TPU v7x, 1024 devices: a whole 4x8x16 slice. The times are simulated.
1024 devices in a mesh: lat: 32 (over y_hi, z), lon: 32 (over x, y_lo, core).
Axes of the slice: x: 4, y: 8 (y_hi: 2, y_lo: 4; y = y_hi * 4 + y_lo), z: 16, core: 2. Of those that a mesh axis runs over, the one named last changes fastest.
Arguments:
- vector: bfloat16 [8, 72, 32, 4096], P(None, None, 'lat', 'lon'), may hold values from -6 to 6
- obs_weight: float32 [72, 32, 4096], P(None, 'lat', 'lon'), may hold values from 0.2 to 5
- departures: int32 [4, 32, 32], P(None, 'lat', 'lon'), may hold values from 0 to 2
- weight_index: int32 [4, 32, 32], P(None, 'lat', 'lon'), may hold values from 0 to 15
- interp_table: bfloat16 [16, 160, 128], replicated, may hold values from -0.5 to 0.5
- column_mix: bfloat16 [4, 32, 72, 72], P(None, 'lat'), may hold values from -0.75 to 0.75
Outputs:
- hess_vec: bfloat16 [8, 72, 32, 4096], P(None, None, 'lat', 'lon')
Inputs may be any that keep to these rules, and one draw needn't show every extreme that they name: `departures`: 0 names the row above the reader row, 1 the reader row, 2 the row below. `weight_index`: an entry of the first dimension of interp_table.
All inputs are finite; a program needn't handle non-finite values.
Results may differ from a plain program's by a relative error of at most 0.022.
Values may be sent and summed in bfloat16 or wider, within the bound.
No kernel may reach another device: no remote copies, remote signals or barrier semaphores. Data moves between devices by JAX's collectives and lax.ppermute only.
A program may use at most 32 MiB of HBM per device.

v0:
```python
import jax
import jax.numpy as jnp
from jax import lax
from jax.sharding import PartitionSpec as P


def with_halo(x, sides, width, wrap):
    for axis, dim in sides:
        size, length = (lax.axis_size(axis), x.shape[dim])
        up = [(i, (i + 1) % size) for i in range(size if wrap else size - 1)]
        down = [(j, i) for i, j in up]
        last = lax.slice_in_dim(x, length - width, length, axis=dim)
        initial = lax.slice_in_dim(x, 0, width, axis=dim)
        before = lax.ppermute(last, axis, up)
        after = lax.ppermute(initial, axis, down)
        x = jnp.concatenate([before, x, after], axis=dim)
    return x


def shifted(x, axis, by):
    length = lax.axis_size(axis)
    pairs = [(i, i + by) for i in range(length) if 0 <= i + by < length]
    return lax.ppermute(x, axis, pairs)


def from_behind(value, axis, steps):
    count = lax.axis_size(axis)
    pairs = [(source, (source + steps) % count) for source in range(count)]
    return lax.ppermute(value, axis, pairs)


def widen_lat(tracer_field):
    return with_halo(tracer_field, (("lat", 2),), 1, False)


def widen_lon(tracer_field, lon_reach):
    return with_halo(tracer_field, (("lon", 3),), lon_reach, True)


def fold_lat(lifted):
    middle = lifted[:, :, 1:-1, :]
    last_row = middle.shape[2] - 1
    for shift_by in (-1, 1):
        outgoing = lifted[:, :, 0:1, :] if shift_by < 0 else lifted[:, :, -1:, :]
        received = shifted(outgoing.astype(jnp.bfloat16), "lat", shift_by).astype(outgoing.dtype)
        target_row = last_row if shift_by < 0 else 0
        middle = middle.at[:, :, target_row : target_row + 1, :].add(received)
    return middle


def fold_lon(lifted, lon_reach):
    middle = lifted[..., lon_reach : lifted.shape[3] - lon_reach]
    block_cols = middle.shape[3]
    for shift_by in (-1, 1):
        outgoing = (
            lifted[..., :lon_reach] if shift_by < 0 else lifted[..., lifted.shape[3] - lon_reach :]
        )
        received = from_behind(outgoing.astype(jnp.bfloat16), "lon", shift_by).astype(
            outgoing.dtype
        )
        first_col = block_cols - lon_reach if shift_by < 0 else 0
        middle = middle.at[..., first_col : first_col + lon_reach].add(received)
    return middle


def advance(tracer_field, offsets, weight_rows, interp_table, mixing, lon_reach):
    widened = widen_lat(widen_lon(tracer_field, lon_reach))
    row_count = tracer_field.shape[2]
    source_rows = jnp.arange(row_count, dtype=jnp.int32) + offsets
    picked = jnp.take(widened, source_rows, axis=2)
    weights = jnp.take(interp_table, weight_rows, axis=0)
    interp = jnp.einsum(
        "tlrj,rjc->tlrc", picked, weights, preferred_element_type=jnp.float32
    ).astype(jnp.bfloat16)
    mixed_cols = jnp.einsum("rkl,tlrc->tkrc", mixing, interp, preferred_element_type=jnp.float32)
    return mixed_cols.astype(jnp.bfloat16)


def retreat(cotangent, offsets, weight_rows, interp_table, mixing, lon_reach):
    back_mixed = jnp.einsum(
        "rkl,tkrc->tlrc", mixing, cotangent, preferred_element_type=jnp.float32
    ).astype(jnp.bfloat16)
    weights = jnp.take(interp_table, weight_rows, axis=0)
    spread = jnp.einsum("tlrc,rjc->tlrj", back_mixed, weights, preferred_element_type=jnp.float32)
    row_count = cotangent.shape[2]
    source_rows = jnp.arange(row_count, dtype=jnp.int32) + offsets
    placing = (jnp.arange(row_count + 2, dtype=jnp.int32)[None, :] == source_rows[:, None]).astype(
        jnp.float32
    )
    lifted = jnp.einsum("tlrj,rp->tlpj", spread, placing, precision=lax.Precision.HIGHEST)
    interior = fold_lat(fold_lon(lifted, lon_reach))
    return interior.astype(jnp.bfloat16)


def on_device(vector, obs_weight, departures, weight_index, interp_table, column_mix):
    lon_reach = (interp_table.shape[1] - interp_table.shape[2]) // 2
    step_count = departures.shape[0]
    tracer_state = vector
    for moment in range(step_count):
        tracer_state = advance(
            tracer_state,
            departures[moment, :, 0],
            weight_index[moment, :, 0],
            interp_table,
            column_mix[moment],
            lon_reach,
        )
    adjoint = (obs_weight[None] * tracer_state.astype(jnp.float32)).astype(jnp.bfloat16)
    for moment in reversed(range(step_count)):
        adjoint = retreat(
            adjoint,
            departures[moment, :, 0],
            weight_index[moment, :, 0],
            interp_table,
            column_mix[moment],
            lon_reach,
        )
    return adjoint


def solution(mesh):
    placed = (
        P(None, None, "lat", "lon"),
        P(None, "lat", "lon"),
        P(None, "lat", "lon"),
        P(None, "lat", "lon"),
        P(),
        P(None, "lat", None, None),
    )
    return jax.shard_map(
        on_device,
        mesh=mesh,
        in_specs=placed,
        out_specs=P(None, None, "lat", "lon"),
        check_vma=False,
    )
```

profile of v0, /device:TPU:57, one launch (start us, length us, event | category | flops | bytes accessed | tf_op | source)
XLA Modules:
  0.0 327.7 jit_solution(3332831295089315369)
XLA Ops:
  1.1 6.0 %collective-permute-start = (bf16[8,72,1,16]{3,1,0,2:T(8,128)(2,1)S(1)}, bf16[8,72,1,16]{3,1,0,2:T(8,128)(2,1)S(1)}, u32[]{:S(2)}, u32[]{:S(2)}) collective-permute-start(bf16[8,72,1,16]{3,1,0,2:T(8,128)(2,1)S(1)} %get-tuple-element.315), channel_id=1, source_target_pairs={{0,1},{1,2},{2,3},{3,4},{4,5},{5,6},{6,7},{7,8},{8,9},{9,10},{10,1... | collective-permute-start | bytes 55304 | tf_op jit(solution)/shard_map/ppermute | solution.py:14
  7.1 1.9 collective-permute-start.1
  10.5 5.8 %collective-permute-done.1 = bf16[8,72,1,16]{3,1,0,2:T(8,128)(2,1)S(1)} collective-permute-done((bf16[8,72,1,16]{3,1,0,2:T(8,128)(2,1)S(1)}, bf16[8,72,1,16]{3,1,0,2:T(8,128)(2,1)S(1)}, u32[]{:S(2)}, u32[]{:S(2)}) %collective-permute-start.1) | collective-permute-done | bytes 18464 | tf_op jit(solution)/shard_map/ppermute | solution.py:15
  17.4 17.5 %collective-permute-start.3 = (bf16[8,72,1,160]{3,1,0,2:T(8,128)(2,1)S(1)}, bf16[8,72,1,160]{3,1,0,2:T(8,128)(2,1)S(1)}, u32[]{:S(2)}, u32[]{:S(2)}) collective-permute-start(bf16[8,72,1,160]{3,1,0,2:T(8,128)(2,1)S(1)} %pad_maximum_fusion), channel_id=1, source_target_pairs={{32,0},{64,32},{96,64},{128,96},{160,128},{192,160},{224,192},{256... | collective-permute-start | bytes 552968 | tf_op jit(solution)/shard_map/ppermute | solution.py:15
  34.9 1.9 collective-permute-start.2
  43.7 9.9 %collective-permute-done.2 = bf16[8,72,1,160]{3,1,0,2:T(8,128)(2,1)S(1)} collective-permute-done((bf16[8,72,1,160]{3,1,0,2:T(8,128)(2,1)S(1)}, bf16[8,72,1,160]{3,1,0,2:T(8,128)(2,1)S(1)}, u32[]{:S(2)}, u32[]{:S(2)}) %collective-permute-start.2) | collective-permute-done | bytes 184352 | tf_op jit(solution)/shard_map/ppermute | solution.py:14
  55.1 5.0 %collective-permute-start.4 = (bf16[8,72,1,16]{3,1,0,2:T(8,128)(2,1)S(1)}, bf16[8,72,1,16]{3,1,0,2:T(8,128)(2,1)S(1)}, u32[]{:S(2)}, u32[]{:S(2)}) collective-permute-start(bf16[8,72,1,16]{3,1,0,2:T(8,128)(2,1)S(1)} %get-tuple-element.313), channel_id=1, source_target_pairs={{0,1},{1,2},{2,3},{3,4},{4,5},{5,6},{6,7},{7,8},{8,9},{9,10},{10,1... | collective-permute-start | bytes 55304 | tf_op jit(solution)/shard_map/ppermute | solution.py:14
  60.1 1.9 collective-permute-start.5
  63.6 5.7 %collective-permute-done.5 = bf16[8,72,1,16]{3,1,0,2:T(8,128)(2,1)S(1)} collective-permute-done((bf16[8,72,1,16]{3,1,0,2:T(8,128)(2,1)S(1)}, bf16[8,72,1,16]{3,1,0,2:T(8,128)(2,1)S(1)}, u32[]{:S(2)}, u32[]{:S(2)}) %collective-permute-start.5) | collective-permute-done | bytes 18464 | tf_op jit(solution)/shard_map/ppermute | solution.py:15
  69.5 1.9 collective-permute-start.7
  71.4 3.4 %collective-permute-start.6 = (bf16[8,72,1,160]{3,1,0,2:T(8,128)(2,1)S(1)}, bf16[8,72,1,160]{3,1,0,2:T(8,128)(2,1)S(1)}, u32[]{:S(2)}, u32[]{:S(2)}) collective-permute-start(bf16[8,72,1,160]{3,1,0,2:T(8,128)(2,1)S(1)} %pad_maximum_fusion.1), channel_id=1, source_target_pairs={{0,32},{32,64},{64,96},{96,128},{128,160},{160,192},{192,224},{224... | collective-permute-start | bytes 552968 | tf_op jit(solution)/shard_map/ppermute | solution.py:14
  78.6 10.8 %collective-permute-done.6 = bf16[8,72,1,160]{3,1,0,2:T(8,128)(2,1)S(1)} collective-permute-done((bf16[8,72,1,160]{3,1,0,2:T(8,128)(2,1)S(1)}, bf16[8,72,1,160]{3,1,0,2:T(8,128)(2,1)S(1)}, u32[]{:S(2)}, u32[]{:S(2)}) %collective-permute-start.6) | collective-permute-done | bytes 184352 | tf_op jit(solution)/shard_map/ppermute | solution.py:14
  90.9 4.7 %collective-permute-start.8 = (bf16[8,72,1,16]{3,1,0,2:T(8,128)(2,1)S(1)}, bf16[8,72,1,16]{3,1,0,2:T(8,128)(2,1)S(1)}, u32[]{:S(2)}, u32[]{:S(2)}) collective-permute-start(bf16[8,72,1,16]{3,1,0,2:T(8,128)(2,1)S(1)} %get-tuple-element.311), channel_id=1, source_target_pairs={{0,1},{1,2},{2,3},{3,4},{4,5},{5,6},{6,7},{7,8},{8,9},{9,10},{10,1... | collective-permute-start | bytes 55304 | tf_op jit(solution)/shard_map/ppermute | solution.py:14
  95.6 1.9 collective-permute-start.9
  99.1 5.6 %collective-permute-done.9 = bf16[8,72,1,16]{3,1,0,2:T(8,128)(2,1)S(1)} collective-permute-done((bf16[8,72,1,16]{3,1,0,2:T(8,128)(2,1)S(1)}, bf16[8,72,1,16]{3,1,0,2:T(8,128)(2,1)S(1)}, u32[]{:S(2)}, u32[]{:S(2)}) %collective-permute-start.9) | collective-permute-done | bytes 18464 | tf_op jit(solution)/shard_map/ppermute | solution.py:15
  106.9 3.4 %collective-permute-start.10 = (bf16[8,72,1,160]{3,1,0,2:T(8,128)(2,1)S(1)}, bf16[8,72,1,160]{3,1,0,2:T(8,128)(2,1)S(1)}, u32[]{:S(2)}, u32[]{:S(2)}) collective-permute-start(bf16[8,72,1,160]{3,1,0,2:T(8,128)(2,1)S(1)} %pad_maximum_fusion.2), channel_id=1, source_target_pairs={{0,32},{32,64},{64,96},{96,128},{128,160},{160,192},{192,224},{224... | collective-permute-start | bytes 552968 | tf_op jit(solution)/shard_map/ppermute | solution.py:14
  114.1 11.2 %collective-permute-done.10 = bf16[8,72,1,160]{3,1,0,2:T(8,128)(2,1)S(1)} collective-permute-done((bf16[8,72,1,160]{3,1,0,2:T(8,128)(2,1)S(1)}, bf16[8,72,1,160]{3,1,0,2:T(8,128)(2,1)S(1)}, u32[]{:S(2)}, u32[]{:S(2)}) %collective-permute-start.10) | collective-permute-done | bytes 184352 | tf_op jit(solution)/shard_map/ppermute | solution.py:14
  126.8 3.2 collective-permute-start.12
  130.1 1.9 collective-permute-start.13
  132.4 6.8 %collective-permute-done.13 = bf16[8,72,1,16]{3,1,0,2:T(8,128)(2,1)S(1)} collective-permute-done((bf16[8,72,1,16]{3,1,0,2:T(8,128)(2,1)S(1)}, bf16[8,72,1,16]{3,1,0,2:T(8,128)(2,1)S(1)}, u32[]{:S(2)}, u32[]{:S(2)}) %collective-permute-start.13) | collective-permute-done | bytes 18464 | tf_op jit(solution)/shard_map/ppermute | solution.py:15
  139.4 1.9 collective-permute-start.15
  141.4 3.4 %collective-permute-start.14 = (bf16[8,72,1,160]{3,1,0,2:T(8,128)(2,1)S(1)}, bf16[8,72,1,160]{3,1,0,2:T(8,128)(2,1)S(1)}, u32[]{:S(2)}, u32[]{:S(2)}) collective-permute-start(bf16[8,72,1,160]{3,1,0,2:T(8,128)(2,1)S(1)} %pad_maximum_fusion.3), channel_id=1, source_target_pairs={{0,32},{32,64},{64,96},{96,128},{128,160},{160,192},{192,224},{224... | collective-permute-start | bytes 552968 | tf_op jit(solution)/shard_map/ppermute | solution.py:14
  149.1 10.5 %collective-permute-done.14 = bf16[8,72,1,160]{3,1,0,2:T(8,128)(2,1)S(1)} collective-permute-done((bf16[8,72,1,160]{3,1,0,2:T(8,128)(2,1)S(1)}, bf16[8,72,1,160]{3,1,0,2:T(8,128)(2,1)S(1)}, u32[]{:S(2)}, u32[]{:S(2)}) %collective-permute-start.14) | collective-permute-done | bytes 184352 | tf_op jit(solution)/shard_map/ppermute | solution.py:14
  164.6 6.3 %collective-permute-start.17 = (bf16[8,72,3,16]{3,1,0,2:T(8,128)(2,1)S(1)}, bf16[8,72,3,16]{3,1,0,2:T(8,128)(2,1)S(1)}, u32[]{:S(2)}, u32[]{:S(2)}) collective-permute-start(bf16[8,72,3,16]{3,1,0,2:T(8,128)(2,1)S(1)} %get-tuple-element.291), channel_id=1, source_target_pairs={{0,1},{1,2},{2,3},{3,4},{4,5},{5,6},{6,7},{7,8},{8,9},{9,10},{10,1... | collective-permute-start | bytes 165896 | tf_op jit(solution)/shard_map/ppermute | solution.py:29
  171.2 5.6 %collective-permute-done.16 = bf16[8,72,3,16]{3,1,0,2:T(8,128)(2,1)S(1)} collective-permute-done((bf16[8,72,3,16]{3,1,0,2:T(8,128)(2,1)S(1)}, bf16[8,72,3,16]{3,1,0,2:T(8,128)(2,1)S(1)}, u32[]{:S(2)}, u32[]{:S(2)}) %collective-permute-start.16) | collective-permute-done | bytes 55328 | tf_op jit(solution)/shard_map/ppermute | solution.py:29
  176.9 5.5 %scatter-add.26 = f32[8,72,3,128]{3,1,0,2:T(8,128)S(1)} dynamic-update-slice(f32[8,72,3,128]{3,1,0,2:T(8,128)S(1)} %slice.668, f32[8,72,3,16]{3,1,0,2:T(8,128)S(1)} %slice_add_fusion.7, s32[]{:T(128)} %constant.447.clone.1, s32[]{:T(128)} %constant.447.clone.1, s32[]{:T(128)} %constant.447.clone.1, s32[]{:T(128)} %constant.448.clone.1) | dynamic-update-slice | bytes 221188 | tf_op jit(solution)/shard_map/scatter-add | solution.py:62
  184.2 1.9 collective-permute-start.18
  186.2 3.4 %collective-permute-start.19 = (bf16[8,72,1,128]{3,1,0,2:T(8,128)(2,1)S(1)}, bf16[8,72,1,128]{3,1,0,2:T(8,128)(2,1)S(1)}, u32[]{:S(2)}, u32[]{:S(2)}) collective-permute-start(bf16[8,72,1,128]{3,1,0,2:T(8,128)(2,1)S(1)} %get-tuple-element.308), channel_id=1, source_target_pairs={{0,32},{32,64},{64,96},{96,128},{128,160},{160,192},{192,224},{224... | collective-permute-start | bytes 442376 | tf_op jit(solution)/shard_map/ppermute | solution.py:23
  190.2 8.1 %collective-permute-done.19 = bf16[8,72,1,128]{3,1,0,2:T(8,128)(2,1)S(1)} collective-permute-done((bf16[8,72,1,128]{3,1,0,2:T(8,128)(2,1)S(1)}, bf16[8,72,1,128]{3,1,0,2:T(8,128)(2,1)S(1)}, u32[]{:S(2)}, u32[]{:S(2)}) %collective-permute-start.19) | collective-permute-done | bytes 147488 | tf_op jit(solution)/shard_map/ppermute | solution.py:23
  201.9 6.3 %collective-permute-start.21 = (bf16[8,72,3,16]{3,1,0,2:T(8,128)(2,1)S(1)}, bf16[8,72,3,16]{3,1,0,2:T(8,128)(2,1)S(1)}, u32[]{:S(2)}, u32[]{:S(2)}) collective-permute-start(bf16[8,72,3,16]{3,1,0,2:T(8,128)(2,1)S(1)} %get-tuple-element.289), channel_id=1, source_target_pairs={{0,1},{1,2},{2,3},{3,4},{4,5},{5,6},{6,7},{7,8},{8,9},{9,10},{10,1... | collective-permute-start | bytes 165896 | tf_op jit(solution)/shard_map/ppermute | solution.py:29
  208.5 8.3 %collective-permute-done.20 = bf16[8,72,3,16]{3,1,0,2:T(8,128)(2,1)S(1)} collective-permute-done((bf16[8,72,3,16]{3,1,0,2:T(8,128)(2,1)S(1)}, bf16[8,72,3,16]{3,1,0,2:T(8,128)(2,1)S(1)}, u32[]{:S(2)}, u32[]{:S(2)}) %collective-permute-start.20) | collective-permute-done | bytes 55328 | tf_op jit(solution)/shard_map/ppermute | solution.py:29
  216.9 5.5 %scatter-add.30 = f32[8,72,3,128]{3,1,0,2:T(8,128)S(1)} dynamic-update-slice(f32[8,72,3,128]{3,1,0,2:T(8,128)S(1)} %slice.676, f32[8,72,3,16]{3,1,0,2:T(8,128)S(1)} %slice_add_fusion.5, s32[]{:T(128)} %constant.447.clone.1, s32[]{:T(128)} %constant.447.clone.1, s32[]{:T(128)} %constant.447.clone.1, s32[]{:T(128)} %constant.448.clone.1) | dynamic-update-slice | bytes 221188 | tf_op jit(solution)/shard_map/scatter-add | solution.py:62
  224.2 1.9 collective-permute-start.22
  226.2 3.5 %collective-permute-start.23 = (bf16[8,72,1,128]{3,1,0,2:T(8,128)(2,1)S(1)}, bf16[8,72,1,128]{3,1,0,2:T(8,128)(2,1)S(1)}, u32[]{:S(2)}, u32[]{:S(2)}) collective-permute-start(bf16[8,72,1,128]{3,1,0,2:T(8,128)(2,1)S(1)} %get-tuple-element.306), channel_id=1, source_target_pairs={{0,32},{32,64},{64,96},{96,128},{128,160},{160,192},{192,224},{224... | collective-permute-start | bytes 442376 | tf_op jit(solution)/shard_map/ppermute | solution.py:23
  230.4 7.8 %collective-permute-done.23 = bf16[8,72,1,128]{3,1,0,2:T(8,128)(2,1)S(1)} collective-permute-done((bf16[8,72,1,128]{3,1,0,2:T(8,128)(2,1)S(1)}, bf16[8,72,1,128]{3,1,0,2:T(8,128)(2,1)S(1)}, u32[]{:S(2)}, u32[]{:S(2)}) %collective-permute-start.23) | collective-permute-done | bytes 147488 | tf_op jit(solution)/shard_map/ppermute | solution.py:23
  241.8 6.3 %collective-permute-start.25 = (bf16[8,72,3,16]{3,1,0,2:T(8,128)(2,1)S(1)}, bf16[8,72,3,16]{3,1,0,2:T(8,128)(2,1)S(1)}, u32[]{:S(2)}, u32[]{:S(2)}) collective-permute-start(bf16[8,72,3,16]{3,1,0,2:T(8,128)(2,1)S(1)} %get-tuple-element.287), channel_id=1, source_target_pairs={{0,1},{1,2},{2,3},{3,4},{4,5},{5,6},{6,7},{7,8},{8,9},{9,10},{10,1... | collective-permute-start | bytes 165896 | tf_op jit(solution)/shard_map/ppermute | solution.py:29
  248.5 6.8 %collective-permute-done.24 = bf16[8,72,3,16]{3,1,0,2:T(8,128)(2,1)S(1)} collective-permute-done((bf16[8,72,3,16]{3,1,0,2:T(8,128)(2,1)S(1)}, bf16[8,72,3,16]{3,1,0,2:T(8,128)(2,1)S(1)}, u32[]{:S(2)}, u32[]{:S(2)}) %collective-permute-start.24) | collective-permute-done | bytes 55328 | tf_op jit(solution)/shard_map/ppermute | solution.py:29
  255.4 5.5 %scatter-add.34 = f32[8,72,3,128]{3,1,0,2:T(8,128)S(1)} dynamic-update-slice(f32[8,72,3,128]{3,1,0,2:T(8,128)S(1)} %slice.684, f32[8,72,3,16]{3,1,0,2:T(8,128)S(1)} %slice_add_fusion.3, s32[]{:T(128)} %constant.447.clone.1, s32[]{:T(128)} %constant.447.clone.1, s32[]{:T(128)} %constant.447.clone.1, s32[]{:T(128)} %constant.448.clone.1) | dynamic-update-slice | bytes 221188 | tf_op jit(solution)/shard_map/scatter-add | solution.py:62
  262.7 1.9 collective-permute-start.26
  264.6 3.4 %collective-permute-start.27 = (bf16[8,72,1,128]{3,1,0,2:T(8,128)(2,1)S(1)}, bf16[8,72,1,128]{3,1,0,2:T(8,128)(2,1)S(1)}, u32[]{:S(2)}, u32[]{:S(2)}) collective-permute-start(bf16[8,72,1,128]{3,1,0,2:T(8,128)(2,1)S(1)} %get-tuple-element.304), channel_id=1, source_target_pairs={{0,32},{32,64},{64,96},{96,128},{128,160},{160,192},{192,224},{224... | collective-permute-start | bytes 442376 | tf_op jit(solution)/shard_map/ppermute | solution.py:23
  268.7 7.9 %collective-permute-done.27 = bf16[8,72,1,128]{3,1,0,2:T(8,128)(2,1)S(1)} collective-permute-done((bf16[8,72,1,128]{3,1,0,2:T(8,128)(2,1)S(1)}, bf16[8,72,1,128]{3,1,0,2:T(8,128)(2,1)S(1)}, u32[]{:S(2)}, u32[]{:S(2)}) %collective-permute-start.27) | collective-permute-done | bytes 147488 | tf_op jit(solution)/shard_map/ppermute | solution.py:23
  280.1 6.3 %collective-permute-start.29 = (bf16[8,72,3,16]{3,1,2,0:T(8,128)(2,1)S(1)}, bf16[8,72,3,16]{3,1,2,0:T(8,128)(2,1)S(1)}, u32[]{:S(2)}, u32[]{:S(2)}) collective-permute-start(bf16[8,72,3,16]{3,1,2,0:T(8,128)(2,1)S(1)} %get-tuple-element.285), channel_id=1, source_target_pairs={{0,1},{1,2},{2,3},{3,4},{4,5},{5,6},{6,7},{7,8},{8,9},{9,10},{10,1... | collective-permute-start | bytes 165896 | tf_op jit(solution)/shard_map/ppermute | solution.py:29
  286.8 6.8 %collective-permute-done.28 = bf16[8,72,3,16]{3,1,2,0:T(8,128)(2,1)S(1)} collective-permute-done((bf16[8,72,3,16]{3,1,2,0:T(8,128)(2,1)S(1)}, bf16[8,72,3,16]{3,1,2,0:T(8,128)(2,1)S(1)}, u32[]{:S(2)}, u32[]{:S(2)}) %collective-permute-start.28) | collective-permute-done | bytes 55328 | tf_op jit(solution)/shard_map/ppermute | solution.py:29
  293.7 11.6 %scatter-add.36 = f32[8,72,3,128]{3,1,2,0:T(8,128)S(1)} dynamic-update-slice(f32[8,72,3,128]{3,1,2,0:T(8,128)S(1)} %slice.692, f32[8,72,3,16]{3,1,2,0:T(8,128)S(1)} %slice_add_fusion.1, s32[]{:T(128)} %constant.447.clone.1, s32[]{:T(128)} %constant.447.clone.1, s32[]{:T(128)} %constant.447.clone.1, s32[]{:T(128)} %constant.448.clone.1) | dynamic-update-slice | bytes 221188 | tf_op jit(solution)/shard_map/scatter-add | solution.py:62
  305.3 7.7 %scatter-add.39 = f32[8,72,3,128]{3,1,2,0:T(8,128)S(1)} dynamic-update-slice(f32[8,72,3,128]{3,1,2,0:T(8,128)S(1)} %scatter-add.36, f32[8,72,3,16]{3,1,2,0:T(8,128)S(1)} %slice_add_fusion, s32[]{:T(128)} %constant.447.clone.1, s32[]{:T(128)} %constant.447.clone.1, s32[]{:T(128)} %constant.447.clone.1, s32[]{:T(128)} %constant.447.clone.1) | dynamic-update-slice | bytes 221188 | tf_op jit(solution)/shard_map/scatter-add | solution.py:62
  313.1 1.9 collective-permute-start.30
  315.1 3.4 %collective-permute-start.31 = (bf16[8,72,1,128]{3,1,2,0:T(8,128)(2,1)S(1)}, bf16[8,72,1,128]{3,1,2,0:T(8,128)(2,1)S(1)}, u32[]{:S(2)}, u32[]{:S(2)}) collective-permute-start(bf16[8,72,1,128]{3,1,2,0:T(8,128)(2,1)S(1)} %get-tuple-element.302), channel_id=1, source_target_pairs={{0,32},{32,64},{64,96},{96,128},{128,160},{160,192},{192,224},{224... | collective-permute-start | bytes 442376 | tf_op jit(solution)/shard_map/ppermute | solution.py:23
  319.0 7.9 %collective-permute-done.31 = bf16[8,72,1,128]{3,1,2,0:T(8,128)(2,1)S(1)} collective-permute-done((bf16[8,72,1,128]{3,1,2,0:T(8,128)(2,1)S(1)}, bf16[8,72,1,128]{3,1,2,0:T(8,128)(2,1)S(1)}, u32[]{:S(2)}, u32[]{:S(2)}) %collective-permute-start.31) | collective-permute-done | bytes 147488 | tf_op jit(solution)/shard_map/ppermute | solution.py:23
  (79 shorter events, 43.8 us)
Async XLA Ops:
  1.1 9.4 %collective-permute-start = (bf16[8,72,1,16]{3,1,0,2:T(8,128)(2,1)S(1)}, bf16[8,72,1,16]{3,1,0,2:T(8,128)(2,1)S(1)}, u32[]{:S(2)}, u32[]{:S(2)}) collective-permute-start(bf16[8,72,1,16]{3,1,0,2:T(8,128)(2,1)S(1)} %get-tuple-element.315), channel_id=1, source_target_pairs={{0,1},{1,2},{2,3},{3,4},{4,5},{5,6},{6,7},{7,8},{8,9},{9,10},{10,1... | collective-permute-start | bytes 55304 | tf_op jit(solution)/shard_map/ppermute | solution.py:14
  7.1 9.2 %collective-permute-start.1 = (bf16[8,72,1,16]{3,1,0,2:T(8,128)(2,1)S(1)}, bf16[8,72,1,16]{3,1,0,2:T(8,128)(2,1)S(1)}, u32[]{:S(2)}, u32[]{:S(2)}) collective-permute-start(bf16[8,72,1,16]{3,1,0,2:T(8,128)(2,1)S(1)} %get-tuple-element.316), channel_id=1, source_target_pairs={{1,0},{2,1},{3,2},{4,3},{5,4},{6,5},{7,6},{8,7},{9,8},{10,9},{11,1... | collective-permute-start | bytes 55304 | tf_op jit(solution)/shard_map/ppermute | solution.py:15
  17.4 26.3 %collective-permute-start.3 = (bf16[8,72,1,160]{3,1,0,2:T(8,128)(2,1)S(1)}, bf16[8,72,1,160]{3,1,0,2:T(8,128)(2,1)S(1)}, u32[]{:S(2)}, u32[]{:S(2)}) collective-permute-start(bf16[8,72,1,160]{3,1,0,2:T(8,128)(2,1)S(1)} %pad_maximum_fusion), channel_id=1, source_target_pairs={{32,0},{64,32},{96,64},{128,96},{160,128},{192,160},{224,192},{256... | collective-permute-start | bytes 552968 | tf_op jit(solution)/shard_map/ppermute | solution.py:15
  34.9 18.7 %collective-permute-start.2 = (bf16[8,72,1,160]{3,1,0,2:T(8,128)(2,1)S(1)}, bf16[8,72,1,160]{3,1,0,2:T(8,128)(2,1)S(1)}, u32[]{:S(2)}, u32[]{:S(2)}) collective-permute-start(bf16[8,72,1,160]{3,1,0,2:T(8,128)(2,1)S(1)} %pad_maximum_fusion), channel_id=1, source_target_pairs={{0,32},{32,64},{64,96},{96,128},{128,160},{160,192},{192,224},{224... | collective-permute-start | bytes 552968 | tf_op jit(solution)/shard_map/ppermute | solution.py:14
  53.6 35.8 %copy-start = (bf16[4,1,72,72]{3,2,1,0:T(8,128)(2,1)S(1)}, bf16[4,1,72,72]{3,2,1,0:T(8,128)(2,1)}, u32[]{:S(2)}) copy-start(bf16[4,1,72,72]{3,2,1,0:T(8,128)(2,1)} %param.63) | copy-start | bytes 124420
  55.1 8.5 %collective-permute-start.4 = (bf16[8,72,1,16]{3,1,0,2:T(8,128)(2,1)S(1)}, bf16[8,72,1,16]{3,1,0,2:T(8,128)(2,1)S(1)}, u32[]{:S(2)}, u32[]{:S(2)}) collective-permute-start(bf16[8,72,1,16]{3,1,0,2:T(8,128)(2,1)S(1)} %get-tuple-element.313), channel_id=1, source_target_pairs={{0,1},{1,2},{2,3},{3,4},{4,5},{5,6},{6,7},{7,8},{8,9},{9,10},{10,1... | collective-permute-start | bytes 55304 | tf_op jit(solution)/shard_map/ppermute | solution.py:14
  60.1 9.2 %collective-permute-start.5 = (bf16[8,72,1,16]{3,1,0,2:T(8,128)(2,1)S(1)}, bf16[8,72,1,16]{3,1,0,2:T(8,128)(2,1)S(1)}, u32[]{:S(2)}, u32[]{:S(2)}) collective-permute-start(bf16[8,72,1,16]{3,1,0,2:T(8,128)(2,1)S(1)} %get-tuple-element.314), channel_id=1, source_target_pairs={{1,0},{2,1},{3,2},{4,3},{5,4},{6,5},{7,6},{8,7},{9,8},{10,9},{11,1... | collective-permute-start | bytes 55304 | tf_op jit(solution)/shard_map/ppermute | solution.py:15
  69.5 9.1 %collective-permute-start.7 = (bf16[8,72,1,160]{3,1,0,2:T(8,128)(2,1)S(1)}, bf16[8,72,1,160]{3,1,0,2:T(8,128)(2,1)S(1)}, u32[]{:S(2)}, u32[]{:S(2)}) collective-permute-start(bf16[8,72,1,160]{3,1,0,2:T(8,128)(2,1)S(1)} %pad_maximum_fusion.1), channel_id=1, source_target_pairs={{32,0},{64,32},{96,64},{128,96},{160,128},{192,160},{224,192},{256... | collective-permute-start | bytes 552968 | tf_op jit(solution)/shard_map/ppermute | solution.py:15
  71.4 17.9 %collective-permute-start.6 = (bf16[8,72,1,160]{3,1,0,2:T(8,128)(2,1)S(1)}, bf16[8,72,1,160]{3,1,0,2:T(8,128)(2,1)S(1)}, u32[]{:S(2)}, u32[]{:S(2)}) collective-permute-start(bf16[8,72,1,160]{3,1,0,2:T(8,128)(2,1)S(1)} %pad_maximum_fusion.1), channel_id=1, source_target_pairs={{0,32},{32,64},{64,96},{96,128},{128,160},{160,192},{192,224},{224... | collective-permute-start | bytes 552968 | tf_op jit(solution)/shard_map/ppermute | solution.py:14
  90.9 8.2 %collective-permute-start.8 = (bf16[8,72,1,16]{3,1,0,2:T(8,128)(2,1)S(1)}, bf16[8,72,1,16]{3,1,0,2:T(8,128)(2,1)S(1)}, u32[]{:S(2)}, u32[]{:S(2)}) collective-permute-start(bf16[8,72,1,16]{3,1,0,2:T(8,128)(2,1)S(1)} %get-tuple-element.311), channel_id=1, source_target_pairs={{0,1},{1,2},{2,3},{3,4},{4,5},{5,6},{6,7},{7,8},{8,9},{9,10},{10,1... | collective-permute-start | bytes 55304 | tf_op jit(solution)/shard_map/ppermute | solution.py:14
  95.6 9.2 %collective-permute-start.9 = (bf16[8,72,1,16]{3,1,0,2:T(8,128)(2,1)S(1)}, bf16[8,72,1,16]{3,1,0,2:T(8,128)(2,1)S(1)}, u32[]{:S(2)}, u32[]{:S(2)}) collective-permute-start(bf16[8,72,1,16]{3,1,0,2:T(8,128)(2,1)S(1)} %get-tuple-element.312), channel_id=1, source_target_pairs={{1,0},{2,1},{3,2},{4,3},{5,4},{6,5},{7,6},{8,7},{9,8},{10,9},{11,1... | collective-permute-start | bytes 55304 | tf_op jit(solution)/shard_map/ppermute | solution.py:15
  104.9 9.2 %collective-permute-start.11 = (bf16[8,72,1,160]{3,1,0,2:T(8,128)(2,1)S(1)}, bf16[8,72,1,160]{3,1,0,2:T(8,128)(2,1)S(1)}, u32[]{:S(2)}, u32[]{:S(2)}) collective-permute-start(bf16[8,72,1,160]{3,1,0,2:T(8,128)(2,1)S(1)} %pad_maximum_fusion.2), channel_id=1, source_target_pairs={{32,0},{64,32},{96,64},{128,96},{160,128},{192,160},{224,192},{256... | collective-permute-start | bytes 552968 | tf_op jit(solution)/shard_map/ppermute | solution.py:15
  106.9 18.4 %collective-permute-start.10 = (bf16[8,72,1,160]{3,1,0,2:T(8,128)(2,1)S(1)}, bf16[8,72,1,160]{3,1,0,2:T(8,128)(2,1)S(1)}, u32[]{:S(2)}, u32[]{:S(2)}) collective-permute-start(bf16[8,72,1,160]{3,1,0,2:T(8,128)(2,1)S(1)} %pad_maximum_fusion.2), channel_id=1, source_target_pairs={{0,32},{32,64},{64,96},{96,128},{128,160},{160,192},{192,224},{224... | collective-permute-start | bytes 552968 | tf_op jit(solution)/shard_map/ppermute | solution.py:14
  125.3 34.3 %copy-start.1 = (f32[72,1,128]{2,1,0:T(1,128)S(1)}, f32[72,1,128]{2,1,0:T(1,128)}, u32[]{:S(2)}) copy-start(f32[72,1,128]{2,1,0:T(1,128)} %param.59) | copy-start | bytes 110596
  126.8 5.6 %collective-permute-start.12 = (bf16[8,72,1,16]{3,1,0,2:T(8,128)(2,1)S(1)}, bf16[8,72,1,16]{3,1,0,2:T(8,128)(2,1)S(1)}, u32[]{:S(2)}, u32[]{:S(2)}) collective-permute-start(bf16[8,72,1,16]{3,1,0,2:T(8,128)(2,1)S(1)} %get-tuple-element.309), channel_id=1, source_target_pairs={{0,1},{1,2},{2,3},{3,4},{4,5},{5,6},{6,7},{7,8},{8,9},{9,10},{10,1... | collective-permute-start | bytes 55304 | tf_op jit(solution)/shard_map/ppermute | solution.py:14
  130.1 9.2 %collective-permute-start.13 = (bf16[8,72,1,16]{3,1,0,2:T(8,128)(2,1)S(1)}, bf16[8,72,1,16]{3,1,0,2:T(8,128)(2,1)S(1)}, u32[]{:S(2)}, u32[]{:S(2)}) collective-permute-start(bf16[8,72,1,16]{3,1,0,2:T(8,128)(2,1)S(1)} %get-tuple-element.310), channel_id=1, source_target_pairs={{1,0},{2,1},{3,2},{4,3},{5,4},{6,5},{7,6},{8,7},{9,8},{10,9},{11,1... | collective-permute-start | bytes 55304 | tf_op jit(solution)/shard_map/ppermute | solution.py:15
  139.4 9.7 %collective-permute-start.15 = (bf16[8,72,1,160]{3,1,0,2:T(8,128)(2,1)S(1)}, bf16[8,72,1,160]{3,1,0,2:T(8,128)(2,1)S(1)}, u32[]{:S(2)}, u32[]{:S(2)}) collective-permute-start(bf16[8,72,1,160]{3,1,0,2:T(8,128)(2,1)S(1)} %pad_maximum_fusion.3), channel_id=1, source_target_pairs={{32,0},{64,32},{96,64},{128,96},{160,128},{192,160},{224,192},{256... | collective-permute-start | bytes 552968 | tf_op jit(solution)/shard_map/ppermute | solution.py:15
  141.4 18.2 %collective-permute-start.14 = (bf16[8,72,1,160]{3,1,0,2:T(8,128)(2,1)S(1)}, bf16[8,72,1,160]{3,1,0,2:T(8,128)(2,1)S(1)}, u32[]{:S(2)}, u32[]{:S(2)}) collective-permute-start(bf16[8,72,1,160]{3,1,0,2:T(8,128)(2,1)S(1)} %pad_maximum_fusion.3), channel_id=1, source_target_pairs={{0,32},{32,64},{64,96},{96,128},{128,160},{160,192},{192,224},{224... | collective-permute-start | bytes 552968 | tf_op jit(solution)/shard_map/ppermute | solution.py:14
  162.7 14.1 %collective-permute-start.16 = (bf16[8,72,3,16]{3,1,0,2:T(8,128)(2,1)S(1)}, bf16[8,72,3,16]{3,1,0,2:T(8,128)(2,1)S(1)}, u32[]{:S(2)}, u32[]{:S(2)}) collective-permute-start(bf16[8,72,3,16]{3,1,0,2:T(8,128)(2,1)S(1)} %get-tuple-element.292), channel_id=1, source_target_pairs={{0,31},{1,0},{2,1},{3,2},{4,3},{5,4},{6,5},{7,6},{8,7},{9,8},{10,9... | collective-permute-start | bytes 165896 | tf_op jit(solution)/shard_map/ppermute | solution.py:29
  164.6 17.8 %collective-permute-start.17 = (bf16[8,72,3,16]{3,1,0,2:T(8,128)(2,1)S(1)}, bf16[8,72,3,16]{3,1,0,2:T(8,128)(2,1)S(1)}, u32[]{:S(2)}, u32[]{:S(2)}) collective-permute-start(bf16[8,72,3,16]{3,1,0,2:T(8,128)(2,1)S(1)} %get-tuple-element.291), channel_id=1, source_target_pairs={{0,1},{1,2},{2,3},{3,4},{4,5},{5,6},{6,7},{7,8},{8,9},{9,10},{10,1... | collective-permute-start | bytes 165896 | tf_op jit(solution)/shard_map/ppermute | solution.py:29
  184.2 5.9 %collective-permute-start.18 = (bf16[8,72,1,128]{3,1,0,2:T(8,128)(2,1)S(1)}, bf16[8,72,1,128]{3,1,0,2:T(8,128)(2,1)S(1)}, u32[]{:S(2)}, u32[]{:S(2)}) collective-permute-start(bf16[8,72,1,128]{3,1,0,2:T(8,128)(2,1)S(1)} %get-tuple-element.307), channel_id=1, source_target_pairs={{32,0},{64,32},{96,64},{128,96},{160,128},{192,160},{224,192},{256... | collective-permute-start | bytes 442376 | tf_op jit(solution)/shard_map/ppermute | solution.py:23
  186.2 12.1 %collective-permute-start.19 = (bf16[8,72,1,128]{3,1,0,2:T(8,128)(2,1)S(1)}, bf16[8,72,1,128]{3,1,0,2:T(8,128)(2,1)S(1)}, u32[]{:S(2)}, u32[]{:S(2)}) collective-permute-start(bf16[8,72,1,128]{3,1,0,2:T(8,128)(2,1)S(1)} %get-tuple-element.308), channel_id=1, source_target_pairs={{0,32},{32,64},{64,96},{96,128},{128,160},{160,192},{192,224},{224... | collective-permute-start | bytes 442376 | tf_op jit(solution)/shard_map/ppermute | solution.py:23
  200.0 16.8 %collective-permute-start.20 = (bf16[8,72,3,16]{3,1,0,2:T(8,128)(2,1)S(1)}, bf16[8,72,3,16]{3,1,0,2:T(8,128)(2,1)S(1)}, u32[]{:S(2)}, u32[]{:S(2)}) collective-permute-start(bf16[8,72,3,16]{3,1,0,2:T(8,128)(2,1)S(1)} %get-tuple-element.290), channel_id=1, source_target_pairs={{0,31},{1,0},{2,1},{3,2},{4,3},{5,4},{6,5},{7,6},{8,7},{9,8},{10,9... | collective-permute-start | bytes 165896 | tf_op jit(solution)/shard_map/ppermute | solution.py:29
  201.9 20.5 %collective-permute-start.21 = (bf16[8,72,3,16]{3,1,0,2:T(8,128)(2,1)S(1)}, bf16[8,72,3,16]{3,1,0,2:T(8,128)(2,1)S(1)}, u32[]{:S(2)}, u32[]{:S(2)}) collective-permute-start(bf16[8,72,3,16]{3,1,0,2:T(8,128)(2,1)S(1)} %get-tuple-element.289), channel_id=1, source_target_pairs={{0,1},{1,2},{2,3},{3,4},{4,5},{5,6},{6,7},{7,8},{8,9},{9,10},{10,1... | collective-permute-start | bytes 165896 | tf_op jit(solution)/shard_map/ppermute | solution.py:29
  224.2 6.1 %collective-permute-start.22 = (bf16[8,72,1,128]{3,1,0,2:T(8,128)(2,1)S(1)}, bf16[8,72,1,128]{3,1,0,2:T(8,128)(2,1)S(1)}, u32[]{:S(2)}, u32[]{:S(2)}) collective-permute-start(bf16[8,72,1,128]{3,1,0,2:T(8,128)(2,1)S(1)} %get-tuple-element.305), channel_id=1, source_target_pairs={{32,0},{64,32},{96,64},{128,96},{160,128},{192,160},{224,192},{256... | collective-permute-start | bytes 442376 | tf_op jit(solution)/shard_map/ppermute | solution.py:23
  226.2 12.0 %collective-permute-start.23 = (bf16[8,72,1,128]{3,1,0,2:T(8,128)(2,1)S(1)}, bf16[8,72,1,128]{3,1,0,2:T(8,128)(2,1)S(1)}, u32[]{:S(2)}, u32[]{:S(2)}) collective-permute-start(bf16[8,72,1,128]{3,1,0,2:T(8,128)(2,1)S(1)} %get-tuple-element.306), channel_id=1, source_target_pairs={{0,32},{32,64},{64,96},{96,128},{128,160},{160,192},{192,224},{224... | collective-permute-start | bytes 442376 | tf_op jit(solution)/shard_map/ppermute | solution.py:23
  239.9 15.4 %collective-permute-start.24 = (bf16[8,72,3,16]{3,1,0,2:T(8,128)(2,1)S(1)}, bf16[8,72,3,16]{3,1,0,2:T(8,128)(2,1)S(1)}, u32[]{:S(2)}, u32[]{:S(2)}) collective-permute-start(bf16[8,72,3,16]{3,1,0,2:T(8,128)(2,1)S(1)} %get-tuple-element.288), channel_id=1, source_target_pairs={{0,31},{1,0},{2,1},{3,2},{4,3},{5,4},{6,5},{7,6},{8,7},{9,8},{10,9... | collective-permute-start | bytes 165896 | tf_op jit(solution)/shard_map/ppermute | solution.py:29
  241.8 19.1 %collective-permute-start.25 = (bf16[8,72,3,16]{3,1,0,2:T(8,128)(2,1)S(1)}, bf16[8,72,3,16]{3,1,0,2:T(8,128)(2,1)S(1)}, u32[]{:S(2)}, u32[]{:S(2)}) collective-permute-start(bf16[8,72,3,16]{3,1,0,2:T(8,128)(2,1)S(1)} %get-tuple-element.287), channel_id=1, source_target_pairs={{0,1},{1,2},{2,3},{3,4},{4,5},{5,6},{6,7},{7,8},{8,9},{9,10},{10,1... | collective-permute-start | bytes 165896 | tf_op jit(solution)/shard_map/ppermute | solution.py:29
  262.7 6.0 %collective-permute-start.26 = (bf16[8,72,1,128]{3,1,0,2:T(8,128)(2,1)S(1)}, bf16[8,72,1,128]{3,1,0,2:T(8,128)(2,1)S(1)}, u32[]{:S(2)}, u32[]{:S(2)}) collective-permute-start(bf16[8,72,1,128]{3,1,0,2:T(8,128)(2,1)S(1)} %get-tuple-element.303), channel_id=1, source_target_pairs={{32,0},{64,32},{96,64},{128,96},{160,128},{192,160},{224,192},{256... | collective-permute-start | bytes 442376 | tf_op jit(solution)/shard_map/ppermute | solution.py:23
  264.6 11.9 %collective-permute-start.27 = (bf16[8,72,1,128]{3,1,0,2:T(8,128)(2,1)S(1)}, bf16[8,72,1,128]{3,1,0,2:T(8,128)(2,1)S(1)}, u32[]{:S(2)}, u32[]{:S(2)}) collective-permute-start(bf16[8,72,1,128]{3,1,0,2:T(8,128)(2,1)S(1)} %get-tuple-element.304), channel_id=1, source_target_pairs={{0,32},{32,64},{64,96},{96,128},{128,160},{160,192},{192,224},{224... | collective-permute-start | bytes 442376 | tf_op jit(solution)/shard_map/ppermute | solution.py:23
  278.2 15.4 %collective-permute-start.28 = (bf16[8,72,3,16]{3,1,2,0:T(8,128)(2,1)S(1)}, bf16[8,72,3,16]{3,1,2,0:T(8,128)(2,1)S(1)}, u32[]{:S(2)}, u32[]{:S(2)}) collective-permute-start(bf16[8,72,3,16]{3,1,2,0:T(8,128)(2,1)S(1)} %get-tuple-element.286), channel_id=1, source_target_pairs={{0,31},{1,0},{2,1},{3,2},{4,3},{5,4},{6,5},{7,6},{8,7},{9,8},{10,9... | collective-permute-start | bytes 165896 | tf_op jit(solution)/shard_map/ppermute | solution.py:29
  280.1 25.1 %collective-permute-start.29 = (bf16[8,72,3,16]{3,1,2,0:T(8,128)(2,1)S(1)}, bf16[8,72,3,16]{3,1,2,0:T(8,128)(2,1)S(1)}, u32[]{:S(2)}, u32[]{:S(2)}) collective-permute-start(bf16[8,72,3,16]{3,1,2,0:T(8,128)(2,1)S(1)} %get-tuple-element.285), channel_id=1, source_target_pairs={{0,1},{1,2},{2,3},{3,4},{4,5},{5,6},{6,7},{7,8},{8,9},{9,10},{10,1... | collective-permute-start | bytes 165896 | tf_op jit(solution)/shard_map/ppermute | solution.py:29
  313.1 5.9 %collective-permute-start.30 = (bf16[8,72,1,128]{3,1,2,0:T(8,128)(2,1)S(1)}, bf16[8,72,1,128]{3,1,2,0:T(8,128)(2,1)S(1)}, u32[]{:S(2)}, u32[]{:S(2)}) collective-permute-start(bf16[8,72,1,128]{3,1,2,0:T(8,128)(2,1)S(1)} %get-tuple-element.301), channel_id=1, source_target_pairs={{32,0},{64,32},{96,64},{128,96},{160,128},{192,160},{224,192},{256... | collective-permute-start | bytes 442376 | tf_op jit(solution)/shard_map/ppermute | solution.py:23
  315.1 11.9 %collective-permute-start.31 = (bf16[8,72,1,128]{3,1,2,0:T(8,128)(2,1)S(1)}, bf16[8,72,1,128]{3,1,2,0:T(8,128)(2,1)S(1)}, u32[]{:S(2)}, u32[]{:S(2)}) collective-permute-start(bf16[8,72,1,128]{3,1,2,0:T(8,128)(2,1)S(1)} %get-tuple-element.302), channel_id=1, source_target_pairs={{0,32},{32,64},{64,96},{96,128},{128,160},{160,192},{192,224},{224... | collective-permute-start | bytes 442376 | tf_op jit(solution)/shard_map/ppermute | solution.py:23
where the time goes:
time: 329 us; the launch traced here: 328 us
  waiting for transfers between devices  131 us (40%)
  starting transfers between devices  116 us (35%)
  local copies, waits for them, and re-layouts  47 us (14%)
  between operations  16.1 us (5%)
  matrix products  10.4 us (3%)
  other arithmetic  6.95 us (2%)
    ppermute x8, waiting for transfers between devices, with_halo(): before = lax.ppermute(last, axis, up)  47.2 us
    scatter-add x8, local copies, waits for them, and re-layouts, fold_lon(): middle = middle.at[..., first_col:first_col + lon_reach].add(received)  40.6 us
    ppermute x8, starting transfers between devices, from_behind(): return lax.ppermute(value, axis, pairs)  33 us
    ppermute x8, waiting for transfers between devices, shifted(): return lax.ppermute(x, axis, pairs)  32.3 us
    ppermute x8, starting transfers between devices, with_halo(): before = lax.ppermute(last, axis, up)  31 us
    ppermute x8, starting transfers between devices, with_halo(): after = lax.ppermute(initial, axis, down)  30.9 us
    ppermute x8, waiting for transfers between devices, from_behind(): return lax.ppermute(value, axis, pairs)  27.5 us
    ppermute x8, waiting for transfers between devices, with_halo(): after = lax.ppermute(initial, axis, down)  24 us
  transfers between devices with their start and end apart: 32, of which 21 were waited for; matrix products, arithmetic and copies ran while one was open for 11% of the time, Pallas kernels for 0%

commit v1 on v0

v1 whole, which is shorter than its diff:
```python
import functools

import jax
import jax.numpy as jnp
from jax import lax
from jax.experimental import pallas as pl
from jax.experimental.pallas import tpu as pltpu
from jax.sharding import PartitionSpec as P

F32, BF16 = jnp.float32, jnp.bfloat16
VMEM = pl.BlockSpec(memory_space=pltpu.VMEM)
SMEM = pl.BlockSpec(memory_space=pltpu.SMEM)
LIMIT = 24 * 1024 * 1024


def right_lanes(shape):
    return lax.broadcasted_iota(jnp.int32, shape, 1) < shape[1] // 2


def forward_kernel(step, first, outs, fold, weighted, par, own, north, south, table, mix, *rest):
    obs, out = rest if weighted else (None, rest[0])
    shape = own.shape[1:]
    rightward = right_lanes(shape)
    blocks = []
    for p in range(outs):
        way, which = par[step, first + p], par[4 + step, first + p]

        def pick(j):
            return jnp.where(way == 1, own[j], jnp.where(way == 0, north[j], south[j]))

        left = p - 1 if p > 0 else outs
        right = p + 1 if p < outs - 1 else outs
        edges = jnp.where(rightward, pick(right), pick(left))
        window = jnp.concatenate([pick(p), edges], axis=1)
        interp = jnp.dot(window, table[which], preferred_element_type=F32).astype(BF16)
        mixed = jnp.dot(mix[step, 0], interp, preferred_element_type=F32).astype(BF16)
        if weighted:
            mixed = (obs[p].astype(F32) * mixed.astype(F32)).astype(BF16)
        if fold and p in (0, outs - 1):
            blocks.append(mixed)
        else:
            out[p - 1 if fold else p] = mixed
    if fold:
        out[outs - 2] = jnp.where(rightward, blocks[1], blocks[0])


def forward(step, outs, fold, par, rows, table, mix, obs=None):
    levels, cols = rows[0].shape[1:]
    first = (par.shape[1] - outs) // 2
    made = outs - 1 if fold else outs
    weighted = obs is not None
    args = (par, *rows, table, mix) + ((obs,) if weighted else ())
    return pl.pallas_call(
        functools.partial(forward_kernel, step, first, outs, fold, weighted),
        out_shape=jax.ShapeDtypeStruct((made, levels, cols), BF16),
        in_specs=[SMEM] + [VMEM] * (len(args) - 1),
        out_specs=VMEM,
        compiler_params=pltpu.CompilerParams(vmem_limit_bytes=LIMIT),
        cost_estimate=pl.CostEstimate(flops=outs * 6_000_000, bytes_accessed=2_000_000, transcendentals=0),
    )(*args)


def adjoint_kernel(step, first, reads, summed, par, *rest):
    parts, (table, mix, to_north, stay, to_south, total) = rest[: 3 if summed else 1], rest[3 if summed else 1 :]
    shape = parts[0].shape[1:]
    rightward = right_lanes(shape)
    nothing = jnp.zeros(shape, F32)
    for way in range(3):
        for p in range(reads):
            total[way, p] = nothing
    for p in range(reads):
        way, which = par[step, first + p], par[4 + step, first + p]
        if summed:
            cot = (parts[0][p] + parts[1][p].astype(F32) + parts[2][p].astype(F32)).astype(BF16)
        else:
            cot = parts[0][p]
        back = lax.dot_general(mix[step, 0], cot, (((0,), (0,)), ((), ())), preferred_element_type=F32).astype(BF16)
        spread = jnp.dot(back, table[which], preferred_element_type=F32)
        main, edges = spread[:, : shape[1]], spread[:, shape[1] :]
        if 0 < p < reads - 1:
            total[way, p] += main
        if p < reads - 2:
            total[way, p + 1] += jnp.where(rightward, edges, nothing)
        if p > 1:
            total[way, p - 1] += jnp.where(rightward, nothing, edges)
    for p in range(1, reads - 1):
        to_north[p - 1] = total[0, p].astype(BF16)
        stay[p - 1] = total[1, p]
        to_south[p - 1] = total[2, p].astype(BF16)


def adjoint(step, par, parts, table, mix):
    reads, levels, cols = parts[0].shape
    first = (par.shape[1] - reads) // 2
    gives = (reads - 2, levels, cols)
    return pl.pallas_call(
        functools.partial(adjoint_kernel, step, first, reads, len(parts) == 3),
        out_shape=[jax.ShapeDtypeStruct(gives, BF16), jax.ShapeDtypeStruct(gives, F32), jax.ShapeDtypeStruct(gives, BF16)],
        in_specs=[SMEM] + [VMEM] * (len(parts) + 2),
        out_specs=[VMEM] * 3,
        scratch_shapes=[pltpu.VMEM((3, reads, levels, cols), F32)],
        compiler_params=pltpu.CompilerParams(vmem_limit_bytes=LIMIT),
        cost_estimate=pl.CostEstimate(flops=reads * 6_000_000, bytes_accessed=2_000_000, transcendentals=0),
    )(par, *parts, table, mix)


def from_lat(value, by):
    length = lax.axis_size("lat")
    return lax.ppermute(value, "lat", [(i, i - by) for i in range(length) if 0 <= i - by < length])


def from_lon(value, by):
    length = lax.axis_size("lon")
    return lax.ppermute(value, "lon", [(i, (i - by) % length) for i in range(length)])


def exchange(value, run):
    length = lax.axis_size("lon")
    groups = [list(range(i, i + run)) for i in range(0, length, run)]
    return lax.all_to_all(value, "lon", 0, 0, axis_index_groups=groups)


def on_device(vector, obs_weight, departures, weight_index, interp_table, column_mix):
    run, levels, _, cols = vector.shape
    reach = (interp_table.shape[1] - cols) // 2
    inner = interp_table[:, reach : reach + cols]
    gap = jnp.zeros((interp_table.shape[0], cols - 2 * reach, cols), BF16)
    table = jnp.concatenate([inner, interp_table[:, reach + cols :], gap, interp_table[:, :reach]], axis=1)
    table_t = jnp.swapaxes(table, 1, 2)

    numbers = jnp.concatenate([departures.reshape(-1), weight_index.reshape(-1)]).astype(BF16)
    count = numbers.shape[0]
    tail = jnp.concatenate([jnp.broadcast_to(numbers[:, None], (count, cols)), jnp.zeros((16 - count, cols), BF16)])
    shared = jnp.concatenate([obs_weight[:, 0].astype(BF16), tail])
    bundle = jnp.concatenate(
        [vector[:, :, 0], jnp.broadcast_to(shared[None], (run, *shared.shape))], axis=1
    )
    bundle = exchange(bundle, run)
    state, obs = bundle[:, :levels], bundle[:, levels : 2 * levels]
    ends = jnp.concatenate([state, bundle[:, 2 * levels :]], axis=1)
    west, east = from_lon(ends[-2:], -run), from_lon(ends[:2], run)
    values = jnp.concatenate(
        [west[:, levels : levels + count, 0], bundle[:, 2 * levels : 2 * levels + count, 0], east[:, levels : levels + count, 0]]
    )
    par = values.astype(jnp.int32).T
    west, east = west[:, :levels], east[:, :levels]

    for step in range(0, 4, 2):
        if step > 0:
            west, east = from_lon(state[-2:], -run), from_lon(state[:2], run)
        rightward = right_lanes((levels, cols))
        outer = jnp.where(rightward, east[1], west[0])
        wide = jnp.concatenate([west[1:], state, east[:1], outer[None]])
        wide = forward(step, run + 2, True, par, (wide, from_lat(wide, -1), from_lat(wide, 1)), table, column_mix)
        state = forward(
            step + 1, run, False, par, (wide, from_lat(wide, -1), from_lat(wide, 1)), table, column_mix,
            obs if step == 2 else None,
        )

    cot = state
    for step in (3, 1):
        west, east = from_lon(cot[-2:], -run), from_lon(cot[:2], run)
        wide = jnp.concatenate([west, cot, east])
        north, stay, south = adjoint(step, par, (wide,), table_t, column_mix)
        parts = (stay, from_lat(north, 1), from_lat(south, -1))
        north, stay, south = adjoint(step - 1, par, parts, table_t, column_mix)
        cot = (stay + from_lat(north, 1).astype(F32) + from_lat(south, -1).astype(F32)).astype(BF16)
    return exchange(cot, run)[:, :, None]


def solution(mesh):
    placed = (
        P(None, None, "lat", "lon"),
        P(None, "lat", "lon"),
        P(None, "lat", "lon"),
        P(None, "lat", "lon"),
        P(),
        P(None, "lat", None, None),
    )
    return jax.shard_map(
        on_device, mesh=mesh, in_specs=placed, out_specs=P(None, None, "lat", "lon"), check_vma=False
    )
```

time: 329 us -> 229 us (0.70)
  the two profiles are of different devices: /device:TPU:57 before, /device:TPU:63 now
where the time goes in v1:
time: 229 us; the launch traced here: 228 us
  waiting for transfers between devices  85.2 us (37%)
  starting transfers between devices  82.7 us (36%)
  blocking collectives  39.1 us (17%)
  Pallas kernels  9.56 us (4%)
  local copies, waits for them, and re-layouts  5.9 us (3%)
  other arithmetic  4.69 us (2%)
    ppermute x16, waiting for transfers between devices, from_lat(): lax.ppermute(value, 'lat', [(i, i - by) for i in range(length) if 0 <= i...  76.1 us
    ppermute x16, starting transfers between devices, from_lat(): lax.ppermute(value, 'lat', [(i, i - by) for i in range(length) if 0 <= i...  58.7 us
    all_to_all x2, blocking collectives, exchange(): return lax.all_to_all(value, 'lon', 0, 0, axis_index_groups=groups)  39.1 us
    ppermute x8, starting transfers between devices, from_lon(): lax.ppermute(value, 'lon', [(i, (i - by) % length) for i in range(length)])  24 us
    ppermute x8, waiting for transfers between devices, from_lon(): lax.ppermute(value, 'lon', [(i, (i - by) % length) for i in range(length)])  9.05 us
    pallas_call x4, Pallas kernels, forward(): pl.pallas_call(functools.partial(forward_kernel, step, first, outs, fold,...  4.83 us
    pallas_call x4, Pallas kernels, adjoint(): pl.pallas_call(functools.partial(adjoint_kernel, step, first, reads, len(...  4.73 us
  transfers between devices with their start and end apart: 24, of which 19 were waited for; matrix products, arithmetic and copies ran while one was open for 3% of the time, Pallas kernels for 0%

profile of v1, /device:TPU:63, one launch (start us, length us, event | category | flops | bytes accessed | tf_op | source)
XLA Modules:
  0.0 227.6 jit_solution(2804377375225201670)
XLA Ops:
  2.7 14.1 %all_to_all.10 = bf16[8,160,128]{2,1,0:T(8,128)(2,1)S(1)} all-to-all(bf16[8,160,128]{2,1,0:T(8,128)(2,1)S(1)} %pad_maximum_fusion.1), channel_id=1, replica_groups={{0,1,2,3,4,5,6,7},{8,9,10,11,12,13,14,15},{16,17,18,19,20,21,22,23},{24..., dimensions={0} | all-to-all | bytes 655360 | tf_op jit(solution)/shard_map/all_to_all | solution.py:120
  17.6 2.2 collective-permute-start
  19.8 3.2 %collective-permute-start.1 = (bf16[2,88,128]{2,1,0:T(8,128)(2,1)S(1)}, bf16[2,88,128]{2,1,0:T(8,128)(2,1)S(1)}, u32[]{:S(2)}, u32[]{:S(2)}) collective-permute-start(bf16[2,88,128]{2,1,0:T(8,128)(2,1)S(1)} %get-tuple-element.32), channel_id=1, source_target_pairs={{0,24},{1,25},{2,26},{3,27},{4,28},{5,29},{6,30},{7,31},{8,0},{9,1... | collective-permute-start | bytes 135176 | tf_op jit(solution)/shard_map/ppermute | solution.py:114
  23.9 1.9 collective-permute-done.1
  25.9 19.8 %collective-permute-start.3 = (bf16[11,72,128]{2,1,0:T(8,128)(2,1)S(1)}, bf16[11,72,128]{2,1,0:T(8,128)(2,1)S(1)}, u32[]{:S(2)}, u32[]{:S(2)}) collective-permute-start(bf16[11,72,128]{2,1,0:T(8,128)(2,1)S(1)} %pad_maximum_fusion.4.own), channel_id=1, source_target_pairs={{32,0},{64,32},{96,64},{128,96},{160,128},{192,160},{224,192},{256... | collective-permute-start | bytes 608264 | tf_op jit(solution)/shard_map/ppermute | solution.py:109
  45.7 1.9 collective-permute-start.2
  47.6 1.4 pad_maximum_fusion
  49.0 1.6 copy.22.table
  52.6 7.4 %collective-permute-done.2.north = bf16[11,72,128]{2,1,0:T(8,128)(2,1)S(1)} collective-permute-done((bf16[11,72,128]{2,1,0:T(8,128)(2,1)S(1)}, bf16[11,72,128]{2,1,0:T(8,128)(2,1)S(1)}, u32[]{:S(2)}, u32[]{:S(2)}) %collective-permute-start.2) | collective-permute-done | bytes 202784 | tf_op jit(solution)/shard_map/ppermute | solution.py:109
  60.0 1.2 shard_map.64.own
  61.3 2.0 collective-permute-start.5
  63.2 3.3 %collective-permute-start.4 = (bf16[9,72,128]{2,1,0:T(8,128)(2,1)S(1)}, bf16[9,72,128]{2,1,0:T(8,128)(2,1)S(1)}, u32[]{:S(2)}, u32[]{:S(2)}) collective-permute-start(bf16[9,72,128]{2,1,0:T(8,128)(2,1)S(1)} %shard_map.64.own), channel_id=1, source_target_pairs={{0,32},{32,64},{64,96},{96,128},{128,160},{160,192},{192,224},{224... | collective-permute-start | bytes 497672 | tf_op jit(solution)/shard_map/ppermute | solution.py:109
  67.3 8.6 %collective-permute-done.4.north = bf16[9,72,128]{2,1,0:T(8,128)(2,1)S(1)} collective-permute-done((bf16[9,72,128]{2,1,0:T(8,128)(2,1)S(1)}, bf16[9,72,128]{2,1,0:T(8,128)(2,1)S(1)}, u32[]{:S(2)}, u32[]{:S(2)}) %collective-permute-start.4) | collective-permute-done | bytes 165920 | tf_op jit(solution)/shard_map/ppermute | solution.py:109
  75.9 1.2 shard_map.65
  77.1 2.0 collective-permute-start.7
  79.1 4.5 %collective-permute-start.6 = (bf16[2,72,128]{2,1,0:T(8,128)(2,1)S(1)}, bf16[2,72,128]{2,1,0:T(8,128)(2,1)S(1)}, u32[]{:S(2)}, u32[]{:S(2)}) collective-permute-start(bf16[2,72,128]{2,1,0:T(8,128)(2,1)S(1)} %get-tuple-element.38), channel_id=1, source_target_pairs={{0,8},{1,9},{2,10},{3,11},{4,12},{5,13},{6,14},{7,15},{8,16},{9,17... | collective-permute-start | bytes 110600 | tf_op jit(solution)/shard_map/ppermute | solution.py:114
  84.7 1.9 collective-permute-start.9
  86.6 3.4 %collective-permute-start.8 = (bf16[11,72,128]{2,1,0:T(8,128)(2,1)S(1)}, bf16[11,72,128]{2,1,0:T(8,128)(2,1)S(1)}, u32[]{:S(2)}, u32[]{:S(2)}) collective-permute-start(bf16[11,72,128]{2,1,0:T(8,128)(2,1)S(1)} %pad_maximum_fusion.5.own), channel_id=1, source_target_pairs={{0,32},{32,64},{64,96},{96,128},{128,160},{160,192},{192,224},{224... | collective-permute-start | bytes 608264 | tf_op jit(solution)/shard_map/ppermute | solution.py:109
  90.0 1.2 collective-permute-done.9.south
  91.2 8.9 %collective-permute-done.8.north = bf16[11,72,128]{2,1,0:T(8,128)(2,1)S(1)} collective-permute-done((bf16[11,72,128]{2,1,0:T(8,128)(2,1)S(1)}, bf16[11,72,128]{2,1,0:T(8,128)(2,1)S(1)}, u32[]{:S(2)}, u32[]{:S(2)}) %collective-permute-start.8) | collective-permute-done | bytes 202784 | tf_op jit(solution)/shard_map/ppermute | solution.py:109
  100.1 1.2 shard_map.66.own
  101.3 1.9 collective-permute-start.11
  103.3 3.4 %collective-permute-start.10 = (bf16[9,72,128]{2,1,0:T(8,128)(2,1)S(1)}, bf16[9,72,128]{2,1,0:T(8,128)(2,1)S(1)}, u32[]{:S(2)}, u32[]{:S(2)}) collective-permute-start(bf16[9,72,128]{2,1,0:T(8,128)(2,1)S(1)} %shard_map.66.own), channel_id=1, source_target_pairs={{0,32},{32,64},{64,96},{96,128},{128,160},{160,192},{192,224},{224... | collective-permute-start | bytes 497672 | tf_op jit(solution)/shard_map/ppermute | solution.py:109
  107.4 8.5 %collective-permute-done.10.north = bf16[9,72,128]{2,1,0:T(8,128)(2,1)S(1)} collective-permute-done((bf16[9,72,128]{2,1,0:T(8,128)(2,1)S(1)}, bf16[9,72,128]{2,1,0:T(8,128)(2,1)S(1)}, u32[]{:S(2)}, u32[]{:S(2)}) %collective-permute-start.10) | collective-permute-done | bytes 165920 | tf_op jit(solution)/shard_map/ppermute | solution.py:109
  115.9 1.2 shard_map.67
  117.1 4.9 %collective-permute-start.12 = (bf16[2,72,128]{2,1,0:T(8,128)(2,1)S(1)}, bf16[2,72,128]{2,1,0:T(8,128)(2,1)S(1)}, u32[]{:S(2)}, u32[]{:S(2)}) collective-permute-start(bf16[2,72,128]{2,1,0:T(8,128)(2,1)S(1)} %get-tuple-element.35), channel_id=1, source_target_pairs={{0,8},{1,9},{2,10},{3,11},{4,12},{5,13},{6,14},{7,15},{8,16},{9,17... | collective-permute-start | bytes 110600 | tf_op jit(solution)/shard_map/ppermute | solution.py:114
  122.0 1.9 collective-permute-start.13
  124.4 3.6 %collective-permute-done.13 = bf16[2,72,128]{2,1,0:T(8,128)(2,1)S(1)} collective-permute-done((bf16[2,72,128]{2,1,0:T(8,128)(2,1)S(1)}, bf16[2,72,128]{2,1,0:T(8,128)(2,1)S(1)}, u32[]{:S(2)}, u32[]{:S(2)}) %collective-permute-start.13) | collective-permute-done | bytes 36896 | tf_op jit(solution)/shard_map/ppermute | solution.py:114
  128.0 1.2 shard_map.68
  129.2 1.9 collective-permute-start.14
  131.1 3.4 %collective-permute-start.15 = (bf16[10,72,128]{2,1,0:T(8,128)(2,1)S(1)}, bf16[10,72,128]{2,1,0:T(8,128)(2,1)S(1)}, u32[]{:S(2)}, u32[]{:S(2)}) collective-permute-start(bf16[10,72,128]{2,1,0:T(8,128)(2,1)S(1)} %get-tuple-element.19), channel_id=1, source_target_pairs={{0,32},{32,64},{64,96},{96,128},{128,160},{160,192},{192,224},{224... | collective-permute-start | bytes 552968 | tf_op jit(solution)/shard_map/ppermute | solution.py:109
  135.5 8.7 %collective-permute-done.15.rest_2_ = bf16[10,72,128]{2,1,0:T(8,128)(2,1)S(1)} collective-permute-done((bf16[10,72,128]{2,1,0:T(8,128)(2,1)S(1)}, bf16[10,72,128]{2,1,0:T(8,128)(2,1)S(1)}, u32[]{:S(2)}, u32[]{:S(2)}) %collective-permute-start.15) | collective-permute-done | bytes 184352 | tf_op jit(solution)/shard_map/ppermute | solution.py:109
  144.2 1.2 shard_map.69
  145.3 1.9 collective-permute-start.16
  147.3 3.4 %collective-permute-start.17 = (bf16[8,72,128]{2,1,0:T(8,128)(2,1)S(1)}, bf16[8,72,128]{2,1,0:T(8,128)(2,1)S(1)}, u32[]{:S(2)}, u32[]{:S(2)}) collective-permute-start(bf16[8,72,128]{2,1,0:T(8,128)(2,1)S(1)} %get-tuple-element.22), channel_id=1, source_target_pairs={{0,32},{32,64},{64,96},{96,128},{128,160},{160,192},{192,224},{224... | collective-permute-start | bytes 442376 | tf_op jit(solution)/shard_map/ppermute | solution.py:109
  151.2 8.3 %collective-permute-done.17 = bf16[8,72,128]{2,1,0:T(8,128)(2,1)S(1)} collective-permute-done((bf16[8,72,128]{2,1,0:T(8,128)(2,1)S(1)}, bf16[8,72,128]{2,1,0:T(8,128)(2,1)S(1)}, u32[]{:S(2)}, u32[]{:S(2)}) %collective-permute-start.17) | collective-permute-done | bytes 147488 | tf_op jit(solution)/shard_map/ppermute | solution.py:109
  159.6 1.9 collective-permute-start.18
  161.5 3.4 %collective-permute-start.19 = (bf16[2,72,128]{2,1,0:T(8,128)(2,1)S(1)}, bf16[2,72,128]{2,1,0:T(8,128)(2,1)S(1)}, u32[]{:S(2)}, u32[]{:S(2)}) collective-permute-start(bf16[2,72,128]{2,1,0:T(8,128)(2,1)S(1)} %get-tuple-element.34), channel_id=1, source_target_pairs={{0,24},{1,25},{2,26},{3,27},{4,28},{5,29},{6,30},{7,31},{8,0},{9,1... | collective-permute-start | bytes 110600 | tf_op jit(solution)/shard_map/ppermute | solution.py:114
  164.9 2.5 %collective-permute-done.19 = bf16[2,72,128]{2,1,0:T(8,128)(2,1)S(1)} collective-permute-done((bf16[2,72,128]{2,1,0:T(8,128)(2,1)S(1)}, bf16[2,72,128]{2,1,0:T(8,128)(2,1)S(1)}, u32[]{:S(2)}, u32[]{:S(2)}) %collective-permute-start.19) | collective-permute-done | bytes 36896 | tf_op jit(solution)/shard_map/ppermute | solution.py:114
  167.5 1.2 shard_map.70
  168.7 1.9 collective-permute-start.20
  170.6 3.4 %collective-permute-start.21 = (bf16[10,72,128]{2,1,0:T(8,128)(2,1)S(1)}, bf16[10,72,128]{2,1,0:T(8,128)(2,1)S(1)}, u32[]{:S(2)}, u32[]{:S(2)}) collective-permute-start(bf16[10,72,128]{2,1,0:T(8,128)(2,1)S(1)} %get-tuple-element.25), channel_id=1, source_target_pairs={{0,32},{32,64},{64,96},{96,128},{128,160},{160,192},{192,224},{224... | collective-permute-start | bytes 552968 | tf_op jit(solution)/shard_map/ppermute | solution.py:109
  175.0 8.7 %collective-permute-done.21.rest_2_ = bf16[10,72,128]{2,1,0:T(8,128)(2,1)S(1)} collective-permute-done((bf16[10,72,128]{2,1,0:T(8,128)(2,1)S(1)}, bf16[10,72,128]{2,1,0:T(8,128)(2,1)S(1)}, u32[]{:S(2)}, u32[]{:S(2)}) %collective-permute-start.21) | collective-permute-done | bytes 184352 | tf_op jit(solution)/shard_map/ppermute | solution.py:109
  184.9 1.9 collective-permute-start.22
  186.8 3.4 %collective-permute-start.23 = (bf16[8,72,128]{2,1,0:T(8,128)(2,1)S(1)}, bf16[8,72,128]{2,1,0:T(8,128)(2,1)S(1)}, u32[]{:S(2)}, u32[]{:S(2)}) collective-permute-start(bf16[8,72,128]{2,1,0:T(8,128)(2,1)S(1)} %get-tuple-element.28), channel_id=1, source_target_pairs={{0,32},{32,64},{64,96},{96,128},{128,160},{160,192},{192,224},{224... | collective-permute-start | bytes 442376 | tf_op jit(solution)/shard_map/ppermute | solution.py:109
  190.2 1.3 collective-permute-done.22
  191.5 10.4 %collective-permute-done.23 = bf16[8,72,128]{2,1,0:T(8,128)(2,1)S(1)} collective-permute-done((bf16[8,72,128]{2,1,0:T(8,128)(2,1)S(1)}, bf16[8,72,128]{2,1,0:T(8,128)(2,1)S(1)}, u32[]{:S(2)}, u32[]{:S(2)}) %collective-permute-start.23) | collective-permute-done | bytes 147488 | tf_op jit(solution)/shard_map/ppermute | solution.py:109
  201.9 25.0 %all_to_all.11 = bf16[8,72,128]{2,1,0:T(8,128)(2,1)S(1)} all-to-all(bf16[8,72,128]{2,1,0:T(8,128)(2,1)S(1)} %add_convert_fusion), channel_id=1, replica_groups={{0,1,2,3,4,5,6,7},{8,9,10,11,12,13,14,15},{16,17,18,19,20,21,22,23},{24..., dimensions={0} | all-to-all | bytes 294912 | tf_op jit(solution)/shard_map/all_to_all | solution.py:120
  (59 shorter events, 13.9 us)
Async XLA Ops:
  16.8 0.7 copy-start.1
  16.8 6.3 %slice-start = ((bf16[16,160,128]{2,1,0:T(8,128)(2,1)}), bf16[16,16,128]{2,1,0:T(8,128)(2,1)S(1)}, s32[]{:S(2)}) async-start(bf16[16,160,128]{2,1,0:T(8,128)(2,1)} %param.10), calls=%async_computation.2 | async-start | bytes 131072 | tf_op jit(solution)/shard_map/slice | solution.py:128
  17.6 5.8 %slice-start.1 = ((bf16[16,160,128]{2,1,0:T(8,128)(2,1)}), bf16[16,144,128]{2,1,0:T(8,128)(2,1)S(1)}, s32[]{:S(2)}) async-start(bf16[16,160,128]{2,1,0:T(8,128)(2,1)} %param.10), calls=%async_computation.3 | async-start | bytes 1179648 | tf_op jit(solution)/shard_map/slice | solution.py:126
  17.6 6.3 %collective-permute-start = (bf16[2,88,128]{2,1,0:T(8,128)(2,1)S(1)}, bf16[2,88,128]{2,1,0:T(8,128)(2,1)S(1)}, u32[]{:S(2)}, u32[]{:S(2)}) collective-permute-start(bf16[2,88,128]{2,1,0:T(8,128)(2,1)S(1)} %get-tuple-element.31), channel_id=1, source_target_pairs={{0,8},{1,9},{2,10},{3,11},{4,12},{5,13},{6,14},{7,15},{8,16},{9,17... | collective-permute-start | bytes 135176 | tf_op jit(solution)/shard_map/ppermute | solution.py:114
  19.8 6.0 %collective-permute-start.1 = (bf16[2,88,128]{2,1,0:T(8,128)(2,1)S(1)}, bf16[2,88,128]{2,1,0:T(8,128)(2,1)S(1)}, u32[]{:S(2)}, u32[]{:S(2)}) collective-permute-start(bf16[2,88,128]{2,1,0:T(8,128)(2,1)S(1)} %get-tuple-element.32), channel_id=1, source_target_pairs={{0,24},{1,25},{2,26},{3,27},{4,28},{5,29},{6,30},{7,31},{8,0},{9,1... | collective-permute-start | bytes 135176 | tf_op jit(solution)/shard_map/ppermute | solution.py:114
  25.8 21.8 %copy-start.2 = (bf16[2,88,128]{2,1,0:T(8,128)(2,1)}, bf16[2,88,128]{2,1,0:T(8,128)(2,1)S(1)}, u32[]{:S(2)}) copy-start(bf16[2,88,128]{2,1,0:T(8,128)(2,1)S(1)} %collective-permute-done.1) | copy-start | bytes 135172
  25.9 26.7 %collective-permute-start.3 = (bf16[11,72,128]{2,1,0:T(8,128)(2,1)S(1)}, bf16[11,72,128]{2,1,0:T(8,128)(2,1)S(1)}, u32[]{:S(2)}, u32[]{:S(2)}) collective-permute-start(bf16[11,72,128]{2,1,0:T(8,128)(2,1)S(1)} %pad_maximum_fusion.4.own), channel_id=1, source_target_pairs={{32,0},{64,32},{96,64},{128,96},{160,128},{192,160},{224,192},{256... | collective-permute-start | bytes 608264 | tf_op jit(solution)/shard_map/ppermute | solution.py:109
  45.7 14.3 %collective-permute-start.2 = (bf16[11,72,128]{2,1,0:T(8,128)(2,1)S(1)}, bf16[11,72,128]{2,1,0:T(8,128)(2,1)S(1)}, u32[]{:S(2)}, u32[]{:S(2)}) collective-permute-start(bf16[11,72,128]{2,1,0:T(8,128)(2,1)S(1)} %pad_maximum_fusion.4.own), channel_id=1, source_target_pairs={{0,32},{32,64},{64,96},{96,128},{128,160},{160,192},{192,224},{224... | collective-permute-start | bytes 608264 | tf_op jit(solution)/shard_map/ppermute | solution.py:109
  49.0 11.0 %copy-start = (bf16[4,1,72,72]{3,2,1,0:T(8,128)(2,1)S(1)}, bf16[4,1,72,72]{3,2,1,0:T(8,128)(2,1)}, u32[]{:S(2)}) copy-start(bf16[4,1,72,72]{3,2,1,0:T(8,128)(2,1)} %rest_4_.3) | copy-start | bytes 124420
  61.3 6.1 %collective-permute-start.5 = (bf16[9,72,128]{2,1,0:T(8,128)(2,1)S(1)}, bf16[9,72,128]{2,1,0:T(8,128)(2,1)S(1)}, u32[]{:S(2)}, u32[]{:S(2)}) collective-permute-start(bf16[9,72,128]{2,1,0:T(8,128)(2,1)S(1)} %shard_map.64.own), channel_id=1, source_target_pairs={{32,0},{64,32},{96,64},{128,96},{160,128},{192,160},{224,192},{256... | collective-permute-start | bytes 497672 | tf_op jit(solution)/shard_map/ppermute | solution.py:109
  63.2 12.7 %collective-permute-start.4 = (bf16[9,72,128]{2,1,0:T(8,128)(2,1)S(1)}, bf16[9,72,128]{2,1,0:T(8,128)(2,1)S(1)}, u32[]{:S(2)}, u32[]{:S(2)}) collective-permute-start(bf16[9,72,128]{2,1,0:T(8,128)(2,1)S(1)} %shard_map.64.own), channel_id=1, source_target_pairs={{0,32},{32,64},{64,96},{96,128},{128,160},{160,192},{192,224},{224... | collective-permute-start | bytes 497672 | tf_op jit(solution)/shard_map/ppermute | solution.py:109
  77.1 6.5 %collective-permute-start.7 = (bf16[2,72,128]{2,1,0:T(8,128)(2,1)S(1)}, bf16[2,72,128]{2,1,0:T(8,128)(2,1)S(1)}, u32[]{:S(2)}, u32[]{:S(2)}) collective-permute-start(bf16[2,72,128]{2,1,0:T(8,128)(2,1)S(1)} %get-tuple-element.37), channel_id=1, source_target_pairs={{0,24},{1,25},{2,26},{3,27},{4,28},{5,29},{6,30},{7,31},{8,0},{9,1... | collective-permute-start | bytes 110600 | tf_op jit(solution)/shard_map/ppermute | solution.py:114
  79.1 5.6 %collective-permute-start.6 = (bf16[2,72,128]{2,1,0:T(8,128)(2,1)S(1)}, bf16[2,72,128]{2,1,0:T(8,128)(2,1)S(1)}, u32[]{:S(2)}, u32[]{:S(2)}) collective-permute-start(bf16[2,72,128]{2,1,0:T(8,128)(2,1)S(1)} %get-tuple-element.38), channel_id=1, source_target_pairs={{0,8},{1,9},{2,10},{3,11},{4,12},{5,13},{6,14},{7,15},{8,16},{9,17... | collective-permute-start | bytes 110600 | tf_op jit(solution)/shard_map/ppermute | solution.py:114
  84.7 6.5 %collective-permute-start.9 = (bf16[11,72,128]{2,1,0:T(8,128)(2,1)S(1)}, bf16[11,72,128]{2,1,0:T(8,128)(2,1)S(1)}, u32[]{:S(2)}, u32[]{:S(2)}) collective-permute-start(bf16[11,72,128]{2,1,0:T(8,128)(2,1)S(1)} %pad_maximum_fusion.5.own), channel_id=1, source_target_pairs={{32,0},{64,32},{96,64},{128,96},{160,128},{192,160},{224,192},{256... | collective-permute-start | bytes 608264 | tf_op jit(solution)/shard_map/ppermute | solution.py:109
  86.6 13.5 %collective-permute-start.8 = (bf16[11,72,128]{2,1,0:T(8,128)(2,1)S(1)}, bf16[11,72,128]{2,1,0:T(8,128)(2,1)S(1)}, u32[]{:S(2)}, u32[]{:S(2)}) collective-permute-start(bf16[11,72,128]{2,1,0:T(8,128)(2,1)S(1)} %pad_maximum_fusion.5.own), channel_id=1, source_target_pairs={{0,32},{32,64},{64,96},{96,128},{128,160},{160,192},{192,224},{224... | collective-permute-start | bytes 608264 | tf_op jit(solution)/shard_map/ppermute | solution.py:109
  101.3 6.1 %collective-permute-start.11 = (bf16[9,72,128]{2,1,0:T(8,128)(2,1)S(1)}, bf16[9,72,128]{2,1,0:T(8,128)(2,1)S(1)}, u32[]{:S(2)}, u32[]{:S(2)}) collective-permute-start(bf16[9,72,128]{2,1,0:T(8,128)(2,1)S(1)} %shard_map.66.own), channel_id=1, source_target_pairs={{32,0},{64,32},{96,64},{128,96},{160,128},{192,160},{224,192},{256... | collective-permute-start | bytes 497672 | tf_op jit(solution)/shard_map/ppermute | solution.py:109
  103.3 12.7 %collective-permute-start.10 = (bf16[9,72,128]{2,1,0:T(8,128)(2,1)S(1)}, bf16[9,72,128]{2,1,0:T(8,128)(2,1)S(1)}, u32[]{:S(2)}, u32[]{:S(2)}) collective-permute-start(bf16[9,72,128]{2,1,0:T(8,128)(2,1)S(1)} %shard_map.66.own), channel_id=1, source_target_pairs={{0,32},{32,64},{64,96},{96,128},{128,160},{160,192},{192,224},{224... | collective-permute-start | bytes 497672 | tf_op jit(solution)/shard_map/ppermute | solution.py:109
  117.1 7.2 %collective-permute-start.12 = (bf16[2,72,128]{2,1,0:T(8,128)(2,1)S(1)}, bf16[2,72,128]{2,1,0:T(8,128)(2,1)S(1)}, u32[]{:S(2)}, u32[]{:S(2)}) collective-permute-start(bf16[2,72,128]{2,1,0:T(8,128)(2,1)S(1)} %get-tuple-element.35), channel_id=1, source_target_pairs={{0,8},{1,9},{2,10},{3,11},{4,12},{5,13},{6,14},{7,15},{8,16},{9,17... | collective-permute-start | bytes 110600 | tf_op jit(solution)/shard_map/ppermute | solution.py:114
  122.0 5.9 %collective-permute-start.13 = (bf16[2,72,128]{2,1,0:T(8,128)(2,1)S(1)}, bf16[2,72,128]{2,1,0:T(8,128)(2,1)S(1)}, u32[]{:S(2)}, u32[]{:S(2)}) collective-permute-start(bf16[2,72,128]{2,1,0:T(8,128)(2,1)S(1)} %get-tuple-element.36), channel_id=1, source_target_pairs={{0,24},{1,25},{2,26},{3,27},{4,28},{5,29},{6,30},{7,31},{8,0},{9,1... | collective-permute-start | bytes 110600 | tf_op jit(solution)/shard_map/ppermute | solution.py:114
  129.2 6.3 %collective-permute-start.14 = (bf16[10,72,128]{2,1,0:T(8,128)(2,1)S(1)}, bf16[10,72,128]{2,1,0:T(8,128)(2,1)S(1)}, u32[]{:S(2)}, u32[]{:S(2)}) collective-permute-start(bf16[10,72,128]{2,1,0:T(8,128)(2,1)S(1)} %get-tuple-element.18), channel_id=1, source_target_pairs={{32,0},{64,32},{96,64},{128,96},{160,128},{192,160},{224,192},{256... | collective-permute-start | bytes 552968 | tf_op jit(solution)/shard_map/ppermute | solution.py:109
  131.1 13.1 %collective-permute-start.15 = (bf16[10,72,128]{2,1,0:T(8,128)(2,1)S(1)}, bf16[10,72,128]{2,1,0:T(8,128)(2,1)S(1)}, u32[]{:S(2)}, u32[]{:S(2)}) collective-permute-start(bf16[10,72,128]{2,1,0:T(8,128)(2,1)S(1)} %get-tuple-element.19), channel_id=1, source_target_pairs={{0,32},{32,64},{64,96},{96,128},{128,160},{160,192},{192,224},{224... | collective-permute-start | bytes 552968 | tf_op jit(solution)/shard_map/ppermute | solution.py:109
  145.3 5.9 %collective-permute-start.16 = (bf16[8,72,128]{2,1,0:T(8,128)(2,1)S(1)}, bf16[8,72,128]{2,1,0:T(8,128)(2,1)S(1)}, u32[]{:S(2)}, u32[]{:S(2)}) collective-permute-start(bf16[8,72,128]{2,1,0:T(8,128)(2,1)S(1)} %get-tuple-element.21), channel_id=1, source_target_pairs={{32,0},{64,32},{96,64},{128,96},{160,128},{192,160},{224,192},{256... | collective-permute-start | bytes 442376 | tf_op jit(solution)/shard_map/ppermute | solution.py:109
  147.3 12.3 %collective-permute-start.17 = (bf16[8,72,128]{2,1,0:T(8,128)(2,1)S(1)}, bf16[8,72,128]{2,1,0:T(8,128)(2,1)S(1)}, u32[]{:S(2)}, u32[]{:S(2)}) collective-permute-start(bf16[8,72,128]{2,1,0:T(8,128)(2,1)S(1)} %get-tuple-element.22), channel_id=1, source_target_pairs={{0,32},{32,64},{64,96},{96,128},{128,160},{160,192},{192,224},{224... | collective-permute-start | bytes 442376 | tf_op jit(solution)/shard_map/ppermute | solution.py:109
  159.6 5.3 %collective-permute-start.18 = (bf16[2,72,128]{2,1,0:T(8,128)(2,1)S(1)}, bf16[2,72,128]{2,1,0:T(8,128)(2,1)S(1)}, u32[]{:S(2)}, u32[]{:S(2)}) collective-permute-start(bf16[2,72,128]{2,1,0:T(8,128)(2,1)S(1)} %get-tuple-element.33), channel_id=1, source_target_pairs={{0,8},{1,9},{2,10},{3,11},{4,12},{5,13},{6,14},{7,15},{8,16},{9,17... | collective-permute-start | bytes 110600 | tf_op jit(solution)/shard_map/ppermute | solution.py:114
  161.5 5.9 %collective-permute-start.19 = (bf16[2,72,128]{2,1,0:T(8,128)(2,1)S(1)}, bf16[2,72,128]{2,1,0:T(8,128)(2,1)S(1)}, u32[]{:S(2)}, u32[]{:S(2)}) collective-permute-start(bf16[2,72,128]{2,1,0:T(8,128)(2,1)S(1)} %get-tuple-element.34), channel_id=1, source_target_pairs={{0,24},{1,25},{2,26},{3,27},{4,28},{5,29},{6,30},{7,31},{8,0},{9,1... | collective-permute-start | bytes 110600 | tf_op jit(solution)/shard_map/ppermute | solution.py:114
  168.7 6.3 %collective-permute-start.20 = (bf16[10,72,128]{2,1,0:T(8,128)(2,1)S(1)}, bf16[10,72,128]{2,1,0:T(8,128)(2,1)S(1)}, u32[]{:S(2)}, u32[]{:S(2)}) collective-permute-start(bf16[10,72,128]{2,1,0:T(8,128)(2,1)S(1)} %get-tuple-element.24), channel_id=1, source_target_pairs={{32,0},{64,32},{96,64},{128,96},{160,128},{192,160},{224,192},{256... | collective-permute-start | bytes 552968 | tf_op jit(solution)/shard_map/ppermute | solution.py:109
  170.6 13.1 %collective-permute-start.21 = (bf16[10,72,128]{2,1,0:T(8,128)(2,1)S(1)}, bf16[10,72,128]{2,1,0:T(8,128)(2,1)S(1)}, u32[]{:S(2)}, u32[]{:S(2)}) collective-permute-start(bf16[10,72,128]{2,1,0:T(8,128)(2,1)S(1)} %get-tuple-element.25), channel_id=1, source_target_pairs={{0,32},{32,64},{64,96},{96,128},{128,160},{160,192},{192,224},{224... | collective-permute-start | bytes 552968 | tf_op jit(solution)/shard_map/ppermute | solution.py:109
  184.9 6.6 %collective-permute-start.22 = (bf16[8,72,128]{2,1,0:T(8,128)(2,1)S(1)}, bf16[8,72,128]{2,1,0:T(8,128)(2,1)S(1)}, u32[]{:S(2)}, u32[]{:S(2)}) collective-permute-start(bf16[8,72,128]{2,1,0:T(8,128)(2,1)S(1)} %get-tuple-element.27), channel_id=1, source_target_pairs={{32,0},{64,32},{96,64},{128,96},{160,128},{192,160},{224,192},{256... | collective-permute-start | bytes 442376 | tf_op jit(solution)/shard_map/ppermute | solution.py:109
  186.8 15.1 %collective-permute-start.23 = (bf16[8,72,128]{2,1,0:T(8,128)(2,1)S(1)}, bf16[8,72,128]{2,1,0:T(8,128)(2,1)S(1)}, u32[]{:S(2)}, u32[]{:S(2)}) collective-permute-start(bf16[8,72,128]{2,1,0:T(8,128)(2,1)S(1)} %get-tuple-element.28), channel_id=1, source_target_pairs={{0,32},{32,64},{64,96},{96,128},{128,160},{160,192},{192,224},{224... | collective-permute-start | bytes 442376 | tf_op jit(solution)/shard_map/ppermute | solution.py:109

commit v2 on v1

v2 whole, which is shorter than its diff:
```python
import functools

import jax
import jax.numpy as jnp
from jax import lax
from jax.experimental import pallas as pl
from jax.experimental.pallas import tpu as pltpu
from jax.sharding import PartitionSpec as P

F32, BF16 = jnp.float32, jnp.bfloat16
VMEM = pl.BlockSpec(memory_space=pltpu.VMEM)
SMEM = pl.BlockSpec(memory_space=pltpu.SMEM)
LIMIT = 24 * 1024 * 1024


def right_lanes(shape):
    return lax.broadcasted_iota(jnp.int32, shape, 1) < shape[1] // 2


def window_weights(table, which):
    weights = table[which]
    cols = weights.shape[1]
    reach = (weights.shape[0] - cols) // 2
    gap = jnp.zeros((cols - 2 * reach, cols), weights.dtype)
    return jnp.concatenate([weights[reach : reach + cols], weights[reach + cols :], gap, weights[:reach]], axis=0)


def forward_kernel(step, first, outs, fold, weighted, par, own, north, south, table, mix, *rest):
    obs, out = rest if weighted else (None, rest[0])
    shape = own.shape[1:]
    rightward = right_lanes(shape)
    blocks = []
    for p in range(outs):
        way, which = par[first + p, step], par[first + p, 4 + step]

        def pick(j):
            return jnp.where(way == 1, own[j], jnp.where(way == 0, north[j], south[j]))

        left = p - 1 if p > 0 else outs
        right = p + 1 if p < outs - 1 else outs
        edges = jnp.where(rightward, pick(right), pick(left))
        window = jnp.concatenate([pick(p), edges], axis=1)
        interp = jnp.dot(window, window_weights(table, which), preferred_element_type=F32).astype(BF16)
        mixed = jnp.dot(mix[step][:, : shape[0]], interp, preferred_element_type=F32).astype(BF16)
        if weighted:
            mixed = (obs[p].astype(F32) * mixed.astype(F32)).astype(BF16)
        if fold and p in (0, outs - 1):
            blocks.append(mixed)
        else:
            out[p - 1 if fold else p] = mixed
    if fold:
        out[outs - 2] = jnp.where(rightward, blocks[1], blocks[0])


def forward(step, outs, fold, par, rows, table, mix, obs=None):
    levels, cols = rows[0].shape[1:]
    first = (par.shape[0] - outs) // 2
    made = outs - 1 if fold else outs
    weighted = obs is not None
    args = (par, *rows, table, mix) + ((obs,) if weighted else ())
    return pl.pallas_call(
        functools.partial(forward_kernel, step, first, outs, fold, weighted),
        out_shape=jax.ShapeDtypeStruct((made, levels, cols), BF16),
        in_specs=[SMEM] + [VMEM] * (len(args) - 1),
        out_specs=VMEM,
        compiler_params=pltpu.CompilerParams(vmem_limit_bytes=LIMIT),
        cost_estimate=pl.CostEstimate(flops=outs * 6_000_000, bytes_accessed=2_000_000, transcendentals=0),
    )(*args)


def adjoint_kernel(step, first, reads, summed, par, *rest):
    parts, (table, mix, to_north, stay, to_south, total) = rest[: 3 if summed else 1], rest[3 if summed else 1 :]
    shape = parts[0].shape[1:]
    rightward = right_lanes(shape)
    nothing = jnp.zeros(shape, F32)
    for way in range(3):
        for p in range(reads):
            total[way, p] = nothing
    for p in range(reads):
        way, which = par[first + p, step], par[first + p, 4 + step]
        if summed:
            cot = (parts[0][p] + parts[1][p].astype(F32) + parts[2][p].astype(F32)).astype(BF16)
        else:
            cot = parts[0][p]
        back = lax.dot_general(mix[step][:, : shape[0]], cot, (((0,), (0,)), ((), ())), preferred_element_type=F32).astype(BF16)
        spread = lax.dot_general(back, window_weights(table, which), (((1,), (1,)), ((), ())), preferred_element_type=F32)
        main, edges = spread[:, : shape[1]], spread[:, shape[1] :]
        if 0 < p < reads - 1:
            total[way, p] += main
        if p < reads - 2:
            total[way, p + 1] += jnp.where(rightward, edges, nothing)
        if p > 1:
            total[way, p - 1] += jnp.where(rightward, nothing, edges)
    for p in range(1, reads - 1):
        to_north[p - 1] = total[0, p].astype(BF16)
        stay[p - 1] = total[1, p]
        to_south[p - 1] = total[2, p].astype(BF16)


def adjoint(step, par, parts, table, mix):
    reads, levels, cols = parts[0].shape
    first = (par.shape[0] - reads) // 2
    gives = (reads - 2, levels, cols)
    return pl.pallas_call(
        functools.partial(adjoint_kernel, step, first, reads, len(parts) == 3),
        out_shape=[jax.ShapeDtypeStruct(gives, BF16), jax.ShapeDtypeStruct(gives, F32), jax.ShapeDtypeStruct(gives, BF16)],
        in_specs=[SMEM] + [VMEM] * (len(parts) + 2),
        out_specs=[VMEM] * 3,
        scratch_shapes=[pltpu.VMEM((3, reads, levels, cols), F32)],
        compiler_params=pltpu.CompilerParams(vmem_limit_bytes=LIMIT),
        cost_estimate=pl.CostEstimate(flops=reads * 6_000_000, bytes_accessed=2_000_000, transcendentals=0),
    )(par, *parts, table, mix)


def homes():
    half, run = lax.axis_size("lat") // 2, 8
    rows, blocks = lax.axis_size("lat"), lax.axis_size("lon")

    def home(row, block):
        upper, z = divmod(row, half)
        column, slot = divmod(block, run)
        y, core = divmod(slot, 2)
        return (core * half + z - z % 2 + upper) * blocks + column * run + y * 2 + z % 2

    return rows, blocks, home


def move(value, pairs):
    return lax.ppermute(value, ("lat", "lon"), pairs)


def go_home(value, back=False):
    rows, blocks, home = homes()
    pairs = [(r * blocks + b, home(r, b)) for r in range(rows) for b in range(blocks)]
    return move(value, [(t, s) for s, t in pairs] if back else pairs)


def from_lat(value, by):
    rows, blocks, home = homes()
    return move(value, [(home(r, b), home(r - by, b)) for r in range(rows) for b in range(blocks) if 0 <= r - by < rows])


def from_lon(value, by):
    rows, blocks, home = homes()
    return move(value, [(home(r, b), home(r, (b - by) % blocks)) for r in range(rows) for b in range(blocks)])


def exchange(value, run):
    rows, blocks, home = homes()
    groups = [[home(r, b + j) for j in range(run)] for r in range(rows) for b in range(0, blocks, run)]
    return lax.all_to_all(value, ("lat", "lon"), 0, 0, axis_index_groups=groups)


def on_device(vector, obs_weight, departures, weight_index, interp_table, column_mix):
    run, levels, _, cols = vector.shape
    numbers = jnp.concatenate([departures.reshape(-1), weight_index.reshape(-1)]).astype(BF16)
    count = numbers.shape[0]
    tail = jnp.concatenate([jnp.broadcast_to(numbers[:, None], (count, cols)), jnp.zeros((16 - count, cols), BF16)])
    mix = jnp.pad(column_mix[:, 0], ((0, 0), (0, 0), (0, cols - levels)))
    steps = mix.shape[0]
    sent = jnp.concatenate([vector.reshape(-1, cols), mix.reshape(-1, cols), obs_weight[:, 0].astype(BF16), tail])
    sent = go_home(sent)
    mix = sent[run * levels : (run + steps) * levels].reshape(steps, levels, cols)
    shared = sent[(run + steps) * levels :]
    bundle = jnp.concatenate(
        [sent[: run * levels].reshape(run, levels, cols), jnp.broadcast_to(shared[None], (run, *shared.shape))], axis=1
    )
    bundle = exchange(bundle, run)
    state, obs = bundle[:, :levels], bundle[:, levels : 2 * levels]
    west, east = from_lon(bundle[-2:], -run), from_lon(bundle[:2], run)

    def read(part):
        return jnp.max(part[:, 2 * levels : 2 * levels + count].astype(F32), axis=2).astype(jnp.int32)

    par = jnp.concatenate([read(west), read(bundle), read(east)])
    west, east = west[:, :levels], east[:, :levels]

    for step in range(0, 4, 2):
        if step > 0:
            west, east = from_lon(state[-2:], -run), from_lon(state[:2], run)
        rightward = right_lanes((levels, cols))
        outer = jnp.where(rightward, east[1], west[0])
        wide = jnp.concatenate([west[1:], state, east[:1], outer[None]])
        wide = forward(step, run + 2, True, par, (wide, from_lat(wide, -1), from_lat(wide, 1)), interp_table, mix)
        state = forward(
            step + 1, run, False, par, (wide, from_lat(wide, -1), from_lat(wide, 1)), interp_table, mix,
            obs if step == 2 else None,
        )

    cot = state
    for step in (3, 1):
        west, east = from_lon(cot[-2:], -run), from_lon(cot[:2], run)
        wide = jnp.concatenate([west, cot, east])
        north, stay, south = adjoint(step, par, (wide,), interp_table, mix)
        parts = (stay, from_lat(north, 1), from_lat(south, -1))
        north, stay, south = adjoint(step - 1, par, parts, interp_table, mix)
        cot = (stay + from_lat(north, 1).astype(F32) + from_lat(south, -1).astype(F32)).astype(BF16)
    return go_home(exchange(cot, run), back=True)[:, :, None]


def solution(mesh):
    placed = (
        P(None, None, "lat", "lon"),
        P(None, "lat", "lon"),
        P(None, "lat", "lon"),
        P(None, "lat", "lon"),
        P(),
        P(None, "lat", None, None),
    )
    return jax.shard_map(
        on_device, mesh=mesh, in_specs=placed, out_specs=P(None, None, "lat", "lon"), check_vma=False
    )
```

time: 229 us -> 222 us (0.969)
  the two profiles are of different devices: /device:TPU:63 before, /device:TPU:1 now
where the time goes in v2:
time: 222 us; the launch traced here: 219 us
  starting transfers between devices  144 us (65%)
  waiting for transfers between devices  45.2 us (20%)
  Pallas kernels  12 us (5%)
  blocking collectives  11.8 us (5%)
  local copies, waits for them, and re-layouts  3.44 us (2%)
    ppermute x26, starting transfers between devices, move(): return lax.ppermute(value, ('lat', 'lon'), pairs)  138 us
    ppermute x26, waiting for transfers between devices, move(): return lax.ppermute(value, ('lat', 'lon'), pairs)  37.9 us
    all_to_all x1, blocking collectives, exchange(): return lax.all_to_all(value, ('lat', 'lon'), 0, 0, axis_index_groups=groups)  11.8 us
    all_to_all x1, waiting for transfers between devices, exchange(): return lax.all_to_all(value, ('lat', 'lon'), 0, 0, axis_index_groups=groups)  7.29 us
    pallas_call x4, Pallas kernels, adjoint(): pl.pallas_call(functools.partial(adjoint_kernel, step, first, reads, len(...  6.92 us
    all_to_all x1, starting transfers between devices, exchange(): return lax.all_to_all(value, ('lat', 'lon'), 0, 0, axis_index_groups=groups)  5.51 us
    pallas_call x4, Pallas kernels, forward(): pl.pallas_call(functools.partial(forward_kernel, step, first, outs, fold,...  5.08 us
  transfers between devices with their start and end apart: 27, of which 23 were waited for; matrix products, arithmetic and copies ran while one was open for 0% of the time, Pallas kernels for 0%

profile of v2, /device:TPU:1, one launch (start us, length us, event | category | flops | bytes accessed | tf_op | source)
XLA Modules:
  0.0 218.9 jit_solution(15654552816880788288)
XLA Ops:
  2.1 8.8 %collective-permute-start = (bf16[952,128]{1,0:T(8,128)(2,1)S(1)}, bf16[952,128]{1,0:T(8,128)(2,1)S(1)}, u32[]{:S(2)}, u32[]{:S(2)}) collective-permute-start(bf16[952,128]{1,0:T(8,128)(2,1)S(1)} %constant_dynamic-update-slice_fusion), channel_id=1, source_target_pairs={{0,0},{1,512},{2,2},{3,514},{4,4},{5,516},{6,6},{7,518},{8,8},{9,5... | collective-permute-start | bytes 731144 | tf_op jit(solution)/shard_map/ppermute | solution.py:129
  10.9 7.7 %collective-permute-done = bf16[952,128]{1,0:T(8,128)(2,1)S(1)} collective-permute-done((bf16[952,128]{1,0:T(8,128)(2,1)S(1)}, bf16[952,128]{1,0:T(8,128)(2,1)S(1)}, u32[]{:S(2)}, u32[]{:S(2)}) %collective-permute-start) | collective-permute-done | bytes 243744 | tf_op jit(solution)/shard_map/ppermute | solution.py:129
  21.0 5.5 %all-to-all-start = ((bf16[8,160,128]{2,1,0:T(8,128)(2,1)}), bf16[8,160,128]{2,1,0:T(8,128)(2,1)S(1)}, u32[]{:S(2)}, u32[]{:S(2)}) async-start(bf16[8,160,128]{2,1,0:T(8,128)(2,1)} %pad_maximum_fusion), calls=%async_computation | async-start | bytes 655360 | tf_op jit(solution)/shard_map/all_to_all | solution.py:151
  26.5 7.3 %all-to-all-done = bf16[8,160,128]{2,1,0:T(8,128)(2,1)S(1)} async-done(((bf16[8,160,128]{2,1,0:T(8,128)(2,1)}), bf16[8,160,128]{2,1,0:T(8,128)(2,1)S(1)}, u32[]{:S(2)}, u32[]{:S(2)}) %all-to-all-start) | async-done | bytes 327712 | tf_op jit(solution)/shard_map/all_to_all | solution.py:151
  33.8 3.3 %collective-permute-start.1 = (bf16[2,160,128]{2,1,0:T(8,128)(2,1)S(1)}, bf16[2,160,128]{2,1,0:T(8,128)(2,1)S(1)}, u32[]{:S(2)}, u32[]{:S(2)}) collective-permute-start(bf16[2,160,128]{2,1,0:T(8,128)(2,1)S(1)} %get-tuple-element.31), channel_id=1, source_target_pairs={{0,8},{512,520},{2,10},{514,522},{4,12},{516,524},{6,14},{518,526}... | collective-permute-start | bytes 245768 | tf_op jit(solution)/shard_map/ppermute | solution.py:129
  37.1 3.4 %collective-permute-start.2 = (bf16[2,160,128]{2,1,0:T(8,128)(2,1)S(1)}, bf16[2,160,128]{2,1,0:T(8,128)(2,1)S(1)}, u32[]{:S(2)}, u32[]{:S(2)}) collective-permute-start(bf16[2,160,128]{2,1,0:T(8,128)(2,1)S(1)} %get-tuple-element.32), channel_id=1, source_target_pairs={{0,24},{512,536},{2,26},{514,538},{4,28},{516,540},{6,30},{518,542... | collective-permute-start | bytes 245768 | tf_op jit(solution)/shard_map/ppermute | solution.py:129
  40.6 1.7 collective-permute-done.2
  42.3 9.5 %collective-permute-start.4 = (bf16[11,72,128]{2,1,0:T(8,128)(2,1)S(1)}, bf16[11,72,128]{2,1,0:T(8,128)(2,1)S(1)}, u32[]{:S(2)}, u32[]{:S(2)}) collective-permute-start(bf16[11,72,128]{2,1,0:T(8,128)(2,1)S(1)} %pad_maximum_fusion.3.own), channel_id=1, source_target_pairs={{1,0},{513,512},{3,2},{515,514},{5,4},{517,516},{7,6},{519,518},{9... | collective-permute-start | bytes 608264 | tf_op jit(solution)/shard_map/ppermute | solution.py:129
  51.8 5.7 %collective-permute-start.3 = (bf16[11,72,128]{2,1,0:T(8,128)(2,1)S(1)}, bf16[11,72,128]{2,1,0:T(8,128)(2,1)S(1)}, u32[]{:S(2)}, u32[]{:S(2)}) collective-permute-start(bf16[11,72,128]{2,1,0:T(8,128)(2,1)S(1)} %pad_maximum_fusion.3.own), channel_id=1, source_target_pairs={{0,1},{512,513},{2,3},{514,515},{4,5},{516,517},{6,7},{518,519},{8... | collective-permute-start | bytes 608264 | tf_op jit(solution)/shard_map/ppermute | solution.py:129
  57.7 1.3 collective-permute-done.4.south
  60.2 1.3 shard_map.64.own
  61.5 1.9 collective-permute-start.6
  63.4 5.3 %collective-permute-start.5 = (bf16[9,72,128]{2,1,0:T(8,128)(2,1)S(1)}, bf16[9,72,128]{2,1,0:T(8,128)(2,1)S(1)}, u32[]{:S(2)}, u32[]{:S(2)}) collective-permute-start(bf16[9,72,128]{2,1,0:T(8,128)(2,1)S(1)} %shard_map.64.own), channel_id=1, source_target_pairs={{0,1},{512,513},{2,3},{514,515},{4,5},{516,517},{6,7},{518,519},{8... | collective-permute-start | bytes 497672 | tf_op jit(solution)/shard_map/ppermute | solution.py:129
  69.8 1.3 collective-permute-done.5.north
  71.1 1.2 shard_map.65
  72.3 4.6 %collective-permute-start.8 = (bf16[2,72,128]{2,1,0:T(8,128)(2,1)S(1)}, bf16[2,72,128]{2,1,0:T(8,128)(2,1)S(1)}, u32[]{:S(2)}, u32[]{:S(2)}) collective-permute-start(bf16[2,72,128]{2,1,0:T(8,128)(2,1)S(1)} %get-tuple-element.37), channel_id=1, source_target_pairs={{0,24},{512,536},{2,26},{514,538},{4,28},{516,540},{6,30},{518,542... | collective-permute-start | bytes 110600 | tf_op jit(solution)/shard_map/ppermute | solution.py:129
  76.9 1.9 collective-permute-start.7
  78.8 4.0 %collective-permute-done.7 = bf16[2,72,128]{2,1,0:T(8,128)(2,1)S(1)} collective-permute-done((bf16[2,72,128]{2,1,0:T(8,128)(2,1)S(1)}, bf16[2,72,128]{2,1,0:T(8,128)(2,1)S(1)}, u32[]{:S(2)}, u32[]{:S(2)}) %collective-permute-start.7) | collective-permute-done | bytes 36896 | tf_op jit(solution)/shard_map/ppermute | solution.py:129
  82.9 1.9 collective-permute-start.10
  84.8 9.1 %collective-permute-start.9 = (bf16[11,72,128]{2,1,0:T(8,128)(2,1)S(1)}, bf16[11,72,128]{2,1,0:T(8,128)(2,1)S(1)}, u32[]{:S(2)}, u32[]{:S(2)}) collective-permute-start(bf16[11,72,128]{2,1,0:T(8,128)(2,1)S(1)} %pad_maximum_fusion.4.own), channel_id=1, source_target_pairs={{0,1},{512,513},{2,3},{514,515},{4,5},{516,517},{6,7},{518,519},{8... | collective-permute-start | bytes 608264 | tf_op jit(solution)/shard_map/ppermute | solution.py:129
  93.9 1.5 collective-permute-done.10.south
  96.6 1.3 shard_map.66.own
  97.9 1.9 collective-permute-start.12
  99.8 5.3 %collective-permute-start.11 = (bf16[9,72,128]{2,1,0:T(8,128)(2,1)S(1)}, bf16[9,72,128]{2,1,0:T(8,128)(2,1)S(1)}, u32[]{:S(2)}, u32[]{:S(2)}) collective-permute-start(bf16[9,72,128]{2,1,0:T(8,128)(2,1)S(1)} %shard_map.66.own), channel_id=1, source_target_pairs={{0,1},{512,513},{2,3},{514,515},{4,5},{516,517},{6,7},{518,519},{8... | collective-permute-start | bytes 497672 | tf_op jit(solution)/shard_map/ppermute | solution.py:129
  105.1 1.4 collective-permute-done.12.south
  107.4 1.3 shard_map.67
  108.7 1.9 collective-permute-start.13
  110.6 4.6 %collective-permute-start.14 = (bf16[2,72,128]{2,1,0:T(8,128)(2,1)S(1)}, bf16[2,72,128]{2,1,0:T(8,128)(2,1)S(1)}, u32[]{:S(2)}, u32[]{:S(2)}) collective-permute-start(bf16[2,72,128]{2,1,0:T(8,128)(2,1)S(1)} %get-tuple-element.36), channel_id=1, source_target_pairs={{0,24},{512,536},{2,26},{514,538},{4,28},{516,540},{6,30},{518,542... | collective-permute-start | bytes 110600 | tf_op jit(solution)/shard_map/ppermute | solution.py:129
  116.3 1.8 shard_map.68
  118.1 1.9 collective-permute-start.15
  120.0 6.5 %collective-permute-start.16 = (bf16[10,72,128]{2,1,0:T(8,128)(2,1)S(1)}, bf16[10,72,128]{2,1,0:T(8,128)(2,1)S(1)}, u32[]{:S(2)}, u32[]{:S(2)}) collective-permute-start(bf16[10,72,128]{2,1,0:T(8,128)(2,1)S(1)} %get-tuple-element.19), channel_id=1, source_target_pairs={{0,1},{512,513},{2,3},{514,515},{4,5},{516,517},{6,7},{518,519},{8... | collective-permute-start | bytes 552968 | tf_op jit(solution)/shard_map/ppermute | solution.py:129
  126.5 1.3 collective-permute-done.15.rest_1_
  128.9 1.7 shard_map.69
  130.6 1.9 collective-permute-start.17
  132.5 5.3 %collective-permute-start.18 = (bf16[8,72,128]{2,1,0:T(8,128)(2,1)S(1)}, bf16[8,72,128]{2,1,0:T(8,128)(2,1)S(1)}, u32[]{:S(2)}, u32[]{:S(2)}) collective-permute-start(bf16[8,72,128]{2,1,0:T(8,128)(2,1)S(1)} %get-tuple-element.22), channel_id=1, source_target_pairs={{0,1},{512,513},{2,3},{514,515},{4,5},{516,517},{6,7},{518,519},{8... | collective-permute-start | bytes 442376 | tf_op jit(solution)/shard_map/ppermute | solution.py:129
  140.0 1.9 collective-permute-start.19
  141.9 5.2 %collective-permute-start.20 = (bf16[2,72,128]{2,1,0:T(8,128)(2,1)S(1)}, bf16[2,72,128]{2,1,0:T(8,128)(2,1)S(1)}, u32[]{:S(2)}, u32[]{:S(2)}) collective-permute-start(bf16[2,72,128]{2,1,0:T(8,128)(2,1)S(1)} %get-tuple-element.34), channel_id=1, source_target_pairs={{0,24},{512,536},{2,26},{514,538},{4,28},{516,540},{6,30},{518,542... | collective-permute-start | bytes 110600 | tf_op jit(solution)/shard_map/ppermute | solution.py:129
  148.2 1.8 shard_map.70
  150.0 1.9 collective-permute-start.21
  151.9 6.1 %collective-permute-start.22 = (bf16[10,72,128]{2,1,0:T(8,128)(2,1)S(1)}, bf16[10,72,128]{2,1,0:T(8,128)(2,1)S(1)}, u32[]{:S(2)}, u32[]{:S(2)}) collective-permute-start(bf16[10,72,128]{2,1,0:T(8,128)(2,1)S(1)} %get-tuple-element.25), channel_id=1, source_target_pairs={{0,1},{512,513},{2,3},{514,515},{4,5},{516,517},{6,7},{518,519},{8... | collective-permute-start | bytes 552968 | tf_op jit(solution)/shard_map/ppermute | solution.py:129
  158.0 1.3 collective-permute-done.21.rest_1_
  159.3 2.8 %collective-permute-done.22.rest_2_ = bf16[10,72,128]{2,1,0:T(8,128)(2,1)S(1)} collective-permute-done((bf16[10,72,128]{2,1,0:T(8,128)(2,1)S(1)}, bf16[10,72,128]{2,1,0:T(8,128)(2,1)S(1)}, u32[]{:S(2)}, u32[]{:S(2)}) %collective-permute-start.22) | collective-permute-done | bytes 184352 | tf_op jit(solution)/shard_map/ppermute | solution.py:129
  162.1 1.6 shard_map.71
  163.7 1.9 collective-permute-start.23
  165.7 5.3 %collective-permute-start.24 = (bf16[8,72,128]{2,1,0:T(8,128)(2,1)S(1)}, bf16[8,72,128]{2,1,0:T(8,128)(2,1)S(1)}, u32[]{:S(2)}, u32[]{:S(2)}) collective-permute-start(bf16[8,72,128]{2,1,0:T(8,128)(2,1)S(1)} %get-tuple-element.28), channel_id=1, source_target_pairs={{0,1},{512,513},{2,3},{514,515},{4,5},{516,517},{6,7},{518,519},{8... | collective-permute-start | bytes 442376 | tf_op jit(solution)/shard_map/ppermute | solution.py:129
  173.1 11.8 %all_to_all.10 = bf16[8,72,128]{2,1,0:T(8,128)(2,1)S(1)} all-to-all(bf16[8,72,128]{2,1,0:T(8,128)(2,1)S(1)} %add_convert_fusion), channel_id=1, replica_groups={{0,512,2,514,4,516,6,518},{8,520,10,522,12,524,14,526},{16,528,18,530,2..., dimensions={0} | all-to-all | bytes 294912 | tf_op jit(solution)/shard_map/all_to_all | solution.py:151
  184.9 31.3 %collective-permute-start.25 = (bf16[8,72,128]{2,1,0:T(8,128)(2,1)S(1)}, bf16[8,72,128]{2,1,0:T(8,128)(2,1)S(1)}, u32[]{:S(2)}, u32[]{:S(2)}) collective-permute-start(bf16[8,72,128]{2,1,0:T(8,128)(2,1)S(1)} %all_to_all.10), channel_id=1, source_target_pairs={{0,0},{512,1},{2,2},{514,3},{4,4},{516,5},{6,6},{518,7},{8,8},{520... | collective-permute-start | bytes 442376 | tf_op jit(solution)/shard_map/ppermute | solution.py:129
  216.2 2.1 collective-permute-done.25
  (64 shorter events, 17.3 us)
Async XLA Ops:
  0.8 1.0 copy-start.4
  0.8 1.0 copy-start.5
  0.8 1.1 copy-start.3
  2.1 16.6 %collective-permute-start = (bf16[952,128]{1,0:T(8,128)(2,1)S(1)}, bf16[952,128]{1,0:T(8,128)(2,1)S(1)}, u32[]{:S(2)}, u32[]{:S(2)}) collective-permute-start(bf16[952,128]{1,0:T(8,128)(2,1)S(1)} %constant_dynamic-update-slice_fusion), channel_id=1, source_target_pairs={{0,0},{1,512},{2,2},{3,514},{4,4},{5,516},{6,6},{7,518},{8,8},{9,5... | collective-permute-start | bytes 731144 | tf_op jit(solution)/shard_map/ppermute | solution.py:129
  18.6 0.7 copy-start.1
  19.3 0.9 slice-start
  21.0 5.5 %copy-start.2 = (bf16[952,128]{1,0:T(8,128)(2,1)S(1)}, bf16[952,128]{1,0:T(8,128)(2,1)}, u32[]{:S(2)}) copy-start(bf16[952,128]{1,0:T(8,128)(2,1)} %copy-done.1) | copy-start | bytes 731140
  21.0 12.8 %all-to-all-start = ((bf16[8,160,128]{2,1,0:T(8,128)(2,1)}), bf16[8,160,128]{2,1,0:T(8,128)(2,1)S(1)}, u32[]{:S(2)}, u32[]{:S(2)}) async-start(bf16[8,160,128]{2,1,0:T(8,128)(2,1)} %pad_maximum_fusion), calls=%async_computation | async-start | bytes 655360 | tf_op jit(solution)/shard_map/all_to_all | solution.py:151
  33.8 26.4 %copy-start = (bf16[16,160,128]{2,1,0:T(8,128)(2,1)S(1)}, bf16[16,160,128]{2,1,0:T(8,128)(2,1)}, u32[]{:S(2)}) copy-start(bf16[16,160,128]{2,1,0:T(8,128)(2,1)} %rest_3_.3) | copy-start | bytes 1966084
  33.8 6.8 %collective-permute-start.1 = (bf16[2,160,128]{2,1,0:T(8,128)(2,1)S(1)}, bf16[2,160,128]{2,1,0:T(8,128)(2,1)S(1)}, u32[]{:S(2)}, u32[]{:S(2)}) collective-permute-start(bf16[2,160,128]{2,1,0:T(8,128)(2,1)S(1)} %get-tuple-element.31), channel_id=1, source_target_pairs={{0,8},{512,520},{2,10},{514,522},{4,12},{516,524},{6,14},{518,526}... | collective-permute-start | bytes 245768 | tf_op jit(solution)/shard_map/ppermute | solution.py:129
  37.1 5.2 %collective-permute-start.2 = (bf16[2,160,128]{2,1,0:T(8,128)(2,1)S(1)}, bf16[2,160,128]{2,1,0:T(8,128)(2,1)S(1)}, u32[]{:S(2)}, u32[]{:S(2)}) collective-permute-start(bf16[2,160,128]{2,1,0:T(8,128)(2,1)S(1)} %get-tuple-element.32), channel_id=1, source_target_pairs={{0,24},{512,536},{2,26},{514,538},{4,28},{516,540},{6,30},{518,542... | collective-permute-start | bytes 245768 | tf_op jit(solution)/shard_map/ppermute | solution.py:129
  42.3 16.7 %collective-permute-start.4 = (bf16[11,72,128]{2,1,0:T(8,128)(2,1)S(1)}, bf16[11,72,128]{2,1,0:T(8,128)(2,1)S(1)}, u32[]{:S(2)}, u32[]{:S(2)}) collective-permute-start(bf16[11,72,128]{2,1,0:T(8,128)(2,1)S(1)} %pad_maximum_fusion.3.own), channel_id=1, source_target_pairs={{1,0},{513,512},{3,2},{515,514},{5,4},{517,516},{7,6},{519,518},{9... | collective-permute-start | bytes 608264 | tf_op jit(solution)/shard_map/ppermute | solution.py:129
  51.8 8.4 %collective-permute-start.3 = (bf16[11,72,128]{2,1,0:T(8,128)(2,1)S(1)}, bf16[11,72,128]{2,1,0:T(8,128)(2,1)S(1)}, u32[]{:S(2)}, u32[]{:S(2)}) collective-permute-start(bf16[11,72,128]{2,1,0:T(8,128)(2,1)S(1)} %pad_maximum_fusion.3.own), channel_id=1, source_target_pairs={{0,1},{512,513},{2,3},{514,515},{4,5},{516,517},{6,7},{518,519},{8... | collective-permute-start | bytes 608264 | tf_op jit(solution)/shard_map/ppermute | solution.py:129
  61.5 8.3 %collective-permute-start.6 = (bf16[9,72,128]{2,1,0:T(8,128)(2,1)S(1)}, bf16[9,72,128]{2,1,0:T(8,128)(2,1)S(1)}, u32[]{:S(2)}, u32[]{:S(2)}) collective-permute-start(bf16[9,72,128]{2,1,0:T(8,128)(2,1)S(1)} %shard_map.64.own), channel_id=1, source_target_pairs={{1,0},{513,512},{3,2},{515,514},{5,4},{517,516},{7,6},{519,518},{9... | collective-permute-start | bytes 497672 | tf_op jit(solution)/shard_map/ppermute | solution.py:129
  63.4 7.7 %collective-permute-start.5 = (bf16[9,72,128]{2,1,0:T(8,128)(2,1)S(1)}, bf16[9,72,128]{2,1,0:T(8,128)(2,1)S(1)}, u32[]{:S(2)}, u32[]{:S(2)}) collective-permute-start(bf16[9,72,128]{2,1,0:T(8,128)(2,1)S(1)} %shard_map.64.own), channel_id=1, source_target_pairs={{0,1},{512,513},{2,3},{514,515},{4,5},{516,517},{6,7},{518,519},{8... | collective-permute-start | bytes 497672 | tf_op jit(solution)/shard_map/ppermute | solution.py:129
  72.3 6.5 %collective-permute-start.8 = (bf16[2,72,128]{2,1,0:T(8,128)(2,1)S(1)}, bf16[2,72,128]{2,1,0:T(8,128)(2,1)S(1)}, u32[]{:S(2)}, u32[]{:S(2)}) collective-permute-start(bf16[2,72,128]{2,1,0:T(8,128)(2,1)S(1)} %get-tuple-element.37), channel_id=1, source_target_pairs={{0,24},{512,536},{2,26},{514,538},{4,28},{516,540},{6,30},{518,542... | collective-permute-start | bytes 110600 | tf_op jit(solution)/shard_map/ppermute | solution.py:129
  76.9 5.9 %collective-permute-start.7 = (bf16[2,72,128]{2,1,0:T(8,128)(2,1)S(1)}, bf16[2,72,128]{2,1,0:T(8,128)(2,1)S(1)}, u32[]{:S(2)}, u32[]{:S(2)}) collective-permute-start(bf16[2,72,128]{2,1,0:T(8,128)(2,1)S(1)} %get-tuple-element.38), channel_id=1, source_target_pairs={{0,8},{512,520},{2,10},{514,522},{4,12},{516,524},{6,14},{518,526}... | collective-permute-start | bytes 110600 | tf_op jit(solution)/shard_map/ppermute | solution.py:129
  82.9 12.5 %collective-permute-start.10 = (bf16[11,72,128]{2,1,0:T(8,128)(2,1)S(1)}, bf16[11,72,128]{2,1,0:T(8,128)(2,1)S(1)}, u32[]{:S(2)}, u32[]{:S(2)}) collective-permute-start(bf16[11,72,128]{2,1,0:T(8,128)(2,1)S(1)} %pad_maximum_fusion.4.own), channel_id=1, source_target_pairs={{1,0},{513,512},{3,2},{515,514},{5,4},{517,516},{7,6},{519,518},{9... | collective-permute-start | bytes 608264 | tf_op jit(solution)/shard_map/ppermute | solution.py:129
  84.8 11.8 %collective-permute-start.9 = (bf16[11,72,128]{2,1,0:T(8,128)(2,1)S(1)}, bf16[11,72,128]{2,1,0:T(8,128)(2,1)S(1)}, u32[]{:S(2)}, u32[]{:S(2)}) collective-permute-start(bf16[11,72,128]{2,1,0:T(8,128)(2,1)S(1)} %pad_maximum_fusion.4.own), channel_id=1, source_target_pairs={{0,1},{512,513},{2,3},{514,515},{4,5},{516,517},{6,7},{518,519},{8... | collective-permute-start | bytes 608264 | tf_op jit(solution)/shard_map/ppermute | solution.py:129
  97.9 8.7 %collective-permute-start.12 = (bf16[9,72,128]{2,1,0:T(8,128)(2,1)S(1)}, bf16[9,72,128]{2,1,0:T(8,128)(2,1)S(1)}, u32[]{:S(2)}, u32[]{:S(2)}) collective-permute-start(bf16[9,72,128]{2,1,0:T(8,128)(2,1)S(1)} %shard_map.66.own), channel_id=1, source_target_pairs={{1,0},{513,512},{3,2},{515,514},{5,4},{517,516},{7,6},{519,518},{9... | collective-permute-start | bytes 497672 | tf_op jit(solution)/shard_map/ppermute | solution.py:129
  99.8 7.6 %collective-permute-start.11 = (bf16[9,72,128]{2,1,0:T(8,128)(2,1)S(1)}, bf16[9,72,128]{2,1,0:T(8,128)(2,1)S(1)}, u32[]{:S(2)}, u32[]{:S(2)}) collective-permute-start(bf16[9,72,128]{2,1,0:T(8,128)(2,1)S(1)} %shard_map.66.own), channel_id=1, source_target_pairs={{0,1},{512,513},{2,3},{514,515},{4,5},{516,517},{6,7},{518,519},{8... | collective-permute-start | bytes 497672 | tf_op jit(solution)/shard_map/ppermute | solution.py:129
  108.7 6.5 %collective-permute-start.13 = (bf16[2,72,128]{2,1,0:T(8,128)(2,1)S(1)}, bf16[2,72,128]{2,1,0:T(8,128)(2,1)S(1)}, u32[]{:S(2)}, u32[]{:S(2)}) collective-permute-start(bf16[2,72,128]{2,1,0:T(8,128)(2,1)S(1)} %get-tuple-element.35), channel_id=1, source_target_pairs={{0,8},{512,520},{2,10},{514,522},{4,12},{516,524},{6,14},{518,526}... | collective-permute-start | bytes 110600 | tf_op jit(solution)/shard_map/ppermute | solution.py:129
  110.6 5.6 %collective-permute-start.14 = (bf16[2,72,128]{2,1,0:T(8,128)(2,1)S(1)}, bf16[2,72,128]{2,1,0:T(8,128)(2,1)S(1)}, u32[]{:S(2)}, u32[]{:S(2)}) collective-permute-start(bf16[2,72,128]{2,1,0:T(8,128)(2,1)S(1)} %get-tuple-element.36), channel_id=1, source_target_pairs={{0,24},{512,536},{2,26},{514,538},{4,28},{516,540},{6,30},{518,542... | collective-permute-start | bytes 110600 | tf_op jit(solution)/shard_map/ppermute | solution.py:129
  118.1 9.7 %collective-permute-start.15 = (bf16[10,72,128]{2,1,0:T(8,128)(2,1)S(1)}, bf16[10,72,128]{2,1,0:T(8,128)(2,1)S(1)}, u32[]{:S(2)}, u32[]{:S(2)}) collective-permute-start(bf16[10,72,128]{2,1,0:T(8,128)(2,1)S(1)} %get-tuple-element.18), channel_id=1, source_target_pairs={{1,0},{513,512},{3,2},{515,514},{5,4},{517,516},{7,6},{519,518},{9... | collective-permute-start | bytes 552968 | tf_op jit(solution)/shard_map/ppermute | solution.py:129
  120.0 8.9 %collective-permute-start.16 = (bf16[10,72,128]{2,1,0:T(8,128)(2,1)S(1)}, bf16[10,72,128]{2,1,0:T(8,128)(2,1)S(1)}, u32[]{:S(2)}, u32[]{:S(2)}) collective-permute-start(bf16[10,72,128]{2,1,0:T(8,128)(2,1)S(1)} %get-tuple-element.19), channel_id=1, source_target_pairs={{0,1},{512,513},{2,3},{514,515},{4,5},{516,517},{6,7},{518,519},{8... | collective-permute-start | bytes 552968 | tf_op jit(solution)/shard_map/ppermute | solution.py:129
  130.6 8.1 %collective-permute-start.17 = (bf16[8,72,128]{2,1,0:T(8,128)(2,1)S(1)}, bf16[8,72,128]{2,1,0:T(8,128)(2,1)S(1)}, u32[]{:S(2)}, u32[]{:S(2)}) collective-permute-start(bf16[8,72,128]{2,1,0:T(8,128)(2,1)S(1)} %get-tuple-element.21), channel_id=1, source_target_pairs={{1,0},{513,512},{3,2},{515,514},{5,4},{517,516},{7,6},{519,518},{9... | collective-permute-start | bytes 442376 | tf_op jit(solution)/shard_map/ppermute | solution.py:129
  132.5 7.4 %collective-permute-start.18 = (bf16[8,72,128]{2,1,0:T(8,128)(2,1)S(1)}, bf16[8,72,128]{2,1,0:T(8,128)(2,1)S(1)}, u32[]{:S(2)}, u32[]{:S(2)}) collective-permute-start(bf16[8,72,128]{2,1,0:T(8,128)(2,1)S(1)} %get-tuple-element.22), channel_id=1, source_target_pairs={{0,1},{512,513},{2,3},{514,515},{4,5},{516,517},{6,7},{518,519},{8... | collective-permute-start | bytes 442376 | tf_op jit(solution)/shard_map/ppermute | solution.py:129
  140.0 7.1 %collective-permute-start.19 = (bf16[2,72,128]{2,1,0:T(8,128)(2,1)S(1)}, bf16[2,72,128]{2,1,0:T(8,128)(2,1)S(1)}, u32[]{:S(2)}, u32[]{:S(2)}) collective-permute-start(bf16[2,72,128]{2,1,0:T(8,128)(2,1)S(1)} %get-tuple-element.33), channel_id=1, source_target_pairs={{0,8},{512,520},{2,10},{514,522},{4,12},{516,524},{6,14},{518,526}... | collective-permute-start | bytes 110600 | tf_op jit(solution)/shard_map/ppermute | solution.py:129
  141.9 6.2 %collective-permute-start.20 = (bf16[2,72,128]{2,1,0:T(8,128)(2,1)S(1)}, bf16[2,72,128]{2,1,0:T(8,128)(2,1)S(1)}, u32[]{:S(2)}, u32[]{:S(2)}) collective-permute-start(bf16[2,72,128]{2,1,0:T(8,128)(2,1)S(1)} %get-tuple-element.34), channel_id=1, source_target_pairs={{0,24},{512,536},{2,26},{514,538},{4,28},{516,540},{6,30},{518,542... | collective-permute-start | bytes 110600 | tf_op jit(solution)/shard_map/ppermute | solution.py:129
  150.0 9.3 %collective-permute-start.21 = (bf16[10,72,128]{2,1,0:T(8,128)(2,1)S(1)}, bf16[10,72,128]{2,1,0:T(8,128)(2,1)S(1)}, u32[]{:S(2)}, u32[]{:S(2)}) collective-permute-start(bf16[10,72,128]{2,1,0:T(8,128)(2,1)S(1)} %get-tuple-element.24), channel_id=1, source_target_pairs={{1,0},{513,512},{3,2},{515,514},{5,4},{517,516},{7,6},{519,518},{9... | collective-permute-start | bytes 552968 | tf_op jit(solution)/shard_map/ppermute | solution.py:129
  151.9 10.2 %collective-permute-start.22 = (bf16[10,72,128]{2,1,0:T(8,128)(2,1)S(1)}, bf16[10,72,128]{2,1,0:T(8,128)(2,1)S(1)}, u32[]{:S(2)}, u32[]{:S(2)}) collective-permute-start(bf16[10,72,128]{2,1,0:T(8,128)(2,1)S(1)} %get-tuple-element.25), channel_id=1, source_target_pairs={{0,1},{512,513},{2,3},{514,515},{4,5},{516,517},{6,7},{518,519},{8... | collective-permute-start | bytes 552968 | tf_op jit(solution)/shard_map/ppermute | solution.py:129
  163.7 8.1 %collective-permute-start.23 = (bf16[8,72,128]{2,1,0:T(8,128)(2,1)S(1)}, bf16[8,72,128]{2,1,0:T(8,128)(2,1)S(1)}, u32[]{:S(2)}, u32[]{:S(2)}) collective-permute-start(bf16[8,72,128]{2,1,0:T(8,128)(2,1)S(1)} %get-tuple-element.27), channel_id=1, source_target_pairs={{1,0},{513,512},{3,2},{515,514},{5,4},{517,516},{7,6},{519,518},{9... | collective-permute-start | bytes 442376 | tf_op jit(solution)/shard_map/ppermute | solution.py:129
  165.7 7.4 %collective-permute-start.24 = (bf16[8,72,128]{2,1,0:T(8,128)(2,1)S(1)}, bf16[8,72,128]{2,1,0:T(8,128)(2,1)S(1)}, u32[]{:S(2)}, u32[]{:S(2)}) collective-permute-start(bf16[8,72,128]{2,1,0:T(8,128)(2,1)S(1)} %get-tuple-element.28), channel_id=1, source_target_pairs={{0,1},{512,513},{2,3},{514,515},{4,5},{516,517},{6,7},{518,519},{8... | collective-permute-start | bytes 442376 | tf_op jit(solution)/shard_map/ppermute | solution.py:129
  184.9 33.4 %collective-permute-start.25 = (bf16[8,72,128]{2,1,0:T(8,128)(2,1)S(1)}, bf16[8,72,128]{2,1,0:T(8,128)(2,1)S(1)}, u32[]{:S(2)}, u32[]{:S(2)}) collective-permute-start(bf16[8,72,128]{2,1,0:T(8,128)(2,1)S(1)} %all_to_all.10), channel_id=1, source_target_pairs={{0,0},{512,1},{2,2},{514,3},{4,4},{516,5},{6,6},{518,7},{8,8},{520... | collective-permute-start | bytes 442376 | tf_op jit(solution)/shard_map/ppermute | solution.py:129

commit v3 on v2

--- a/solution.py
+++ b/solution.py
@@ -117,10 +117,10 @@
     rows, blocks = lax.axis_size("lat"), lax.axis_size("lon")
 
     def home(row, block):
-        upper, z = divmod(row, half)
+        z, side = divmod(row, 2)
         column, slot = divmod(block, run)
         y, core = divmod(slot, 2)
-        return (core * half + z - z % 2 + upper) * blocks + column * run + y * 2 + z % 2
+        return (core * half + z) * blocks + column * run + y * 2 + side
 
     return rows, blocks, home
 

time: 222 us -> 240 us (1.081)
  the two profiles are of different devices: /device:TPU:1 before, /device:TPU:310 now
where the time goes in v3:
time: 240 us; the launch traced here: 239 us
  waiting for transfers between devices  125 us (52%)
  starting transfers between devices  84.6 us (35%)
  Pallas kernels  12 us (5%)
  blocking collectives  11.3 us (5%)
  local copies, waits for them, and re-layouts  3.44 us (1%)
    ppermute x26, waiting for transfers between devices, move(): return lax.ppermute(value, ('lat', 'lon'), pairs)  118 us
    ppermute x26, starting transfers between devices, move(): return lax.ppermute(value, ('lat', 'lon'), pairs)  78.9 us
    all_to_all x1, blocking collectives, exchange(): return lax.all_to_all(value, ('lat', 'lon'), 0, 0, axis_index_groups=groups)  11.3 us
    all_to_all x1, waiting for transfers between devices, exchange(): return lax.all_to_all(value, ('lat', 'lon'), 0, 0, axis_index_groups=groups)  7.15 us
    pallas_call x4, Pallas kernels, adjoint(): pl.pallas_call(functools.partial(adjoint_kernel, step, first, reads, len(...  6.93 us
    all_to_all x1, starting transfers between devices, exchange(): return lax.all_to_all(value, ('lat', 'lon'), 0, 0, axis_index_groups=groups)  5.7 us
    pallas_call x4, Pallas kernels, forward(): pl.pallas_call(functools.partial(forward_kernel, step, first, outs, fold,...  5.09 us
  transfers between devices with their start and end apart: 27, of which 24 were waited for; matrix products, arithmetic and copies ran while one was open for 0% of the time, Pallas kernels for 0%

profile of v3, /device:TPU:310, one launch (start us, length us, event | category | flops | bytes accessed | tf_op | source)
XLA Modules:
  0.0 239.2 jit_solution(5779039466568930307)
XLA Ops:
  2.1 14.1 %collective-permute-start = (bf16[952,128]{1,0:T(8,128)(2,1)S(1)}, bf16[952,128]{1,0:T(8,128)(2,1)S(1)}, u32[]{:S(2)}, u32[]{:S(2)}) collective-permute-start(bf16[952,128]{1,0:T(8,128)(2,1)S(1)} %constant_dynamic-update-slice_fusion), channel_id=1, source_target_pairs={{0,0},{1,512},{2,2},{3,514},{4,4},{5,516},{6,6},{7,518},{8,8},{9,5... | collective-permute-start | bytes 731144 | tf_op jit(solution)/shard_map/ppermute | solution.py:129
  16.1 42.0 %collective-permute-done = bf16[952,128]{1,0:T(8,128)(2,1)S(1)} collective-permute-done((bf16[952,128]{1,0:T(8,128)(2,1)S(1)}, bf16[952,128]{1,0:T(8,128)(2,1)S(1)}, u32[]{:S(2)}, u32[]{:S(2)}) %collective-permute-start) | collective-permute-done | bytes 243744 | tf_op jit(solution)/shard_map/ppermute | solution.py:129
  60.5 5.7 %all-to-all-start = ((bf16[8,160,128]{2,1,0:T(8,128)(2,1)}), bf16[8,160,128]{2,1,0:T(8,128)(2,1)S(1)}, u32[]{:S(2)}, u32[]{:S(2)}) async-start(bf16[8,160,128]{2,1,0:T(8,128)(2,1)} %pad_maximum_fusion), calls=%async_computation | async-start | bytes 655360 | tf_op jit(solution)/shard_map/all_to_all | solution.py:151
  66.2 7.2 %all-to-all-done = bf16[8,160,128]{2,1,0:T(8,128)(2,1)S(1)} async-done(((bf16[8,160,128]{2,1,0:T(8,128)(2,1)}), bf16[8,160,128]{2,1,0:T(8,128)(2,1)S(1)}, u32[]{:S(2)}, u32[]{:S(2)}) %all-to-all-start) | async-done | bytes 327712 | tf_op jit(solution)/shard_map/all_to_all | solution.py:151
  73.4 2.5 %collective-permute-start.1 = (bf16[2,160,128]{2,1,0:T(8,128)(2,1)S(1)}, bf16[2,160,128]{2,1,0:T(8,128)(2,1)S(1)}, u32[]{:S(2)}, u32[]{:S(2)}) collective-permute-start(bf16[2,160,128]{2,1,0:T(8,128)(2,1)S(1)} %get-tuple-element.31), channel_id=1, source_target_pairs={{0,8},{512,520},{2,10},{514,522},{4,12},{516,524},{6,14},{518,526}... | collective-permute-start | bytes 245768 | tf_op jit(solution)/shard_map/ppermute | solution.py:129
  75.9 3.5 %collective-permute-start.2 = (bf16[2,160,128]{2,1,0:T(8,128)(2,1)S(1)}, bf16[2,160,128]{2,1,0:T(8,128)(2,1)S(1)}, u32[]{:S(2)}, u32[]{:S(2)}) collective-permute-start(bf16[2,160,128]{2,1,0:T(8,128)(2,1)S(1)} %get-tuple-element.32), channel_id=1, source_target_pairs={{0,24},{512,536},{2,26},{514,538},{4,28},{516,540},{6,30},{518,542... | collective-permute-start | bytes 245768 | tf_op jit(solution)/shard_map/ppermute | solution.py:129
  79.9 3.6 %collective-permute-done.2 = bf16[2,160,128]{2,1,0:T(8,128)(2,1)S(1)} collective-permute-done((bf16[2,160,128]{2,1,0:T(8,128)(2,1)S(1)}, bf16[2,160,128]{2,1,0:T(8,128)(2,1)S(1)}, u32[]{:S(2)}, u32[]{:S(2)}) %collective-permute-start.2) | collective-permute-done | bytes 81952 | tf_op jit(solution)/shard_map/ppermute | solution.py:129
  83.5 1.9 collective-permute-start.4
  85.4 2.4 %collective-permute-start.3 = (bf16[11,72,128]{2,1,0:T(8,128)(2,1)S(1)}, bf16[11,72,128]{2,1,0:T(8,128)(2,1)S(1)}, u32[]{:S(2)}, u32[]{:S(2)}) collective-permute-start(bf16[11,72,128]{2,1,0:T(8,128)(2,1)S(1)} %pad_maximum_fusion.3.own), channel_id=1, source_target_pairs={{0,1},{512,513},{2,3},{514,515},{4,5},{516,517},{6,7},{518,519},{8... | collective-permute-start | bytes 608264 | tf_op jit(solution)/shard_map/ppermute | solution.py:129
  88.7 5.0 %collective-permute-done.3.north = bf16[11,72,128]{2,1,0:T(8,128)(2,1)S(1)} collective-permute-done((bf16[11,72,128]{2,1,0:T(8,128)(2,1)S(1)}, bf16[11,72,128]{2,1,0:T(8,128)(2,1)S(1)}, u32[]{:S(2)}, u32[]{:S(2)}) %collective-permute-start.3) | collective-permute-done | bytes 202784 | tf_op jit(solution)/shard_map/ppermute | solution.py:129
  93.7 1.3 shard_map.64.own
  95.0 1.9 collective-permute-start.6
  96.9 2.4 %collective-permute-start.5 = (bf16[9,72,128]{2,1,0:T(8,128)(2,1)S(1)}, bf16[9,72,128]{2,1,0:T(8,128)(2,1)S(1)}, u32[]{:S(2)}, u32[]{:S(2)}) collective-permute-start(bf16[9,72,128]{2,1,0:T(8,128)(2,1)S(1)} %shard_map.64.own), channel_id=1, source_target_pairs={{0,1},{512,513},{2,3},{514,515},{4,5},{516,517},{6,7},{518,519},{8... | collective-permute-start | bytes 497672 | tf_op jit(solution)/shard_map/ppermute | solution.py:129
  99.8 5.0 %collective-permute-done.5.north = bf16[9,72,128]{2,1,0:T(8,128)(2,1)S(1)} collective-permute-done((bf16[9,72,128]{2,1,0:T(8,128)(2,1)S(1)}, bf16[9,72,128]{2,1,0:T(8,128)(2,1)S(1)}, u32[]{:S(2)}, u32[]{:S(2)}) %collective-permute-start.5) | collective-permute-done | bytes 165920 | tf_op jit(solution)/shard_map/ppermute | solution.py:129
  106.1 2.2 collective-permute-start.8
  108.3 4.8 %collective-permute-start.7 = (bf16[2,72,128]{2,1,0:T(8,128)(2,1)S(1)}, bf16[2,72,128]{2,1,0:T(8,128)(2,1)S(1)}, u32[]{:S(2)}, u32[]{:S(2)}) collective-permute-start(bf16[2,72,128]{2,1,0:T(8,128)(2,1)S(1)} %get-tuple-element.38), channel_id=1, source_target_pairs={{0,8},{512,520},{2,10},{514,522},{4,12},{516,524},{6,14},{518,526}... | collective-permute-start | bytes 110600 | tf_op jit(solution)/shard_map/ppermute | solution.py:129
  113.1 1.6 collective-permute-done.7
  114.8 1.9 collective-permute-start.10
  116.7 2.4 %collective-permute-start.9 = (bf16[11,72,128]{2,1,0:T(8,128)(2,1)S(1)}, bf16[11,72,128]{2,1,0:T(8,128)(2,1)S(1)}, u32[]{:S(2)}, u32[]{:S(2)}) collective-permute-start(bf16[11,72,128]{2,1,0:T(8,128)(2,1)S(1)} %pad_maximum_fusion.4.own), channel_id=1, source_target_pairs={{0,1},{512,513},{2,3},{514,515},{4,5},{516,517},{6,7},{518,519},{8... | collective-permute-start | bytes 608264 | tf_op jit(solution)/shard_map/ppermute | solution.py:129
  120.0 5.0 %collective-permute-done.9.north = bf16[11,72,128]{2,1,0:T(8,128)(2,1)S(1)} collective-permute-done((bf16[11,72,128]{2,1,0:T(8,128)(2,1)S(1)}, bf16[11,72,128]{2,1,0:T(8,128)(2,1)S(1)}, u32[]{:S(2)}, u32[]{:S(2)}) %collective-permute-start.9) | collective-permute-done | bytes 202784 | tf_op jit(solution)/shard_map/ppermute | solution.py:129
  126.3 1.9 collective-permute-start.12
  128.2 2.4 %collective-permute-start.11 = (bf16[9,72,128]{2,1,0:T(8,128)(2,1)S(1)}, bf16[9,72,128]{2,1,0:T(8,128)(2,1)S(1)}, u32[]{:S(2)}, u32[]{:S(2)}) collective-permute-start(bf16[9,72,128]{2,1,0:T(8,128)(2,1)S(1)} %shard_map.66.own), channel_id=1, source_target_pairs={{0,1},{512,513},{2,3},{514,515},{4,5},{516,517},{6,7},{518,519},{8... | collective-permute-start | bytes 497672 | tf_op jit(solution)/shard_map/ppermute | solution.py:129
  131.1 5.0 %collective-permute-done.11.north = bf16[9,72,128]{2,1,0:T(8,128)(2,1)S(1)} collective-permute-done((bf16[9,72,128]{2,1,0:T(8,128)(2,1)S(1)}, bf16[9,72,128]{2,1,0:T(8,128)(2,1)S(1)}, u32[]{:S(2)}, u32[]{:S(2)}) %collective-permute-start.11) | collective-permute-done | bytes 165920 | tf_op jit(solution)/shard_map/ppermute | solution.py:129
  137.4 5.4 %collective-permute-start.13 = (bf16[2,72,128]{2,1,0:T(8,128)(2,1)S(1)}, bf16[2,72,128]{2,1,0:T(8,128)(2,1)S(1)}, u32[]{:S(2)}, u32[]{:S(2)}) collective-permute-start(bf16[2,72,128]{2,1,0:T(8,128)(2,1)S(1)} %get-tuple-element.35), channel_id=1, source_target_pairs={{0,8},{512,520},{2,10},{514,522},{4,12},{516,524},{6,14},{518,526}... | collective-permute-start | bytes 110600 | tf_op jit(solution)/shard_map/ppermute | solution.py:129
  142.8 1.9 collective-permute-start.14
  144.8 5.1 %collective-permute-done.14 = bf16[2,72,128]{2,1,0:T(8,128)(2,1)S(1)} collective-permute-done((bf16[2,72,128]{2,1,0:T(8,128)(2,1)S(1)}, bf16[2,72,128]{2,1,0:T(8,128)(2,1)S(1)}, u32[]{:S(2)}, u32[]{:S(2)}) %collective-permute-start.14) | collective-permute-done | bytes 36896 | tf_op jit(solution)/shard_map/ppermute | solution.py:129
  149.9 1.8 shard_map.68
  151.7 1.9 collective-permute-start.15
  153.7 2.4 %collective-permute-start.16 = (bf16[10,72,128]{2,1,0:T(8,128)(2,1)S(1)}, bf16[10,72,128]{2,1,0:T(8,128)(2,1)S(1)}, u32[]{:S(2)}, u32[]{:S(2)}) collective-permute-start(bf16[10,72,128]{2,1,0:T(8,128)(2,1)S(1)} %get-tuple-element.19), channel_id=1, source_target_pairs={{0,1},{512,513},{2,3},{514,515},{4,5},{516,517},{6,7},{518,519},{8... | collective-permute-start | bytes 552968 | tf_op jit(solution)/shard_map/ppermute | solution.py:129
  156.7 5.0 %collective-permute-done.16.rest_2_ = bf16[10,72,128]{2,1,0:T(8,128)(2,1)S(1)} collective-permute-done((bf16[10,72,128]{2,1,0:T(8,128)(2,1)S(1)}, bf16[10,72,128]{2,1,0:T(8,128)(2,1)S(1)}, u32[]{:S(2)}, u32[]{:S(2)}) %collective-permute-start.16) | collective-permute-done | bytes 184352 | tf_op jit(solution)/shard_map/ppermute | solution.py:129
  161.7 1.6 shard_map.69
  163.4 1.9 collective-permute-start.17
  165.3 2.4 %collective-permute-start.18 = (bf16[8,72,128]{2,1,0:T(8,128)(2,1)S(1)}, bf16[8,72,128]{2,1,0:T(8,128)(2,1)S(1)}, u32[]{:S(2)}, u32[]{:S(2)}) collective-permute-start(bf16[8,72,128]{2,1,0:T(8,128)(2,1)S(1)} %get-tuple-element.22), channel_id=1, source_target_pairs={{0,1},{512,513},{2,3},{514,515},{4,5},{516,517},{6,7},{518,519},{8... | collective-permute-start | bytes 442376 | tf_op jit(solution)/shard_map/ppermute | solution.py:129
  168.0 5.0 %collective-permute-done.18 = bf16[8,72,128]{2,1,0:T(8,128)(2,1)S(1)} collective-permute-done((bf16[8,72,128]{2,1,0:T(8,128)(2,1)S(1)}, bf16[8,72,128]{2,1,0:T(8,128)(2,1)S(1)}, u32[]{:S(2)}, u32[]{:S(2)}) %collective-permute-start.18) | collective-permute-done | bytes 147488 | tf_op jit(solution)/shard_map/ppermute | solution.py:129
  173.1 1.9 collective-permute-start.19
  175.0 3.9 %collective-permute-start.20 = (bf16[2,72,128]{2,1,0:T(8,128)(2,1)S(1)}, bf16[2,72,128]{2,1,0:T(8,128)(2,1)S(1)}, u32[]{:S(2)}, u32[]{:S(2)}) collective-permute-start(bf16[2,72,128]{2,1,0:T(8,128)(2,1)S(1)} %get-tuple-element.34), channel_id=1, source_target_pairs={{0,24},{512,536},{2,26},{514,538},{4,28},{516,540},{6,30},{518,542... | collective-permute-start | bytes 110600 | tf_op jit(solution)/shard_map/ppermute | solution.py:129
  178.9 3.1 %collective-permute-done.20 = bf16[2,72,128]{2,1,0:T(8,128)(2,1)S(1)} collective-permute-done((bf16[2,72,128]{2,1,0:T(8,128)(2,1)S(1)}, bf16[2,72,128]{2,1,0:T(8,128)(2,1)S(1)}, u32[]{:S(2)}, u32[]{:S(2)}) %collective-permute-start.20) | collective-permute-done | bytes 36896 | tf_op jit(solution)/shard_map/ppermute | solution.py:129
  182.1 1.8 shard_map.70
  183.9 1.9 collective-permute-start.21
  185.8 2.4 %collective-permute-start.22 = (bf16[10,72,128]{2,1,0:T(8,128)(2,1)S(1)}, bf16[10,72,128]{2,1,0:T(8,128)(2,1)S(1)}, u32[]{:S(2)}, u32[]{:S(2)}) collective-permute-start(bf16[10,72,128]{2,1,0:T(8,128)(2,1)S(1)} %get-tuple-element.25), channel_id=1, source_target_pairs={{0,1},{512,513},{2,3},{514,515},{4,5},{516,517},{6,7},{518,519},{8... | collective-permute-start | bytes 552968 | tf_op jit(solution)/shard_map/ppermute | solution.py:129
  188.9 5.0 %collective-permute-done.22.rest_2_ = bf16[10,72,128]{2,1,0:T(8,128)(2,1)S(1)} collective-permute-done((bf16[10,72,128]{2,1,0:T(8,128)(2,1)S(1)}, bf16[10,72,128]{2,1,0:T(8,128)(2,1)S(1)}, u32[]{:S(2)}, u32[]{:S(2)}) %collective-permute-start.22) | collective-permute-done | bytes 184352 | tf_op jit(solution)/shard_map/ppermute | solution.py:129
  193.9 1.7 shard_map.71
  195.6 1.9 collective-permute-start.23
  197.5 2.4 %collective-permute-start.24 = (bf16[8,72,128]{2,1,0:T(8,128)(2,1)S(1)}, bf16[8,72,128]{2,1,0:T(8,128)(2,1)S(1)}, u32[]{:S(2)}, u32[]{:S(2)}) collective-permute-start(bf16[8,72,128]{2,1,0:T(8,128)(2,1)S(1)} %get-tuple-element.28), channel_id=1, source_target_pairs={{0,1},{512,513},{2,3},{514,515},{4,5},{516,517},{6,7},{518,519},{8... | collective-permute-start | bytes 442376 | tf_op jit(solution)/shard_map/ppermute | solution.py:129
  200.1 5.0 %collective-permute-done.24 = bf16[8,72,128]{2,1,0:T(8,128)(2,1)S(1)} collective-permute-done((bf16[8,72,128]{2,1,0:T(8,128)(2,1)S(1)}, bf16[8,72,128]{2,1,0:T(8,128)(2,1)S(1)}, u32[]{:S(2)}, u32[]{:S(2)}) %collective-permute-start.24) | collective-permute-done | bytes 147488 | tf_op jit(solution)/shard_map/ppermute | solution.py:129
  205.2 11.3 %all_to_all.10 = bf16[8,72,128]{2,1,0:T(8,128)(2,1)S(1)} all-to-all(bf16[8,72,128]{2,1,0:T(8,128)(2,1)S(1)} %add_convert_fusion), channel_id=1, replica_groups={{0,512,2,514,4,516,6,518},{8,520,10,522,12,524,14,526},{16,528,18,530,2..., dimensions={0} | all-to-all | bytes 294912 | tf_op jit(solution)/shard_map/all_to_all | solution.py:151
  216.5 4.0 %collective-permute-start.25 = (bf16[8,72,128]{2,1,0:T(8,128)(2,1)S(1)}, bf16[8,72,128]{2,1,0:T(8,128)(2,1)S(1)}, u32[]{:S(2)}, u32[]{:S(2)}) collective-permute-start(bf16[8,72,128]{2,1,0:T(8,128)(2,1)S(1)} %all_to_all.10), channel_id=1, source_target_pairs={{0,0},{512,1},{2,2},{514,3},{4,4},{516,5},{6,6},{518,7},{8,8},{520... | collective-permute-start | bytes 442376 | tf_op jit(solution)/shard_map/ppermute | solution.py:129
  220.5 18.0 %collective-permute-done.25 = bf16[8,72,128]{2,1,0:T(8,128)(2,1)S(1)} collective-permute-done((bf16[8,72,128]{2,1,0:T(8,128)(2,1)S(1)}, bf16[8,72,128]{2,1,0:T(8,128)(2,1)S(1)}, u32[]{:S(2)}, u32[]{:S(2)}) %collective-permute-start.25) | collective-permute-done | bytes 147488 | tf_op jit(solution)/shard_map/ppermute | solution.py:129
  (64 shorter events, 13.7 us)
Async XLA Ops:
  0.8 1.0 copy-start.4
  0.8 1.0 copy-start.5
  0.8 1.1 copy-start.3
  2.1 56.1 %collective-permute-start = (bf16[952,128]{1,0:T(8,128)(2,1)S(1)}, bf16[952,128]{1,0:T(8,128)(2,1)S(1)}, u32[]{:S(2)}, u32[]{:S(2)}) collective-permute-start(bf16[952,128]{1,0:T(8,128)(2,1)S(1)} %constant_dynamic-update-slice_fusion), channel_id=1, source_target_pairs={{0,0},{1,512},{2,2},{3,514},{4,4},{5,516},{6,6},{7,518},{8,8},{9,5... | collective-permute-start | bytes 731144 | tf_op jit(solution)/shard_map/ppermute | solution.py:129
  58.1 0.7 copy-start.1
  58.8 0.9 slice-start
  60.5 5.7 %copy-start.2 = (bf16[952,128]{1,0:T(8,128)(2,1)S(1)}, bf16[952,128]{1,0:T(8,128)(2,1)}, u32[]{:S(2)}) copy-start(bf16[952,128]{1,0:T(8,128)(2,1)} %copy-done.1) | copy-start | bytes 731140
  60.5 12.9 %all-to-all-start = ((bf16[8,160,128]{2,1,0:T(8,128)(2,1)}), bf16[8,160,128]{2,1,0:T(8,128)(2,1)S(1)}, u32[]{:S(2)}, u32[]{:S(2)}) async-start(bf16[8,160,128]{2,1,0:T(8,128)(2,1)} %pad_maximum_fusion), calls=%async_computation | async-start | bytes 655360 | tf_op jit(solution)/shard_map/all_to_all | solution.py:151
  73.4 20.3 %copy-start = (bf16[16,160,128]{2,1,0:T(8,128)(2,1)S(1)}, bf16[16,160,128]{2,1,0:T(8,128)(2,1)}, u32[]{:S(2)}) copy-start(bf16[16,160,128]{2,1,0:T(8,128)(2,1)} %rest_3_.3) | copy-start | bytes 1966084
  73.4 6.5 %collective-permute-start.1 = (bf16[2,160,128]{2,1,0:T(8,128)(2,1)S(1)}, bf16[2,160,128]{2,1,0:T(8,128)(2,1)S(1)}, u32[]{:S(2)}, u32[]{:S(2)}) collective-permute-start(bf16[2,160,128]{2,1,0:T(8,128)(2,1)S(1)} %get-tuple-element.31), channel_id=1, source_target_pairs={{0,8},{512,520},{2,10},{514,522},{4,12},{516,524},{6,14},{518,526}... | collective-permute-start | bytes 245768 | tf_op jit(solution)/shard_map/ppermute | solution.py:129
  75.9 7.5 %collective-permute-start.2 = (bf16[2,160,128]{2,1,0:T(8,128)(2,1)S(1)}, bf16[2,160,128]{2,1,0:T(8,128)(2,1)S(1)}, u32[]{:S(2)}, u32[]{:S(2)}) collective-permute-start(bf16[2,160,128]{2,1,0:T(8,128)(2,1)S(1)} %get-tuple-element.32), channel_id=1, source_target_pairs={{0,24},{512,536},{2,26},{514,538},{4,28},{516,540},{6,30},{518,542... | collective-permute-start | bytes 245768 | tf_op jit(solution)/shard_map/ppermute | solution.py:129
  83.5 5.2 %collective-permute-start.4 = (bf16[11,72,128]{2,1,0:T(8,128)(2,1)S(1)}, bf16[11,72,128]{2,1,0:T(8,128)(2,1)S(1)}, u32[]{:S(2)}, u32[]{:S(2)}) collective-permute-start(bf16[11,72,128]{2,1,0:T(8,128)(2,1)S(1)} %pad_maximum_fusion.3.own), channel_id=1, source_target_pairs={{1,0},{513,512},{3,2},{515,514},{5,4},{517,516},{7,6},{519,518},{9... | collective-permute-start | bytes 608264 | tf_op jit(solution)/shard_map/ppermute | solution.py:129
  85.4 8.3 %collective-permute-start.3 = (bf16[11,72,128]{2,1,0:T(8,128)(2,1)S(1)}, bf16[11,72,128]{2,1,0:T(8,128)(2,1)S(1)}, u32[]{:S(2)}, u32[]{:S(2)}) collective-permute-start(bf16[11,72,128]{2,1,0:T(8,128)(2,1)S(1)} %pad_maximum_fusion.3.own), channel_id=1, source_target_pairs={{0,1},{512,513},{2,3},{514,515},{4,5},{516,517},{6,7},{518,519},{8... | collective-permute-start | bytes 608264 | tf_op jit(solution)/shard_map/ppermute | solution.py:129
  95.0 4.8 %collective-permute-start.6 = (bf16[9,72,128]{2,1,0:T(8,128)(2,1)S(1)}, bf16[9,72,128]{2,1,0:T(8,128)(2,1)S(1)}, u32[]{:S(2)}, u32[]{:S(2)}) collective-permute-start(bf16[9,72,128]{2,1,0:T(8,128)(2,1)S(1)} %shard_map.64.own), channel_id=1, source_target_pairs={{1,0},{513,512},{3,2},{515,514},{5,4},{517,516},{7,6},{519,518},{9... | collective-permute-start | bytes 497672 | tf_op jit(solution)/shard_map/ppermute | solution.py:129
  96.9 7.9 %collective-permute-start.5 = (bf16[9,72,128]{2,1,0:T(8,128)(2,1)S(1)}, bf16[9,72,128]{2,1,0:T(8,128)(2,1)S(1)}, u32[]{:S(2)}, u32[]{:S(2)}) collective-permute-start(bf16[9,72,128]{2,1,0:T(8,128)(2,1)S(1)} %shard_map.64.own), channel_id=1, source_target_pairs={{0,1},{512,513},{2,3},{514,515},{4,5},{516,517},{6,7},{518,519},{8... | collective-permute-start | bytes 497672 | tf_op jit(solution)/shard_map/ppermute | solution.py:129
  106.1 7.1 %collective-permute-start.8 = (bf16[2,72,128]{2,1,0:T(8,128)(2,1)S(1)}, bf16[2,72,128]{2,1,0:T(8,128)(2,1)S(1)}, u32[]{:S(2)}, u32[]{:S(2)}) collective-permute-start(bf16[2,72,128]{2,1,0:T(8,128)(2,1)S(1)} %get-tuple-element.37), channel_id=1, source_target_pairs={{0,24},{512,536},{2,26},{514,538},{4,28},{516,540},{6,30},{518,542... | collective-permute-start | bytes 110600 | tf_op jit(solution)/shard_map/ppermute | solution.py:129
  108.3 6.4 %collective-permute-start.7 = (bf16[2,72,128]{2,1,0:T(8,128)(2,1)S(1)}, bf16[2,72,128]{2,1,0:T(8,128)(2,1)S(1)}, u32[]{:S(2)}, u32[]{:S(2)}) collective-permute-start(bf16[2,72,128]{2,1,0:T(8,128)(2,1)S(1)} %get-tuple-element.38), channel_id=1, source_target_pairs={{0,8},{512,520},{2,10},{514,522},{4,12},{516,524},{6,14},{518,526}... | collective-permute-start | bytes 110600 | tf_op jit(solution)/shard_map/ppermute | solution.py:129
  114.8 5.2 %collective-permute-start.10 = (bf16[11,72,128]{2,1,0:T(8,128)(2,1)S(1)}, bf16[11,72,128]{2,1,0:T(8,128)(2,1)S(1)}, u32[]{:S(2)}, u32[]{:S(2)}) collective-permute-start(bf16[11,72,128]{2,1,0:T(8,128)(2,1)S(1)} %pad_maximum_fusion.4.own), channel_id=1, source_target_pairs={{1,0},{513,512},{3,2},{515,514},{5,4},{517,516},{7,6},{519,518},{9... | collective-permute-start | bytes 608264 | tf_op jit(solution)/shard_map/ppermute | solution.py:129
  116.7 8.3 %collective-permute-start.9 = (bf16[11,72,128]{2,1,0:T(8,128)(2,1)S(1)}, bf16[11,72,128]{2,1,0:T(8,128)(2,1)S(1)}, u32[]{:S(2)}, u32[]{:S(2)}) collective-permute-start(bf16[11,72,128]{2,1,0:T(8,128)(2,1)S(1)} %pad_maximum_fusion.4.own), channel_id=1, source_target_pairs={{0,1},{512,513},{2,3},{514,515},{4,5},{516,517},{6,7},{518,519},{8... | collective-permute-start | bytes 608264 | tf_op jit(solution)/shard_map/ppermute | solution.py:129
  126.3 4.8 %collective-permute-start.12 = (bf16[9,72,128]{2,1,0:T(8,128)(2,1)S(1)}, bf16[9,72,128]{2,1,0:T(8,128)(2,1)S(1)}, u32[]{:S(2)}, u32[]{:S(2)}) collective-permute-start(bf16[9,72,128]{2,1,0:T(8,128)(2,1)S(1)} %shard_map.66.own), channel_id=1, source_target_pairs={{1,0},{513,512},{3,2},{515,514},{5,4},{517,516},{7,6},{519,518},{9... | collective-permute-start | bytes 497672 | tf_op jit(solution)/shard_map/ppermute | solution.py:129
  128.2 7.9 %collective-permute-start.11 = (bf16[9,72,128]{2,1,0:T(8,128)(2,1)S(1)}, bf16[9,72,128]{2,1,0:T(8,128)(2,1)S(1)}, u32[]{:S(2)}, u32[]{:S(2)}) collective-permute-start(bf16[9,72,128]{2,1,0:T(8,128)(2,1)S(1)} %shard_map.66.own), channel_id=1, source_target_pairs={{0,1},{512,513},{2,3},{514,515},{4,5},{516,517},{6,7},{518,519},{8... | collective-permute-start | bytes 497672 | tf_op jit(solution)/shard_map/ppermute | solution.py:129
  137.4 7.4 %collective-permute-start.13 = (bf16[2,72,128]{2,1,0:T(8,128)(2,1)S(1)}, bf16[2,72,128]{2,1,0:T(8,128)(2,1)S(1)}, u32[]{:S(2)}, u32[]{:S(2)}) collective-permute-start(bf16[2,72,128]{2,1,0:T(8,128)(2,1)S(1)} %get-tuple-element.35), channel_id=1, source_target_pairs={{0,8},{512,520},{2,10},{514,522},{4,12},{516,524},{6,14},{518,526}... | collective-permute-start | bytes 110600 | tf_op jit(solution)/shard_map/ppermute | solution.py:129
  142.8 7.1 %collective-permute-start.14 = (bf16[2,72,128]{2,1,0:T(8,128)(2,1)S(1)}, bf16[2,72,128]{2,1,0:T(8,128)(2,1)S(1)}, u32[]{:S(2)}, u32[]{:S(2)}) collective-permute-start(bf16[2,72,128]{2,1,0:T(8,128)(2,1)S(1)} %get-tuple-element.36), channel_id=1, source_target_pairs={{0,24},{512,536},{2,26},{514,538},{4,28},{516,540},{6,30},{518,542... | collective-permute-start | bytes 110600 | tf_op jit(solution)/shard_map/ppermute | solution.py:129
  151.7 5.0 %collective-permute-start.15 = (bf16[10,72,128]{2,1,0:T(8,128)(2,1)S(1)}, bf16[10,72,128]{2,1,0:T(8,128)(2,1)S(1)}, u32[]{:S(2)}, u32[]{:S(2)}) collective-permute-start(bf16[10,72,128]{2,1,0:T(8,128)(2,1)S(1)} %get-tuple-element.18), channel_id=1, source_target_pairs={{1,0},{513,512},{3,2},{515,514},{5,4},{517,516},{7,6},{519,518},{9... | collective-permute-start | bytes 552968 | tf_op jit(solution)/shard_map/ppermute | solution.py:129
  153.7 8.1 %collective-permute-start.16 = (bf16[10,72,128]{2,1,0:T(8,128)(2,1)S(1)}, bf16[10,72,128]{2,1,0:T(8,128)(2,1)S(1)}, u32[]{:S(2)}, u32[]{:S(2)}) collective-permute-start(bf16[10,72,128]{2,1,0:T(8,128)(2,1)S(1)} %get-tuple-element.19), channel_id=1, source_target_pairs={{0,1},{512,513},{2,3},{514,515},{4,5},{516,517},{6,7},{518,519},{8... | collective-permute-start | bytes 552968 | tf_op jit(solution)/shard_map/ppermute | solution.py:129
  163.4 4.6 %collective-permute-start.17 = (bf16[8,72,128]{2,1,0:T(8,128)(2,1)S(1)}, bf16[8,72,128]{2,1,0:T(8,128)(2,1)S(1)}, u32[]{:S(2)}, u32[]{:S(2)}) collective-permute-start(bf16[8,72,128]{2,1,0:T(8,128)(2,1)S(1)} %get-tuple-element.21), channel_id=1, source_target_pairs={{1,0},{513,512},{3,2},{515,514},{5,4},{517,516},{7,6},{519,518},{9... | collective-permute-start | bytes 442376 | tf_op jit(solution)/shard_map/ppermute | solution.py:129
  165.3 7.7 %collective-permute-start.18 = (bf16[8,72,128]{2,1,0:T(8,128)(2,1)S(1)}, bf16[8,72,128]{2,1,0:T(8,128)(2,1)S(1)}, u32[]{:S(2)}, u32[]{:S(2)}) collective-permute-start(bf16[8,72,128]{2,1,0:T(8,128)(2,1)S(1)} %get-tuple-element.22), channel_id=1, source_target_pairs={{0,1},{512,513},{2,3},{514,515},{4,5},{516,517},{6,7},{518,519},{8... | collective-permute-start | bytes 442376 | tf_op jit(solution)/shard_map/ppermute | solution.py:129
  173.1 5.9 %collective-permute-start.19 = (bf16[2,72,128]{2,1,0:T(8,128)(2,1)S(1)}, bf16[2,72,128]{2,1,0:T(8,128)(2,1)S(1)}, u32[]{:S(2)}, u32[]{:S(2)}) collective-permute-start(bf16[2,72,128]{2,1,0:T(8,128)(2,1)S(1)} %get-tuple-element.33), channel_id=1, source_target_pairs={{0,8},{512,520},{2,10},{514,522},{4,12},{516,524},{6,14},{518,526}... | collective-permute-start | bytes 110600 | tf_op jit(solution)/shard_map/ppermute | solution.py:129
  175.0 7.1 %collective-permute-start.20 = (bf16[2,72,128]{2,1,0:T(8,128)(2,1)S(1)}, bf16[2,72,128]{2,1,0:T(8,128)(2,1)S(1)}, u32[]{:S(2)}, u32[]{:S(2)}) collective-permute-start(bf16[2,72,128]{2,1,0:T(8,128)(2,1)S(1)} %get-tuple-element.34), channel_id=1, source_target_pairs={{0,24},{512,536},{2,26},{514,538},{4,28},{516,540},{6,30},{518,542... | collective-permute-start | bytes 110600 | tf_op jit(solution)/shard_map/ppermute | solution.py:129
  183.9 5.0 %collective-permute-start.21 = (bf16[10,72,128]{2,1,0:T(8,128)(2,1)S(1)}, bf16[10,72,128]{2,1,0:T(8,128)(2,1)S(1)}, u32[]{:S(2)}, u32[]{:S(2)}) collective-permute-start(bf16[10,72,128]{2,1,0:T(8,128)(2,1)S(1)} %get-tuple-element.24), channel_id=1, source_target_pairs={{1,0},{513,512},{3,2},{515,514},{5,4},{517,516},{7,6},{519,518},{9... | collective-permute-start | bytes 552968 | tf_op jit(solution)/shard_map/ppermute | solution.py:129
  185.8 8.1 %collective-permute-start.22 = (bf16[10,72,128]{2,1,0:T(8,128)(2,1)S(1)}, bf16[10,72,128]{2,1,0:T(8,128)(2,1)S(1)}, u32[]{:S(2)}, u32[]{:S(2)}) collective-permute-start(bf16[10,72,128]{2,1,0:T(8,128)(2,1)S(1)} %get-tuple-element.25), channel_id=1, source_target_pairs={{0,1},{512,513},{2,3},{514,515},{4,5},{516,517},{6,7},{518,519},{8... | collective-permute-start | bytes 552968 | tf_op jit(solution)/shard_map/ppermute | solution.py:129
  195.6 4.6 %collective-permute-start.23 = (bf16[8,72,128]{2,1,0:T(8,128)(2,1)S(1)}, bf16[8,72,128]{2,1,0:T(8,128)(2,1)S(1)}, u32[]{:S(2)}, u32[]{:S(2)}) collective-permute-start(bf16[8,72,128]{2,1,0:T(8,128)(2,1)S(1)} %get-tuple-element.27), channel_id=1, source_target_pairs={{1,0},{513,512},{3,2},{515,514},{5,4},{517,516},{7,6},{519,518},{9... | collective-permute-start | bytes 442376 | tf_op jit(solution)/shard_map/ppermute | solution.py:129
  197.5 7.7 %collective-permute-start.24 = (bf16[8,72,128]{2,1,0:T(8,128)(2,1)S(1)}, bf16[8,72,128]{2,1,0:T(8,128)(2,1)S(1)}, u32[]{:S(2)}, u32[]{:S(2)}) collective-permute-start(bf16[8,72,128]{2,1,0:T(8,128)(2,1)S(1)} %get-tuple-element.28), channel_id=1, source_target_pairs={{0,1},{512,513},{2,3},{514,515},{4,5},{516,517},{6,7},{518,519},{8... | collective-permute-start | bytes 442376 | tf_op jit(solution)/shard_map/ppermute | solution.py:129
  216.5 22.0 %collective-permute-start.25 = (bf16[8,72,128]{2,1,0:T(8,128)(2,1)S(1)}, bf16[8,72,128]{2,1,0:T(8,128)(2,1)S(1)}, u32[]{:S(2)}, u32[]{:S(2)}) collective-permute-start(bf16[8,72,128]{2,1,0:T(8,128)(2,1)S(1)} %all_to_all.10), channel_id=1, source_target_pairs={{0,0},{512,1},{2,2},{514,3},{4,4},{516,5},{6,6},{518,7},{8,8},{520... | collective-permute-start | bytes 442376 | tf_op jit(solution)/shard_map/ppermute | solution.py:129

commit v4 on v3

--- a/solution.py
+++ b/solution.py
@@ -11,6 +11,7 @@
 VMEM = pl.BlockSpec(memory_space=pltpu.VMEM)
 SMEM = pl.BlockSpec(memory_space=pltpu.SMEM)
 LIMIT = 24 * 1024 * 1024
+RUN = 8
 
 
 def right_lanes(shape):
@@ -113,26 +114,23 @@
 
 
 def homes():
-    half, run = lax.axis_size("lat") // 2, 8
     rows, blocks = lax.axis_size("lat"), lax.axis_size("lon")
 
     def home(row, block):
-        z, side = divmod(row, 2)
-        column, slot = divmod(block, run)
-        y, core = divmod(slot, 2)
-        return (core * half + z) * blocks + column * run + y * 2 + side
+        half, z = divmod(row, rows // 2)
+        column, tracer = divmod(block, RUN)
+        return place(rows, blocks, z, column, tracer, half)
 
     return rows, blocks, home
+
+
+def place(rows, blocks, z, column, y, core):
+    upper, y = divmod(y, RUN // 2)
+    return (upper * (rows // 2) + z) * blocks + column * RUN + y * 2 + core
 
 
 def move(value, pairs):
     return lax.ppermute(value, ("lat", "lon"), pairs)
-
-
-def go_home(value, back=False):
-    rows, blocks, home = homes()
-    pairs = [(r * blocks + b, home(r, b)) for r in range(rows) for b in range(blocks)]
-    return move(value, [(t, s) for s, t in pairs] if back else pairs)
 
 
 def from_lat(value, by):
@@ -145,27 +143,39 @@
     return move(value, [(home(r, b), home(r, (b - by) % blocks)) for r in range(rows) for b in range(blocks)])
 
 
-def exchange(value, run):
-    rows, blocks, home = homes()
-    groups = [[home(r, b + j) for j in range(run)] for r in range(rows) for b in range(0, blocks, run)]
+def along_y(value):
+    rows, blocks, _ = homes()
+    groups = [
+        [place(rows, blocks, z, column, y, core) for y in range(RUN)]
+        for z in range(rows // 2)
+        for column in range(blocks // RUN)
+        for core in range(2)
+    ]
     return lax.all_to_all(value, ("lat", "lon"), 0, 0, axis_index_groups=groups)
+
+
+def swap_cores(value, first):
+    keep, give = jnp.where(first, value[0], value[1]), jnp.where(first, value[1], value[0])
+    blocks = lax.axis_size("lon")
+    both = lax.all_gather(give, "lon", axis_index_groups=[[i, i + 1] for i in range(0, blocks, 2)])
+    return jnp.where(first, keep, both[0]), jnp.where(first, both[1], keep)
 
 
 def on_device(vector, obs_weight, departures, weight_index, interp_table, column_mix):
     run, levels, _, cols = vector.shape
+    first = lax.axis_index("lon") % 2 == 0
     numbers = jnp.concatenate([departures.reshape(-1), weight_index.reshape(-1)]).astype(BF16)
     count = numbers.shape[0]
     tail = jnp.concatenate([jnp.broadcast_to(numbers[:, None], (count, cols)), jnp.zeros((16 - count, cols), BF16)])
-    mix = jnp.pad(column_mix[:, 0], ((0, 0), (0, 0), (0, cols - levels)))
-    steps = mix.shape[0]
-    sent = jnp.concatenate([vector.reshape(-1, cols), mix.reshape(-1, cols), obs_weight[:, 0].astype(BF16), tail])
-    sent = go_home(sent)
-    mix = sent[run * levels : (run + steps) * levels].reshape(steps, levels, cols)
-    shared = sent[(run + steps) * levels :]
-    bundle = jnp.concatenate(
-        [sent[: run * levels].reshape(run, levels, cols), jnp.broadcast_to(shared[None], (run, *shared.shape))], axis=1
+    part = lax.dynamic_index_in_dim(column_mix[:, 0], lax.axis_index("lon") // 2 % column_mix.shape[0], keepdims=False)
+    part = jnp.pad(part, ((0, 0), (0, cols - levels)))
+    shared = jnp.concatenate([obs_weight[:, 0].astype(BF16), tail, part])
+    bundle = along_y(
+        jnp.concatenate([vector[:, :, 0], jnp.broadcast_to(shared[None], (run, *shared.shape))], axis=1)
     )
-    bundle = exchange(bundle, run)
+    bundle = bundle.reshape(2, run // 2, *bundle.shape[1:])
+    mix = jnp.where(first, bundle[0, :, -levels:], bundle[1, :, -levels:])
+    bundle = jnp.stack(swap_cores(bundle[:, :, :-levels], first), axis=1).reshape(run, -1, cols)
     state, obs = bundle[:, :levels], bundle[:, levels : 2 * levels]
     west, east = from_lon(bundle[-2:], -run), from_lon(bundle[:2], run)
 
@@ -195,7 +205,9 @@
         parts = (stay, from_lat(north, 1), from_lat(south, -1))
         north, stay, south = adjoint(step - 1, par, parts, interp_table, mix)
         cot = (stay + from_lat(north, 1).astype(F32) + from_lat(south, -1).astype(F32)).astype(BF16)
-    return go_home(exchange(cot, run), back=True)[:, :, None]
+    cot = cot.reshape(run // 2, 2, levels, cols)
+    lower, upper = swap_cores((cot[:, 0], cot[:, 1]), first)
+    return along_y(jnp.concatenate([lower, upper]))[:, :, None]
 
 
 def solution(mesh):

time: 240 us -> 198 us (0.82)
  the two profiles are of different devices: /device:TPU:310 before, /device:TPU:1 now
where the time goes in v4:
time: 198 us; the launch traced here: 196 us
  starting transfers between devices  89 us (45%)
  waiting for transfers between devices  63.7 us (32%)
  blocking collectives  26.2 us (13%)
  Pallas kernels  12 us (6%)
  local copies, waits for them, and re-layouts  3.11 us (2%)
    ppermute x24, starting transfers between devices, move(): return lax.ppermute(value, ('lat', 'lon'), pairs)  81.3 us
    ppermute x24, waiting for transfers between devices, move(): return lax.ppermute(value, ('lat', 'lon'), pairs)  52.1 us
    all_gather x2, blocking collectives, swap_cores(): lax.all_gather(give, 'lon', axis_index_groups=[[i, i + 1] for i in range(...  14.6 us
    all_to_all x1, waiting for transfers between devices, along_y(): return lax.all_to_all(value, ('lat', 'lon'), 0, 0, axis_index_groups=groups)  11.6 us
    all_to_all x1, blocking collectives, along_y(): return lax.all_to_all(value, ('lat', 'lon'), 0, 0, axis_index_groups=groups)  11.6 us
    all_to_all x1, starting transfers between devices, along_y(): return lax.all_to_all(value, ('lat', 'lon'), 0, 0, axis_index_groups=groups)  7.65 us
    pallas_call x4, Pallas kernels, adjoint(): pl.pallas_call(functools.partial(adjoint_kernel, step, first, reads, len(...  6.92 us
    pallas_call x4, Pallas kernels, forward(): pl.pallas_call(functools.partial(forward_kernel, step, first, outs, fold,...  5.09 us
  transfers between devices with their start and end apart: 25, of which 22 were waited for; matrix products, arithmetic and copies ran while one was open for 0% of the time, Pallas kernels for 0%

profile of v4, /device:TPU:1, one launch (start us, length us, event | category | flops | bytes accessed | tf_op | source)
XLA Modules:
  0.0 196.2 jit_solution(13882040384037058546)
XLA Ops:
  3.5 7.7 %all-to-all-start = ((bf16[8,232,128]{2,1,0:T(8,128)(2,1)}), bf16[8,232,128]{2,1,0:T(8,128)(2,1)S(1)}, u32[]{:S(2)}, u32[]{:S(2)}) async-start(bf16[8,232,128]{2,1,0:T(8,128)(2,1)} %pad_maximum_fusion), calls=%async_computation | async-start | bytes 950272 | tf_op jit(solution)/shard_map/all_to_all | solution.py:154
  11.1 11.6 %all-to-all-done = bf16[8,232,128]{2,1,0:T(8,128)(2,1)S(1)} async-done(((bf16[8,232,128]{2,1,0:T(8,128)(2,1)}), bf16[8,232,128]{2,1,0:T(8,128)(2,1)S(1)}, u32[]{:S(2)}, u32[]{:S(2)}) %all-to-all-start) | async-done | bytes 475168 | tf_op jit(solution)/shard_map/all_to_all | solution.py:154
  22.8 12.7 %all_gather.8 = bf16[2,4,160,128]{3,2,1,0:T(8,128)(2,1)S(1)} all-gather(bf16[1,4,160,128]{3,2,1,0:T(8,128)(2,1)S(1)} %broadcast_select_fusion), channel_id=1, replica_groups={{0,1},{2,3},{4,5},{6,7},{8,9},{10,11},{12,13},{14,15},{16,17},{18,19},{..., dimensions={0}, use_global_device_ids=true | all-gather | bytes 491520 | tf_op jit(solution)/shard_map/all_gather | solution.py:160
  35.8 2.1 %collective-permute-start.1 = (bf16[2,160,128]{2,1,0:T(8,128)(2,1)S(1)}, bf16[2,160,128]{2,1,0:T(8,128)(2,1)S(1)}, u32[]{:S(2)}, u32[]{:S(2)}) collective-permute-start(bf16[2,160,128]{2,1,0:T(8,128)(2,1)S(1)} %fusion.3), channel_id=1, source_target_pairs={{0,24},{2,26},{4,28},{6,30},{512,536},{514,538},{516,540},{518,542... | collective-permute-start | bytes 245768 | tf_op jit(solution)/shard_map/ppermute | solution.py:133
  37.9 3.4 %collective-permute-start = (bf16[2,160,128]{2,1,0:T(8,128)(2,1)S(1)}, bf16[2,160,128]{2,1,0:T(8,128)(2,1)S(1)}, u32[]{:S(2)}, u32[]{:S(2)}) collective-permute-start(bf16[2,160,128]{2,1,0:T(8,128)(2,1)S(1)} %slice_bitcast_fusion), channel_id=1, source_target_pairs={{0,8},{2,10},{4,12},{6,14},{512,520},{514,522},{516,524},{518,526}... | collective-permute-start | bytes 245768 | tf_op jit(solution)/shard_map/ppermute | solution.py:133
  41.5 3.1 %collective-permute-done = bf16[2,160,128]{2,1,0:T(8,128)(2,1)S(1)} collective-permute-done((bf16[2,160,128]{2,1,0:T(8,128)(2,1)S(1)}, bf16[2,160,128]{2,1,0:T(8,128)(2,1)S(1)}, u32[]{:S(2)}, u32[]{:S(2)}) %collective-permute-start) | collective-permute-done | bytes 81952 | tf_op jit(solution)/shard_map/ppermute | solution.py:133
  44.7 16.5 %collective-permute-start.3 = (bf16[11,72,128]{2,1,0:T(8,128)(2,1)S(1)}, bf16[11,72,128]{2,1,0:T(8,128)(2,1)S(1)}, u32[]{:S(2)}, u32[]{:S(2)}) collective-permute-start(bf16[11,72,128]{2,1,0:T(8,128)(2,1)S(1)} %pad_maximum_fusion.4.own), channel_id=1, source_target_pairs={{32,0},{34,2},{36,4},{38,6},{544,512},{546,514},{548,516},{550,518... | collective-permute-start | bytes 608264 | tf_op jit(solution)/shard_map/ppermute | solution.py:133
  61.1 1.9 collective-permute-start.2
  63.8 5.6 %collective-permute-done.2.north = bf16[11,72,128]{2,1,0:T(8,128)(2,1)S(1)} collective-permute-done((bf16[11,72,128]{2,1,0:T(8,128)(2,1)S(1)}, bf16[11,72,128]{2,1,0:T(8,128)(2,1)S(1)}, u32[]{:S(2)}, u32[]{:S(2)}) %collective-permute-start.2) | collective-permute-done | bytes 202784 | tf_op jit(solution)/shard_map/ppermute | solution.py:133
  69.4 1.3 shard_map.64.own
  70.7 1.9 collective-permute-start.5
  72.6 3.4 %collective-permute-start.4 = (bf16[9,72,128]{2,1,0:T(8,128)(2,1)S(1)}, bf16[9,72,128]{2,1,0:T(8,128)(2,1)S(1)}, u32[]{:S(2)}, u32[]{:S(2)}) collective-permute-start(bf16[9,72,128]{2,1,0:T(8,128)(2,1)S(1)} %shard_map.64.own), channel_id=1, source_target_pairs={{0,32},{2,34},{4,36},{6,38},{512,544},{514,546},{516,548},{518,550... | collective-permute-start | bytes 497672 | tf_op jit(solution)/shard_map/ppermute | solution.py:133
  76.8 3.7 %collective-permute-done.4.north = bf16[9,72,128]{2,1,0:T(8,128)(2,1)S(1)} collective-permute-done((bf16[9,72,128]{2,1,0:T(8,128)(2,1)S(1)}, bf16[9,72,128]{2,1,0:T(8,128)(2,1)S(1)}, u32[]{:S(2)}, u32[]{:S(2)}) %collective-permute-start.4) | collective-permute-done | bytes 165920 | tf_op jit(solution)/shard_map/ppermute | solution.py:133
  80.5 1.2 shard_map.65
  81.8 1.9 collective-permute-start.7
  83.7 3.4 %collective-permute-start.6 = (bf16[2,72,128]{2,1,0:T(8,128)(2,1)S(1)}, bf16[2,72,128]{2,1,0:T(8,128)(2,1)S(1)}, u32[]{:S(2)}, u32[]{:S(2)}) collective-permute-start(bf16[2,72,128]{2,1,0:T(8,128)(2,1)S(1)} %get-tuple-element.38), channel_id=1, source_target_pairs={{0,8},{2,10},{4,12},{6,14},{512,520},{514,522},{516,524},{518,526}... | collective-permute-start | bytes 110600 | tf_op jit(solution)/shard_map/ppermute | solution.py:133
  87.1 2.5 %collective-permute-done.6 = bf16[2,72,128]{2,1,0:T(8,128)(2,1)S(1)} collective-permute-done((bf16[2,72,128]{2,1,0:T(8,128)(2,1)S(1)}, bf16[2,72,128]{2,1,0:T(8,128)(2,1)S(1)}, u32[]{:S(2)}, u32[]{:S(2)}) %collective-permute-start.6) | collective-permute-done | bytes 36896 | tf_op jit(solution)/shard_map/ppermute | solution.py:133
  89.6 2.9 %collective-permute-start.9 = (bf16[11,72,128]{2,1,0:T(8,128)(2,1)S(1)}, bf16[11,72,128]{2,1,0:T(8,128)(2,1)S(1)}, u32[]{:S(2)}, u32[]{:S(2)}) collective-permute-start(bf16[11,72,128]{2,1,0:T(8,128)(2,1)S(1)} %pad_maximum_fusion.5.own), channel_id=1, source_target_pairs={{32,0},{34,2},{36,4},{38,6},{544,512},{546,514},{548,516},{550,518... | collective-permute-start | bytes 608264 | tf_op jit(solution)/shard_map/ppermute | solution.py:133
  92.5 2.4 %collective-permute-start.8 = (bf16[11,72,128]{2,1,0:T(8,128)(2,1)S(1)}, bf16[11,72,128]{2,1,0:T(8,128)(2,1)S(1)}, u32[]{:S(2)}, u32[]{:S(2)}) collective-permute-start(bf16[11,72,128]{2,1,0:T(8,128)(2,1)S(1)} %pad_maximum_fusion.5.own), channel_id=1, source_target_pairs={{0,32},{2,34},{4,36},{6,38},{512,544},{514,546},{516,548},{518,550... | collective-permute-start | bytes 608264 | tf_op jit(solution)/shard_map/ppermute | solution.py:133
  94.9 2.3 %collective-permute-done.9.south = bf16[11,72,128]{2,1,0:T(8,128)(2,1)S(1)} collective-permute-done((bf16[11,72,128]{2,1,0:T(8,128)(2,1)S(1)}, bf16[11,72,128]{2,1,0:T(8,128)(2,1)S(1)}, u32[]{:S(2)}, u32[]{:S(2)}) %collective-permute-start.9) | collective-permute-done | bytes 202784 | tf_op jit(solution)/shard_map/ppermute | solution.py:133
  97.2 3.6 %collective-permute-done.8.north = bf16[11,72,128]{2,1,0:T(8,128)(2,1)S(1)} collective-permute-done((bf16[11,72,128]{2,1,0:T(8,128)(2,1)S(1)}, bf16[11,72,128]{2,1,0:T(8,128)(2,1)S(1)}, u32[]{:S(2)}, u32[]{:S(2)}) %collective-permute-start.8) | collective-permute-done | bytes 202784 | tf_op jit(solution)/shard_map/ppermute | solution.py:133
  100.8 1.3 shard_map.66.own
  102.1 2.8 %collective-permute-start.11 = (bf16[9,72,128]{2,1,0:T(8,128)(2,1)S(1)}, bf16[9,72,128]{2,1,0:T(8,128)(2,1)S(1)}, u32[]{:S(2)}, u32[]{:S(2)}) collective-permute-start(bf16[9,72,128]{2,1,0:T(8,128)(2,1)S(1)} %shard_map.66.own), channel_id=1, source_target_pairs={{32,0},{34,2},{36,4},{38,6},{544,512},{546,514},{548,516},{550,518... | collective-permute-start | bytes 497672 | tf_op jit(solution)/shard_map/ppermute | solution.py:133
  104.9 2.5 %collective-permute-start.10 = (bf16[9,72,128]{2,1,0:T(8,128)(2,1)S(1)}, bf16[9,72,128]{2,1,0:T(8,128)(2,1)S(1)}, u32[]{:S(2)}, u32[]{:S(2)}) collective-permute-start(bf16[9,72,128]{2,1,0:T(8,128)(2,1)S(1)} %shard_map.66.own), channel_id=1, source_target_pairs={{0,32},{2,34},{4,36},{6,38},{512,544},{514,546},{516,548},{518,550... | collective-permute-start | bytes 497672 | tf_op jit(solution)/shard_map/ppermute | solution.py:133
  108.4 4.4 %collective-permute-done.10.north = bf16[9,72,128]{2,1,0:T(8,128)(2,1)S(1)} collective-permute-done((bf16[9,72,128]{2,1,0:T(8,128)(2,1)S(1)}, bf16[9,72,128]{2,1,0:T(8,128)(2,1)S(1)}, u32[]{:S(2)}, u32[]{:S(2)}) %collective-permute-start.10) | collective-permute-done | bytes 165920 | tf_op jit(solution)/shard_map/ppermute | solution.py:133
  112.8 1.3 shard_map.67
  114.0 2.4 %collective-permute-start.12 = (bf16[2,72,128]{2,1,0:T(8,128)(2,1)S(1)}, bf16[2,72,128]{2,1,0:T(8,128)(2,1)S(1)}, u32[]{:S(2)}, u32[]{:S(2)}) collective-permute-start(bf16[2,72,128]{2,1,0:T(8,128)(2,1)S(1)} %get-tuple-element.35), channel_id=1, source_target_pairs={{0,8},{2,10},{4,12},{6,14},{512,520},{514,522},{516,524},{518,526}... | collective-permute-start | bytes 110600 | tf_op jit(solution)/shard_map/ppermute | solution.py:133
  116.5 4.1 %collective-permute-start.13 = (bf16[2,72,128]{2,1,0:T(8,128)(2,1)S(1)}, bf16[2,72,128]{2,1,0:T(8,128)(2,1)S(1)}, u32[]{:S(2)}, u32[]{:S(2)}) collective-permute-start(bf16[2,72,128]{2,1,0:T(8,128)(2,1)S(1)} %get-tuple-element.36), channel_id=1, source_target_pairs={{0,24},{2,26},{4,28},{6,30},{512,536},{514,538},{516,540},{518,542... | collective-permute-start | bytes 110600 | tf_op jit(solution)/shard_map/ppermute | solution.py:133
  121.6 1.8 shard_map.68
  123.4 4.4 %collective-permute-start.14 = (bf16[10,72,128]{2,1,0:T(8,128)(2,1)S(1)}, bf16[10,72,128]{2,1,0:T(8,128)(2,1)S(1)}, u32[]{:S(2)}, u32[]{:S(2)}) collective-permute-start(bf16[10,72,128]{2,1,0:T(8,128)(2,1)S(1)} %get-tuple-element.18), channel_id=1, source_target_pairs={{32,0},{34,2},{36,4},{38,6},{544,512},{546,514},{548,516},{550,518... | collective-permute-start | bytes 552968 | tf_op jit(solution)/shard_map/ppermute | solution.py:133
  127.9 1.9 collective-permute-start.15
  130.4 5.5 %collective-permute-done.15.rest_2_ = bf16[10,72,128]{2,1,0:T(8,128)(2,1)S(1)} collective-permute-done((bf16[10,72,128]{2,1,0:T(8,128)(2,1)S(1)}, bf16[10,72,128]{2,1,0:T(8,128)(2,1)S(1)}, u32[]{:S(2)}, u32[]{:S(2)}) %collective-permute-start.15) | collective-permute-done | bytes 184352 | tf_op jit(solution)/shard_map/ppermute | solution.py:133
  135.9 1.6 shard_map.69
  137.6 3.7 %collective-permute-start.16 = (bf16[8,72,128]{2,1,0:T(8,128)(2,1)S(1)}, bf16[8,72,128]{2,1,0:T(8,128)(2,1)S(1)}, u32[]{:S(2)}, u32[]{:S(2)}) collective-permute-start(bf16[8,72,128]{2,1,0:T(8,128)(2,1)S(1)} %get-tuple-element.21), channel_id=1, source_target_pairs={{32,0},{34,2},{36,4},{38,6},{544,512},{546,514},{548,516},{550,518... | collective-permute-start | bytes 442376 | tf_op jit(solution)/shard_map/ppermute | solution.py:133
  141.3 1.9 collective-permute-start.17
  143.5 5.5 %collective-permute-done.17 = bf16[8,72,128]{2,1,0:T(8,128)(2,1)S(1)} collective-permute-done((bf16[8,72,128]{2,1,0:T(8,128)(2,1)S(1)}, bf16[8,72,128]{2,1,0:T(8,128)(2,1)S(1)}, u32[]{:S(2)}, u32[]{:S(2)}) %collective-permute-start.17) | collective-permute-done | bytes 147488 | tf_op jit(solution)/shard_map/ppermute | solution.py:133
  149.0 1.9 collective-permute-start.18
  150.9 5.5 %collective-permute-start.19 = (bf16[2,72,128]{2,1,0:T(8,128)(2,1)S(1)}, bf16[2,72,128]{2,1,0:T(8,128)(2,1)S(1)}, u32[]{:S(2)}, u32[]{:S(2)}) collective-permute-start(bf16[2,72,128]{2,1,0:T(8,128)(2,1)S(1)} %get-tuple-element.34), channel_id=1, source_target_pairs={{0,24},{2,26},{4,28},{6,30},{512,536},{514,538},{516,540},{518,542... | collective-permute-start | bytes 110600 | tf_op jit(solution)/shard_map/ppermute | solution.py:133
  157.5 1.8 shard_map.70
  159.3 3.0 %collective-permute-start.20 = (bf16[10,72,128]{2,1,0:T(8,128)(2,1)S(1)}, bf16[10,72,128]{2,1,0:T(8,128)(2,1)S(1)}, u32[]{:S(2)}, u32[]{:S(2)}) collective-permute-start(bf16[10,72,128]{2,1,0:T(8,128)(2,1)S(1)} %get-tuple-element.24), channel_id=1, source_target_pairs={{32,0},{34,2},{36,4},{38,6},{544,512},{546,514},{548,516},{550,518... | collective-permute-start | bytes 552968 | tf_op jit(solution)/shard_map/ppermute | solution.py:133
  162.4 2.3 %collective-permute-start.21 = (bf16[10,72,128]{2,1,0:T(8,128)(2,1)S(1)}, bf16[10,72,128]{2,1,0:T(8,128)(2,1)S(1)}, u32[]{:S(2)}, u32[]{:S(2)}) collective-permute-start(bf16[10,72,128]{2,1,0:T(8,128)(2,1)S(1)} %get-tuple-element.25), channel_id=1, source_target_pairs={{0,32},{2,34},{4,36},{6,38},{512,544},{514,546},{516,548},{518,550... | collective-permute-start | bytes 552968 | tf_op jit(solution)/shard_map/ppermute | solution.py:133
  165.6 4.8 %collective-permute-done.21.rest_2_ = bf16[10,72,128]{2,1,0:T(8,128)(2,1)S(1)} collective-permute-done((bf16[10,72,128]{2,1,0:T(8,128)(2,1)S(1)}, bf16[10,72,128]{2,1,0:T(8,128)(2,1)S(1)}, u32[]{:S(2)}, u32[]{:S(2)}) %collective-permute-start.21) | collective-permute-done | bytes 184352 | tf_op jit(solution)/shard_map/ppermute | solution.py:133
  170.4 1.7 shard_map.71
  172.1 2.2 %collective-permute-start.22 = (bf16[8,72,128]{2,1,0:T(8,128)(2,1)S(1)}, bf16[8,72,128]{2,1,0:T(8,128)(2,1)S(1)}, u32[]{:S(2)}, u32[]{:S(2)}) collective-permute-start(bf16[8,72,128]{2,1,0:T(8,128)(2,1)S(1)} %get-tuple-element.27), channel_id=1, source_target_pairs={{32,0},{34,2},{36,4},{38,6},{544,512},{546,514},{548,516},{550,518... | collective-permute-start | bytes 442376 | tf_op jit(solution)/shard_map/ppermute | solution.py:133
  174.3 3.1 %collective-permute-start.23 = (bf16[8,72,128]{2,1,0:T(8,128)(2,1)S(1)}, bf16[8,72,128]{2,1,0:T(8,128)(2,1)S(1)}, u32[]{:S(2)}, u32[]{:S(2)}) collective-permute-start(bf16[8,72,128]{2,1,0:T(8,128)(2,1)S(1)} %get-tuple-element.28), channel_id=1, source_target_pairs={{0,32},{2,34},{4,36},{6,38},{512,544},{514,546},{516,548},{518,550... | collective-permute-start | bytes 442376 | tf_op jit(solution)/shard_map/ppermute | solution.py:133
  178.0 4.0 %collective-permute-done.23 = bf16[8,72,128]{2,1,0:T(8,128)(2,1)S(1)} collective-permute-done((bf16[8,72,128]{2,1,0:T(8,128)(2,1)S(1)}, bf16[8,72,128]{2,1,0:T(8,128)(2,1)S(1)}, u32[]{:S(2)}, u32[]{:S(2)}) %collective-permute-start.23) | collective-permute-done | bytes 147488 | tf_op jit(solution)/shard_map/ppermute | solution.py:133
  182.0 1.9 all-gather
  184.0 11.6 %all_to_all.10 = bf16[8,72,128]{2,1,0:T(8,128)(2,1)S(1)} all-to-all(bf16[8,72,128]{2,1,0:T(8,128)(2,1)S(1)} %pad_maximum_fusion.6), channel_id=1, replica_groups={{0,2,4,6,512,514,516,518},{1,3,5,7,513,515,517,519},{8,10,12,14,520,522..., dimensions={0} | all-to-all | bytes 294912 | tf_op jit(solution)/shard_map/all_to_all | solution.py:154
  (67 shorter events, 11.9 us)
Async XLA Ops:
  0.0 1.6 copy-start
  0.0 0.8 copy-start.3
  0.9 0.7 copy-start.4
  0.9 0.7 copy-start.5
  1.7 0.9 copy-start.2
  3.5 19.3 %all-to-all-start = ((bf16[8,232,128]{2,1,0:T(8,128)(2,1)}), bf16[8,232,128]{2,1,0:T(8,128)(2,1)S(1)}, u32[]{:S(2)}, u32[]{:S(2)}) async-start(bf16[8,232,128]{2,1,0:T(8,128)(2,1)} %pad_maximum_fusion), calls=%async_computation | async-start | bytes 950272 | tf_op jit(solution)/shard_map/all_to_all | solution.py:154
  35.7 33.7 %copy-start.1 = (bf16[16,160,128]{2,1,0:T(8,128)(2,1)S(1)}, bf16[16,160,128]{2,1,0:T(8,128)(2,1)}, u32[]{:S(2)}) copy-start(bf16[16,160,128]{2,1,0:T(8,128)(2,1)} %rest_3_.3) | copy-start | bytes 1966084
  35.8 5.7 %collective-permute-start.1 = (bf16[2,160,128]{2,1,0:T(8,128)(2,1)S(1)}, bf16[2,160,128]{2,1,0:T(8,128)(2,1)S(1)}, u32[]{:S(2)}, u32[]{:S(2)}) collective-permute-start(bf16[2,160,128]{2,1,0:T(8,128)(2,1)S(1)} %fusion.3), channel_id=1, source_target_pairs={{0,24},{2,26},{4,28},{6,30},{512,536},{514,538},{516,540},{518,542... | collective-permute-start | bytes 245768 | tf_op jit(solution)/shard_map/ppermute | solution.py:133
  37.9 6.8 %collective-permute-start = (bf16[2,160,128]{2,1,0:T(8,128)(2,1)S(1)}, bf16[2,160,128]{2,1,0:T(8,128)(2,1)S(1)}, u32[]{:S(2)}, u32[]{:S(2)}) collective-permute-start(bf16[2,160,128]{2,1,0:T(8,128)(2,1)S(1)} %slice_bitcast_fusion), channel_id=1, source_target_pairs={{0,8},{2,10},{4,12},{6,14},{512,520},{514,522},{516,524},{518,526}... | collective-permute-start | bytes 245768 | tf_op jit(solution)/shard_map/ppermute | solution.py:133
  44.7 19.1 %collective-permute-start.3 = (bf16[11,72,128]{2,1,0:T(8,128)(2,1)S(1)}, bf16[11,72,128]{2,1,0:T(8,128)(2,1)S(1)}, u32[]{:S(2)}, u32[]{:S(2)}) collective-permute-start(bf16[11,72,128]{2,1,0:T(8,128)(2,1)S(1)} %pad_maximum_fusion.4.own), channel_id=1, source_target_pairs={{32,0},{34,2},{36,4},{38,6},{544,512},{546,514},{548,516},{550,518... | collective-permute-start | bytes 608264 | tf_op jit(solution)/shard_map/ppermute | solution.py:133
  61.1 8.3 %collective-permute-start.2 = (bf16[11,72,128]{2,1,0:T(8,128)(2,1)S(1)}, bf16[11,72,128]{2,1,0:T(8,128)(2,1)S(1)}, u32[]{:S(2)}, u32[]{:S(2)}) collective-permute-start(bf16[11,72,128]{2,1,0:T(8,128)(2,1)S(1)} %pad_maximum_fusion.4.own), channel_id=1, source_target_pairs={{0,32},{2,34},{4,36},{6,38},{512,544},{514,546},{516,548},{518,550... | collective-permute-start | bytes 608264 | tf_op jit(solution)/shard_map/ppermute | solution.py:133
  70.7 6.1 %collective-permute-start.5 = (bf16[9,72,128]{2,1,0:T(8,128)(2,1)S(1)}, bf16[9,72,128]{2,1,0:T(8,128)(2,1)S(1)}, u32[]{:S(2)}, u32[]{:S(2)}) collective-permute-start(bf16[9,72,128]{2,1,0:T(8,128)(2,1)S(1)} %shard_map.64.own), channel_id=1, source_target_pairs={{32,0},{34,2},{36,4},{38,6},{544,512},{546,514},{548,516},{550,518... | collective-permute-start | bytes 497672 | tf_op jit(solution)/shard_map/ppermute | solution.py:133
  72.6 7.9 %collective-permute-start.4 = (bf16[9,72,128]{2,1,0:T(8,128)(2,1)S(1)}, bf16[9,72,128]{2,1,0:T(8,128)(2,1)S(1)}, u32[]{:S(2)}, u32[]{:S(2)}) collective-permute-start(bf16[9,72,128]{2,1,0:T(8,128)(2,1)S(1)} %shard_map.64.own), channel_id=1, source_target_pairs={{0,32},{2,34},{4,36},{6,38},{512,544},{514,546},{516,548},{518,550... | collective-permute-start | bytes 497672 | tf_op jit(solution)/shard_map/ppermute | solution.py:133
  81.8 5.3 %collective-permute-start.7 = (bf16[2,72,128]{2,1,0:T(8,128)(2,1)S(1)}, bf16[2,72,128]{2,1,0:T(8,128)(2,1)S(1)}, u32[]{:S(2)}, u32[]{:S(2)}) collective-permute-start(bf16[2,72,128]{2,1,0:T(8,128)(2,1)S(1)} %get-tuple-element.37), channel_id=1, source_target_pairs={{0,24},{2,26},{4,28},{6,30},{512,536},{514,538},{516,540},{518,542... | collective-permute-start | bytes 110600 | tf_op jit(solution)/shard_map/ppermute | solution.py:133
  83.7 5.9 %collective-permute-start.6 = (bf16[2,72,128]{2,1,0:T(8,128)(2,1)S(1)}, bf16[2,72,128]{2,1,0:T(8,128)(2,1)S(1)}, u32[]{:S(2)}, u32[]{:S(2)}) collective-permute-start(bf16[2,72,128]{2,1,0:T(8,128)(2,1)S(1)} %get-tuple-element.38), channel_id=1, source_target_pairs={{0,8},{2,10},{4,12},{6,14},{512,520},{514,522},{516,524},{518,526}... | collective-permute-start | bytes 110600 | tf_op jit(solution)/shard_map/ppermute | solution.py:133
  89.6 7.6 %collective-permute-start.9 = (bf16[11,72,128]{2,1,0:T(8,128)(2,1)S(1)}, bf16[11,72,128]{2,1,0:T(8,128)(2,1)S(1)}, u32[]{:S(2)}, u32[]{:S(2)}) collective-permute-start(bf16[11,72,128]{2,1,0:T(8,128)(2,1)S(1)} %pad_maximum_fusion.5.own), channel_id=1, source_target_pairs={{32,0},{34,2},{36,4},{38,6},{544,512},{546,514},{548,516},{550,518... | collective-permute-start | bytes 608264 | tf_op jit(solution)/shard_map/ppermute | solution.py:133
  92.5 8.3 %collective-permute-start.8 = (bf16[11,72,128]{2,1,0:T(8,128)(2,1)S(1)}, bf16[11,72,128]{2,1,0:T(8,128)(2,1)S(1)}, u32[]{:S(2)}, u32[]{:S(2)}) collective-permute-start(bf16[11,72,128]{2,1,0:T(8,128)(2,1)S(1)} %pad_maximum_fusion.5.own), channel_id=1, source_target_pairs={{0,32},{2,34},{4,36},{6,38},{512,544},{514,546},{516,548},{518,550... | collective-permute-start | bytes 608264 | tf_op jit(solution)/shard_map/ppermute | solution.py:133
  102.1 6.2 %collective-permute-start.11 = (bf16[9,72,128]{2,1,0:T(8,128)(2,1)S(1)}, bf16[9,72,128]{2,1,0:T(8,128)(2,1)S(1)}, u32[]{:S(2)}, u32[]{:S(2)}) collective-permute-start(bf16[9,72,128]{2,1,0:T(8,128)(2,1)S(1)} %shard_map.66.own), channel_id=1, source_target_pairs={{32,0},{34,2},{36,4},{38,6},{544,512},{546,514},{548,516},{550,518... | collective-permute-start | bytes 497672 | tf_op jit(solution)/shard_map/ppermute | solution.py:133
  104.9 7.9 %collective-permute-start.10 = (bf16[9,72,128]{2,1,0:T(8,128)(2,1)S(1)}, bf16[9,72,128]{2,1,0:T(8,128)(2,1)S(1)}, u32[]{:S(2)}, u32[]{:S(2)}) collective-permute-start(bf16[9,72,128]{2,1,0:T(8,128)(2,1)S(1)} %shard_map.66.own), channel_id=1, source_target_pairs={{0,32},{2,34},{4,36},{6,38},{512,544},{514,546},{516,548},{518,550... | collective-permute-start | bytes 497672 | tf_op jit(solution)/shard_map/ppermute | solution.py:133
  114.0 6.5 %collective-permute-start.12 = (bf16[2,72,128]{2,1,0:T(8,128)(2,1)S(1)}, bf16[2,72,128]{2,1,0:T(8,128)(2,1)S(1)}, u32[]{:S(2)}, u32[]{:S(2)}) collective-permute-start(bf16[2,72,128]{2,1,0:T(8,128)(2,1)S(1)} %get-tuple-element.35), channel_id=1, source_target_pairs={{0,8},{2,10},{4,12},{6,14},{512,520},{514,522},{516,524},{518,526}... | collective-permute-start | bytes 110600 | tf_op jit(solution)/shard_map/ppermute | solution.py:133
  116.5 5.1 %collective-permute-start.13 = (bf16[2,72,128]{2,1,0:T(8,128)(2,1)S(1)}, bf16[2,72,128]{2,1,0:T(8,128)(2,1)S(1)}, u32[]{:S(2)}, u32[]{:S(2)}) collective-permute-start(bf16[2,72,128]{2,1,0:T(8,128)(2,1)S(1)} %get-tuple-element.36), channel_id=1, source_target_pairs={{0,24},{2,26},{4,28},{6,30},{512,536},{514,538},{516,540},{518,542... | collective-permute-start | bytes 110600 | tf_op jit(solution)/shard_map/ppermute | solution.py:133
  123.4 7.0 %collective-permute-start.14 = (bf16[10,72,128]{2,1,0:T(8,128)(2,1)S(1)}, bf16[10,72,128]{2,1,0:T(8,128)(2,1)S(1)}, u32[]{:S(2)}, u32[]{:S(2)}) collective-permute-start(bf16[10,72,128]{2,1,0:T(8,128)(2,1)S(1)} %get-tuple-element.18), channel_id=1, source_target_pairs={{32,0},{34,2},{36,4},{38,6},{544,512},{546,514},{548,516},{550,518... | collective-permute-start | bytes 552968 | tf_op jit(solution)/shard_map/ppermute | solution.py:133
  127.9 8.1 %collective-permute-start.15 = (bf16[10,72,128]{2,1,0:T(8,128)(2,1)S(1)}, bf16[10,72,128]{2,1,0:T(8,128)(2,1)S(1)}, u32[]{:S(2)}, u32[]{:S(2)}) collective-permute-start(bf16[10,72,128]{2,1,0:T(8,128)(2,1)S(1)} %get-tuple-element.19), channel_id=1, source_target_pairs={{0,32},{2,34},{4,36},{6,38},{512,544},{514,546},{516,548},{518,550... | collective-permute-start | bytes 552968 | tf_op jit(solution)/shard_map/ppermute | solution.py:133
  137.6 5.9 %collective-permute-start.16 = (bf16[8,72,128]{2,1,0:T(8,128)(2,1)S(1)}, bf16[8,72,128]{2,1,0:T(8,128)(2,1)S(1)}, u32[]{:S(2)}, u32[]{:S(2)}) collective-permute-start(bf16[8,72,128]{2,1,0:T(8,128)(2,1)S(1)} %get-tuple-element.21), channel_id=1, source_target_pairs={{32,0},{34,2},{36,4},{38,6},{544,512},{546,514},{548,516},{550,518... | collective-permute-start | bytes 442376 | tf_op jit(solution)/shard_map/ppermute | solution.py:133
  141.3 7.7 %collective-permute-start.17 = (bf16[8,72,128]{2,1,0:T(8,128)(2,1)S(1)}, bf16[8,72,128]{2,1,0:T(8,128)(2,1)S(1)}, u32[]{:S(2)}, u32[]{:S(2)}) collective-permute-start(bf16[8,72,128]{2,1,0:T(8,128)(2,1)S(1)} %get-tuple-element.22), channel_id=1, source_target_pairs={{0,32},{2,34},{4,36},{6,38},{512,544},{514,546},{516,548},{518,550... | collective-permute-start | bytes 442376 | tf_op jit(solution)/shard_map/ppermute | solution.py:133
  149.0 7.4 %collective-permute-start.18 = (bf16[2,72,128]{2,1,0:T(8,128)(2,1)S(1)}, bf16[2,72,128]{2,1,0:T(8,128)(2,1)S(1)}, u32[]{:S(2)}, u32[]{:S(2)}) collective-permute-start(bf16[2,72,128]{2,1,0:T(8,128)(2,1)S(1)} %get-tuple-element.33), channel_id=1, source_target_pairs={{0,8},{2,10},{4,12},{6,14},{512,520},{514,522},{516,524},{518,526}... | collective-permute-start | bytes 110600 | tf_op jit(solution)/shard_map/ppermute | solution.py:133
  150.9 6.5 %collective-permute-start.19 = (bf16[2,72,128]{2,1,0:T(8,128)(2,1)S(1)}, bf16[2,72,128]{2,1,0:T(8,128)(2,1)S(1)}, u32[]{:S(2)}, u32[]{:S(2)}) collective-permute-start(bf16[2,72,128]{2,1,0:T(8,128)(2,1)S(1)} %get-tuple-element.34), channel_id=1, source_target_pairs={{0,24},{2,26},{4,28},{6,30},{512,536},{514,538},{516,540},{518,542... | collective-permute-start | bytes 110600 | tf_op jit(solution)/shard_map/ppermute | solution.py:133
  159.3 6.3 %collective-permute-start.20 = (bf16[10,72,128]{2,1,0:T(8,128)(2,1)S(1)}, bf16[10,72,128]{2,1,0:T(8,128)(2,1)S(1)}, u32[]{:S(2)}, u32[]{:S(2)}) collective-permute-start(bf16[10,72,128]{2,1,0:T(8,128)(2,1)S(1)} %get-tuple-element.24), channel_id=1, source_target_pairs={{32,0},{34,2},{36,4},{38,6},{544,512},{546,514},{548,516},{550,518... | collective-permute-start | bytes 552968 | tf_op jit(solution)/shard_map/ppermute | solution.py:133
  162.4 8.1 %collective-permute-start.21 = (bf16[10,72,128]{2,1,0:T(8,128)(2,1)S(1)}, bf16[10,72,128]{2,1,0:T(8,128)(2,1)S(1)}, u32[]{:S(2)}, u32[]{:S(2)}) collective-permute-start(bf16[10,72,128]{2,1,0:T(8,128)(2,1)S(1)} %get-tuple-element.25), channel_id=1, source_target_pairs={{0,32},{2,34},{4,36},{6,38},{512,544},{514,546},{516,548},{518,550... | collective-permute-start | bytes 552968 | tf_op jit(solution)/shard_map/ppermute | solution.py:133
  172.1 5.9 %collective-permute-start.22 = (bf16[8,72,128]{2,1,0:T(8,128)(2,1)S(1)}, bf16[8,72,128]{2,1,0:T(8,128)(2,1)S(1)}, u32[]{:S(2)}, u32[]{:S(2)}) collective-permute-start(bf16[8,72,128]{2,1,0:T(8,128)(2,1)S(1)} %get-tuple-element.27), channel_id=1, source_target_pairs={{32,0},{34,2},{36,4},{38,6},{544,512},{546,514},{548,516},{550,518... | collective-permute-start | bytes 442376 | tf_op jit(solution)/shard_map/ppermute | solution.py:133
  174.3 7.7 %collective-permute-start.23 = (bf16[8,72,128]{2,1,0:T(8,128)(2,1)S(1)}, bf16[8,72,128]{2,1,0:T(8,128)(2,1)S(1)}, u32[]{:S(2)}, u32[]{:S(2)}) collective-permute-start(bf16[8,72,128]{2,1,0:T(8,128)(2,1)S(1)} %get-tuple-element.28), channel_id=1, source_target_pairs={{0,32},{2,34},{4,36},{6,38},{512,544},{514,546},{516,548},{518,550... | collective-permute-start | bytes 442376 | tf_op jit(solution)/shard_map/ppermute | solution.py:133

commit v5 on v4

--- a/solution.py
+++ b/solution.py
@@ -169,42 +169,35 @@
     tail = jnp.concatenate([jnp.broadcast_to(numbers[:, None], (count, cols)), jnp.zeros((16 - count, cols), BF16)])
     part = lax.dynamic_index_in_dim(column_mix[:, 0], lax.axis_index("lon") // 2 % column_mix.shape[0], keepdims=False)
     part = jnp.pad(part, ((0, 0), (0, cols - levels)))
-    shared = jnp.concatenate([obs_weight[:, 0].astype(BF16), tail, part])
+    shared = jnp.concatenate([tail, obs_weight[:, 0].astype(BF16), part])
     bundle = along_y(
         jnp.concatenate([vector[:, :, 0], jnp.broadcast_to(shared[None], (run, *shared.shape))], axis=1)
     )
     bundle = bundle.reshape(2, run // 2, *bundle.shape[1:])
     mix = jnp.where(first, bundle[0, :, -levels:], bundle[1, :, -levels:])
     bundle = jnp.stack(swap_cores(bundle[:, :, :-levels], first), axis=1).reshape(run, -1, cols)
-    state, obs = bundle[:, :levels], bundle[:, levels : 2 * levels]
-    west, east = from_lon(bundle[-2:], -run), from_lon(bundle[:2], run)
+    marked = levels + tail.shape[0]
+    state, obs = bundle[:, :levels], bundle[:, marked:]
+    reach = column_mix.shape[0]
+    west, east = from_lon(bundle[-reach:, :marked], -run), from_lon(bundle[:reach, :marked], run)
 
     def read(part):
-        return jnp.max(part[:, 2 * levels : 2 * levels + count].astype(F32), axis=2).astype(jnp.int32)
+        return jnp.max(part[:, levels : levels + count].astype(F32), axis=2).astype(jnp.int32)
 
     par = jnp.concatenate([read(west), read(bundle), read(east)])
-    west, east = west[:, :levels], east[:, :levels]
-
-    for step in range(0, 4, 2):
-        if step > 0:
-            west, east = from_lon(state[-2:], -run), from_lon(state[:2], run)
-        rightward = right_lanes((levels, cols))
-        outer = jnp.where(rightward, east[1], west[0])
-        wide = jnp.concatenate([west[1:], state, east[:1], outer[None]])
-        wide = forward(step, run + 2, True, par, (wide, from_lat(wide, -1), from_lat(wide, 1)), interp_table, mix)
-        state = forward(
-            step + 1, run, False, par, (wide, from_lat(wide, -1), from_lat(wide, 1)), interp_table, mix,
-            obs if step == 2 else None,
-        )
-
-    cot = state
-    for step in (3, 1):
-        west, east = from_lon(cot[-2:], -run), from_lon(cot[:2], run)
-        wide = jnp.concatenate([west, cot, east])
-        north, stay, south = adjoint(step, par, (wide,), interp_table, mix)
+    outer = jnp.where(right_lanes((levels, cols)), east[-1, :levels], west[0, :levels])
+    state = jnp.concatenate([west[1:, :levels], state, east[:-1, :levels], outer[None]])
+    for step in range(reach):
+        last = step == reach - 1
+        rows = (state, from_lat(state, -1), from_lat(state, 1))
+        state = forward(step, run + 2 * (reach - 1 - step), not last, par, rows, interp_table, mix, obs if last else None)
+
+    west, east = from_lon(state[-reach:], -run), from_lon(state[:reach], run)
+    parts = (jnp.concatenate([west, state, east]),)
+    for step in reversed(range(reach)):
+        north, stay, south = adjoint(step, par, parts, interp_table, mix)
         parts = (stay, from_lat(north, 1), from_lat(south, -1))
-        north, stay, south = adjoint(step - 1, par, parts, interp_table, mix)
-        cot = (stay + from_lat(north, 1).astype(F32) + from_lat(south, -1).astype(F32)).astype(BF16)
+    cot = sum(part.astype(F32) for part in parts).astype(BF16)
     cot = cot.reshape(run // 2, 2, levels, cols)
     lower, upper = swap_cores((cot[:, 0], cot[:, 1]), first)
     return along_y(jnp.concatenate([lower, upper]))[:, :, None]

time: 198 us -> 183 us (0.924)
  starting transfers between devices: 89 us -> 76.5 us
  waiting for transfers between devices: 63.7 us -> 61.5 us
    ppermute x24 -> x20, starting transfers between devices: 81.3 us -> 68.8 us  [move(): return lax.ppermute(value, ('lat', 'lon'), pairs)]
    ppermute x24 -> x20, waiting for transfers between devices: 52.1 us -> 49.9 us  [move(): return lax.ppermute(value, ('lat', 'lon'), pairs)]
  transfers between devices with their start and end apart: 25 -> 21, of which waited for: 22 -> 20; matrix products, arithmetic and copies ran while one was open for 0% -> 0% of each run, Pallas kernels for 0% -> 0%
where the time goes in v5:
time: 183 us; the launch traced here: 182 us
  starting transfers between devices  76.5 us (42%)
  waiting for transfers between devices  61.5 us (34%)
  blocking collectives  26.2 us (14%)
  Pallas kernels  12.9 us (7%)
  local copies, waits for them, and re-layouts  3.13 us (2%)
    ppermute x20, starting transfers between devices, move(): return lax.ppermute(value, ('lat', 'lon'), pairs)  68.8 us
    ppermute x20, waiting for transfers between devices, move(): return lax.ppermute(value, ('lat', 'lon'), pairs)  49.9 us
    all_gather x2, blocking collectives, swap_cores(): lax.all_gather(give, 'lon', axis_index_groups=[[i, i + 1] for i in range(...  14.6 us
    all_to_all x1, waiting for transfers between devices, along_y(): return lax.all_to_all(value, ('lat', 'lon'), 0, 0, axis_index_groups=groups)  11.6 us
    all_to_all x1, blocking collectives, along_y(): return lax.all_to_all(value, ('lat', 'lon'), 0, 0, axis_index_groups=groups)  11.6 us
    all_to_all x1, starting transfers between devices, along_y(): return lax.all_to_all(value, ('lat', 'lon'), 0, 0, axis_index_groups=groups)  7.65 us
    pallas_call x4, Pallas kernels, adjoint(): pl.pallas_call(functools.partial(adjoint_kernel, step, first, reads, len(...  7.64 us
    pallas_call x4, Pallas kernels, forward(): pl.pallas_call(functools.partial(forward_kernel, step, first, outs, fold,...  5.27 us
  transfers between devices with their start and end apart: 21, of which 20 were waited for; matrix products, arithmetic and copies ran while one was open for 0% of the time, Pallas kernels for 0%

profile of v5, /device:TPU:1, one launch (start us, length us, event | category | flops | bytes accessed | tf_op | source)
XLA Modules:
  0.0 182.3 jit_solution(9894650618171268766)
XLA Ops:
  3.5 7.7 %all-to-all-start = ((bf16[8,232,128]{2,1,0:T(8,128)(2,1)}), bf16[8,232,128]{2,1,0:T(8,128)(2,1)S(1)}, u32[]{:S(2)}, u32[]{:S(2)}) async-start(bf16[8,232,128]{2,1,0:T(8,128)(2,1)} %pad_maximum_fusion), calls=%async_computation | async-start | bytes 950272 | tf_op jit(solution)/shard_map/all_to_all | solution.py:154
  11.1 11.6 %all-to-all-done = bf16[8,232,128]{2,1,0:T(8,128)(2,1)S(1)} async-done(((bf16[8,232,128]{2,1,0:T(8,128)(2,1)}), bf16[8,232,128]{2,1,0:T(8,128)(2,1)S(1)}, u32[]{:S(2)}, u32[]{:S(2)}) %all-to-all-start) | async-done | bytes 475168 | tf_op jit(solution)/shard_map/all_to_all | solution.py:154
  22.8 12.7 %all_gather.8 = bf16[2,4,160,128]{3,2,1,0:T(8,128)(2,1)S(1)} all-gather(bf16[1,4,160,128]{3,2,1,0:T(8,128)(2,1)S(1)} %broadcast_select_fusion), channel_id=1, replica_groups={{0,1},{2,3},{4,5},{6,7},{8,9},{10,11},{12,13},{14,15},{16,17},{18,19},{..., dimensions={0}, use_global_device_ids=true | all-gather | bytes 491520 | tf_op jit(solution)/shard_map/all_gather | solution.py:160
  35.8 2.1 %collective-permute-start = (bf16[4,88,128]{2,1,0:T(8,128)(2,1)S(1)}, bf16[4,88,128]{2,1,0:T(8,128)(2,1)S(1)}, u32[]{:S(2)}, u32[]{:S(2)}) collective-permute-start(bf16[4,88,128]{2,1,0:T(8,128)(2,1)S(1)} %get-tuple-element.33), channel_id=1, source_target_pairs={{0,8},{2,10},{4,12},{6,14},{512,520},{514,522},{516,524},{518,526}... | collective-permute-start | bytes 270344 | tf_op jit(solution)/shard_map/ppermute | solution.py:133
  37.8 4.6 %collective-permute-start.1 = (bf16[4,88,128]{2,1,0:T(8,128)(2,1)S(1)}, bf16[4,88,128]{2,1,0:T(8,128)(2,1)S(1)}, u32[]{:S(2)}, u32[]{:S(2)}) collective-permute-start(bf16[4,88,128]{2,1,0:T(8,128)(2,1)S(1)} %get-tuple-element.34), channel_id=1, source_target_pairs={{0,24},{2,26},{4,28},{6,30},{512,536},{514,538},{516,540},{518,542... | collective-permute-start | bytes 270344 | tf_op jit(solution)/shard_map/ppermute | solution.py:133
  44.0 14.7 %collective-permute-start.3 = (bf16[15,72,128]{2,1,0:T(8,128)(2,1)S(1)}, bf16[15,72,128]{2,1,0:T(8,128)(2,1)S(1)}, u32[]{:S(2)}, u32[]{:S(2)}) collective-permute-start(bf16[15,72,128]{2,1,0:T(8,128)(2,1)S(1)} %pad_maximum_fusion.3.own), channel_id=1, source_target_pairs={{32,0},{34,2},{36,4},{38,6},{544,512},{546,514},{548,516},{550,518... | collective-permute-start | bytes 829448 | tf_op jit(solution)/shard_map/ppermute | solution.py:133
  58.7 1.9 %collective-permute-start.2 = (bf16[15,72,128]{2,1,0:T(8,128)(2,1)S(1)}, bf16[15,72,128]{2,1,0:T(8,128)(2,1)S(1)}, u32[]{:S(2)}, u32[]{:S(2)}) collective-permute-start(bf16[15,72,128]{2,1,0:T(8,128)(2,1)S(1)} %pad_maximum_fusion.3.own), channel_id=1, source_target_pairs={{0,32},{2,34},{4,36},{6,38},{512,544},{514,546},{516,548},{518,550... | collective-permute-start | bytes 829448 | tf_op jit(solution)/shard_map/ppermute | solution.py:133
  60.9 1.3 collective-permute-done.3.south
  62.2 5.6 %collective-permute-done.2.north = bf16[15,72,128]{2,1,0:T(8,128)(2,1)S(1)} collective-permute-done((bf16[15,72,128]{2,1,0:T(8,128)(2,1)S(1)}, bf16[15,72,128]{2,1,0:T(8,128)(2,1)S(1)}, u32[]{:S(2)}, u32[]{:S(2)}) %collective-permute-start.2) | collective-permute-done | bytes 276512 | tf_op jit(solution)/shard_map/ppermute | solution.py:133
  67.8 1.4 shard_map.64.own
  69.2 2.3 %collective-permute-start.5 = (bf16[13,72,128]{2,1,0:T(8,128)(2,1)S(1)}, bf16[13,72,128]{2,1,0:T(8,128)(2,1)S(1)}, u32[]{:S(2)}, u32[]{:S(2)}) collective-permute-start(bf16[13,72,128]{2,1,0:T(8,128)(2,1)S(1)} %shard_map.64.own), channel_id=1, source_target_pairs={{32,0},{34,2},{36,4},{38,6},{544,512},{546,514},{548,516},{550,518... | collective-permute-start | bytes 718856 | tf_op jit(solution)/shard_map/ppermute | solution.py:133
  71.5 3.0 %collective-permute-start.4 = (bf16[13,72,128]{2,1,0:T(8,128)(2,1)S(1)}, bf16[13,72,128]{2,1,0:T(8,128)(2,1)S(1)}, u32[]{:S(2)}, u32[]{:S(2)}) collective-permute-start(bf16[13,72,128]{2,1,0:T(8,128)(2,1)S(1)} %shard_map.64.own), channel_id=1, source_target_pairs={{0,32},{2,34},{4,36},{6,38},{512,544},{514,546},{516,548},{518,550... | collective-permute-start | bytes 718856 | tf_op jit(solution)/shard_map/ppermute | solution.py:133
  74.5 3.8 %collective-permute-done.5.south = bf16[13,72,128]{2,1,0:T(8,128)(2,1)S(1)} collective-permute-done((bf16[13,72,128]{2,1,0:T(8,128)(2,1)S(1)}, bf16[13,72,128]{2,1,0:T(8,128)(2,1)S(1)}, u32[]{:S(2)}, u32[]{:S(2)}) %collective-permute-start.5) | collective-permute-done | bytes 239648 | tf_op jit(solution)/shard_map/ppermute | solution.py:133
  78.3 1.8 collective-permute-done.4.north
  80.1 1.3 shard_map.65.own
  81.5 1.9 %collective-permute-start.7 = (bf16[11,72,128]{2,1,0:T(8,128)(2,1)S(1)}, bf16[11,72,128]{2,1,0:T(8,128)(2,1)S(1)}, u32[]{:S(2)}, u32[]{:S(2)}) collective-permute-start(bf16[11,72,128]{2,1,0:T(8,128)(2,1)S(1)} %shard_map.65.own), channel_id=1, source_target_pairs={{32,0},{34,2},{36,4},{38,6},{544,512},{546,514},{548,516},{550,518... | collective-permute-start | bytes 608264 | tf_op jit(solution)/shard_map/ppermute | solution.py:133
  83.4 3.7 %collective-permute-start.6 = (bf16[11,72,128]{2,1,0:T(8,128)(2,1)S(1)}, bf16[11,72,128]{2,1,0:T(8,128)(2,1)S(1)}, u32[]{:S(2)}, u32[]{:S(2)}) collective-permute-start(bf16[11,72,128]{2,1,0:T(8,128)(2,1)S(1)} %shard_map.65.own), channel_id=1, source_target_pairs={{0,32},{2,34},{4,36},{6,38},{512,544},{514,546},{516,548},{518,550... | collective-permute-start | bytes 608264 | tf_op jit(solution)/shard_map/ppermute | solution.py:133
  87.1 3.2 %collective-permute-done.7.south = bf16[11,72,128]{2,1,0:T(8,128)(2,1)S(1)} collective-permute-done((bf16[11,72,128]{2,1,0:T(8,128)(2,1)S(1)}, bf16[11,72,128]{2,1,0:T(8,128)(2,1)S(1)}, u32[]{:S(2)}, u32[]{:S(2)}) %collective-permute-start.7) | collective-permute-done | bytes 202784 | tf_op jit(solution)/shard_map/ppermute | solution.py:133
  90.3 1.4 collective-permute-done.6.north
  91.7 1.3 shard_map.66.own
  93.0 2.7 %collective-permute-start.9 = (bf16[9,72,128]{2,1,0:T(8,128)(2,1)S(1)}, bf16[9,72,128]{2,1,0:T(8,128)(2,1)S(1)}, u32[]{:S(2)}, u32[]{:S(2)}) collective-permute-start(bf16[9,72,128]{2,1,0:T(8,128)(2,1)S(1)} %shard_map.66.own), channel_id=1, source_target_pairs={{32,0},{34,2},{36,4},{38,6},{544,512},{546,514},{548,516},{550,518... | collective-permute-start | bytes 497672 | tf_op jit(solution)/shard_map/ppermute | solution.py:133
  95.6 2.8 %collective-permute-start.8 = (bf16[9,72,128]{2,1,0:T(8,128)(2,1)S(1)}, bf16[9,72,128]{2,1,0:T(8,128)(2,1)S(1)}, u32[]{:S(2)}, u32[]{:S(2)}) collective-permute-start(bf16[9,72,128]{2,1,0:T(8,128)(2,1)S(1)} %shard_map.66.own), channel_id=1, source_target_pairs={{0,32},{2,34},{4,36},{6,38},{512,544},{514,546},{516,548},{518,550... | collective-permute-start | bytes 497672 | tf_op jit(solution)/shard_map/ppermute | solution.py:133
  99.6 4.0 %collective-permute-done.8.north = bf16[9,72,128]{2,1,0:T(8,128)(2,1)S(1)} collective-permute-done((bf16[9,72,128]{2,1,0:T(8,128)(2,1)S(1)}, bf16[9,72,128]{2,1,0:T(8,128)(2,1)S(1)}, u32[]{:S(2)}, u32[]{:S(2)}) %collective-permute-start.8) | collective-permute-done | bytes 165920 | tf_op jit(solution)/shard_map/ppermute | solution.py:133
  103.5 1.3 shard_map.67
  104.8 3.1 %collective-permute-start.10 = (bf16[4,72,128]{2,1,0:T(8,128)(2,1)S(1)}, bf16[4,72,128]{2,1,0:T(8,128)(2,1)S(1)}, u32[]{:S(2)}, u32[]{:S(2)}) collective-permute-start(bf16[4,72,128]{2,1,0:T(8,128)(2,1)S(1)} %get-tuple-element.35), channel_id=1, source_target_pairs={{0,8},{2,10},{4,12},{6,14},{512,520},{514,522},{516,524},{518,526}... | collective-permute-start | bytes 221192 | tf_op jit(solution)/shard_map/ppermute | solution.py:133
  107.9 3.4 %collective-permute-start.11 = (bf16[4,72,128]{2,1,0:T(8,128)(2,1)S(1)}, bf16[4,72,128]{2,1,0:T(8,128)(2,1)S(1)}, u32[]{:S(2)}, u32[]{:S(2)}) collective-permute-start(bf16[4,72,128]{2,1,0:T(8,128)(2,1)S(1)} %get-tuple-element.36), channel_id=1, source_target_pairs={{0,24},{2,26},{4,28},{6,30},{512,536},{514,538},{516,540},{518,542... | collective-permute-start | bytes 221192 | tf_op jit(solution)/shard_map/ppermute | solution.py:133
  111.3 1.7 collective-permute-done.11
  113.1 2.1 %shard_map.68 = (bf16[14,72,128]{2,1,0:T(8,128)(2,1)S(1)}, f32[14,72,128]{2,1,0:T(8,128)S(1)}, bf16[14,72,128]{2,1,0:T(8,128)(2,1)S(1)}) custom-call(s32[16,8]{1,0:T(8,128)S(1)} %pad_add_fusion.par, bf16[16,72,128]{2,1,0:T(8,128)(2,1)S(1)} %pad_maximum_fusion.2.rest_0_, bf16[16,160,128]{2,1,0:T(8,128)(2,1)S(1)} %copy-done.1, ...), custom_call_target="tpu_custom_call" | custom-call | flops 96000000 | bytes 2000000 | tf_op jit(solution)/shard_map/pallas_call | solution.py:105
  115.2 4.7 %collective-permute-start.12 = (bf16[14,72,128]{2,1,0:T(8,128)(2,1)S(1)}, bf16[14,72,128]{2,1,0:T(8,128)(2,1)S(1)}, u32[]{:S(2)}, u32[]{:S(2)}) collective-permute-start(bf16[14,72,128]{2,1,0:T(8,128)(2,1)S(1)} %get-tuple-element.18), channel_id=1, source_target_pairs={{32,0},{34,2},{36,4},{38,6},{544,512},{546,514},{548,516},{550,518... | collective-permute-start | bytes 774152 | tf_op jit(solution)/shard_map/ppermute | solution.py:133
  119.9 1.9 %collective-permute-start.13 = (bf16[14,72,128]{2,1,0:T(8,128)(2,1)S(1)}, bf16[14,72,128]{2,1,0:T(8,128)(2,1)S(1)}, u32[]{:S(2)}, u32[]{:S(2)}) collective-permute-start(bf16[14,72,128]{2,1,0:T(8,128)(2,1)S(1)} %get-tuple-element.19), channel_id=1, source_target_pairs={{0,32},{2,34},{4,36},{6,38},{512,544},{514,546},{516,548},{518,550... | collective-permute-start | bytes 774152 | tf_op jit(solution)/shard_map/ppermute | solution.py:133
  121.9 1.3 collective-permute-done.12.rest_1_
  123.2 5.6 %collective-permute-done.13.rest_2_ = bf16[14,72,128]{2,1,0:T(8,128)(2,1)S(1)} collective-permute-done((bf16[14,72,128]{2,1,0:T(8,128)(2,1)S(1)}, bf16[14,72,128]{2,1,0:T(8,128)(2,1)S(1)}, u32[]{:S(2)}, u32[]{:S(2)}) %collective-permute-start.13) | collective-permute-done | bytes 258080 | tf_op jit(solution)/shard_map/ppermute | solution.py:133
  128.8 2.0 %shard_map.69 = (bf16[12,72,128]{2,1,0:T(8,128)(2,1)S(1)}, f32[12,72,128]{2,1,0:T(8,128)S(1)}, bf16[12,72,128]{2,1,0:T(8,128)(2,1)S(1)}) custom-call(s32[16,8]{1,0:T(8,128)S(1)} %pad_add_fusion.par, f32[14,72,128]{2,1,0:T(8,128)S(1)} %get-tuple-element.17.rest_0_, bf16[14,72,128]{2,1,0:T(8,128)(2,1)S(1)} %collective-permute-done.12.rest_1_, ...), custom_call_target="tpu_custom_call" | custom-call | flops 84000000 | bytes 2000000 | tf_op jit(solution)/shard_map/pallas_call | solution.py:105
  130.8 2.5 %collective-permute-start.14 = (bf16[12,72,128]{2,1,0:T(8,128)(2,1)S(1)}, bf16[12,72,128]{2,1,0:T(8,128)(2,1)S(1)}, u32[]{:S(2)}, u32[]{:S(2)}) collective-permute-start(bf16[12,72,128]{2,1,0:T(8,128)(2,1)S(1)} %get-tuple-element.21), channel_id=1, source_target_pairs={{32,0},{34,2},{36,4},{38,6},{544,512},{546,514},{548,516},{550,518... | collective-permute-start | bytes 663560 | tf_op jit(solution)/shard_map/ppermute | solution.py:133
  133.3 2.8 %collective-permute-start.15 = (bf16[12,72,128]{2,1,0:T(8,128)(2,1)S(1)}, bf16[12,72,128]{2,1,0:T(8,128)(2,1)S(1)}, u32[]{:S(2)}, u32[]{:S(2)}) collective-permute-start(bf16[12,72,128]{2,1,0:T(8,128)(2,1)S(1)} %get-tuple-element.22), channel_id=1, source_target_pairs={{0,32},{2,34},{4,36},{6,38},{512,544},{514,546},{516,548},{518,550... | collective-permute-start | bytes 663560 | tf_op jit(solution)/shard_map/ppermute | solution.py:133
  136.1 3.2 %collective-permute-done.14.rest_1_ = bf16[12,72,128]{2,1,0:T(8,128)(2,1)S(1)} collective-permute-done((bf16[12,72,128]{2,1,0:T(8,128)(2,1)S(1)}, bf16[12,72,128]{2,1,0:T(8,128)(2,1)S(1)}, u32[]{:S(2)}, u32[]{:S(2)}) %collective-permute-start.14) | collective-permute-done | bytes 221216 | tf_op jit(solution)/shard_map/ppermute | solution.py:133
  139.3 2.5 %collective-permute-done.15.rest_2_ = bf16[12,72,128]{2,1,0:T(8,128)(2,1)S(1)} collective-permute-done((bf16[12,72,128]{2,1,0:T(8,128)(2,1)S(1)}, bf16[12,72,128]{2,1,0:T(8,128)(2,1)S(1)}, u32[]{:S(2)}, u32[]{:S(2)}) %collective-permute-start.15) | collective-permute-done | bytes 221216 | tf_op jit(solution)/shard_map/ppermute | solution.py:133
  141.8 1.8 %shard_map.70 = (bf16[10,72,128]{2,1,0:T(8,128)(2,1)S(1)}, f32[10,72,128]{2,1,0:T(8,128)S(1)}, bf16[10,72,128]{2,1,0:T(8,128)(2,1)S(1)}) custom-call(s32[16,8]{1,0:T(8,128)S(1)} %pad_add_fusion.par, f32[12,72,128]{2,1,0:T(8,128)S(1)} %get-tuple-element.20.rest_0_, bf16[12,72,128]{2,1,0:T(8,128)(2,1)S(1)} %collective-permute-done.14.rest_1_, ...), custom_call_target="tpu_custom_call" | custom-call | flops 72000000 | bytes 2000000 | tf_op jit(solution)/shard_map/pallas_call | solution.py:105
  143.6 3.5 %collective-permute-start.16 = (bf16[10,72,128]{2,1,0:T(8,128)(2,1)S(1)}, bf16[10,72,128]{2,1,0:T(8,128)(2,1)S(1)}, u32[]{:S(2)}, u32[]{:S(2)}) collective-permute-start(bf16[10,72,128]{2,1,0:T(8,128)(2,1)S(1)} %get-tuple-element.24), channel_id=1, source_target_pairs={{32,0},{34,2},{36,4},{38,6},{544,512},{546,514},{548,516},{550,518... | collective-permute-start | bytes 552968 | tf_op jit(solution)/shard_map/ppermute | solution.py:133
  147.1 1.9 %collective-permute-start.17 = (bf16[10,72,128]{2,1,0:T(8,128)(2,1)S(1)}, bf16[10,72,128]{2,1,0:T(8,128)(2,1)S(1)}, u32[]{:S(2)}, u32[]{:S(2)}) collective-permute-start(bf16[10,72,128]{2,1,0:T(8,128)(2,1)S(1)} %get-tuple-element.25), channel_id=1, source_target_pairs={{0,32},{2,34},{4,36},{6,38},{512,544},{514,546},{516,548},{518,550... | collective-permute-start | bytes 552968 | tf_op jit(solution)/shard_map/ppermute | solution.py:133
  149.0 2.5 %collective-permute-done.16.rest_1_ = bf16[10,72,128]{2,1,0:T(8,128)(2,1)S(1)} collective-permute-done((bf16[10,72,128]{2,1,0:T(8,128)(2,1)S(1)}, bf16[10,72,128]{2,1,0:T(8,128)(2,1)S(1)}, u32[]{:S(2)}, u32[]{:S(2)}) %collective-permute-start.16) | collective-permute-done | bytes 184352 | tf_op jit(solution)/shard_map/ppermute | solution.py:133
  151.5 3.7 %collective-permute-done.17.rest_2_ = bf16[10,72,128]{2,1,0:T(8,128)(2,1)S(1)} collective-permute-done((bf16[10,72,128]{2,1,0:T(8,128)(2,1)S(1)}, bf16[10,72,128]{2,1,0:T(8,128)(2,1)S(1)}, u32[]{:S(2)}, u32[]{:S(2)}) %collective-permute-start.17) | collective-permute-done | bytes 184352 | tf_op jit(solution)/shard_map/ppermute | solution.py:133
  155.2 1.6 shard_map.71
  156.8 3.5 %collective-permute-start.18 = (bf16[8,72,128]{2,1,0:T(8,128)(2,1)S(1)}, bf16[8,72,128]{2,1,0:T(8,128)(2,1)S(1)}, u32[]{:S(2)}, u32[]{:S(2)}) collective-permute-start(bf16[8,72,128]{2,1,0:T(8,128)(2,1)S(1)} %get-tuple-element.27), channel_id=1, source_target_pairs={{32,0},{34,2},{36,4},{38,6},{544,512},{546,514},{548,516},{550,518... | collective-permute-start | bytes 442376 | tf_op jit(solution)/shard_map/ppermute | solution.py:133
  160.3 1.9 %collective-permute-start.19 = (bf16[8,72,128]{2,1,0:T(8,128)(2,1)S(1)}, bf16[8,72,128]{2,1,0:T(8,128)(2,1)S(1)}, u32[]{:S(2)}, u32[]{:S(2)}) collective-permute-start(bf16[8,72,128]{2,1,0:T(8,128)(2,1)S(1)} %get-tuple-element.28), channel_id=1, source_target_pairs={{0,32},{2,34},{4,36},{6,38},{512,544},{514,546},{516,548},{518,550... | collective-permute-start | bytes 442376 | tf_op jit(solution)/shard_map/ppermute | solution.py:133
  162.7 5.3 %collective-permute-done.19 = bf16[8,72,128]{2,1,0:T(8,128)(2,1)S(1)} collective-permute-done((bf16[8,72,128]{2,1,0:T(8,128)(2,1)S(1)}, bf16[8,72,128]{2,1,0:T(8,128)(2,1)S(1)}, u32[]{:S(2)}, u32[]{:S(2)}) %collective-permute-start.19) | collective-permute-done | bytes 147488 | tf_op jit(solution)/shard_map/ppermute | solution.py:133
  168.1 1.9 %all-gather = bf16[8,1,72,128]{3,2,1,0:T(8,128)(2,1)S(1)} all-gather(bf16[4,1,72,128]{3,2,1,0:T(8,128)(2,1)S(1)} %bitcast_select_fusion), channel_id=2, replica_groups={{0,1},{2,3},{4,5},{6,7},{8,9},{10,11},{12,13},{14,15},{16,17},{18,19},{..., dimensions={0}, use_global_device_ids=true | all-gather | bytes 221184 | tf_op jit(solution)/shard_map/all_gather | solution.py:160
  170.0 11.6 %all_to_all.10 = bf16[8,72,128]{2,1,0:T(8,128)(2,1)S(1)} all-to-all(bf16[8,72,128]{2,1,0:T(8,128)(2,1)S(1)} %pad_maximum_fusion.4), channel_id=1, replica_groups={{0,2,4,6,512,514,516,518},{1,3,5,7,513,515,517,519},{8,10,12,14,520,522..., dimensions={0} | all-to-all | bytes 294912 | tf_op jit(solution)/shard_map/all_to_all | solution.py:154
  (53 shorter events, 7.8 us)
Async XLA Ops:
  0.0 1.5 copy-start
  0.0 0.8 copy-start.3
  0.8 0.7 copy-start.4
  0.9 0.7 copy-start.5
  1.7 0.9 copy-start.2
  3.5 19.3 %all-to-all-start = ((bf16[8,232,128]{2,1,0:T(8,128)(2,1)}), bf16[8,232,128]{2,1,0:T(8,128)(2,1)S(1)}, u32[]{:S(2)}, u32[]{:S(2)}) async-start(bf16[8,232,128]{2,1,0:T(8,128)(2,1)} %pad_maximum_fusion), calls=%async_computation | async-start | bytes 950272 | tf_op jit(solution)/shard_map/all_to_all | solution.py:154
  35.7 32.0 %copy-start.1 = (bf16[16,160,128]{2,1,0:T(8,128)(2,1)S(1)}, bf16[16,160,128]{2,1,0:T(8,128)(2,1)}, u32[]{:S(2)}) copy-start(bf16[16,160,128]{2,1,0:T(8,128)(2,1)} %rest_3_.5) | copy-start | bytes 1966084
  35.8 7.1 %collective-permute-start = (bf16[4,88,128]{2,1,0:T(8,128)(2,1)S(1)}, bf16[4,88,128]{2,1,0:T(8,128)(2,1)S(1)}, u32[]{:S(2)}, u32[]{:S(2)}) collective-permute-start(bf16[4,88,128]{2,1,0:T(8,128)(2,1)S(1)} %get-tuple-element.33), channel_id=1, source_target_pairs={{0,8},{2,10},{4,12},{6,14},{512,520},{514,522},{516,524},{518,526}... | collective-permute-start | bytes 270344 | tf_op jit(solution)/shard_map/ppermute | solution.py:133
  37.8 6.1 %collective-permute-start.1 = (bf16[4,88,128]{2,1,0:T(8,128)(2,1)S(1)}, bf16[4,88,128]{2,1,0:T(8,128)(2,1)S(1)}, u32[]{:S(2)}, u32[]{:S(2)}) collective-permute-start(bf16[4,88,128]{2,1,0:T(8,128)(2,1)S(1)} %get-tuple-element.34), channel_id=1, source_target_pairs={{0,24},{2,26},{4,28},{6,30},{512,536},{514,538},{516,540},{518,542... | collective-permute-start | bytes 270344 | tf_op jit(solution)/shard_map/ppermute | solution.py:133
  44.0 18.2 %collective-permute-start.3 = (bf16[15,72,128]{2,1,0:T(8,128)(2,1)S(1)}, bf16[15,72,128]{2,1,0:T(8,128)(2,1)S(1)}, u32[]{:S(2)}, u32[]{:S(2)}) collective-permute-start(bf16[15,72,128]{2,1,0:T(8,128)(2,1)S(1)} %pad_maximum_fusion.3.own), channel_id=1, source_target_pairs={{32,0},{34,2},{36,4},{38,6},{544,512},{546,514},{548,516},{550,518... | collective-permute-start | bytes 829448 | tf_op jit(solution)/shard_map/ppermute | solution.py:133
  58.7 9.1 %collective-permute-start.2 = (bf16[15,72,128]{2,1,0:T(8,128)(2,1)S(1)}, bf16[15,72,128]{2,1,0:T(8,128)(2,1)S(1)}, u32[]{:S(2)}, u32[]{:S(2)}) collective-permute-start(bf16[15,72,128]{2,1,0:T(8,128)(2,1)S(1)} %pad_maximum_fusion.3.own), channel_id=1, source_target_pairs={{0,32},{2,34},{4,36},{6,38},{512,544},{514,546},{516,548},{518,550... | collective-permute-start | bytes 829448 | tf_op jit(solution)/shard_map/ppermute | solution.py:133
  69.2 9.1 %collective-permute-start.5 = (bf16[13,72,128]{2,1,0:T(8,128)(2,1)S(1)}, bf16[13,72,128]{2,1,0:T(8,128)(2,1)S(1)}, u32[]{:S(2)}, u32[]{:S(2)}) collective-permute-start(bf16[13,72,128]{2,1,0:T(8,128)(2,1)S(1)} %shard_map.64.own), channel_id=1, source_target_pairs={{32,0},{34,2},{36,4},{38,6},{544,512},{546,514},{548,516},{550,518... | collective-permute-start | bytes 718856 | tf_op jit(solution)/shard_map/ppermute | solution.py:133
  71.5 8.7 %collective-permute-start.4 = (bf16[13,72,128]{2,1,0:T(8,128)(2,1)S(1)}, bf16[13,72,128]{2,1,0:T(8,128)(2,1)S(1)}, u32[]{:S(2)}, u32[]{:S(2)}) collective-permute-start(bf16[13,72,128]{2,1,0:T(8,128)(2,1)S(1)} %shard_map.64.own), channel_id=1, source_target_pairs={{0,32},{2,34},{4,36},{6,38},{512,544},{514,546},{516,548},{518,550... | collective-permute-start | bytes 718856 | tf_op jit(solution)/shard_map/ppermute | solution.py:133
  81.5 8.8 %collective-permute-start.7 = (bf16[11,72,128]{2,1,0:T(8,128)(2,1)S(1)}, bf16[11,72,128]{2,1,0:T(8,128)(2,1)S(1)}, u32[]{:S(2)}, u32[]{:S(2)}) collective-permute-start(bf16[11,72,128]{2,1,0:T(8,128)(2,1)S(1)} %shard_map.65.own), channel_id=1, source_target_pairs={{32,0},{34,2},{36,4},{38,6},{544,512},{546,514},{548,516},{550,518... | collective-permute-start | bytes 608264 | tf_op jit(solution)/shard_map/ppermute | solution.py:133
  83.4 8.3 %collective-permute-start.6 = (bf16[11,72,128]{2,1,0:T(8,128)(2,1)S(1)}, bf16[11,72,128]{2,1,0:T(8,128)(2,1)S(1)}, u32[]{:S(2)}, u32[]{:S(2)}) collective-permute-start(bf16[11,72,128]{2,1,0:T(8,128)(2,1)S(1)} %shard_map.65.own), channel_id=1, source_target_pairs={{0,32},{2,34},{4,36},{6,38},{512,544},{514,546},{516,548},{518,550... | collective-permute-start | bytes 608264 | tf_op jit(solution)/shard_map/ppermute | solution.py:133
  93.0 6.6 %collective-permute-start.9 = (bf16[9,72,128]{2,1,0:T(8,128)(2,1)S(1)}, bf16[9,72,128]{2,1,0:T(8,128)(2,1)S(1)}, u32[]{:S(2)}, u32[]{:S(2)}) collective-permute-start(bf16[9,72,128]{2,1,0:T(8,128)(2,1)S(1)} %shard_map.66.own), channel_id=1, source_target_pairs={{32,0},{34,2},{36,4},{38,6},{544,512},{546,514},{548,516},{550,518... | collective-permute-start | bytes 497672 | tf_op jit(solution)/shard_map/ppermute | solution.py:133
  95.6 7.9 %collective-permute-start.8 = (bf16[9,72,128]{2,1,0:T(8,128)(2,1)S(1)}, bf16[9,72,128]{2,1,0:T(8,128)(2,1)S(1)}, u32[]{:S(2)}, u32[]{:S(2)}) collective-permute-start(bf16[9,72,128]{2,1,0:T(8,128)(2,1)S(1)} %shard_map.66.own), channel_id=1, source_target_pairs={{0,32},{2,34},{4,36},{6,38},{512,544},{514,546},{516,548},{518,550... | collective-permute-start | bytes 497672 | tf_op jit(solution)/shard_map/ppermute | solution.py:133
  104.8 6.5 %collective-permute-start.10 = (bf16[4,72,128]{2,1,0:T(8,128)(2,1)S(1)}, bf16[4,72,128]{2,1,0:T(8,128)(2,1)S(1)}, u32[]{:S(2)}, u32[]{:S(2)}) collective-permute-start(bf16[4,72,128]{2,1,0:T(8,128)(2,1)S(1)} %get-tuple-element.35), channel_id=1, source_target_pairs={{0,8},{2,10},{4,12},{6,14},{512,520},{514,522},{516,524},{518,526}... | collective-permute-start | bytes 221192 | tf_op jit(solution)/shard_map/ppermute | solution.py:133
  107.9 5.1 %collective-permute-start.11 = (bf16[4,72,128]{2,1,0:T(8,128)(2,1)S(1)}, bf16[4,72,128]{2,1,0:T(8,128)(2,1)S(1)}, u32[]{:S(2)}, u32[]{:S(2)}) collective-permute-start(bf16[4,72,128]{2,1,0:T(8,128)(2,1)S(1)} %get-tuple-element.36), channel_id=1, source_target_pairs={{0,24},{2,26},{4,28},{6,30},{512,536},{514,538},{516,540},{518,542... | collective-permute-start | bytes 221192 | tf_op jit(solution)/shard_map/ppermute | solution.py:133
  115.2 8.0 %collective-permute-start.12 = (bf16[14,72,128]{2,1,0:T(8,128)(2,1)S(1)}, bf16[14,72,128]{2,1,0:T(8,128)(2,1)S(1)}, u32[]{:S(2)}, u32[]{:S(2)}) collective-permute-start(bf16[14,72,128]{2,1,0:T(8,128)(2,1)S(1)} %get-tuple-element.18), channel_id=1, source_target_pairs={{32,0},{34,2},{36,4},{38,6},{544,512},{546,514},{548,516},{550,518... | collective-permute-start | bytes 774152 | tf_op jit(solution)/shard_map/ppermute | solution.py:133
  119.9 8.9 %collective-permute-start.13 = (bf16[14,72,128]{2,1,0:T(8,128)(2,1)S(1)}, bf16[14,72,128]{2,1,0:T(8,128)(2,1)S(1)}, u32[]{:S(2)}, u32[]{:S(2)}) collective-permute-start(bf16[14,72,128]{2,1,0:T(8,128)(2,1)S(1)} %get-tuple-element.19), channel_id=1, source_target_pairs={{0,32},{2,34},{4,36},{6,38},{512,544},{514,546},{516,548},{518,550... | collective-permute-start | bytes 774152 | tf_op jit(solution)/shard_map/ppermute | solution.py:133
  130.8 8.5 %collective-permute-start.14 = (bf16[12,72,128]{2,1,0:T(8,128)(2,1)S(1)}, bf16[12,72,128]{2,1,0:T(8,128)(2,1)S(1)}, u32[]{:S(2)}, u32[]{:S(2)}) collective-permute-start(bf16[12,72,128]{2,1,0:T(8,128)(2,1)S(1)} %get-tuple-element.21), channel_id=1, source_target_pairs={{32,0},{34,2},{36,4},{38,6},{544,512},{546,514},{548,516},{550,518... | collective-permute-start | bytes 663560 | tf_op jit(solution)/shard_map/ppermute | solution.py:133
  133.3 8.5 %collective-permute-start.15 = (bf16[12,72,128]{2,1,0:T(8,128)(2,1)S(1)}, bf16[12,72,128]{2,1,0:T(8,128)(2,1)S(1)}, u32[]{:S(2)}, u32[]{:S(2)}) collective-permute-start(bf16[12,72,128]{2,1,0:T(8,128)(2,1)S(1)} %get-tuple-element.22), channel_id=1, source_target_pairs={{0,32},{2,34},{4,36},{6,38},{512,544},{514,546},{516,548},{518,550... | collective-permute-start | bytes 663560 | tf_op jit(solution)/shard_map/ppermute | solution.py:133
  143.6 7.9 %collective-permute-start.16 = (bf16[10,72,128]{2,1,0:T(8,128)(2,1)S(1)}, bf16[10,72,128]{2,1,0:T(8,128)(2,1)S(1)}, u32[]{:S(2)}, u32[]{:S(2)}) collective-permute-start(bf16[10,72,128]{2,1,0:T(8,128)(2,1)S(1)} %get-tuple-element.24), channel_id=1, source_target_pairs={{32,0},{34,2},{36,4},{38,6},{544,512},{546,514},{548,516},{550,518... | collective-permute-start | bytes 552968 | tf_op jit(solution)/shard_map/ppermute | solution.py:133
  147.1 8.1 %collective-permute-start.17 = (bf16[10,72,128]{2,1,0:T(8,128)(2,1)S(1)}, bf16[10,72,128]{2,1,0:T(8,128)(2,1)S(1)}, u32[]{:S(2)}, u32[]{:S(2)}) collective-permute-start(bf16[10,72,128]{2,1,0:T(8,128)(2,1)S(1)} %get-tuple-element.25), channel_id=1, source_target_pairs={{0,32},{2,34},{4,36},{6,38},{512,544},{514,546},{516,548},{518,550... | collective-permute-start | bytes 552968 | tf_op jit(solution)/shard_map/ppermute | solution.py:133
  156.8 5.9 %collective-permute-start.18 = (bf16[8,72,128]{2,1,0:T(8,128)(2,1)S(1)}, bf16[8,72,128]{2,1,0:T(8,128)(2,1)S(1)}, u32[]{:S(2)}, u32[]{:S(2)}) collective-permute-start(bf16[8,72,128]{2,1,0:T(8,128)(2,1)S(1)} %get-tuple-element.27), channel_id=1, source_target_pairs={{32,0},{34,2},{36,4},{38,6},{544,512},{546,514},{548,516},{550,518... | collective-permute-start | bytes 442376 | tf_op jit(solution)/shard_map/ppermute | solution.py:133
  160.3 7.7 %collective-permute-start.19 = (bf16[8,72,128]{2,1,0:T(8,128)(2,1)S(1)}, bf16[8,72,128]{2,1,0:T(8,128)(2,1)S(1)}, u32[]{:S(2)}, u32[]{:S(2)}) collective-permute-start(bf16[8,72,128]{2,1,0:T(8,128)(2,1)S(1)} %get-tuple-element.28), channel_id=1, source_target_pairs={{0,32},{2,34},{4,36},{6,38},{512,544},{514,546},{516,548},{518,550... | collective-permute-start | bytes 442376 | tf_op jit(solution)/shard_map/ppermute | solution.py:133

commit v6 on v5

v6 whole, which is shorter than its diff:
```python
import functools

import jax
import jax.numpy as jnp
from jax import lax
from jax.experimental import pallas as pl
from jax.experimental.pallas import tpu as pltpu
from jax.sharding import PartitionSpec as P

F32, BF16 = jnp.float32, jnp.bfloat16
VMEM = pl.BlockSpec(memory_space=pltpu.VMEM)
SMEM = pl.BlockSpec(memory_space=pltpu.SMEM)
LIMIT = 24 * 1024 * 1024
RUN = 8


def right_lanes(shape):
    return lax.broadcasted_iota(jnp.int32, shape, 1) < shape[1] // 2


def window_weights(weights):
    cols = weights.shape[1]
    reach = (weights.shape[0] - cols) // 2
    gap = jnp.zeros((cols - 2 * reach, cols), weights.dtype)
    return jnp.concatenate([weights[reach : reach + cols], weights[reach + cols :], gap, weights[:reach]], axis=0)


def turn_kernel(table, out):
    for i in range(table.shape[0]):
        out[i] = window_weights(table[i]).astype(F32).T.astype(BF16)


def turn(table):
    count, _, cols = table.shape
    return pl.pallas_call(
        turn_kernel,
        out_shape=jax.ShapeDtypeStruct((count, cols, 2 * cols), BF16),
        in_specs=[VMEM],
        out_specs=VMEM,
        compiler_params=pltpu.CompilerParams(vmem_limit_bytes=LIMIT),
        cost_estimate=pl.CostEstimate(flops=0, bytes_accessed=6_000_000, transcendentals=0),
    )(table)


def choose_kernel(outside, par, table, out):
    steps, blocks = out.shape[:2]
    for step in range(steps):
        for p in range(outside(step), blocks - outside(step)):
            out[step, p] = table[par[p, steps + step]]


def choose(par, table, steps, outside):
    return pl.pallas_call(
        functools.partial(choose_kernel, outside),
        out_shape=jax.ShapeDtypeStruct((steps, par.shape[0], *table.shape[1:]), BF16),
        in_specs=[SMEM, VMEM],
        out_specs=VMEM,
        compiler_params=pltpu.CompilerParams(vmem_limit_bytes=LIMIT),
        cost_estimate=pl.CostEstimate(flops=0, bytes_accessed=6_000_000, transcendentals=0),
    )(par, table)


def forward_kernel(step, first, outs, fold, weighted, marks, own, north, south, weights, mix, *rest):
    obs, out = rest if weighted else (None, rest[0])
    shape = own.shape[1:]
    rightward = right_lanes(shape)
    mixing = mix[step][:, : shape[0]]
    blocks = []
    for p in range(outs):
        way = jnp.broadcast_to(marks[first + p][step : step + 1].astype(F32), shape)
        stay, up = way == 1, way == 0

        def pick(j):
            return jnp.where(stay, own[j], jnp.where(up, north[j], south[j]))

        left = p - 1 if p > 0 else outs
        right = p + 1 if p < outs - 1 else outs
        edges = jnp.where(rightward, pick(right), pick(left))
        window = jnp.concatenate([pick(p), edges], axis=1)
        interp = jnp.dot(window, window_weights(weights[step, first + p]), preferred_element_type=F32).astype(BF16)
        mixed = jnp.dot(mixing, interp, preferred_element_type=F32).astype(BF16)
        if weighted:
            mixed = (obs[p].astype(F32) * mixed.astype(F32)).astype(BF16)
        if fold and p in (0, outs - 1):
            blocks.append(mixed)
        else:
            out[p - 1 if fold else p] = mixed
    if fold:
        out[outs - 2] = jnp.where(rightward, blocks[1], blocks[0])


def forward(step, outs, fold, marks, rows, weights, mix, obs=None):
    levels, cols = rows[0].shape[1:]
    first = (marks.shape[0] - outs) // 2
    made = outs - 1 if fold else outs
    weighted = obs is not None
    args = (marks, *rows, weights, mix) + ((obs,) if weighted else ())
    return pl.pallas_call(
        functools.partial(forward_kernel, step, first, outs, fold, weighted),
        out_shape=jax.ShapeDtypeStruct((made, levels, cols), BF16),
        in_specs=[VMEM] * len(args),
        out_specs=VMEM,
        compiler_params=pltpu.CompilerParams(vmem_limit_bytes=LIMIT),
        cost_estimate=pl.CostEstimate(flops=outs * 6_000_000, bytes_accessed=2_000_000, transcendentals=0),
    )(*args)


def adjoint_kernel(step, first, reads, summed, marks, *rest):
    parts, (weights, mix, to_north, stay, to_south, spreads) = rest[: 3 if summed else 1], rest[3 if summed else 1 :]
    shape = parts[0].shape[1:]
    cols = shape[1]
    rightward = right_lanes(shape)
    mixing = mix[step].astype(F32).T[: shape[0]].astype(BF16)
    for p in range(reads):
        if summed:
            cot = (parts[0][p] + parts[1][p].astype(F32) + parts[2][p].astype(F32)).astype(BF16)
        else:
            cot = parts[0][p]
        back = jnp.dot(mixing, cot, preferred_element_type=F32).astype(BF16)
        spreads[p] = jnp.dot(back, weights[step, first + p], preferred_element_type=F32)
    nothing = jnp.zeros(shape, F32)

    def way(p):
        return jnp.broadcast_to(marks[first + p][step : step + 1].astype(F32), shape)

    for p in range(1, reads - 1):
        main, to = spreads[p, :, :cols], way(p)
        edges = jnp.where(rightward, spreads[p - 1, :, cols:], spreads[p + 1, :, cols:])
        edges_to = jnp.where(rightward, way(p - 1), way(p + 1))
        total = [jnp.where(to == i, main, nothing) + jnp.where(edges_to == i, edges, nothing) for i in range(3)]
        to_north[p - 1] = total[0].astype(BF16)
        stay[p - 1] = total[1]
        to_south[p - 1] = total[2].astype(BF16)


def adjoint(step, marks, parts, weights, mix):
    reads, levels, cols = parts[0].shape
    first = (marks.shape[0] - reads) // 2
    gives = (reads - 2, levels, cols)
    return pl.pallas_call(
        functools.partial(adjoint_kernel, step, first, reads, len(parts) == 3),
        out_shape=[jax.ShapeDtypeStruct(gives, BF16), jax.ShapeDtypeStruct(gives, F32), jax.ShapeDtypeStruct(gives, BF16)],
        in_specs=[VMEM] * (len(parts) + 3),
        out_specs=[VMEM] * 3,
        scratch_shapes=[pltpu.VMEM((reads, levels, 2 * cols), F32)],
        compiler_params=pltpu.CompilerParams(vmem_limit_bytes=LIMIT),
        cost_estimate=pl.CostEstimate(flops=reads * 6_000_000, bytes_accessed=2_000_000, transcendentals=0),
    )(marks, *parts, weights, mix)


def homes():
    rows, blocks = lax.axis_size("lat"), lax.axis_size("lon")

    def home(row, block):
        half, z = divmod(row, rows // 2)
        column, tracer = divmod(block, RUN)
        return place(rows, blocks, z, column, tracer, half)

    return rows, blocks, home


def place(rows, blocks, z, column, y, core):
    upper, y = divmod(y, RUN // 2)
    return (upper * (rows // 2) + z) * blocks + column * RUN + y * 2 + core


def move(value, pairs):
    return lax.ppermute(value, ("lat", "lon"), pairs)


def from_lat(value, by):
    rows, blocks, home = homes()
    return move(value, [(home(r, b), home(r - by, b)) for r in range(rows) for b in range(blocks) if 0 <= r - by < rows])


def from_lon(value, by):
    rows, blocks, home = homes()
    return move(value, [(home(r, b), home(r, (b - by) % blocks)) for r in range(rows) for b in range(blocks)])


def along_y(value):
    rows, blocks, _ = homes()
    groups = [
        [place(rows, blocks, z, column, y, core) for y in range(RUN)]
        for z in range(rows // 2)
        for column in range(blocks // RUN)
        for core in range(2)
    ]
    return lax.all_to_all(value, ("lat", "lon"), 0, 0, axis_index_groups=groups)


def swap_cores(value, first):
    keep, give = jnp.where(first, value[0], value[1]), jnp.where(first, value[1], value[0])
    blocks = lax.axis_size("lon")
    both = lax.all_gather(give, "lon", axis_index_groups=[[i, i + 1] for i in range(0, blocks, 2)])
    return jnp.where(first, keep, both[0]), jnp.where(first, both[1], keep)


def on_device(vector, obs_weight, departures, weight_index, interp_table, column_mix):
    run, levels, _, cols = vector.shape
    first = lax.axis_index("lon") % 2 == 0
    numbers = jnp.concatenate([departures.reshape(-1), weight_index.reshape(-1)]).astype(BF16)
    count = numbers.shape[0]
    tail = jnp.broadcast_to(numbers[:, None], (count, cols))
    part = lax.dynamic_index_in_dim(column_mix[:, 0], lax.axis_index("lon") // 2 % column_mix.shape[0], keepdims=False)
    part = jnp.pad(part, ((0, 0), (0, cols - levels)))
    shared = jnp.concatenate([tail, obs_weight[:, 0].astype(BF16), part])
    bundle = along_y(
        jnp.concatenate([vector[:, :, 0], jnp.broadcast_to(shared[None], (run, *shared.shape))], axis=1)
    )
    bundle = bundle.reshape(2, run // 2, *bundle.shape[1:])
    mix = jnp.where(first, bundle[0, :, -levels:], bundle[1, :, -levels:])
    bundle = jnp.stack(swap_cores(bundle[:, :, :-levels], first), axis=1).reshape(run, -1, cols)
    marked = levels + count
    state, obs = bundle[:, :levels], bundle[:, marked:]
    reach = column_mix.shape[0]
    west, east = from_lon(bundle[-reach:, :marked], -run), from_lon(bundle[:reach, :marked], run)

    marks = jnp.concatenate([part[:, levels:marked] for part in (west, bundle, east)])
    par = jnp.max(marks.astype(F32), axis=2).astype(jnp.int32)
    weights = choose(par, interp_table, reach, lambda step: 1 + step)
    turned = choose(par, turn(interp_table), reach, lambda step: reach - 1 - step)
    outer = jnp.where(right_lanes((levels, cols)), east[-1, :levels], west[0, :levels])
    state = jnp.concatenate([west[1:, :levels], state, east[:-1, :levels], outer[None]])
    for step in range(reach):
        last = step == reach - 1
        rows = (state, from_lat(state, -1), from_lat(state, 1))
        state = forward(step, run + 2 * (reach - 1 - step), not last, marks, rows, weights, mix, obs if last else None)

    west, east = from_lon(state[-reach:], -run), from_lon(state[:reach], run)
    parts = (jnp.concatenate([west, state, east]),)
    for step in reversed(range(reach)):
        north, stay, south = adjoint(step, marks, parts, turned, mix)
        parts = (stay, from_lat(north, 1), from_lat(south, -1))
    cot = sum(part.astype(F32) for part in parts).astype(BF16)
    cot = cot.reshape(run // 2, 2, levels, cols)
    lower, upper = swap_cores((cot[:, 0], cot[:, 1]), first)
    return along_y(jnp.concatenate([lower, upper]))[:, :, None]


def solution(mesh):
    placed = (
        P(None, None, "lat", "lon"),
        P(None, "lat", "lon"),
        P(None, "lat", "lon"),
        P(None, "lat", "lon"),
        P(),
        P(None, "lat", None, None),
    )
    return jax.shard_map(
        on_device, mesh=mesh, in_specs=placed, out_specs=P(None, None, "lat", "lon"), check_vma=False
    )
```

time: 183 us -> 175 us (0.956)
  Pallas kernels: 12.9 us -> 6.98 us
  local copies, waits for them, and re-layouts: 3.13 us -> 0.81 us
  waiting for transfers between devices: 61.5 us -> 59.3 us
  other arithmetic: 1.62 us -> 3.82 us
    pallas_call x4, Pallas kernels: 7.64 us -> 2.35 us  [adjoint(): pl.pallas_call(functools.partial(adjoint_kernel, step, first, reads, len(...]
    pallas_call x4, Pallas kernels: 5.27 us -> 2.62 us  [forward(): pl.pallas_call(functools.partial(forward_kernel, step, first, outs, fold,...]
    unnamed x14 -> x6, local copies, waits for them, and re-layouts: 2.98 us -> 0.67 us
    ppermute x20, waiting for transfers between devices: 49.9 us -> 47.8 us  [move(): return lax.ppermute(value, ('lat', 'lon'), pairs)]
    pallas_call x0 -> x3, Pallas kernels: none -> 2.02 us  [the longest x2 1.68 us: choose(): pl.pallas_call(functools.partial(choose_kernel, outside), out_shape=jax.S...]
  transfers between devices with their start and end apart: 21 -> 21, of which waited for: 20 -> 20; matrix products, arithmetic and copies ran while one was open for 0% -> 0% of each run, Pallas kernels for 0% -> 1%
where the time goes in v6:
time: 175 us; the launch traced here: 174 us
  starting transfers between devices  77 us (44%)
  waiting for transfers between devices  59.3 us (34%)
  blocking collectives  26.2 us (15%)
  Pallas kernels  6.98 us (4%)
  other arithmetic  3.82 us (2%)
    ppermute x20, starting transfers between devices, move(): return lax.ppermute(value, ('lat', 'lon'), pairs)  69.3 us
    ppermute x20, waiting for transfers between devices, move(): return lax.ppermute(value, ('lat', 'lon'), pairs)  47.8 us
    all_gather x2, blocking collectives, swap_cores(): lax.all_gather(give, 'lon', axis_index_groups=[[i, i + 1] for i in range(...  14.6 us
    all_to_all x1, blocking collectives, along_y(): return lax.all_to_all(value, ('lat', 'lon'), 0, 0, axis_index_groups=groups)  11.6 us
    all_to_all x1, waiting for transfers between devices, along_y(): return lax.all_to_all(value, ('lat', 'lon'), 0, 0, axis_index_groups=groups)  11.4 us
    all_to_all x1, starting transfers between devices, along_y(): return lax.all_to_all(value, ('lat', 'lon'), 0, 0, axis_index_groups=groups)  7.65 us
  transfers between devices with their start and end apart: 21, of which 20 were waited for; matrix products, arithmetic and copies ran while one was open for 0% of the time, Pallas kernels for 1%

profile of v6, /device:TPU:1, one launch (start us, length us, event | category | flops | bytes accessed | tf_op | source)
XLA Modules:
  0.0 174.5 jit_solution(16663569221561925984)
XLA Ops:
  0.0 0.9 convert_element_type.26
  0.9 0.7 convert_bitcast_fusion
  1.8 1.7 pad_maximum_fusion
  3.5 7.7 %all-to-all-start = ((bf16[8,224,128]{2,1,0:T(8,128)(2,1)}), bf16[8,224,128]{2,1,0:T(8,128)(2,1)S(1)}, u32[]{:S(2)}, u32[]{:S(2)}) async-start(bf16[8,224,128]{2,1,0:T(8,128)(2,1)} %pad_maximum_fusion), calls=%async_computation | async-start | bytes 917504 | tf_op jit(solution)/shard_map/all_to_all | solution.py:189
  11.2 11.4 %all-to-all-done = bf16[8,224,128]{2,1,0:T(8,128)(2,1)S(1)} async-done(((bf16[8,224,128]{2,1,0:T(8,128)(2,1)}), bf16[8,224,128]{2,1,0:T(8,128)(2,1)S(1)}, u32[]{:S(2)}, u32[]{:S(2)}) %all-to-all-start) | async-done | bytes 458784 | tf_op jit(solution)/shard_map/all_to_all | solution.py:189
  22.6 12.7 %all_gather.8 = bf16[2,4,152,128]{3,2,1,0:T(8,128)(2,1)S(1)} all-gather(bf16[1,4,152,128]{3,2,1,0:T(8,128)(2,1)S(1)} %broadcast_select_fusion), channel_id=1, replica_groups={{0,1},{2,3},{4,5},{6,7},{8,9},{10,11},{12,13},{14,15},{16,17},{18,19},{..., dimensions={0}, use_global_device_ids=true | all-gather | bytes 466944 | tf_op jit(solution)/shard_map/all_gather | solution.py:195
  35.5 1.9 %collective-permute-start = (bf16[4,80,128]{2,1,0:T(8,128)(2,1)S(1)}, bf16[4,80,128]{2,1,0:T(8,128)(2,1)S(1)}, u32[]{:S(2)}, u32[]{:S(2)}) collective-permute-start(bf16[4,80,128]{2,1,0:T(8,128)(2,1)S(1)} %get-tuple-element.35), channel_id=1, source_target_pairs={{0,8},{2,10},{4,12},{6,14},{512,520},{514,522},{516,524},{518,526}... | collective-permute-start | bytes 245768 | tf_op jit(solution)/shard_map/ppermute | solution.py:168
  37.4 4.6 %collective-permute-start.1 = (bf16[4,80,128]{2,1,0:T(8,128)(2,1)S(1)}, bf16[4,80,128]{2,1,0:T(8,128)(2,1)S(1)}, u32[]{:S(2)}, u32[]{:S(2)}) collective-permute-start(bf16[4,80,128]{2,1,0:T(8,128)(2,1)S(1)} %get-tuple-element.36), channel_id=1, source_target_pairs={{0,24},{2,26},{4,28},{6,30},{512,536},{514,538},{516,540},{518,542... | collective-permute-start | bytes 245768 | tf_op jit(solution)/shard_map/ppermute | solution.py:168
  42.3 1.2 collective-permute-done.1
  43.5 14.5 %collective-permute-start.3 = (bf16[15,72,128]{2,1,0:T(8,128)(2,1)S(1)}, bf16[15,72,128]{2,1,0:T(8,128)(2,1)S(1)}, u32[]{:S(2)}, u32[]{:S(2)}) collective-permute-start(bf16[15,72,128]{2,1,0:T(8,128)(2,1)S(1)} %pad_maximum_fusion.3.own), channel_id=1, source_target_pairs={{32,0},{34,2},{36,4},{38,6},{544,512},{546,514},{548,516},{550,518... | collective-permute-start | bytes 829448 | tf_op jit(solution)/shard_map/ppermute | solution.py:168
  58.1 1.9 %collective-permute-start.2 = (bf16[15,72,128]{2,1,0:T(8,128)(2,1)S(1)}, bf16[15,72,128]{2,1,0:T(8,128)(2,1)S(1)}, u32[]{:S(2)}, u32[]{:S(2)}) collective-permute-start(bf16[15,72,128]{2,1,0:T(8,128)(2,1)S(1)} %pad_maximum_fusion.3.own), channel_id=1, source_target_pairs={{0,32},{2,34},{4,36},{6,38},{512,544},{514,546},{516,548},{518,550... | collective-permute-start | bytes 829448 | tf_op jit(solution)/shard_map/ppermute | solution.py:168
  60.1 0.8 shard_map.64.weights
  61.5 5.6 %collective-permute-done.2.north = bf16[15,72,128]{2,1,0:T(8,128)(2,1)S(1)} collective-permute-done((bf16[15,72,128]{2,1,0:T(8,128)(2,1)S(1)}, bf16[15,72,128]{2,1,0:T(8,128)(2,1)S(1)}, u32[]{:S(2)}, u32[]{:S(2)}) %collective-permute-start.2) | collective-permute-done | bytes 276512 | tf_op jit(solution)/shard_map/ppermute | solution.py:168
  67.1 0.7 shard_map.65.own
  67.9 2.3 %collective-permute-start.5 = (bf16[13,72,128]{2,1,0:T(8,128)(2,1)S(1)}, bf16[13,72,128]{2,1,0:T(8,128)(2,1)S(1)}, u32[]{:S(2)}, u32[]{:S(2)}) collective-permute-start(bf16[13,72,128]{2,1,0:T(8,128)(2,1)S(1)} %shard_map.65.own), channel_id=1, source_target_pairs={{32,0},{34,2},{36,4},{38,6},{544,512},{546,514},{548,516},{550,518... | collective-permute-start | bytes 718856 | tf_op jit(solution)/shard_map/ppermute | solution.py:168
  70.1 3.0 %collective-permute-start.4 = (bf16[13,72,128]{2,1,0:T(8,128)(2,1)S(1)}, bf16[13,72,128]{2,1,0:T(8,128)(2,1)S(1)}, u32[]{:S(2)}, u32[]{:S(2)}) collective-permute-start(bf16[13,72,128]{2,1,0:T(8,128)(2,1)S(1)} %shard_map.65.own), channel_id=1, source_target_pairs={{0,32},{2,34},{4,36},{6,38},{512,544},{514,546},{516,548},{518,550... | collective-permute-start | bytes 718856 | tf_op jit(solution)/shard_map/ppermute | solution.py:168
  73.2 3.8 %collective-permute-done.5.south = bf16[13,72,128]{2,1,0:T(8,128)(2,1)S(1)} collective-permute-done((bf16[13,72,128]{2,1,0:T(8,128)(2,1)S(1)}, bf16[13,72,128]{2,1,0:T(8,128)(2,1)S(1)}, u32[]{:S(2)}, u32[]{:S(2)}) %collective-permute-start.5) | collective-permute-done | bytes 239648 | tf_op jit(solution)/shard_map/ppermute | solution.py:168
  77.0 1.8 %collective-permute-done.4.north = bf16[13,72,128]{2,1,0:T(8,128)(2,1)S(1)} collective-permute-done((bf16[13,72,128]{2,1,0:T(8,128)(2,1)S(1)}, bf16[13,72,128]{2,1,0:T(8,128)(2,1)S(1)}, u32[]{:S(2)}, u32[]{:S(2)}) %collective-permute-start.4) | collective-permute-done | bytes 239648 | tf_op jit(solution)/shard_map/ppermute | solution.py:168
  78.8 0.7 shard_map.66.own
  79.5 1.9 %collective-permute-start.7 = (bf16[11,72,128]{2,1,0:T(8,128)(2,1)S(1)}, bf16[11,72,128]{2,1,0:T(8,128)(2,1)S(1)}, u32[]{:S(2)}, u32[]{:S(2)}) collective-permute-start(bf16[11,72,128]{2,1,0:T(8,128)(2,1)S(1)} %shard_map.66.own), channel_id=1, source_target_pairs={{32,0},{34,2},{36,4},{38,6},{544,512},{546,514},{548,516},{550,518... | collective-permute-start | bytes 608264 | tf_op jit(solution)/shard_map/ppermute | solution.py:168
  81.4 3.7 %collective-permute-start.6 = (bf16[11,72,128]{2,1,0:T(8,128)(2,1)S(1)}, bf16[11,72,128]{2,1,0:T(8,128)(2,1)S(1)}, u32[]{:S(2)}, u32[]{:S(2)}) collective-permute-start(bf16[11,72,128]{2,1,0:T(8,128)(2,1)S(1)} %shard_map.66.own), channel_id=1, source_target_pairs={{0,32},{2,34},{4,36},{6,38},{512,544},{514,546},{516,548},{518,550... | collective-permute-start | bytes 608264 | tf_op jit(solution)/shard_map/ppermute | solution.py:168
  85.1 3.2 %collective-permute-done.7.south = bf16[11,72,128]{2,1,0:T(8,128)(2,1)S(1)} collective-permute-done((bf16[11,72,128]{2,1,0:T(8,128)(2,1)S(1)}, bf16[11,72,128]{2,1,0:T(8,128)(2,1)S(1)}, u32[]{:S(2)}, u32[]{:S(2)}) %collective-permute-start.7) | collective-permute-done | bytes 202784 | tf_op jit(solution)/shard_map/ppermute | solution.py:168
  88.3 1.4 collective-permute-done.6.north
  90.3 2.7 %collective-permute-start.9 = (bf16[9,72,128]{2,1,0:T(8,128)(2,1)S(1)}, bf16[9,72,128]{2,1,0:T(8,128)(2,1)S(1)}, u32[]{:S(2)}, u32[]{:S(2)}) collective-permute-start(bf16[9,72,128]{2,1,0:T(8,128)(2,1)S(1)} %shard_map.67.own), channel_id=1, source_target_pairs={{32,0},{34,2},{36,4},{38,6},{544,512},{546,514},{548,516},{550,518... | collective-permute-start | bytes 497672 | tf_op jit(solution)/shard_map/ppermute | solution.py:168
  93.0 2.8 %collective-permute-start.8 = (bf16[9,72,128]{2,1,0:T(8,128)(2,1)S(1)}, bf16[9,72,128]{2,1,0:T(8,128)(2,1)S(1)}, u32[]{:S(2)}, u32[]{:S(2)}) collective-permute-start(bf16[9,72,128]{2,1,0:T(8,128)(2,1)S(1)} %shard_map.67.own), channel_id=1, source_target_pairs={{0,32},{2,34},{4,36},{6,38},{512,544},{514,546},{516,548},{518,550... | collective-permute-start | bytes 497672 | tf_op jit(solution)/shard_map/ppermute | solution.py:168
  95.8 1.1 collective-permute-done.9.south
  96.9 3.9 %collective-permute-done.8.north = bf16[9,72,128]{2,1,0:T(8,128)(2,1)S(1)} collective-permute-done((bf16[9,72,128]{2,1,0:T(8,128)(2,1)S(1)}, bf16[9,72,128]{2,1,0:T(8,128)(2,1)S(1)}, u32[]{:S(2)}, u32[]{:S(2)}) %collective-permute-start.8) | collective-permute-done | bytes 165920 | tf_op jit(solution)/shard_map/ppermute | solution.py:168
  101.5 3.1 %collective-permute-start.10 = (bf16[4,72,128]{2,1,0:T(8,128)(2,1)S(1)}, bf16[4,72,128]{2,1,0:T(8,128)(2,1)S(1)}, u32[]{:S(2)}, u32[]{:S(2)}) collective-permute-start(bf16[4,72,128]{2,1,0:T(8,128)(2,1)S(1)} %get-tuple-element.37), channel_id=1, source_target_pairs={{0,8},{2,10},{4,12},{6,14},{512,520},{514,522},{516,524},{518,526}... | collective-permute-start | bytes 221192 | tf_op jit(solution)/shard_map/ppermute | solution.py:168
  104.6 3.4 %collective-permute-start.11 = (bf16[4,72,128]{2,1,0:T(8,128)(2,1)S(1)}, bf16[4,72,128]{2,1,0:T(8,128)(2,1)S(1)}, u32[]{:S(2)}, u32[]{:S(2)}) collective-permute-start(bf16[4,72,128]{2,1,0:T(8,128)(2,1)S(1)} %get-tuple-element.38), channel_id=1, source_target_pairs={{0,24},{2,26},{4,28},{6,30},{512,536},{514,538},{516,540},{518,542... | collective-permute-start | bytes 221192 | tf_op jit(solution)/shard_map/ppermute | solution.py:168
  108.3 0.9 shard_map.70.rest_1_.rest_3_
  110.4 4.7 %collective-permute-start.12 = (bf16[14,72,128]{2,1,0:T(8,128)(2,1)S(1)}, bf16[14,72,128]{2,1,0:T(8,128)(2,1)S(1)}, u32[]{:S(2)}, u32[]{:S(2)}) collective-permute-start(bf16[14,72,128]{2,1,0:T(8,128)(2,1)S(1)} %get-tuple-element.18), channel_id=1, source_target_pairs={{32,0},{34,2},{36,4},{38,6},{544,512},{546,514},{548,516},{550,518... | collective-permute-start | bytes 774152 | tf_op jit(solution)/shard_map/ppermute | solution.py:168
  115.1 1.9 %collective-permute-start.13 = (bf16[14,72,128]{2,1,0:T(8,128)(2,1)S(1)}, bf16[14,72,128]{2,1,0:T(8,128)(2,1)S(1)}, u32[]{:S(2)}, u32[]{:S(2)}) collective-permute-start(bf16[14,72,128]{2,1,0:T(8,128)(2,1)S(1)} %get-tuple-element.19), channel_id=1, source_target_pairs={{0,32},{2,34},{4,36},{6,38},{512,544},{514,546},{516,548},{518,550... | collective-permute-start | bytes 774152 | tf_op jit(solution)/shard_map/ppermute | solution.py:168
  117.0 1.9 %collective-permute-done.12.rest_1_ = bf16[14,72,128]{2,1,0:T(8,128)(2,1)S(1)} collective-permute-done((bf16[14,72,128]{2,1,0:T(8,128)(2,1)S(1)}, bf16[14,72,128]{2,1,0:T(8,128)(2,1)S(1)}, u32[]{:S(2)}, u32[]{:S(2)}) %collective-permute-start.12) | collective-permute-done | bytes 258080 | tf_op jit(solution)/shard_map/ppermute | solution.py:168
  118.9 5.1 %collective-permute-done.13.rest_2_ = bf16[14,72,128]{2,1,0:T(8,128)(2,1)S(1)} collective-permute-done((bf16[14,72,128]{2,1,0:T(8,128)(2,1)S(1)}, bf16[14,72,128]{2,1,0:T(8,128)(2,1)S(1)}, u32[]{:S(2)}, u32[]{:S(2)}) %collective-permute-start.13) | collective-permute-done | bytes 258080 | tf_op jit(solution)/shard_map/ppermute | solution.py:168
  124.6 3.5 %collective-permute-start.14 = (bf16[12,72,128]{2,1,0:T(8,128)(2,1)S(1)}, bf16[12,72,128]{2,1,0:T(8,128)(2,1)S(1)}, u32[]{:S(2)}, u32[]{:S(2)}) collective-permute-start(bf16[12,72,128]{2,1,0:T(8,128)(2,1)S(1)} %get-tuple-element.21), channel_id=1, source_target_pairs={{32,0},{34,2},{36,4},{38,6},{544,512},{546,514},{548,516},{550,518... | collective-permute-start | bytes 663560 | tf_op jit(solution)/shard_map/ppermute | solution.py:168
  128.1 1.9 %collective-permute-start.15 = (bf16[12,72,128]{2,1,0:T(8,128)(2,1)S(1)}, bf16[12,72,128]{2,1,0:T(8,128)(2,1)S(1)}, u32[]{:S(2)}, u32[]{:S(2)}) collective-permute-start(bf16[12,72,128]{2,1,0:T(8,128)(2,1)S(1)} %get-tuple-element.22), channel_id=1, source_target_pairs={{0,32},{2,34},{4,36},{6,38},{512,544},{514,546},{516,548},{518,550... | collective-permute-start | bytes 663560 | tf_op jit(solution)/shard_map/ppermute | solution.py:168
  130.1 3.2 %collective-permute-done.14.rest_1_ = bf16[12,72,128]{2,1,0:T(8,128)(2,1)S(1)} collective-permute-done((bf16[12,72,128]{2,1,0:T(8,128)(2,1)S(1)}, bf16[12,72,128]{2,1,0:T(8,128)(2,1)S(1)}, u32[]{:S(2)}, u32[]{:S(2)}) %collective-permute-start.14) | collective-permute-done | bytes 221216 | tf_op jit(solution)/shard_map/ppermute | solution.py:168
  133.2 3.4 %collective-permute-done.15.rest_2_ = bf16[12,72,128]{2,1,0:T(8,128)(2,1)S(1)} collective-permute-done((bf16[12,72,128]{2,1,0:T(8,128)(2,1)S(1)}, bf16[12,72,128]{2,1,0:T(8,128)(2,1)S(1)}, u32[]{:S(2)}, u32[]{:S(2)}) %collective-permute-start.15) | collective-permute-done | bytes 221216 | tf_op jit(solution)/shard_map/ppermute | solution.py:168
  137.2 4.2 %collective-permute-start.16 = (bf16[10,72,128]{2,1,0:T(8,128)(2,1)S(1)}, bf16[10,72,128]{2,1,0:T(8,128)(2,1)S(1)}, u32[]{:S(2)}, u32[]{:S(2)}) collective-permute-start(bf16[10,72,128]{2,1,0:T(8,128)(2,1)S(1)} %get-tuple-element.24), channel_id=1, source_target_pairs={{32,0},{34,2},{36,4},{38,6},{544,512},{546,514},{548,516},{550,518... | collective-permute-start | bytes 552968 | tf_op jit(solution)/shard_map/ppermute | solution.py:168
  141.4 1.9 %collective-permute-start.17 = (bf16[10,72,128]{2,1,0:T(8,128)(2,1)S(1)}, bf16[10,72,128]{2,1,0:T(8,128)(2,1)S(1)}, u32[]{:S(2)}, u32[]{:S(2)}) collective-permute-start(bf16[10,72,128]{2,1,0:T(8,128)(2,1)S(1)} %get-tuple-element.25), channel_id=1, source_target_pairs={{0,32},{2,34},{4,36},{6,38},{512,544},{514,546},{516,548},{518,550... | collective-permute-start | bytes 552968 | tf_op jit(solution)/shard_map/ppermute | solution.py:168
  143.3 1.0 collective-permute-done.16.rest_1_
  144.3 5.2 %collective-permute-done.17.rest_2_ = bf16[10,72,128]{2,1,0:T(8,128)(2,1)S(1)} collective-permute-done((bf16[10,72,128]{2,1,0:T(8,128)(2,1)S(1)}, bf16[10,72,128]{2,1,0:T(8,128)(2,1)S(1)}, u32[]{:S(2)}, u32[]{:S(2)}) %collective-permute-start.17) | collective-permute-done | bytes 184352 | tf_op jit(solution)/shard_map/ppermute | solution.py:168
  150.0 2.5 %collective-permute-start.18 = (bf16[8,72,128]{2,1,0:T(8,128)(2,1)S(1)}, bf16[8,72,128]{2,1,0:T(8,128)(2,1)S(1)}, u32[]{:S(2)}, u32[]{:S(2)}) collective-permute-start(bf16[8,72,128]{2,1,0:T(8,128)(2,1)S(1)} %get-tuple-element.27), channel_id=1, source_target_pairs={{32,0},{34,2},{36,4},{38,6},{544,512},{546,514},{548,516},{550,518... | collective-permute-start | bytes 442376 | tf_op jit(solution)/shard_map/ppermute | solution.py:168
  152.5 2.7 %collective-permute-start.19 = (bf16[8,72,128]{2,1,0:T(8,128)(2,1)S(1)}, bf16[8,72,128]{2,1,0:T(8,128)(2,1)S(1)}, u32[]{:S(2)}, u32[]{:S(2)}) collective-permute-start(bf16[8,72,128]{2,1,0:T(8,128)(2,1)S(1)} %get-tuple-element.28), channel_id=1, source_target_pairs={{0,32},{2,34},{4,36},{6,38},{512,544},{514,546},{516,548},{518,550... | collective-permute-start | bytes 442376 | tf_op jit(solution)/shard_map/ppermute | solution.py:168
  155.9 4.3 %collective-permute-done.19 = bf16[8,72,128]{2,1,0:T(8,128)(2,1)S(1)} collective-permute-done((bf16[8,72,128]{2,1,0:T(8,128)(2,1)S(1)}, bf16[8,72,128]{2,1,0:T(8,128)(2,1)S(1)}, u32[]{:S(2)}, u32[]{:S(2)}) %collective-permute-start.19) | collective-permute-done | bytes 147488 | tf_op jit(solution)/shard_map/ppermute | solution.py:168
  160.3 1.9 %all-gather = bf16[8,1,72,128]{3,2,1,0:T(8,128)(2,1)S(1)} all-gather(bf16[4,1,72,128]{3,2,1,0:T(8,128)(2,1)S(1)} %bitcast_select_fusion), channel_id=2, replica_groups={{0,1},{2,3},{4,5},{6,7},{8,9},{10,11},{12,13},{14,15},{16,17},{18,19},{..., dimensions={0}, use_global_device_ids=true | all-gather | bytes 221184 | tf_op jit(solution)/shard_map/all_gather | solution.py:195
  162.3 11.6 %all_to_all.10 = bf16[8,72,128]{2,1,0:T(8,128)(2,1)S(1)} all-to-all(bf16[8,72,128]{2,1,0:T(8,128)(2,1)S(1)} %pad_maximum_fusion.4), channel_id=1, replica_groups={{0,2,4,6,512,514,516,518},{1,3,5,7,513,515,517,519},{8,10,12,14,520,522..., dimensions={0} | all-to-all | bytes 294912 | tf_op jit(solution)/shard_map/all_to_all | solution.py:189
  173.8 0.7 copy.23
  (45 shorter events, 6.5 us)
Async XLA Ops:
  0.0 1.7 copy-start
  0.0 60.1 %copy-start.1 = (bf16[16,160,128]{2,1,0:T(8,128)(2,1)S(1)}, bf16[16,160,128]{2,1,0:T(8,128)(2,1)}, u32[]{:S(2)}) copy-start(bf16[16,160,128]{2,1,0:T(8,128)(2,1)} %table.3) | copy-start | bytes 1966084
  3.5 19.1 %all-to-all-start = ((bf16[8,224,128]{2,1,0:T(8,128)(2,1)}), bf16[8,224,128]{2,1,0:T(8,128)(2,1)S(1)}, u32[]{:S(2)}, u32[]{:S(2)}) async-start(bf16[8,224,128]{2,1,0:T(8,128)(2,1)} %pad_maximum_fusion), calls=%async_computation | async-start | bytes 917504 | tf_op jit(solution)/shard_map/all_to_all | solution.py:189
  35.5 6.8 %collective-permute-start = (bf16[4,80,128]{2,1,0:T(8,128)(2,1)S(1)}, bf16[4,80,128]{2,1,0:T(8,128)(2,1)S(1)}, u32[]{:S(2)}, u32[]{:S(2)}) collective-permute-start(bf16[4,80,128]{2,1,0:T(8,128)(2,1)S(1)} %get-tuple-element.35), channel_id=1, source_target_pairs={{0,8},{2,10},{4,12},{6,14},{512,520},{514,522},{516,524},{518,526}... | collective-permute-start | bytes 245768 | tf_op jit(solution)/shard_map/ppermute | solution.py:168
  37.4 6.0 %collective-permute-start.1 = (bf16[4,80,128]{2,1,0:T(8,128)(2,1)S(1)}, bf16[4,80,128]{2,1,0:T(8,128)(2,1)S(1)}, u32[]{:S(2)}, u32[]{:S(2)}) collective-permute-start(bf16[4,80,128]{2,1,0:T(8,128)(2,1)S(1)} %get-tuple-element.36), channel_id=1, source_target_pairs={{0,24},{2,26},{4,28},{6,30},{512,536},{514,538},{516,540},{518,542... | collective-permute-start | bytes 245768 | tf_op jit(solution)/shard_map/ppermute | solution.py:168
  43.5 18.0 %collective-permute-start.3 = (bf16[15,72,128]{2,1,0:T(8,128)(2,1)S(1)}, bf16[15,72,128]{2,1,0:T(8,128)(2,1)S(1)}, u32[]{:S(2)}, u32[]{:S(2)}) collective-permute-start(bf16[15,72,128]{2,1,0:T(8,128)(2,1)S(1)} %pad_maximum_fusion.3.own), channel_id=1, source_target_pairs={{32,0},{34,2},{36,4},{38,6},{544,512},{546,514},{548,516},{550,518... | collective-permute-start | bytes 829448 | tf_op jit(solution)/shard_map/ppermute | solution.py:168
  58.1 9.1 %collective-permute-start.2 = (bf16[15,72,128]{2,1,0:T(8,128)(2,1)S(1)}, bf16[15,72,128]{2,1,0:T(8,128)(2,1)S(1)}, u32[]{:S(2)}, u32[]{:S(2)}) collective-permute-start(bf16[15,72,128]{2,1,0:T(8,128)(2,1)S(1)} %pad_maximum_fusion.3.own), channel_id=1, source_target_pairs={{0,32},{2,34},{4,36},{6,38},{512,544},{514,546},{516,548},{518,550... | collective-permute-start | bytes 829448 | tf_op jit(solution)/shard_map/ppermute | solution.py:168
  67.9 9.1 %collective-permute-start.5 = (bf16[13,72,128]{2,1,0:T(8,128)(2,1)S(1)}, bf16[13,72,128]{2,1,0:T(8,128)(2,1)S(1)}, u32[]{:S(2)}, u32[]{:S(2)}) collective-permute-start(bf16[13,72,128]{2,1,0:T(8,128)(2,1)S(1)} %shard_map.65.own), channel_id=1, source_target_pairs={{32,0},{34,2},{36,4},{38,6},{544,512},{546,514},{548,516},{550,518... | collective-permute-start | bytes 718856 | tf_op jit(solution)/shard_map/ppermute | solution.py:168
  70.1 8.7 %collective-permute-start.4 = (bf16[13,72,128]{2,1,0:T(8,128)(2,1)S(1)}, bf16[13,72,128]{2,1,0:T(8,128)(2,1)S(1)}, u32[]{:S(2)}, u32[]{:S(2)}) collective-permute-start(bf16[13,72,128]{2,1,0:T(8,128)(2,1)S(1)} %shard_map.65.own), channel_id=1, source_target_pairs={{0,32},{2,34},{4,36},{6,38},{512,544},{514,546},{516,548},{518,550... | collective-permute-start | bytes 718856 | tf_op jit(solution)/shard_map/ppermute | solution.py:168
  79.5 8.8 %collective-permute-start.7 = (bf16[11,72,128]{2,1,0:T(8,128)(2,1)S(1)}, bf16[11,72,128]{2,1,0:T(8,128)(2,1)S(1)}, u32[]{:S(2)}, u32[]{:S(2)}) collective-permute-start(bf16[11,72,128]{2,1,0:T(8,128)(2,1)S(1)} %shard_map.66.own), channel_id=1, source_target_pairs={{32,0},{34,2},{36,4},{38,6},{544,512},{546,514},{548,516},{550,518... | collective-permute-start | bytes 608264 | tf_op jit(solution)/shard_map/ppermute | solution.py:168
  81.4 8.3 %collective-permute-start.6 = (bf16[11,72,128]{2,1,0:T(8,128)(2,1)S(1)}, bf16[11,72,128]{2,1,0:T(8,128)(2,1)S(1)}, u32[]{:S(2)}, u32[]{:S(2)}) collective-permute-start(bf16[11,72,128]{2,1,0:T(8,128)(2,1)S(1)} %shard_map.66.own), channel_id=1, source_target_pairs={{0,32},{2,34},{4,36},{6,38},{512,544},{514,546},{516,548},{518,550... | collective-permute-start | bytes 608264 | tf_op jit(solution)/shard_map/ppermute | solution.py:168
  90.3 6.6 %collective-permute-start.9 = (bf16[9,72,128]{2,1,0:T(8,128)(2,1)S(1)}, bf16[9,72,128]{2,1,0:T(8,128)(2,1)S(1)}, u32[]{:S(2)}, u32[]{:S(2)}) collective-permute-start(bf16[9,72,128]{2,1,0:T(8,128)(2,1)S(1)} %shard_map.67.own), channel_id=1, source_target_pairs={{32,0},{34,2},{36,4},{38,6},{544,512},{546,514},{548,516},{550,518... | collective-permute-start | bytes 497672 | tf_op jit(solution)/shard_map/ppermute | solution.py:168
  93.0 7.9 %collective-permute-start.8 = (bf16[9,72,128]{2,1,0:T(8,128)(2,1)S(1)}, bf16[9,72,128]{2,1,0:T(8,128)(2,1)S(1)}, u32[]{:S(2)}, u32[]{:S(2)}) collective-permute-start(bf16[9,72,128]{2,1,0:T(8,128)(2,1)S(1)} %shard_map.67.own), channel_id=1, source_target_pairs={{0,32},{2,34},{4,36},{6,38},{512,544},{514,546},{516,548},{518,550... | collective-permute-start | bytes 497672 | tf_op jit(solution)/shard_map/ppermute | solution.py:168
  101.5 7.8 %collective-permute-start.10 = (bf16[4,72,128]{2,1,0:T(8,128)(2,1)S(1)}, bf16[4,72,128]{2,1,0:T(8,128)(2,1)S(1)}, u32[]{:S(2)}, u32[]{:S(2)}) collective-permute-start(bf16[4,72,128]{2,1,0:T(8,128)(2,1)S(1)} %get-tuple-element.37), channel_id=1, source_target_pairs={{0,8},{2,10},{4,12},{6,14},{512,520},{514,522},{516,524},{518,526}... | collective-permute-start | bytes 221192 | tf_op jit(solution)/shard_map/ppermute | solution.py:168
  104.6 5.1 %collective-permute-start.11 = (bf16[4,72,128]{2,1,0:T(8,128)(2,1)S(1)}, bf16[4,72,128]{2,1,0:T(8,128)(2,1)S(1)}, u32[]{:S(2)}, u32[]{:S(2)}) collective-permute-start(bf16[4,72,128]{2,1,0:T(8,128)(2,1)S(1)} %get-tuple-element.38), channel_id=1, source_target_pairs={{0,24},{2,26},{4,28},{6,30},{512,536},{514,538},{516,540},{518,542... | collective-permute-start | bytes 221192 | tf_op jit(solution)/shard_map/ppermute | solution.py:168
  110.4 8.5 %collective-permute-start.12 = (bf16[14,72,128]{2,1,0:T(8,128)(2,1)S(1)}, bf16[14,72,128]{2,1,0:T(8,128)(2,1)S(1)}, u32[]{:S(2)}, u32[]{:S(2)}) collective-permute-start(bf16[14,72,128]{2,1,0:T(8,128)(2,1)S(1)} %get-tuple-element.18), channel_id=1, source_target_pairs={{32,0},{34,2},{36,4},{38,6},{544,512},{546,514},{548,516},{550,518... | collective-permute-start | bytes 774152 | tf_op jit(solution)/shard_map/ppermute | solution.py:168
  115.1 8.9 %collective-permute-start.13 = (bf16[14,72,128]{2,1,0:T(8,128)(2,1)S(1)}, bf16[14,72,128]{2,1,0:T(8,128)(2,1)S(1)}, u32[]{:S(2)}, u32[]{:S(2)}) collective-permute-start(bf16[14,72,128]{2,1,0:T(8,128)(2,1)S(1)} %get-tuple-element.19), channel_id=1, source_target_pairs={{0,32},{2,34},{4,36},{6,38},{512,544},{514,546},{516,548},{518,550... | collective-permute-start | bytes 774152 | tf_op jit(solution)/shard_map/ppermute | solution.py:168
  124.6 8.6 %collective-permute-start.14 = (bf16[12,72,128]{2,1,0:T(8,128)(2,1)S(1)}, bf16[12,72,128]{2,1,0:T(8,128)(2,1)S(1)}, u32[]{:S(2)}, u32[]{:S(2)}) collective-permute-start(bf16[12,72,128]{2,1,0:T(8,128)(2,1)S(1)} %get-tuple-element.21), channel_id=1, source_target_pairs={{32,0},{34,2},{36,4},{38,6},{544,512},{546,514},{548,516},{550,518... | collective-permute-start | bytes 663560 | tf_op jit(solution)/shard_map/ppermute | solution.py:168
  128.1 8.5 %collective-permute-start.15 = (bf16[12,72,128]{2,1,0:T(8,128)(2,1)S(1)}, bf16[12,72,128]{2,1,0:T(8,128)(2,1)S(1)}, u32[]{:S(2)}, u32[]{:S(2)}) collective-permute-start(bf16[12,72,128]{2,1,0:T(8,128)(2,1)S(1)} %get-tuple-element.22), channel_id=1, source_target_pairs={{0,32},{2,34},{4,36},{6,38},{512,544},{514,546},{516,548},{518,550... | collective-permute-start | bytes 663560 | tf_op jit(solution)/shard_map/ppermute | solution.py:168
  137.2 7.1 %collective-permute-start.16 = (bf16[10,72,128]{2,1,0:T(8,128)(2,1)S(1)}, bf16[10,72,128]{2,1,0:T(8,128)(2,1)S(1)}, u32[]{:S(2)}, u32[]{:S(2)}) collective-permute-start(bf16[10,72,128]{2,1,0:T(8,128)(2,1)S(1)} %get-tuple-element.24), channel_id=1, source_target_pairs={{32,0},{34,2},{36,4},{38,6},{544,512},{546,514},{548,516},{550,518... | collective-permute-start | bytes 552968 | tf_op jit(solution)/shard_map/ppermute | solution.py:168
  141.4 8.1 %collective-permute-start.17 = (bf16[10,72,128]{2,1,0:T(8,128)(2,1)S(1)}, bf16[10,72,128]{2,1,0:T(8,128)(2,1)S(1)}, u32[]{:S(2)}, u32[]{:S(2)}) collective-permute-start(bf16[10,72,128]{2,1,0:T(8,128)(2,1)S(1)} %get-tuple-element.25), channel_id=1, source_target_pairs={{0,32},{2,34},{4,36},{6,38},{512,544},{514,546},{516,548},{518,550... | collective-permute-start | bytes 552968 | tf_op jit(solution)/shard_map/ppermute | solution.py:168
  150.0 5.9 %collective-permute-start.18 = (bf16[8,72,128]{2,1,0:T(8,128)(2,1)S(1)}, bf16[8,72,128]{2,1,0:T(8,128)(2,1)S(1)}, u32[]{:S(2)}, u32[]{:S(2)}) collective-permute-start(bf16[8,72,128]{2,1,0:T(8,128)(2,1)S(1)} %get-tuple-element.27), channel_id=1, source_target_pairs={{32,0},{34,2},{36,4},{38,6},{544,512},{546,514},{548,516},{550,518... | collective-permute-start | bytes 442376 | tf_op jit(solution)/shard_map/ppermute | solution.py:168
  152.5 7.7 %collective-permute-start.19 = (bf16[8,72,128]{2,1,0:T(8,128)(2,1)S(1)}, bf16[8,72,128]{2,1,0:T(8,128)(2,1)S(1)}, u32[]{:S(2)}, u32[]{:S(2)}) collective-permute-start(bf16[8,72,128]{2,1,0:T(8,128)(2,1)S(1)} %get-tuple-element.28), channel_id=1, source_target_pairs={{0,32},{2,34},{4,36},{6,38},{512,544},{514,546},{516,548},{518,550... | collective-permute-start | bytes 442376 | tf_op jit(solution)/shard_map/ppermute | solution.py:168

commit v7 on v6

--- a/solution.py
+++ b/solution.py
@@ -16,6 +16,39 @@
 
 def right_lanes(shape):
     return lax.broadcasted_iota(jnp.int32, shape, 1) < shape[1] // 2
+
+
+def bundle_kernel(mine, *refs):
+    given, out, held, done = refs[:5], refs[5], refs[6:11], refs[11]
+    copies = [pltpu.make_async_copy(given[i], held[i], done.at[i]) for i in range(5)]
+    for copy in copies:
+        copy.start()
+    for copy in copies:
+        copy.wait()
+    departures, weight_index, vector, obs, mix = held
+    run, levels, cols = vector.shape
+    marks = [jnp.full((1, cols), ref[i]) for ref in (departures, weight_index) for i in range(ref.shape[0])]
+    part = mix[mine[0]].astype(F32)
+    part = jnp.concatenate([part, jnp.zeros((levels, cols - levels), F32)], axis=1)
+    shared = jnp.concatenate([jnp.concatenate(marks).astype(F32), obs[...], part])
+    for tracer in range(run):
+        out[tracer] = jnp.concatenate([vector[tracer].astype(F32), shared]).astype(BF16)
+
+
+def bundled(mine, departures, weight_index, vector, obs, mix):
+    run, levels, cols = vector.shape
+    rows = 3 * levels + departures.shape[0] + weight_index.shape[0]
+    spaces = (pltpu.SMEM, pltpu.SMEM, pltpu.VMEM, pltpu.VMEM, pltpu.VMEM)
+    given = (departures, weight_index, vector, obs, mix)
+    return pl.pallas_call(
+        bundle_kernel,
+        out_shape=jax.ShapeDtypeStruct((run, rows, cols), BF16),
+        in_specs=[SMEM] + [pl.BlockSpec(memory_space=pltpu.HBM)] * 5,
+        out_specs=VMEM,
+        scratch_shapes=[space(x.shape, x.dtype) for space, x in zip(spaces, given)] + [pltpu.SemaphoreType.DMA((5,))],
+        compiler_params=pltpu.CompilerParams(vmem_limit_bytes=60 * 1024 * 1024),
+        cost_estimate=pl.CostEstimate(flops=0, bytes_accessed=1_000_000, transcendentals=0),
+    )(mine, *given)
 
 
 def window_weights(weights):
@@ -199,21 +232,20 @@
 def on_device(vector, obs_weight, departures, weight_index, interp_table, column_mix):
     run, levels, _, cols = vector.shape
     first = lax.axis_index("lon") % 2 == 0
-    numbers = jnp.concatenate([departures.reshape(-1), weight_index.reshape(-1)]).astype(BF16)
-    count = numbers.shape[0]
-    tail = jnp.broadcast_to(numbers[:, None], (count, cols))
-    part = lax.dynamic_index_in_dim(column_mix[:, 0], lax.axis_index("lon") // 2 % column_mix.shape[0], keepdims=False)
-    part = jnp.pad(part, ((0, 0), (0, cols - levels)))
-    shared = jnp.concatenate([tail, obs_weight[:, 0].astype(BF16), part])
+    steps = column_mix.shape[0]
+    count = 2 * steps
+    mine = (lax.axis_index("lon") // 2 % steps).reshape(1).astype(jnp.int32)
     bundle = along_y(
-        jnp.concatenate([vector[:, :, 0], jnp.broadcast_to(shared[None], (run, *shared.shape))], axis=1)
+        bundled(
+            mine, departures.reshape(-1), weight_index.reshape(-1), vector[:, :, 0], obs_weight[:, 0], column_mix[:, 0]
+        )
     )
     bundle = bundle.reshape(2, run // 2, *bundle.shape[1:])
     mix = jnp.where(first, bundle[0, :, -levels:], bundle[1, :, -levels:])
     bundle = jnp.stack(swap_cores(bundle[:, :, :-levels], first), axis=1).reshape(run, -1, cols)
     marked = levels + count
     state, obs = bundle[:, :levels], bundle[:, marked:]
-    reach = column_mix.shape[0]
+    reach = steps
     west, east = from_lon(bundle[-reach:, :marked], -run), from_lon(bundle[:reach, :marked], run)
 
     marks = jnp.concatenate([part[:, levels:marked] for part in (west, bundle, east)])

time: 175 us -> 174 us (level)
  other arithmetic: 3.82 us -> 0.4 us
  Pallas kernels: 6.98 us -> 8.87 us
    concatenate x4 -> x0, other arithmetic: 2.56 us -> none  [the longest x1 1.72 us: on_device(): jnp.concatenate([vector[:, :, 0], jnp.broadcast_to(shared[None], (run, *s...]
    pallas_call x0 -> x1, Pallas kernels: none -> 1.89 us  [bundled(): pl.pallas_call(bundle_kernel, out_shape=jax.ShapeDtypeStruct((run, rows,...]
where the time goes in v7:
time: 174 us; the launch traced here: 173 us
  starting transfers between devices  77 us (44%)
  waiting for transfers between devices  59.3 us (34%)
  blocking collectives  26.2 us (15%)
  Pallas kernels  8.87 us (5%)
    ppermute x20, starting transfers between devices, move(): return lax.ppermute(value, ('lat', 'lon'), pairs)  69.3 us
    ppermute x20, waiting for transfers between devices, move(): return lax.ppermute(value, ('lat', 'lon'), pairs)  47.8 us
    all_gather x2, blocking collectives, swap_cores(): lax.all_gather(give, 'lon', axis_index_groups=[[i, i + 1] for i in range(...  14.6 us
    all_to_all x1, blocking collectives, along_y(): return lax.all_to_all(value, ('lat', 'lon'), 0, 0, axis_index_groups=groups)  11.6 us
    all_to_all x1, waiting for transfers between devices, along_y(): return lax.all_to_all(value, ('lat', 'lon'), 0, 0, axis_index_groups=groups)  11.4 us
    all_to_all x1, starting transfers between devices, along_y(): return lax.all_to_all(value, ('lat', 'lon'), 0, 0, axis_index_groups=groups)  7.66 us
  transfers between devices with their start and end apart: 21, of which 20 were waited for; matrix products, arithmetic and copies ran while one was open for 0% of the time, Pallas kernels for 1%

profile of v7, /device:TPU:1, one launch (start us, length us, event | category | flops | bytes accessed | tf_op | source)
XLA Modules:
  0.0 172.9 jit_solution(4332134335774574070)
XLA Ops:
  0.0 1.9 %shard_map.64 = bf16[8,224,128]{2,1,0:T(8,128)(2,1)} custom-call(s32[1]{0:T(128)} %bitcast.1.mine, s32[4]{0:T(128)} %bitcast.49, s32[4]{0:T(128)} %bitcast.50, bf16[8,72,128]{2,1,0:T(8,128)(2,1)} %bitcast.46, f32[72,128]{1,0:T(8,128)} %bitcast.48, bf16[4,72,72]{2,1,0:T(8,128)(2,1)} %bitcast.47), custom_call_target="tpu_custom_call" | custom-call | bytes 1000000 | tf_op jit(solution)/shard_map/pallas_call | solution.py:43
  1.9 7.7 %all-to-all-start = ((bf16[8,224,128]{2,1,0:T(8,128)(2,1)}), bf16[8,224,128]{2,1,0:T(8,128)(2,1)S(1)}, u32[]{:S(2)}, u32[]{:S(2)}) async-start(bf16[8,224,128]{2,1,0:T(8,128)(2,1)} %shard_map.64), calls=%async_computation | async-start | bytes 917504 | tf_op jit(solution)/shard_map/all_to_all | solution.py:222
  9.6 11.4 %all-to-all-done = bf16[8,224,128]{2,1,0:T(8,128)(2,1)S(1)} async-done(((bf16[8,224,128]{2,1,0:T(8,128)(2,1)}), bf16[8,224,128]{2,1,0:T(8,128)(2,1)S(1)}, u32[]{:S(2)}, u32[]{:S(2)}) %all-to-all-start) | async-done | bytes 458784 | tf_op jit(solution)/shard_map/all_to_all | solution.py:222
  21.0 12.7 %all_gather.8 = bf16[2,4,152,128]{3,2,1,0:T(8,128)(2,1)S(1)} all-gather(bf16[1,4,152,128]{3,2,1,0:T(8,128)(2,1)S(1)} %broadcast_select_fusion), channel_id=1, replica_groups={{0,1},{2,3},{4,5},{6,7},{8,9},{10,11},{12,13},{14,15},{16,17},{18,19},{..., dimensions={0}, use_global_device_ids=true | all-gather | bytes 466944 | tf_op jit(solution)/shard_map/all_gather | solution.py:228
  33.9 1.9 %collective-permute-start = (bf16[4,80,128]{2,1,0:T(8,128)(2,1)S(1)}, bf16[4,80,128]{2,1,0:T(8,128)(2,1)S(1)}, u32[]{:S(2)}, u32[]{:S(2)}) collective-permute-start(bf16[4,80,128]{2,1,0:T(8,128)(2,1)S(1)} %get-tuple-element.35), channel_id=1, source_target_pairs={{0,8},{2,10},{4,12},{6,14},{512,520},{514,522},{516,524},{518,526}... | collective-permute-start | bytes 245768 | tf_op jit(solution)/shard_map/ppermute | solution.py:201
  35.8 4.6 %collective-permute-start.1 = (bf16[4,80,128]{2,1,0:T(8,128)(2,1)S(1)}, bf16[4,80,128]{2,1,0:T(8,128)(2,1)S(1)}, u32[]{:S(2)}, u32[]{:S(2)}) collective-permute-start(bf16[4,80,128]{2,1,0:T(8,128)(2,1)S(1)} %get-tuple-element.36), channel_id=1, source_target_pairs={{0,24},{2,26},{4,28},{6,30},{512,536},{514,538},{516,540},{518,542... | collective-permute-start | bytes 245768 | tf_op jit(solution)/shard_map/ppermute | solution.py:201
  40.7 1.2 collective-permute-done.1
  41.9 14.5 %collective-permute-start.3 = (bf16[15,72,128]{2,1,0:T(8,128)(2,1)S(1)}, bf16[15,72,128]{2,1,0:T(8,128)(2,1)S(1)}, u32[]{:S(2)}, u32[]{:S(2)}) collective-permute-start(bf16[15,72,128]{2,1,0:T(8,128)(2,1)S(1)} %pad_maximum_fusion.2.own), channel_id=1, source_target_pairs={{32,0},{34,2},{36,4},{38,6},{544,512},{546,514},{548,516},{550,518... | collective-permute-start | bytes 829448 | tf_op jit(solution)/shard_map/ppermute | solution.py:201
  56.5 1.9 %collective-permute-start.2 = (bf16[15,72,128]{2,1,0:T(8,128)(2,1)S(1)}, bf16[15,72,128]{2,1,0:T(8,128)(2,1)S(1)}, u32[]{:S(2)}, u32[]{:S(2)}) collective-permute-start(bf16[15,72,128]{2,1,0:T(8,128)(2,1)S(1)} %pad_maximum_fusion.2.own), channel_id=1, source_target_pairs={{0,32},{2,34},{4,36},{6,38},{512,544},{514,546},{516,548},{518,550... | collective-permute-start | bytes 829448 | tf_op jit(solution)/shard_map/ppermute | solution.py:201
  58.5 0.8 shard_map.65.weights
  59.9 5.6 %collective-permute-done.2.north = bf16[15,72,128]{2,1,0:T(8,128)(2,1)S(1)} collective-permute-done((bf16[15,72,128]{2,1,0:T(8,128)(2,1)S(1)}, bf16[15,72,128]{2,1,0:T(8,128)(2,1)S(1)}, u32[]{:S(2)}, u32[]{:S(2)}) %collective-permute-start.2) | collective-permute-done | bytes 276512 | tf_op jit(solution)/shard_map/ppermute | solution.py:201
  65.5 0.7 shard_map.66.own
  66.2 2.3 %collective-permute-start.5 = (bf16[13,72,128]{2,1,0:T(8,128)(2,1)S(1)}, bf16[13,72,128]{2,1,0:T(8,128)(2,1)S(1)}, u32[]{:S(2)}, u32[]{:S(2)}) collective-permute-start(bf16[13,72,128]{2,1,0:T(8,128)(2,1)S(1)} %shard_map.66.own), channel_id=1, source_target_pairs={{32,0},{34,2},{36,4},{38,6},{544,512},{546,514},{548,516},{550,518... | collective-permute-start | bytes 718856 | tf_op jit(solution)/shard_map/ppermute | solution.py:201
  68.5 3.0 %collective-permute-start.4 = (bf16[13,72,128]{2,1,0:T(8,128)(2,1)S(1)}, bf16[13,72,128]{2,1,0:T(8,128)(2,1)S(1)}, u32[]{:S(2)}, u32[]{:S(2)}) collective-permute-start(bf16[13,72,128]{2,1,0:T(8,128)(2,1)S(1)} %shard_map.66.own), channel_id=1, source_target_pairs={{0,32},{2,34},{4,36},{6,38},{512,544},{514,546},{516,548},{518,550... | collective-permute-start | bytes 718856 | tf_op jit(solution)/shard_map/ppermute | solution.py:201
  71.5 3.8 %collective-permute-done.5.south = bf16[13,72,128]{2,1,0:T(8,128)(2,1)S(1)} collective-permute-done((bf16[13,72,128]{2,1,0:T(8,128)(2,1)S(1)}, bf16[13,72,128]{2,1,0:T(8,128)(2,1)S(1)}, u32[]{:S(2)}, u32[]{:S(2)}) %collective-permute-start.5) | collective-permute-done | bytes 239648 | tf_op jit(solution)/shard_map/ppermute | solution.py:201
  75.4 1.8 %collective-permute-done.4.north = bf16[13,72,128]{2,1,0:T(8,128)(2,1)S(1)} collective-permute-done((bf16[13,72,128]{2,1,0:T(8,128)(2,1)S(1)}, bf16[13,72,128]{2,1,0:T(8,128)(2,1)S(1)}, u32[]{:S(2)}, u32[]{:S(2)}) %collective-permute-start.4) | collective-permute-done | bytes 239648 | tf_op jit(solution)/shard_map/ppermute | solution.py:201
  77.2 0.7 shard_map.67.own
  77.9 1.9 %collective-permute-start.7 = (bf16[11,72,128]{2,1,0:T(8,128)(2,1)S(1)}, bf16[11,72,128]{2,1,0:T(8,128)(2,1)S(1)}, u32[]{:S(2)}, u32[]{:S(2)}) collective-permute-start(bf16[11,72,128]{2,1,0:T(8,128)(2,1)S(1)} %shard_map.67.own), channel_id=1, source_target_pairs={{32,0},{34,2},{36,4},{38,6},{544,512},{546,514},{548,516},{550,518... | collective-permute-start | bytes 608264 | tf_op jit(solution)/shard_map/ppermute | solution.py:201
  79.8 3.7 %collective-permute-start.6 = (bf16[11,72,128]{2,1,0:T(8,128)(2,1)S(1)}, bf16[11,72,128]{2,1,0:T(8,128)(2,1)S(1)}, u32[]{:S(2)}, u32[]{:S(2)}) collective-permute-start(bf16[11,72,128]{2,1,0:T(8,128)(2,1)S(1)} %shard_map.67.own), channel_id=1, source_target_pairs={{0,32},{2,34},{4,36},{6,38},{512,544},{514,546},{516,548},{518,550... | collective-permute-start | bytes 608264 | tf_op jit(solution)/shard_map/ppermute | solution.py:201
  83.5 3.2 %collective-permute-done.7.south = bf16[11,72,128]{2,1,0:T(8,128)(2,1)S(1)} collective-permute-done((bf16[11,72,128]{2,1,0:T(8,128)(2,1)S(1)}, bf16[11,72,128]{2,1,0:T(8,128)(2,1)S(1)}, u32[]{:S(2)}, u32[]{:S(2)}) %collective-permute-start.7) | collective-permute-done | bytes 202784 | tf_op jit(solution)/shard_map/ppermute | solution.py:201
  86.7 1.4 collective-permute-done.6.north
  88.1 0.6 shard_map.68.own
  88.7 2.7 %collective-permute-start.9 = (bf16[9,72,128]{2,1,0:T(8,128)(2,1)S(1)}, bf16[9,72,128]{2,1,0:T(8,128)(2,1)S(1)}, u32[]{:S(2)}, u32[]{:S(2)}) collective-permute-start(bf16[9,72,128]{2,1,0:T(8,128)(2,1)S(1)} %shard_map.68.own), channel_id=1, source_target_pairs={{32,0},{34,2},{36,4},{38,6},{544,512},{546,514},{548,516},{550,518... | collective-permute-start | bytes 497672 | tf_op jit(solution)/shard_map/ppermute | solution.py:201
  91.4 2.8 %collective-permute-start.8 = (bf16[9,72,128]{2,1,0:T(8,128)(2,1)S(1)}, bf16[9,72,128]{2,1,0:T(8,128)(2,1)S(1)}, u32[]{:S(2)}, u32[]{:S(2)}) collective-permute-start(bf16[9,72,128]{2,1,0:T(8,128)(2,1)S(1)} %shard_map.68.own), channel_id=1, source_target_pairs={{0,32},{2,34},{4,36},{6,38},{512,544},{514,546},{516,548},{518,550... | collective-permute-start | bytes 497672 | tf_op jit(solution)/shard_map/ppermute | solution.py:201
  94.2 1.1 collective-permute-done.9.south
  95.3 4.0 %collective-permute-done.8.north = bf16[9,72,128]{2,1,0:T(8,128)(2,1)S(1)} collective-permute-done((bf16[9,72,128]{2,1,0:T(8,128)(2,1)S(1)}, bf16[9,72,128]{2,1,0:T(8,128)(2,1)S(1)}, u32[]{:S(2)}, u32[]{:S(2)}) %collective-permute-start.8) | collective-permute-done | bytes 165920 | tf_op jit(solution)/shard_map/ppermute | solution.py:201
  99.9 3.1 %collective-permute-start.10 = (bf16[4,72,128]{2,1,0:T(8,128)(2,1)S(1)}, bf16[4,72,128]{2,1,0:T(8,128)(2,1)S(1)}, u32[]{:S(2)}, u32[]{:S(2)}) collective-permute-start(bf16[4,72,128]{2,1,0:T(8,128)(2,1)S(1)} %get-tuple-element.37), channel_id=1, source_target_pairs={{0,8},{2,10},{4,12},{6,14},{512,520},{514,522},{516,524},{518,526}... | collective-permute-start | bytes 221192 | tf_op jit(solution)/shard_map/ppermute | solution.py:201
  103.0 3.4 %collective-permute-start.11 = (bf16[4,72,128]{2,1,0:T(8,128)(2,1)S(1)}, bf16[4,72,128]{2,1,0:T(8,128)(2,1)S(1)}, u32[]{:S(2)}, u32[]{:S(2)}) collective-permute-start(bf16[4,72,128]{2,1,0:T(8,128)(2,1)S(1)} %get-tuple-element.38), channel_id=1, source_target_pairs={{0,24},{2,26},{4,28},{6,30},{512,536},{514,538},{516,540},{518,542... | collective-permute-start | bytes 221192 | tf_op jit(solution)/shard_map/ppermute | solution.py:201
  106.7 0.9 shard_map.71.rest_1_.rest_3_
  108.1 0.7 shard_map.72
  108.8 4.7 %collective-permute-start.12 = (bf16[14,72,128]{2,1,0:T(8,128)(2,1)S(1)}, bf16[14,72,128]{2,1,0:T(8,128)(2,1)S(1)}, u32[]{:S(2)}, u32[]{:S(2)}) collective-permute-start(bf16[14,72,128]{2,1,0:T(8,128)(2,1)S(1)} %get-tuple-element.18), channel_id=1, source_target_pairs={{32,0},{34,2},{36,4},{38,6},{544,512},{546,514},{548,516},{550,518... | collective-permute-start | bytes 774152 | tf_op jit(solution)/shard_map/ppermute | solution.py:201
  113.5 1.9 %collective-permute-start.13 = (bf16[14,72,128]{2,1,0:T(8,128)(2,1)S(1)}, bf16[14,72,128]{2,1,0:T(8,128)(2,1)S(1)}, u32[]{:S(2)}, u32[]{:S(2)}) collective-permute-start(bf16[14,72,128]{2,1,0:T(8,128)(2,1)S(1)} %get-tuple-element.19), channel_id=1, source_target_pairs={{0,32},{2,34},{4,36},{6,38},{512,544},{514,546},{516,548},{518,550... | collective-permute-start | bytes 774152 | tf_op jit(solution)/shard_map/ppermute | solution.py:201
  115.4 1.9 %collective-permute-done.12.rest_1_ = bf16[14,72,128]{2,1,0:T(8,128)(2,1)S(1)} collective-permute-done((bf16[14,72,128]{2,1,0:T(8,128)(2,1)S(1)}, bf16[14,72,128]{2,1,0:T(8,128)(2,1)S(1)}, u32[]{:S(2)}, u32[]{:S(2)}) %collective-permute-start.12) | collective-permute-done | bytes 258080 | tf_op jit(solution)/shard_map/ppermute | solution.py:201
  117.3 5.1 %collective-permute-done.13.rest_2_ = bf16[14,72,128]{2,1,0:T(8,128)(2,1)S(1)} collective-permute-done((bf16[14,72,128]{2,1,0:T(8,128)(2,1)S(1)}, bf16[14,72,128]{2,1,0:T(8,128)(2,1)S(1)}, u32[]{:S(2)}, u32[]{:S(2)}) %collective-permute-start.13) | collective-permute-done | bytes 258080 | tf_op jit(solution)/shard_map/ppermute | solution.py:201
  123.0 3.5 %collective-permute-start.14 = (bf16[12,72,128]{2,1,0:T(8,128)(2,1)S(1)}, bf16[12,72,128]{2,1,0:T(8,128)(2,1)S(1)}, u32[]{:S(2)}, u32[]{:S(2)}) collective-permute-start(bf16[12,72,128]{2,1,0:T(8,128)(2,1)S(1)} %get-tuple-element.21), channel_id=1, source_target_pairs={{32,0},{34,2},{36,4},{38,6},{544,512},{546,514},{548,516},{550,518... | collective-permute-start | bytes 663560 | tf_op jit(solution)/shard_map/ppermute | solution.py:201
  126.5 1.9 %collective-permute-start.15 = (bf16[12,72,128]{2,1,0:T(8,128)(2,1)S(1)}, bf16[12,72,128]{2,1,0:T(8,128)(2,1)S(1)}, u32[]{:S(2)}, u32[]{:S(2)}) collective-permute-start(bf16[12,72,128]{2,1,0:T(8,128)(2,1)S(1)} %get-tuple-element.22), channel_id=1, source_target_pairs={{0,32},{2,34},{4,36},{6,38},{512,544},{514,546},{516,548},{518,550... | collective-permute-start | bytes 663560 | tf_op jit(solution)/shard_map/ppermute | solution.py:201
  128.5 3.1 %collective-permute-done.14.rest_1_ = bf16[12,72,128]{2,1,0:T(8,128)(2,1)S(1)} collective-permute-done((bf16[12,72,128]{2,1,0:T(8,128)(2,1)S(1)}, bf16[12,72,128]{2,1,0:T(8,128)(2,1)S(1)}, u32[]{:S(2)}, u32[]{:S(2)}) %collective-permute-start.14) | collective-permute-done | bytes 221216 | tf_op jit(solution)/shard_map/ppermute | solution.py:201
  131.6 3.4 %collective-permute-done.15.rest_2_ = bf16[12,72,128]{2,1,0:T(8,128)(2,1)S(1)} collective-permute-done((bf16[12,72,128]{2,1,0:T(8,128)(2,1)S(1)}, bf16[12,72,128]{2,1,0:T(8,128)(2,1)S(1)}, u32[]{:S(2)}, u32[]{:S(2)}) %collective-permute-start.15) | collective-permute-done | bytes 221216 | tf_op jit(solution)/shard_map/ppermute | solution.py:201
  135.6 4.2 %collective-permute-start.16 = (bf16[10,72,128]{2,1,0:T(8,128)(2,1)S(1)}, bf16[10,72,128]{2,1,0:T(8,128)(2,1)S(1)}, u32[]{:S(2)}, u32[]{:S(2)}) collective-permute-start(bf16[10,72,128]{2,1,0:T(8,128)(2,1)S(1)} %get-tuple-element.24), channel_id=1, source_target_pairs={{32,0},{34,2},{36,4},{38,6},{544,512},{546,514},{548,516},{550,518... | collective-permute-start | bytes 552968 | tf_op jit(solution)/shard_map/ppermute | solution.py:201
  139.8 1.9 %collective-permute-start.17 = (bf16[10,72,128]{2,1,0:T(8,128)(2,1)S(1)}, bf16[10,72,128]{2,1,0:T(8,128)(2,1)S(1)}, u32[]{:S(2)}, u32[]{:S(2)}) collective-permute-start(bf16[10,72,128]{2,1,0:T(8,128)(2,1)S(1)} %get-tuple-element.25), channel_id=1, source_target_pairs={{0,32},{2,34},{4,36},{6,38},{512,544},{514,546},{516,548},{518,550... | collective-permute-start | bytes 552968 | tf_op jit(solution)/shard_map/ppermute | solution.py:201
  141.7 1.0 collective-permute-done.16.rest_1_
  142.7 5.2 %collective-permute-done.17.rest_2_ = bf16[10,72,128]{2,1,0:T(8,128)(2,1)S(1)} collective-permute-done((bf16[10,72,128]{2,1,0:T(8,128)(2,1)S(1)}, bf16[10,72,128]{2,1,0:T(8,128)(2,1)S(1)}, u32[]{:S(2)}, u32[]{:S(2)}) %collective-permute-start.17) | collective-permute-done | bytes 184352 | tf_op jit(solution)/shard_map/ppermute | solution.py:201
  148.4 2.5 %collective-permute-start.18 = (bf16[8,72,128]{2,1,0:T(8,128)(2,1)S(1)}, bf16[8,72,128]{2,1,0:T(8,128)(2,1)S(1)}, u32[]{:S(2)}, u32[]{:S(2)}) collective-permute-start(bf16[8,72,128]{2,1,0:T(8,128)(2,1)S(1)} %get-tuple-element.27), channel_id=1, source_target_pairs={{32,0},{34,2},{36,4},{38,6},{544,512},{546,514},{548,516},{550,518... | collective-permute-start | bytes 442376 | tf_op jit(solution)/shard_map/ppermute | solution.py:201
  150.9 2.7 %collective-permute-start.19 = (bf16[8,72,128]{2,1,0:T(8,128)(2,1)S(1)}, bf16[8,72,128]{2,1,0:T(8,128)(2,1)S(1)}, u32[]{:S(2)}, u32[]{:S(2)}) collective-permute-start(bf16[8,72,128]{2,1,0:T(8,128)(2,1)S(1)} %get-tuple-element.28), channel_id=1, source_target_pairs={{0,32},{2,34},{4,36},{6,38},{512,544},{514,546},{516,548},{518,550... | collective-permute-start | bytes 442376 | tf_op jit(solution)/shard_map/ppermute | solution.py:201
  154.2 4.3 %collective-permute-done.19 = bf16[8,72,128]{2,1,0:T(8,128)(2,1)S(1)} collective-permute-done((bf16[8,72,128]{2,1,0:T(8,128)(2,1)S(1)}, bf16[8,72,128]{2,1,0:T(8,128)(2,1)S(1)}, u32[]{:S(2)}, u32[]{:S(2)}) %collective-permute-start.19) | collective-permute-done | bytes 147488 | tf_op jit(solution)/shard_map/ppermute | solution.py:201
  158.7 1.9 %all-gather = bf16[8,1,72,128]{3,2,1,0:T(8,128)(2,1)S(1)} all-gather(bf16[4,1,72,128]{3,2,1,0:T(8,128)(2,1)S(1)} %bitcast_select_fusion), channel_id=2, replica_groups={{0,1},{2,3},{4,5},{6,7},{8,9},{10,11},{12,13},{14,15},{16,17},{18,19},{..., dimensions={0}, use_global_device_ids=true | all-gather | bytes 221184 | tf_op jit(solution)/shard_map/all_gather | solution.py:228
  160.7 11.6 %all_to_all.10 = bf16[8,72,128]{2,1,0:T(8,128)(2,1)S(1)} all-to-all(bf16[8,72,128]{2,1,0:T(8,128)(2,1)S(1)} %pad_maximum_fusion.3), channel_id=1, replica_groups={{0,2,4,6,512,514,516,518},{1,3,5,7,513,515,517,519},{8,10,12,14,520,522..., dimensions={0} | all-to-all | bytes 294912 | tf_op jit(solution)/shard_map/all_to_all | solution.py:222
  172.2 0.7 copy.20
  (36 shorter events, 5.0 us)
Async XLA Ops:
  0.0 58.5 %copy-start = (bf16[16,160,128]{2,1,0:T(8,128)(2,1)S(1)}, bf16[16,160,128]{2,1,0:T(8,128)(2,1)}, u32[]{:S(2)}) copy-start(bf16[16,160,128]{2,1,0:T(8,128)(2,1)} %table.3) | copy-start | bytes 1966084
  1.9 19.1 %all-to-all-start = ((bf16[8,224,128]{2,1,0:T(8,128)(2,1)}), bf16[8,224,128]{2,1,0:T(8,128)(2,1)S(1)}, u32[]{:S(2)}, u32[]{:S(2)}) async-start(bf16[8,224,128]{2,1,0:T(8,128)(2,1)} %shard_map.64), calls=%async_computation | async-start | bytes 917504 | tf_op jit(solution)/shard_map/all_to_all | solution.py:222
  33.9 6.8 %collective-permute-start = (bf16[4,80,128]{2,1,0:T(8,128)(2,1)S(1)}, bf16[4,80,128]{2,1,0:T(8,128)(2,1)S(1)}, u32[]{:S(2)}, u32[]{:S(2)}) collective-permute-start(bf16[4,80,128]{2,1,0:T(8,128)(2,1)S(1)} %get-tuple-element.35), channel_id=1, source_target_pairs={{0,8},{2,10},{4,12},{6,14},{512,520},{514,522},{516,524},{518,526}... | collective-permute-start | bytes 245768 | tf_op jit(solution)/shard_map/ppermute | solution.py:201
  35.8 6.0 %collective-permute-start.1 = (bf16[4,80,128]{2,1,0:T(8,128)(2,1)S(1)}, bf16[4,80,128]{2,1,0:T(8,128)(2,1)S(1)}, u32[]{:S(2)}, u32[]{:S(2)}) collective-permute-start(bf16[4,80,128]{2,1,0:T(8,128)(2,1)S(1)} %get-tuple-element.36), channel_id=1, source_target_pairs={{0,24},{2,26},{4,28},{6,30},{512,536},{514,538},{516,540},{518,542... | collective-permute-start | bytes 245768 | tf_op jit(solution)/shard_map/ppermute | solution.py:201
  41.9 18.0 %collective-permute-start.3 = (bf16[15,72,128]{2,1,0:T(8,128)(2,1)S(1)}, bf16[15,72,128]{2,1,0:T(8,128)(2,1)S(1)}, u32[]{:S(2)}, u32[]{:S(2)}) collective-permute-start(bf16[15,72,128]{2,1,0:T(8,128)(2,1)S(1)} %pad_maximum_fusion.2.own), channel_id=1, source_target_pairs={{32,0},{34,2},{36,4},{38,6},{544,512},{546,514},{548,516},{550,518... | collective-permute-start | bytes 829448 | tf_op jit(solution)/shard_map/ppermute | solution.py:201
  56.5 9.1 %collective-permute-start.2 = (bf16[15,72,128]{2,1,0:T(8,128)(2,1)S(1)}, bf16[15,72,128]{2,1,0:T(8,128)(2,1)S(1)}, u32[]{:S(2)}, u32[]{:S(2)}) collective-permute-start(bf16[15,72,128]{2,1,0:T(8,128)(2,1)S(1)} %pad_maximum_fusion.2.own), channel_id=1, source_target_pairs={{0,32},{2,34},{4,36},{6,38},{512,544},{514,546},{516,548},{518,550... | collective-permute-start | bytes 829448 | tf_op jit(solution)/shard_map/ppermute | solution.py:201
  66.2 9.1 %collective-permute-start.5 = (bf16[13,72,128]{2,1,0:T(8,128)(2,1)S(1)}, bf16[13,72,128]{2,1,0:T(8,128)(2,1)S(1)}, u32[]{:S(2)}, u32[]{:S(2)}) collective-permute-start(bf16[13,72,128]{2,1,0:T(8,128)(2,1)S(1)} %shard_map.66.own), channel_id=1, source_target_pairs={{32,0},{34,2},{36,4},{38,6},{544,512},{546,514},{548,516},{550,518... | collective-permute-start | bytes 718856 | tf_op jit(solution)/shard_map/ppermute | solution.py:201
  68.5 8.7 %collective-permute-start.4 = (bf16[13,72,128]{2,1,0:T(8,128)(2,1)S(1)}, bf16[13,72,128]{2,1,0:T(8,128)(2,1)S(1)}, u32[]{:S(2)}, u32[]{:S(2)}) collective-permute-start(bf16[13,72,128]{2,1,0:T(8,128)(2,1)S(1)} %shard_map.66.own), channel_id=1, source_target_pairs={{0,32},{2,34},{4,36},{6,38},{512,544},{514,546},{516,548},{518,550... | collective-permute-start | bytes 718856 | tf_op jit(solution)/shard_map/ppermute | solution.py:201
  77.9 8.8 %collective-permute-start.7 = (bf16[11,72,128]{2,1,0:T(8,128)(2,1)S(1)}, bf16[11,72,128]{2,1,0:T(8,128)(2,1)S(1)}, u32[]{:S(2)}, u32[]{:S(2)}) collective-permute-start(bf16[11,72,128]{2,1,0:T(8,128)(2,1)S(1)} %shard_map.67.own), channel_id=1, source_target_pairs={{32,0},{34,2},{36,4},{38,6},{544,512},{546,514},{548,516},{550,518... | collective-permute-start | bytes 608264 | tf_op jit(solution)/shard_map/ppermute | solution.py:201
  79.8 8.3 %collective-permute-start.6 = (bf16[11,72,128]{2,1,0:T(8,128)(2,1)S(1)}, bf16[11,72,128]{2,1,0:T(8,128)(2,1)S(1)}, u32[]{:S(2)}, u32[]{:S(2)}) collective-permute-start(bf16[11,72,128]{2,1,0:T(8,128)(2,1)S(1)} %shard_map.67.own), channel_id=1, source_target_pairs={{0,32},{2,34},{4,36},{6,38},{512,544},{514,546},{516,548},{518,550... | collective-permute-start | bytes 608264 | tf_op jit(solution)/shard_map/ppermute | solution.py:201
  88.7 6.6 %collective-permute-start.9 = (bf16[9,72,128]{2,1,0:T(8,128)(2,1)S(1)}, bf16[9,72,128]{2,1,0:T(8,128)(2,1)S(1)}, u32[]{:S(2)}, u32[]{:S(2)}) collective-permute-start(bf16[9,72,128]{2,1,0:T(8,128)(2,1)S(1)} %shard_map.68.own), channel_id=1, source_target_pairs={{32,0},{34,2},{36,4},{38,6},{544,512},{546,514},{548,516},{550,518... | collective-permute-start | bytes 497672 | tf_op jit(solution)/shard_map/ppermute | solution.py:201
  91.4 7.9 %collective-permute-start.8 = (bf16[9,72,128]{2,1,0:T(8,128)(2,1)S(1)}, bf16[9,72,128]{2,1,0:T(8,128)(2,1)S(1)}, u32[]{:S(2)}, u32[]{:S(2)}) collective-permute-start(bf16[9,72,128]{2,1,0:T(8,128)(2,1)S(1)} %shard_map.68.own), channel_id=1, source_target_pairs={{0,32},{2,34},{4,36},{6,38},{512,544},{514,546},{516,548},{518,550... | collective-permute-start | bytes 497672 | tf_op jit(solution)/shard_map/ppermute | solution.py:201
  99.9 7.8 %collective-permute-start.10 = (bf16[4,72,128]{2,1,0:T(8,128)(2,1)S(1)}, bf16[4,72,128]{2,1,0:T(8,128)(2,1)S(1)}, u32[]{:S(2)}, u32[]{:S(2)}) collective-permute-start(bf16[4,72,128]{2,1,0:T(8,128)(2,1)S(1)} %get-tuple-element.37), channel_id=1, source_target_pairs={{0,8},{2,10},{4,12},{6,14},{512,520},{514,522},{516,524},{518,526}... | collective-permute-start | bytes 221192 | tf_op jit(solution)/shard_map/ppermute | solution.py:201
  103.0 5.1 %collective-permute-start.11 = (bf16[4,72,128]{2,1,0:T(8,128)(2,1)S(1)}, bf16[4,72,128]{2,1,0:T(8,128)(2,1)S(1)}, u32[]{:S(2)}, u32[]{:S(2)}) collective-permute-start(bf16[4,72,128]{2,1,0:T(8,128)(2,1)S(1)} %get-tuple-element.38), channel_id=1, source_target_pairs={{0,24},{2,26},{4,28},{6,30},{512,536},{514,538},{516,540},{518,542... | collective-permute-start | bytes 221192 | tf_op jit(solution)/shard_map/ppermute | solution.py:201
  108.8 8.5 %collective-permute-start.12 = (bf16[14,72,128]{2,1,0:T(8,128)(2,1)S(1)}, bf16[14,72,128]{2,1,0:T(8,128)(2,1)S(1)}, u32[]{:S(2)}, u32[]{:S(2)}) collective-permute-start(bf16[14,72,128]{2,1,0:T(8,128)(2,1)S(1)} %get-tuple-element.18), channel_id=1, source_target_pairs={{32,0},{34,2},{36,4},{38,6},{544,512},{546,514},{548,516},{550,518... | collective-permute-start | bytes 774152 | tf_op jit(solution)/shard_map/ppermute | solution.py:201
  113.5 8.9 %collective-permute-start.13 = (bf16[14,72,128]{2,1,0:T(8,128)(2,1)S(1)}, bf16[14,72,128]{2,1,0:T(8,128)(2,1)S(1)}, u32[]{:S(2)}, u32[]{:S(2)}) collective-permute-start(bf16[14,72,128]{2,1,0:T(8,128)(2,1)S(1)} %get-tuple-element.19), channel_id=1, source_target_pairs={{0,32},{2,34},{4,36},{6,38},{512,544},{514,546},{516,548},{518,550... | collective-permute-start | bytes 774152 | tf_op jit(solution)/shard_map/ppermute | solution.py:201
  123.0 8.6 %collective-permute-start.14 = (bf16[12,72,128]{2,1,0:T(8,128)(2,1)S(1)}, bf16[12,72,128]{2,1,0:T(8,128)(2,1)S(1)}, u32[]{:S(2)}, u32[]{:S(2)}) collective-permute-start(bf16[12,72,128]{2,1,0:T(8,128)(2,1)S(1)} %get-tuple-element.21), channel_id=1, source_target_pairs={{32,0},{34,2},{36,4},{38,6},{544,512},{546,514},{548,516},{550,518... | collective-permute-start | bytes 663560 | tf_op jit(solution)/shard_map/ppermute | solution.py:201
  126.5 8.5 %collective-permute-start.15 = (bf16[12,72,128]{2,1,0:T(8,128)(2,1)S(1)}, bf16[12,72,128]{2,1,0:T(8,128)(2,1)S(1)}, u32[]{:S(2)}, u32[]{:S(2)}) collective-permute-start(bf16[12,72,128]{2,1,0:T(8,128)(2,1)S(1)} %get-tuple-element.22), channel_id=1, source_target_pairs={{0,32},{2,34},{4,36},{6,38},{512,544},{514,546},{516,548},{518,550... | collective-permute-start | bytes 663560 | tf_op jit(solution)/shard_map/ppermute | solution.py:201
  135.6 7.1 %collective-permute-start.16 = (bf16[10,72,128]{2,1,0:T(8,128)(2,1)S(1)}, bf16[10,72,128]{2,1,0:T(8,128)(2,1)S(1)}, u32[]{:S(2)}, u32[]{:S(2)}) collective-permute-start(bf16[10,72,128]{2,1,0:T(8,128)(2,1)S(1)} %get-tuple-element.24), channel_id=1, source_target_pairs={{32,0},{34,2},{36,4},{38,6},{544,512},{546,514},{548,516},{550,518... | collective-permute-start | bytes 552968 | tf_op jit(solution)/shard_map/ppermute | solution.py:201
  139.8 8.1 %collective-permute-start.17 = (bf16[10,72,128]{2,1,0:T(8,128)(2,1)S(1)}, bf16[10,72,128]{2,1,0:T(8,128)(2,1)S(1)}, u32[]{:S(2)}, u32[]{:S(2)}) collective-permute-start(bf16[10,72,128]{2,1,0:T(8,128)(2,1)S(1)} %get-tuple-element.25), channel_id=1, source_target_pairs={{0,32},{2,34},{4,36},{6,38},{512,544},{514,546},{516,548},{518,550... | collective-permute-start | bytes 552968 | tf_op jit(solution)/shard_map/ppermute | solution.py:201
  148.4 5.9 %collective-permute-start.18 = (bf16[8,72,128]{2,1,0:T(8,128)(2,1)S(1)}, bf16[8,72,128]{2,1,0:T(8,128)(2,1)S(1)}, u32[]{:S(2)}, u32[]{:S(2)}) collective-permute-start(bf16[8,72,128]{2,1,0:T(8,128)(2,1)S(1)} %get-tuple-element.27), channel_id=1, source_target_pairs={{32,0},{34,2},{36,4},{38,6},{544,512},{546,514},{548,516},{550,518... | collective-permute-start | bytes 442376 | tf_op jit(solution)/shard_map/ppermute | solution.py:201
  150.9 7.7 %collective-permute-start.19 = (bf16[8,72,128]{2,1,0:T(8,128)(2,1)S(1)}, bf16[8,72,128]{2,1,0:T(8,128)(2,1)S(1)}, u32[]{:S(2)}, u32[]{:S(2)}) collective-permute-start(bf16[8,72,128]{2,1,0:T(8,128)(2,1)S(1)} %get-tuple-element.28), channel_id=1, source_target_pairs={{0,32},{2,34},{4,36},{6,38},{512,544},{514,546},{516,548},{518,550... | collective-permute-start | bytes 442376 | tf_op jit(solution)/shard_map/ppermute | solution.py:201

commit v8 on v7

--- a/solution.py
+++ b/solution.py
@@ -28,16 +28,18 @@
     departures, weight_index, vector, obs, mix = held
     run, levels, cols = vector.shape
     marks = [jnp.full((1, cols), ref[i]) for ref in (departures, weight_index) for i in range(ref.shape[0])]
-    part = mix[mine[0]].astype(F32)
-    part = jnp.concatenate([part, jnp.zeros((levels, cols - levels), F32)], axis=1)
+    part = mix[mine[0] >> 1].astype(F32)
+    share = out.shape[1] - 2 * levels - len(marks)
+    part = jnp.where((mine[0] & 1) == 0, part[:share], part[levels - share :])
+    part = jnp.concatenate([part, jnp.zeros((share, cols - levels), F32)], axis=1)
     shared = jnp.concatenate([jnp.concatenate(marks).astype(F32), obs[...], part])
     for tracer in range(run):
         out[tracer] = jnp.concatenate([vector[tracer].astype(F32), shared]).astype(BF16)
 
 
-def bundled(mine, departures, weight_index, vector, obs, mix):
+def bundled(mine, share, departures, weight_index, vector, obs, mix):
     run, levels, cols = vector.shape
-    rows = 3 * levels + departures.shape[0] + weight_index.shape[0]
+    rows = 2 * levels + departures.shape[0] + weight_index.shape[0] + share
     spaces = (pltpu.SMEM, pltpu.SMEM, pltpu.VMEM, pltpu.VMEM, pltpu.VMEM)
     given = (departures, weight_index, vector, obs, mix)
     return pl.pallas_call(
@@ -234,15 +236,16 @@
     first = lax.axis_index("lon") % 2 == 0
     steps = column_mix.shape[0]
     count = 2 * steps
-    mine = (lax.axis_index("lon") // 2 % steps).reshape(1).astype(jnp.int32)
+    share = -(-levels // 16) * 8
+    mine = (lax.axis_index("lon") & run - 1).reshape(1)
     bundle = along_y(
         bundled(
-            mine, departures.reshape(-1), weight_index.reshape(-1), vector[:, :, 0], obs_weight[:, 0], column_mix[:, 0]
+            mine, share, departures.reshape(-1), weight_index.reshape(-1), vector[:, :, 0], obs_weight[:, 0], column_mix[:, 0]
         )
     )
-    bundle = bundle.reshape(2, run // 2, *bundle.shape[1:])
-    mix = jnp.where(first, bundle[0, :, -levels:], bundle[1, :, -levels:])
-    bundle = jnp.stack(swap_cores(bundle[:, :, :-levels], first), axis=1).reshape(run, -1, cols)
+    halves = swap_cores(bundle.reshape(2, run // 2, *bundle.shape[1:]), first)
+    mix = jnp.concatenate([halves[0][:, -share:], halves[1][:, share - levels :]], axis=1)
+    bundle = jnp.stack([half[:, :-share] for half in halves], axis=1).reshape(run, -1, cols)
     marked = levels + count
     state, obs = bundle[:, :levels], bundle[:, marked:]
     reach = steps

time: 174 us -> 172 us (0.989)
  no operation moved by 1% of the time
where the time goes in v8:
time: 172 us
  starting transfers between devices  76.3 us (44%)
  waiting for transfers between devices  58.6 us (34%)
  blocking collectives  26.2 us (15%)
  Pallas kernels  8.86 us (5%)
    ppermute x20, starting transfers between devices, move(): return lax.ppermute(value, ('lat', 'lon'), pairs)  68.7 us
    ppermute x20, waiting for transfers between devices, move(): return lax.ppermute(value, ('lat', 'lon'), pairs)  47.8 us
    all_gather x2, blocking collectives, swap_cores(): lax.all_gather(give, 'lon', axis_index_groups=[[i, i + 1] for i in range(...  14.7 us
    all_to_all x1, blocking collectives, along_y(): return lax.all_to_all(value, ('lat', 'lon'), 0, 0, axis_index_groups=groups)  11.6 us
    all_to_all x1, waiting for transfers between devices, along_y(): return lax.all_to_all(value, ('lat', 'lon'), 0, 0, axis_index_groups=groups)  10.7 us
    all_to_all x1, starting transfers between devices, along_y(): return lax.all_to_all(value, ('lat', 'lon'), 0, 0, axis_index_groups=groups)  7.66 us
  transfers between devices with their start and end apart: 21, of which 20 were waited for; matrix products, arithmetic and copies ran while one was open for 0% of the time, Pallas kernels for 1%

profile of v8, /device:TPU:1, one launch (start us, length us, event | category | flops | bytes accessed | tf_op | source)
XLA Modules:
  0.0 171.6 jit_solution(304261712582913778)
XLA Ops:
  0.0 1.9 %shard_map.64 = bf16[8,192,128]{2,1,0:T(8,128)(2,1)} custom-call(s32[1]{0:T(128)} %bitcast.1.mine, s32[4]{0:T(128)} %bitcast.43, s32[4]{0:T(128)} %bitcast.44, bf16[8,72,128]{2,1,0:T(8,128)(2,1)} %bitcast.40, f32[72,128]{1,0:T(8,128)} %bitcast.42, bf16[4,72,72]{2,1,0:T(8,128)(2,1)} %bitcast.41), custom_call_target="tpu_custom_call" | custom-call | bytes 1000000 | tf_op jit(solution)/shard_map/pallas_call | solution.py:45
  1.9 7.7 %all-to-all-start = ((bf16[8,192,128]{2,1,0:T(8,128)(2,1)}), bf16[8,192,128]{2,1,0:T(8,128)(2,1)S(1)}, u32[]{:S(2)}, u32[]{:S(2)}) async-start(bf16[8,192,128]{2,1,0:T(8,128)(2,1)} %shard_map.64), calls=%async_computation | async-start | bytes 786432 | tf_op jit(solution)/shard_map/all_to_all | solution.py:224
  9.6 10.7 %all-to-all-done = bf16[8,192,128]{2,1,0:T(8,128)(2,1)S(1)} async-done(((bf16[8,192,128]{2,1,0:T(8,128)(2,1)}), bf16[8,192,128]{2,1,0:T(8,128)(2,1)S(1)}, u32[]{:S(2)}, u32[]{:S(2)}) %all-to-all-start) | async-done | bytes 393248 | tf_op jit(solution)/shard_map/all_to_all | solution.py:224
  20.3 12.7 %all-gather = bf16[8,192,128]{2,1,0:T(8,128)(2,1)S(1)} all-gather(bf16[4,192,128]{2,1,0:T(8,128)(2,1)S(1)} %broadcast_select_fusion), channel_id=2, replica_groups={{0,1},{2,3},{4,5},{6,7},{8,9},{10,11},{12,13},{14,15},{16,17},{18,19},{..., dimensions={0}, use_global_device_ids=true | all-gather | bytes 589824 | tf_op jit(solution)/shard_map/all_gather | solution.py:230
  33.3 1.9 %collective-permute-start = (bf16[4,80,128]{2,1,0:T(8,128)(2,1)S(1)}, bf16[4,80,128]{2,1,0:T(8,128)(2,1)S(1)}, u32[]{:S(2)}, u32[]{:S(2)}) collective-permute-start(bf16[4,80,128]{2,1,0:T(8,128)(2,1)S(1)} %get-tuple-element.35), channel_id=1, source_target_pairs={{0,8},{2,10},{4,12},{6,14},{512,520},{514,522},{516,524},{518,526}... | collective-permute-start | bytes 245768 | tf_op jit(solution)/shard_map/ppermute | solution.py:203
  35.2 4.6 %collective-permute-start.1 = (bf16[4,80,128]{2,1,0:T(8,128)(2,1)S(1)}, bf16[4,80,128]{2,1,0:T(8,128)(2,1)S(1)}, u32[]{:S(2)}, u32[]{:S(2)}) collective-permute-start(bf16[4,80,128]{2,1,0:T(8,128)(2,1)S(1)} %get-tuple-element.36), channel_id=1, source_target_pairs={{0,24},{2,26},{4,28},{6,30},{512,536},{514,538},{516,540},{518,542... | collective-permute-start | bytes 245768 | tf_op jit(solution)/shard_map/ppermute | solution.py:203
  40.1 1.2 collective-permute-done.1
  41.3 13.8 %collective-permute-start.3 = (bf16[15,72,128]{2,1,0:T(8,128)(2,1)S(1)}, bf16[15,72,128]{2,1,0:T(8,128)(2,1)S(1)}, u32[]{:S(2)}, u32[]{:S(2)}) collective-permute-start(bf16[15,72,128]{2,1,0:T(8,128)(2,1)S(1)} %pad_maximum_fusion.2.own), channel_id=1, source_target_pairs={{32,0},{34,2},{36,4},{38,6},{544,512},{546,514},{548,516},{550,518... | collective-permute-start | bytes 829448 | tf_op jit(solution)/shard_map/ppermute | solution.py:203
  55.2 1.9 %collective-permute-start.2 = (bf16[15,72,128]{2,1,0:T(8,128)(2,1)S(1)}, bf16[15,72,128]{2,1,0:T(8,128)(2,1)S(1)}, u32[]{:S(2)}, u32[]{:S(2)}) collective-permute-start(bf16[15,72,128]{2,1,0:T(8,128)(2,1)S(1)} %pad_maximum_fusion.2.own), channel_id=1, source_target_pairs={{0,32},{2,34},{4,36},{6,38},{512,544},{514,546},{516,548},{518,550... | collective-permute-start | bytes 829448 | tf_op jit(solution)/shard_map/ppermute | solution.py:203
  57.3 0.8 shard_map.65.weights
  58.6 5.6 %collective-permute-done.2.north = bf16[15,72,128]{2,1,0:T(8,128)(2,1)S(1)} collective-permute-done((bf16[15,72,128]{2,1,0:T(8,128)(2,1)S(1)}, bf16[15,72,128]{2,1,0:T(8,128)(2,1)S(1)}, u32[]{:S(2)}, u32[]{:S(2)}) %collective-permute-start.2) | collective-permute-done | bytes 276512 | tf_op jit(solution)/shard_map/ppermute | solution.py:203
  64.3 0.7 shard_map.66.own
  65.0 2.3 %collective-permute-start.5 = (bf16[13,72,128]{2,1,0:T(8,128)(2,1)S(1)}, bf16[13,72,128]{2,1,0:T(8,128)(2,1)S(1)}, u32[]{:S(2)}, u32[]{:S(2)}) collective-permute-start(bf16[13,72,128]{2,1,0:T(8,128)(2,1)S(1)} %shard_map.66.own), channel_id=1, source_target_pairs={{32,0},{34,2},{36,4},{38,6},{544,512},{546,514},{548,516},{550,518... | collective-permute-start | bytes 718856 | tf_op jit(solution)/shard_map/ppermute | solution.py:203
  67.2 3.0 %collective-permute-start.4 = (bf16[13,72,128]{2,1,0:T(8,128)(2,1)S(1)}, bf16[13,72,128]{2,1,0:T(8,128)(2,1)S(1)}, u32[]{:S(2)}, u32[]{:S(2)}) collective-permute-start(bf16[13,72,128]{2,1,0:T(8,128)(2,1)S(1)} %shard_map.66.own), channel_id=1, source_target_pairs={{0,32},{2,34},{4,36},{6,38},{512,544},{514,546},{516,548},{518,550... | collective-permute-start | bytes 718856 | tf_op jit(solution)/shard_map/ppermute | solution.py:203
  70.3 3.8 %collective-permute-done.5.south = bf16[13,72,128]{2,1,0:T(8,128)(2,1)S(1)} collective-permute-done((bf16[13,72,128]{2,1,0:T(8,128)(2,1)S(1)}, bf16[13,72,128]{2,1,0:T(8,128)(2,1)S(1)}, u32[]{:S(2)}, u32[]{:S(2)}) %collective-permute-start.5) | collective-permute-done | bytes 239648 | tf_op jit(solution)/shard_map/ppermute | solution.py:203
  74.1 1.8 %collective-permute-done.4.north = bf16[13,72,128]{2,1,0:T(8,128)(2,1)S(1)} collective-permute-done((bf16[13,72,128]{2,1,0:T(8,128)(2,1)S(1)}, bf16[13,72,128]{2,1,0:T(8,128)(2,1)S(1)}, u32[]{:S(2)}, u32[]{:S(2)}) %collective-permute-start.4) | collective-permute-done | bytes 239648 | tf_op jit(solution)/shard_map/ppermute | solution.py:203
  75.9 0.7 shard_map.67.own
  76.6 1.9 %collective-permute-start.7 = (bf16[11,72,128]{2,1,0:T(8,128)(2,1)S(1)}, bf16[11,72,128]{2,1,0:T(8,128)(2,1)S(1)}, u32[]{:S(2)}, u32[]{:S(2)}) collective-permute-start(bf16[11,72,128]{2,1,0:T(8,128)(2,1)S(1)} %shard_map.67.own), channel_id=1, source_target_pairs={{32,0},{34,2},{36,4},{38,6},{544,512},{546,514},{548,516},{550,518... | collective-permute-start | bytes 608264 | tf_op jit(solution)/shard_map/ppermute | solution.py:203
  78.5 3.7 %collective-permute-start.6 = (bf16[11,72,128]{2,1,0:T(8,128)(2,1)S(1)}, bf16[11,72,128]{2,1,0:T(8,128)(2,1)S(1)}, u32[]{:S(2)}, u32[]{:S(2)}) collective-permute-start(bf16[11,72,128]{2,1,0:T(8,128)(2,1)S(1)} %shard_map.67.own), channel_id=1, source_target_pairs={{0,32},{2,34},{4,36},{6,38},{512,544},{514,546},{516,548},{518,550... | collective-permute-start | bytes 608264 | tf_op jit(solution)/shard_map/ppermute | solution.py:203
  82.2 3.2 %collective-permute-done.7.south = bf16[11,72,128]{2,1,0:T(8,128)(2,1)S(1)} collective-permute-done((bf16[11,72,128]{2,1,0:T(8,128)(2,1)S(1)}, bf16[11,72,128]{2,1,0:T(8,128)(2,1)S(1)}, u32[]{:S(2)}, u32[]{:S(2)}) %collective-permute-start.7) | collective-permute-done | bytes 202784 | tf_op jit(solution)/shard_map/ppermute | solution.py:203
  85.4 1.4 collective-permute-done.6.north
  86.8 0.6 shard_map.68.own
  87.4 2.7 %collective-permute-start.9 = (bf16[9,72,128]{2,1,0:T(8,128)(2,1)S(1)}, bf16[9,72,128]{2,1,0:T(8,128)(2,1)S(1)}, u32[]{:S(2)}, u32[]{:S(2)}) collective-permute-start(bf16[9,72,128]{2,1,0:T(8,128)(2,1)S(1)} %shard_map.68.own), channel_id=1, source_target_pairs={{32,0},{34,2},{36,4},{38,6},{544,512},{546,514},{548,516},{550,518... | collective-permute-start | bytes 497672 | tf_op jit(solution)/shard_map/ppermute | solution.py:203
  90.1 2.8 %collective-permute-start.8 = (bf16[9,72,128]{2,1,0:T(8,128)(2,1)S(1)}, bf16[9,72,128]{2,1,0:T(8,128)(2,1)S(1)}, u32[]{:S(2)}, u32[]{:S(2)}) collective-permute-start(bf16[9,72,128]{2,1,0:T(8,128)(2,1)S(1)} %shard_map.68.own), channel_id=1, source_target_pairs={{0,32},{2,34},{4,36},{6,38},{512,544},{514,546},{516,548},{518,550... | collective-permute-start | bytes 497672 | tf_op jit(solution)/shard_map/ppermute | solution.py:203
  92.9 1.1 collective-permute-done.9.south
  94.0 4.0 %collective-permute-done.8.north = bf16[9,72,128]{2,1,0:T(8,128)(2,1)S(1)} collective-permute-done((bf16[9,72,128]{2,1,0:T(8,128)(2,1)S(1)}, bf16[9,72,128]{2,1,0:T(8,128)(2,1)S(1)}, u32[]{:S(2)}, u32[]{:S(2)}) %collective-permute-start.8) | collective-permute-done | bytes 165920 | tf_op jit(solution)/shard_map/ppermute | solution.py:203
  98.6 3.1 %collective-permute-start.10 = (bf16[4,72,128]{2,1,0:T(8,128)(2,1)S(1)}, bf16[4,72,128]{2,1,0:T(8,128)(2,1)S(1)}, u32[]{:S(2)}, u32[]{:S(2)}) collective-permute-start(bf16[4,72,128]{2,1,0:T(8,128)(2,1)S(1)} %get-tuple-element.37), channel_id=1, source_target_pairs={{0,8},{2,10},{4,12},{6,14},{512,520},{514,522},{516,524},{518,526}... | collective-permute-start | bytes 221192 | tf_op jit(solution)/shard_map/ppermute | solution.py:203
  101.7 3.4 %collective-permute-start.11 = (bf16[4,72,128]{2,1,0:T(8,128)(2,1)S(1)}, bf16[4,72,128]{2,1,0:T(8,128)(2,1)S(1)}, u32[]{:S(2)}, u32[]{:S(2)}) collective-permute-start(bf16[4,72,128]{2,1,0:T(8,128)(2,1)S(1)} %get-tuple-element.38), channel_id=1, source_target_pairs={{0,24},{2,26},{4,28},{6,30},{512,536},{514,538},{516,540},{518,542... | collective-permute-start | bytes 221192 | tf_op jit(solution)/shard_map/ppermute | solution.py:203
  105.5 0.9 shard_map.71.rest_1_.rest_3_
  106.9 0.7 shard_map.72
  107.5 4.7 %collective-permute-start.12 = (bf16[14,72,128]{2,1,0:T(8,128)(2,1)S(1)}, bf16[14,72,128]{2,1,0:T(8,128)(2,1)S(1)}, u32[]{:S(2)}, u32[]{:S(2)}) collective-permute-start(bf16[14,72,128]{2,1,0:T(8,128)(2,1)S(1)} %get-tuple-element.18), channel_id=1, source_target_pairs={{32,0},{34,2},{36,4},{38,6},{544,512},{546,514},{548,516},{550,518... | collective-permute-start | bytes 774152 | tf_op jit(solution)/shard_map/ppermute | solution.py:203
  112.2 1.9 %collective-permute-start.13 = (bf16[14,72,128]{2,1,0:T(8,128)(2,1)S(1)}, bf16[14,72,128]{2,1,0:T(8,128)(2,1)S(1)}, u32[]{:S(2)}, u32[]{:S(2)}) collective-permute-start(bf16[14,72,128]{2,1,0:T(8,128)(2,1)S(1)} %get-tuple-element.19), channel_id=1, source_target_pairs={{0,32},{2,34},{4,36},{6,38},{512,544},{514,546},{516,548},{518,550... | collective-permute-start | bytes 774152 | tf_op jit(solution)/shard_map/ppermute | solution.py:203
  114.2 1.4 collective-permute-done.12.rest_1_
  115.6 5.5 %collective-permute-done.13.rest_2_ = bf16[14,72,128]{2,1,0:T(8,128)(2,1)S(1)} collective-permute-done((bf16[14,72,128]{2,1,0:T(8,128)(2,1)S(1)}, bf16[14,72,128]{2,1,0:T(8,128)(2,1)S(1)}, u32[]{:S(2)}, u32[]{:S(2)}) %collective-permute-start.13) | collective-permute-done | bytes 258080 | tf_op jit(solution)/shard_map/ppermute | solution.py:203
  121.7 3.5 %collective-permute-start.14 = (bf16[12,72,128]{2,1,0:T(8,128)(2,1)S(1)}, bf16[12,72,128]{2,1,0:T(8,128)(2,1)S(1)}, u32[]{:S(2)}, u32[]{:S(2)}) collective-permute-start(bf16[12,72,128]{2,1,0:T(8,128)(2,1)S(1)} %get-tuple-element.21), channel_id=1, source_target_pairs={{32,0},{34,2},{36,4},{38,6},{544,512},{546,514},{548,516},{550,518... | collective-permute-start | bytes 663560 | tf_op jit(solution)/shard_map/ppermute | solution.py:203
  125.3 1.9 %collective-permute-start.15 = (bf16[12,72,128]{2,1,0:T(8,128)(2,1)S(1)}, bf16[12,72,128]{2,1,0:T(8,128)(2,1)S(1)}, u32[]{:S(2)}, u32[]{:S(2)}) collective-permute-start(bf16[12,72,128]{2,1,0:T(8,128)(2,1)S(1)} %get-tuple-element.22), channel_id=1, source_target_pairs={{0,32},{2,34},{4,36},{6,38},{512,544},{514,546},{516,548},{518,550... | collective-permute-start | bytes 663560 | tf_op jit(solution)/shard_map/ppermute | solution.py:203
  127.2 3.1 %collective-permute-done.14.rest_1_ = bf16[12,72,128]{2,1,0:T(8,128)(2,1)S(1)} collective-permute-done((bf16[12,72,128]{2,1,0:T(8,128)(2,1)S(1)}, bf16[12,72,128]{2,1,0:T(8,128)(2,1)S(1)}, u32[]{:S(2)}, u32[]{:S(2)}) %collective-permute-start.14) | collective-permute-done | bytes 221216 | tf_op jit(solution)/shard_map/ppermute | solution.py:203
  130.3 3.4 %collective-permute-done.15.rest_2_ = bf16[12,72,128]{2,1,0:T(8,128)(2,1)S(1)} collective-permute-done((bf16[12,72,128]{2,1,0:T(8,128)(2,1)S(1)}, bf16[12,72,128]{2,1,0:T(8,128)(2,1)S(1)}, u32[]{:S(2)}, u32[]{:S(2)}) %collective-permute-start.15) | collective-permute-done | bytes 221216 | tf_op jit(solution)/shard_map/ppermute | solution.py:203
  134.3 4.2 %collective-permute-start.16 = (bf16[10,72,128]{2,1,0:T(8,128)(2,1)S(1)}, bf16[10,72,128]{2,1,0:T(8,128)(2,1)S(1)}, u32[]{:S(2)}, u32[]{:S(2)}) collective-permute-start(bf16[10,72,128]{2,1,0:T(8,128)(2,1)S(1)} %get-tuple-element.24), channel_id=1, source_target_pairs={{32,0},{34,2},{36,4},{38,6},{544,512},{546,514},{548,516},{550,518... | collective-permute-start | bytes 552968 | tf_op jit(solution)/shard_map/ppermute | solution.py:203
  138.5 1.9 %collective-permute-start.17 = (bf16[10,72,128]{2,1,0:T(8,128)(2,1)S(1)}, bf16[10,72,128]{2,1,0:T(8,128)(2,1)S(1)}, u32[]{:S(2)}, u32[]{:S(2)}) collective-permute-start(bf16[10,72,128]{2,1,0:T(8,128)(2,1)S(1)} %get-tuple-element.25), channel_id=1, source_target_pairs={{0,32},{2,34},{4,36},{6,38},{512,544},{514,546},{516,548},{518,550... | collective-permute-start | bytes 552968 | tf_op jit(solution)/shard_map/ppermute | solution.py:203
  140.4 1.0 collective-permute-done.16.rest_1_
  141.4 5.2 %collective-permute-done.17.rest_2_ = bf16[10,72,128]{2,1,0:T(8,128)(2,1)S(1)} collective-permute-done((bf16[10,72,128]{2,1,0:T(8,128)(2,1)S(1)}, bf16[10,72,128]{2,1,0:T(8,128)(2,1)S(1)}, u32[]{:S(2)}, u32[]{:S(2)}) %collective-permute-start.17) | collective-permute-done | bytes 184352 | tf_op jit(solution)/shard_map/ppermute | solution.py:203
  147.1 2.5 %collective-permute-start.18 = (bf16[8,72,128]{2,1,0:T(8,128)(2,1)S(1)}, bf16[8,72,128]{2,1,0:T(8,128)(2,1)S(1)}, u32[]{:S(2)}, u32[]{:S(2)}) collective-permute-start(bf16[8,72,128]{2,1,0:T(8,128)(2,1)S(1)} %get-tuple-element.27), channel_id=1, source_target_pairs={{32,0},{34,2},{36,4},{38,6},{544,512},{546,514},{548,516},{550,518... | collective-permute-start | bytes 442376 | tf_op jit(solution)/shard_map/ppermute | solution.py:203
  149.6 2.7 %collective-permute-start.19 = (bf16[8,72,128]{2,1,0:T(8,128)(2,1)S(1)}, bf16[8,72,128]{2,1,0:T(8,128)(2,1)S(1)}, u32[]{:S(2)}, u32[]{:S(2)}) collective-permute-start(bf16[8,72,128]{2,1,0:T(8,128)(2,1)S(1)} %get-tuple-element.28), channel_id=1, source_target_pairs={{0,32},{2,34},{4,36},{6,38},{512,544},{514,546},{516,548},{518,550... | collective-permute-start | bytes 442376 | tf_op jit(solution)/shard_map/ppermute | solution.py:203
  153.0 4.3 %collective-permute-done.19 = bf16[8,72,128]{2,1,0:T(8,128)(2,1)S(1)} collective-permute-done((bf16[8,72,128]{2,1,0:T(8,128)(2,1)S(1)}, bf16[8,72,128]{2,1,0:T(8,128)(2,1)S(1)}, u32[]{:S(2)}, u32[]{:S(2)}) %collective-permute-start.19) | collective-permute-done | bytes 147488 | tf_op jit(solution)/shard_map/ppermute | solution.py:203
  157.4 1.9 %all-gather.1 = bf16[8,1,72,128]{3,2,1,0:T(8,128)(2,1)S(1)} all-gather(bf16[4,1,72,128]{3,2,1,0:T(8,128)(2,1)S(1)} %bitcast_select_fusion), channel_id=3, replica_groups={{0,1},{2,3},{4,5},{6,7},{8,9},{10,11},{12,13},{14,15},{16,17},{18,19},{..., dimensions={0}, use_global_device_ids=true | all-gather | bytes 221184 | tf_op jit(solution)/shard_map/all_gather | solution.py:230
  159.4 11.6 %all_to_all.10 = bf16[8,72,128]{2,1,0:T(8,128)(2,1)S(1)} all-to-all(bf16[8,72,128]{2,1,0:T(8,128)(2,1)S(1)} %pad_maximum_fusion.3), channel_id=1, replica_groups={{0,2,4,6,512,514,516,518},{1,3,5,7,513,515,517,519},{8,10,12,14,520,522..., dimensions={0} | all-to-all | bytes 294912 | tf_op jit(solution)/shard_map/all_to_all | solution.py:224
  170.9 0.7 copy.20
  (39 shorter events, 5.0 us)
Async XLA Ops:
  0.0 57.3 %copy-start = (bf16[16,160,128]{2,1,0:T(8,128)(2,1)S(1)}, bf16[16,160,128]{2,1,0:T(8,128)(2,1)}, u32[]{:S(2)}) copy-start(bf16[16,160,128]{2,1,0:T(8,128)(2,1)} %table.3) | copy-start | bytes 1966084
  1.9 18.4 %all-to-all-start = ((bf16[8,192,128]{2,1,0:T(8,128)(2,1)}), bf16[8,192,128]{2,1,0:T(8,128)(2,1)S(1)}, u32[]{:S(2)}, u32[]{:S(2)}) async-start(bf16[8,192,128]{2,1,0:T(8,128)(2,1)} %shard_map.64), calls=%async_computation | async-start | bytes 786432 | tf_op jit(solution)/shard_map/all_to_all | solution.py:224
  33.3 6.8 %collective-permute-start = (bf16[4,80,128]{2,1,0:T(8,128)(2,1)S(1)}, bf16[4,80,128]{2,1,0:T(8,128)(2,1)S(1)}, u32[]{:S(2)}, u32[]{:S(2)}) collective-permute-start(bf16[4,80,128]{2,1,0:T(8,128)(2,1)S(1)} %get-tuple-element.35), channel_id=1, source_target_pairs={{0,8},{2,10},{4,12},{6,14},{512,520},{514,522},{516,524},{518,526}... | collective-permute-start | bytes 245768 | tf_op jit(solution)/shard_map/ppermute | solution.py:203
  35.2 6.0 %collective-permute-start.1 = (bf16[4,80,128]{2,1,0:T(8,128)(2,1)S(1)}, bf16[4,80,128]{2,1,0:T(8,128)(2,1)S(1)}, u32[]{:S(2)}, u32[]{:S(2)}) collective-permute-start(bf16[4,80,128]{2,1,0:T(8,128)(2,1)S(1)} %get-tuple-element.36), channel_id=1, source_target_pairs={{0,24},{2,26},{4,28},{6,30},{512,536},{514,538},{516,540},{518,542... | collective-permute-start | bytes 245768 | tf_op jit(solution)/shard_map/ppermute | solution.py:203
  41.3 17.3 %collective-permute-start.3 = (bf16[15,72,128]{2,1,0:T(8,128)(2,1)S(1)}, bf16[15,72,128]{2,1,0:T(8,128)(2,1)S(1)}, u32[]{:S(2)}, u32[]{:S(2)}) collective-permute-start(bf16[15,72,128]{2,1,0:T(8,128)(2,1)S(1)} %pad_maximum_fusion.2.own), channel_id=1, source_target_pairs={{32,0},{34,2},{36,4},{38,6},{544,512},{546,514},{548,516},{550,518... | collective-permute-start | bytes 829448 | tf_op jit(solution)/shard_map/ppermute | solution.py:203
  55.2 9.1 %collective-permute-start.2 = (bf16[15,72,128]{2,1,0:T(8,128)(2,1)S(1)}, bf16[15,72,128]{2,1,0:T(8,128)(2,1)S(1)}, u32[]{:S(2)}, u32[]{:S(2)}) collective-permute-start(bf16[15,72,128]{2,1,0:T(8,128)(2,1)S(1)} %pad_maximum_fusion.2.own), channel_id=1, source_target_pairs={{0,32},{2,34},{4,36},{6,38},{512,544},{514,546},{516,548},{518,550... | collective-permute-start | bytes 829448 | tf_op jit(solution)/shard_map/ppermute | solution.py:203
  65.0 9.1 %collective-permute-start.5 = (bf16[13,72,128]{2,1,0:T(8,128)(2,1)S(1)}, bf16[13,72,128]{2,1,0:T(8,128)(2,1)S(1)}, u32[]{:S(2)}, u32[]{:S(2)}) collective-permute-start(bf16[13,72,128]{2,1,0:T(8,128)(2,1)S(1)} %shard_map.66.own), channel_id=1, source_target_pairs={{32,0},{34,2},{36,4},{38,6},{544,512},{546,514},{548,516},{550,518... | collective-permute-start | bytes 718856 | tf_op jit(solution)/shard_map/ppermute | solution.py:203
  67.2 8.7 %collective-permute-start.4 = (bf16[13,72,128]{2,1,0:T(8,128)(2,1)S(1)}, bf16[13,72,128]{2,1,0:T(8,128)(2,1)S(1)}, u32[]{:S(2)}, u32[]{:S(2)}) collective-permute-start(bf16[13,72,128]{2,1,0:T(8,128)(2,1)S(1)} %shard_map.66.own), channel_id=1, source_target_pairs={{0,32},{2,34},{4,36},{6,38},{512,544},{514,546},{516,548},{518,550... | collective-permute-start | bytes 718856 | tf_op jit(solution)/shard_map/ppermute | solution.py:203
  76.6 8.8 %collective-permute-start.7 = (bf16[11,72,128]{2,1,0:T(8,128)(2,1)S(1)}, bf16[11,72,128]{2,1,0:T(8,128)(2,1)S(1)}, u32[]{:S(2)}, u32[]{:S(2)}) collective-permute-start(bf16[11,72,128]{2,1,0:T(8,128)(2,1)S(1)} %shard_map.67.own), channel_id=1, source_target_pairs={{32,0},{34,2},{36,4},{38,6},{544,512},{546,514},{548,516},{550,518... | collective-permute-start | bytes 608264 | tf_op jit(solution)/shard_map/ppermute | solution.py:203
  78.5 8.3 %collective-permute-start.6 = (bf16[11,72,128]{2,1,0:T(8,128)(2,1)S(1)}, bf16[11,72,128]{2,1,0:T(8,128)(2,1)S(1)}, u32[]{:S(2)}, u32[]{:S(2)}) collective-permute-start(bf16[11,72,128]{2,1,0:T(8,128)(2,1)S(1)} %shard_map.67.own), channel_id=1, source_target_pairs={{0,32},{2,34},{4,36},{6,38},{512,544},{514,546},{516,548},{518,550... | collective-permute-start | bytes 608264 | tf_op jit(solution)/shard_map/ppermute | solution.py:203
  87.4 6.6 %collective-permute-start.9 = (bf16[9,72,128]{2,1,0:T(8,128)(2,1)S(1)}, bf16[9,72,128]{2,1,0:T(8,128)(2,1)S(1)}, u32[]{:S(2)}, u32[]{:S(2)}) collective-permute-start(bf16[9,72,128]{2,1,0:T(8,128)(2,1)S(1)} %shard_map.68.own), channel_id=1, source_target_pairs={{32,0},{34,2},{36,4},{38,6},{544,512},{546,514},{548,516},{550,518... | collective-permute-start | bytes 497672 | tf_op jit(solution)/shard_map/ppermute | solution.py:203
  90.1 7.9 %collective-permute-start.8 = (bf16[9,72,128]{2,1,0:T(8,128)(2,1)S(1)}, bf16[9,72,128]{2,1,0:T(8,128)(2,1)S(1)}, u32[]{:S(2)}, u32[]{:S(2)}) collective-permute-start(bf16[9,72,128]{2,1,0:T(8,128)(2,1)S(1)} %shard_map.68.own), channel_id=1, source_target_pairs={{0,32},{2,34},{4,36},{6,38},{512,544},{514,546},{516,548},{518,550... | collective-permute-start | bytes 497672 | tf_op jit(solution)/shard_map/ppermute | solution.py:203
  98.6 7.8 %collective-permute-start.10 = (bf16[4,72,128]{2,1,0:T(8,128)(2,1)S(1)}, bf16[4,72,128]{2,1,0:T(8,128)(2,1)S(1)}, u32[]{:S(2)}, u32[]{:S(2)}) collective-permute-start(bf16[4,72,128]{2,1,0:T(8,128)(2,1)S(1)} %get-tuple-element.37), channel_id=1, source_target_pairs={{0,8},{2,10},{4,12},{6,14},{512,520},{514,522},{516,524},{518,526}... | collective-permute-start | bytes 221192 | tf_op jit(solution)/shard_map/ppermute | solution.py:203
  101.7 5.1 %collective-permute-start.11 = (bf16[4,72,128]{2,1,0:T(8,128)(2,1)S(1)}, bf16[4,72,128]{2,1,0:T(8,128)(2,1)S(1)}, u32[]{:S(2)}, u32[]{:S(2)}) collective-permute-start(bf16[4,72,128]{2,1,0:T(8,128)(2,1)S(1)} %get-tuple-element.38), channel_id=1, source_target_pairs={{0,24},{2,26},{4,28},{6,30},{512,536},{514,538},{516,540},{518,542... | collective-permute-start | bytes 221192 | tf_op jit(solution)/shard_map/ppermute | solution.py:203
  107.5 8.1 %collective-permute-start.12 = (bf16[14,72,128]{2,1,0:T(8,128)(2,1)S(1)}, bf16[14,72,128]{2,1,0:T(8,128)(2,1)S(1)}, u32[]{:S(2)}, u32[]{:S(2)}) collective-permute-start(bf16[14,72,128]{2,1,0:T(8,128)(2,1)S(1)} %get-tuple-element.18), channel_id=1, source_target_pairs={{32,0},{34,2},{36,4},{38,6},{544,512},{546,514},{548,516},{550,518... | collective-permute-start | bytes 774152 | tf_op jit(solution)/shard_map/ppermute | solution.py:203
  112.2 8.9 %collective-permute-start.13 = (bf16[14,72,128]{2,1,0:T(8,128)(2,1)S(1)}, bf16[14,72,128]{2,1,0:T(8,128)(2,1)S(1)}, u32[]{:S(2)}, u32[]{:S(2)}) collective-permute-start(bf16[14,72,128]{2,1,0:T(8,128)(2,1)S(1)} %get-tuple-element.19), channel_id=1, source_target_pairs={{0,32},{2,34},{4,36},{6,38},{512,544},{514,546},{516,548},{518,550... | collective-permute-start | bytes 774152 | tf_op jit(solution)/shard_map/ppermute | solution.py:203
  121.7 8.6 %collective-permute-start.14 = (bf16[12,72,128]{2,1,0:T(8,128)(2,1)S(1)}, bf16[12,72,128]{2,1,0:T(8,128)(2,1)S(1)}, u32[]{:S(2)}, u32[]{:S(2)}) collective-permute-start(bf16[12,72,128]{2,1,0:T(8,128)(2,1)S(1)} %get-tuple-element.21), channel_id=1, source_target_pairs={{32,0},{34,2},{36,4},{38,6},{544,512},{546,514},{548,516},{550,518... | collective-permute-start | bytes 663560 | tf_op jit(solution)/shard_map/ppermute | solution.py:203
  125.3 8.5 %collective-permute-start.15 = (bf16[12,72,128]{2,1,0:T(8,128)(2,1)S(1)}, bf16[12,72,128]{2,1,0:T(8,128)(2,1)S(1)}, u32[]{:S(2)}, u32[]{:S(2)}) collective-permute-start(bf16[12,72,128]{2,1,0:T(8,128)(2,1)S(1)} %get-tuple-element.22), channel_id=1, source_target_pairs={{0,32},{2,34},{4,36},{6,38},{512,544},{514,546},{516,548},{518,550... | collective-permute-start | bytes 663560 | tf_op jit(solution)/shard_map/ppermute | solution.py:203
  134.3 7.1 %collective-permute-start.16 = (bf16[10,72,128]{2,1,0:T(8,128)(2,1)S(1)}, bf16[10,72,128]{2,1,0:T(8,128)(2,1)S(1)}, u32[]{:S(2)}, u32[]{:S(2)}) collective-permute-start(bf16[10,72,128]{2,1,0:T(8,128)(2,1)S(1)} %get-tuple-element.24), channel_id=1, source_target_pairs={{32,0},{34,2},{36,4},{38,6},{544,512},{546,514},{548,516},{550,518... | collective-permute-start | bytes 552968 | tf_op jit(solution)/shard_map/ppermute | solution.py:203
  138.5 8.1 %collective-permute-start.17 = (bf16[10,72,128]{2,1,0:T(8,128)(2,1)S(1)}, bf16[10,72,128]{2,1,0:T(8,128)(2,1)S(1)}, u32[]{:S(2)}, u32[]{:S(2)}) collective-permute-start(bf16[10,72,128]{2,1,0:T(8,128)(2,1)S(1)} %get-tuple-element.25), channel_id=1, source_target_pairs={{0,32},{2,34},{4,36},{6,38},{512,544},{514,546},{516,548},{518,550... | collective-permute-start | bytes 552968 | tf_op jit(solution)/shard_map/ppermute | solution.py:203
  147.1 5.9 %collective-permute-start.18 = (bf16[8,72,128]{2,1,0:T(8,128)(2,1)S(1)}, bf16[8,72,128]{2,1,0:T(8,128)(2,1)S(1)}, u32[]{:S(2)}, u32[]{:S(2)}) collective-permute-start(bf16[8,72,128]{2,1,0:T(8,128)(2,1)S(1)} %get-tuple-element.27), channel_id=1, source_target_pairs={{32,0},{34,2},{36,4},{38,6},{544,512},{546,514},{548,516},{550,518... | collective-permute-start | bytes 442376 | tf_op jit(solution)/shard_map/ppermute | solution.py:203
  149.6 7.7 %collective-permute-start.19 = (bf16[8,72,128]{2,1,0:T(8,128)(2,1)S(1)}, bf16[8,72,128]{2,1,0:T(8,128)(2,1)S(1)}, u32[]{:S(2)}, u32[]{:S(2)}) collective-permute-start(bf16[8,72,128]{2,1,0:T(8,128)(2,1)S(1)} %get-tuple-element.28), channel_id=1, source_target_pairs={{0,32},{2,34},{4,36},{6,38},{512,544},{514,546},{516,548},{518,550... | collective-permute-start | bytes 442376 | tf_op jit(solution)/shard_map/ppermute | solution.py:203

commit v9 on v8

--- a/solution.py
+++ b/solution.py
@@ -81,7 +81,7 @@
     steps, blocks = out.shape[:2]
     for step in range(steps):
         for p in range(outside(step), blocks - outside(step)):
-            out[step, p] = table[par[p, steps + step]]
+            out[step, p] = table[par[p, par.shape[1] // 2 + step]]
 
 
 def choose(par, table, steps, outside):
@@ -95,8 +95,7 @@
     )(par, table)
 
 
-def forward_kernel(step, first, outs, fold, weighted, marks, own, north, south, weights, mix, *rest):
-    obs, out = rest if weighted else (None, rest[0])
+def forward_kernel(step, first, outs, fold, marks, own, north, south, weights, mix, out):
     shape = own.shape[1:]
     rightward = right_lanes(shape)
     mixing = mix[step][:, : shape[0]]
@@ -114,8 +113,6 @@
         window = jnp.concatenate([pick(p), edges], axis=1)
         interp = jnp.dot(window, window_weights(weights[step, first + p]), preferred_element_type=F32).astype(BF16)
         mixed = jnp.dot(mixing, interp, preferred_element_type=F32).astype(BF16)
-        if weighted:
-            mixed = (obs[p].astype(F32) * mixed.astype(F32)).astype(BF16)
         if fold and p in (0, outs - 1):
             blocks.append(mixed)
         else:
@@ -124,14 +121,13 @@
         out[outs - 2] = jnp.where(rightward, blocks[1], blocks[0])
 
 
-def forward(step, outs, fold, marks, rows, weights, mix, obs=None):
+def forward(step, outs, fold, marks, rows, weights, mix):
     levels, cols = rows[0].shape[1:]
     first = (marks.shape[0] - outs) // 2
     made = outs - 1 if fold else outs
-    weighted = obs is not None
-    args = (marks, *rows, weights, mix) + ((obs,) if weighted else ())
-    return pl.pallas_call(
-        functools.partial(forward_kernel, step, first, outs, fold, weighted),
+    args = (marks, *rows, weights, mix)
+    return pl.pallas_call(
+        functools.partial(forward_kernel, step, first, outs, fold),
         out_shape=jax.ShapeDtypeStruct((made, levels, cols), BF16),
         in_specs=[VMEM] * len(args),
         out_specs=VMEM,
@@ -181,6 +177,49 @@
         compiler_params=pltpu.CompilerParams(vmem_limit_bytes=LIMIT),
         cost_estimate=pl.CostEstimate(flops=reads * 6_000_000, bytes_accessed=2_000_000, transcendentals=0),
     )(marks, *parts, weights, mix)
+
+
+def middle_kernel(step, par, line, above, beside, below, table, turned, out, spreads):
+    reads = spreads.shape[0]
+    shape = line.shape[1:]
+    levels, cols = shape
+    rightward = right_lanes(shape)
+    rows = (above, beside, below)
+    marks = [jnp.concatenate([row[reads + 1].astype(F32), row[reads + 2].astype(F32)]) for row in rows]
+    mixing = [row[reads][:, :levels] for row in rows]
+    unmixing = [row[reads].astype(F32).T[:levels].astype(BF16) for row in rows]
+    count = 2 * (step + 1)
+    for p in range(reads):
+        left = p - 1 if p > 0 else reads
+        right = p + 1 if p < reads - 1 else reads
+        window = jnp.concatenate([line[p], jnp.where(rightward, line[right], line[left])], axis=1)
+        total = jnp.zeros((levels, 2 * cols), F32)
+        for i, row in enumerate(rows):
+            which = par[i, p]
+            interp = jnp.dot(window, window_weights(table[which]), preferred_element_type=F32).astype(BF16)
+            mixed = jnp.dot(mixing[i], interp, preferred_element_type=F32).astype(BF16)
+            cot = row[p].astype(F32) * mixed.astype(F32)
+            way = jnp.broadcast_to(marks[i][count * p + step : count * p + step + 1], shape)
+            cot = jnp.where(way == 2 - i, cot, 0.0).astype(BF16)
+            back = jnp.dot(unmixing[i], cot, preferred_element_type=F32).astype(BF16)
+            total += jnp.dot(back, turned[which], preferred_element_type=F32)
+        spreads[p] = total
+    for p in range(1, reads - 1):
+        edges = jnp.where(rightward, spreads[p - 1, :, cols:], spreads[p + 1, :, cols:])
+        out[p - 1] = (spreads[p, :, :cols] + edges).astype(BF16)
+
+
+def middle(step, par, line, rows, table, turned):
+    reads, (levels, cols) = par.shape[1], line.shape[1:]
+    return pl.pallas_call(
+        functools.partial(middle_kernel, step),
+        out_shape=jax.ShapeDtypeStruct((reads - 2, levels, cols), BF16),
+        in_specs=[SMEM] + [VMEM] * 6,
+        out_specs=VMEM,
+        scratch_shapes=[pltpu.VMEM((reads, levels, 2 * cols), F32)],
+        compiler_params=pltpu.CompilerParams(vmem_limit_bytes=LIMIT),
+        cost_estimate=pl.CostEstimate(flops=reads * 30_000_000, bytes_accessed=4_000_000, transcendentals=0),
+    )(par, line, *rows, table, turned)
 
 
 def homes():
@@ -247,24 +286,45 @@
     mix = jnp.concatenate([halves[0][:, -share:], halves[1][:, share - levels :]], axis=1)
     bundle = jnp.stack([half[:, :-share] for half in halves], axis=1).reshape(run, -1, cols)
     marked = levels + count
-    state, obs = bundle[:, :levels], bundle[:, marked:]
     reach = steps
-    west, east = from_lon(bundle[-reach:, :marked], -run), from_lon(bundle[:reach, :marked], run)
-
-    marks = jnp.concatenate([part[:, levels:marked] for part in (west, bundle, east)])
+    west, east = from_lon(bundle[-reach:], -run), from_lon(bundle[:reach], run)
+    line = jnp.concatenate([west, bundle, east])
+    marks = line[:, levels:marked]
     par = jnp.max(marks.astype(F32), axis=2).astype(jnp.int32)
-    weights = choose(par, interp_table, reach, lambda step: 1 + step)
-    turned = choose(par, turn(interp_table), reach, lambda step: reach - 1 - step)
-    outer = jnp.where(right_lanes((levels, cols)), east[-1, :levels], west[0, :levels])
-    state = jnp.concatenate([west[1:, :levels], state, east[:-1, :levels], outer[None]])
-    for step in range(reach):
-        last = step == reach - 1
-        rows = (state, from_lat(state, -1), from_lat(state, 1))
-        state = forward(step, run + 2 * (reach - 1 - step), not last, marks, rows, weights, mix, obs if last else None)
-
-    west, east = from_lon(state[-reach:], -run), from_lon(state[:reach], run)
-    parts = (jnp.concatenate([west, state, east]),)
-    for step in reversed(range(reach)):
+    last = steps - 1
+    weights = choose(par, interp_table, last, lambda step: 2 + step)
+    table = turn(interp_table)
+    turned = choose(par, table, last, lambda step: reach - 1 - step)
+
+    span = line.shape[0]
+    room = -(-span * count // levels) * levels - span * count
+    flat = jnp.concatenate([marks.reshape(-1, cols), jnp.zeros((room, cols), BF16)]).reshape(-1, levels, cols)
+    beside = jnp.concatenate([line[:, marked:], mix[last][None], flat])
+    cuts = (0, 4, 10, beside.shape[0])
+
+    outer = jnp.where(right_lanes((levels, cols)), line[-2, :levels], line[1, :levels])
+    state = jnp.concatenate([line[2:-2, :levels], outer[None]])
+    above, below = [], []
+    for step in range(last):
+        sent = jnp.concatenate([state, beside[cuts[step] : cuts[step + 1]]])
+        north, south = from_lat(sent, -1), from_lat(sent, 1)
+        above.append(north[state.shape[0] :])
+        below.append(south[state.shape[0] :])
+        outs = run + 2 * (last - 1 - step)
+        state = forward(step, outs, step < last - 1, marks, (state, north, south), weights, mix)
+
+    west, east = from_lon(state[-reach - 1 :], -run), from_lon(state[: reach + 1], run)
+    outer = jnp.where(right_lanes((levels, cols)), east[-1], west[0])
+    line = jnp.concatenate([west[1:], state, east[:-1], outer[None]])
+    rows = (jnp.concatenate(above), beside, jnp.concatenate(below))
+
+    def chosen(row):
+        numbers = row[span + 1 :].reshape(-1, cols)[: span * count].reshape(span, count, cols)[:, -1]
+        return jnp.max(numbers.astype(F32), axis=1).astype(jnp.int32)
+
+    par = jnp.stack([chosen(row) for row in rows])
+    parts = (middle(last, par, line, rows, interp_table, table),)
+    for step in reversed(range(last)):
         north, stay, south = adjoint(step, marks, parts, turned, mix)
         parts = (stay, from_lat(north, 1), from_lat(south, -1))
     cot = sum(part.astype(F32) for part in parts).astype(BF16)

time: 172 us -> 167 us (0.971)
  starting transfers between devices: 76.3 us -> 62.8 us
  Pallas kernels: 8.86 us -> 18.1 us
  waiting for transfers between devices: 58.6 us -> 55.9 us
    ppermute x20 -> x16, starting transfers between devices: 68.7 us -> 55.2 us  [move(): return lax.ppermute(value, ('lat', 'lon'), pairs)]
    pallas_call x4, Pallas kernels: 2.6 us -> 12.7 us  [the longest x1 10.8 us: middle(): pl.pallas_call(functools.partial(middle_kernel, step), out_shape=jax.Shap...]
    ppermute x20 -> x16, waiting for transfers between devices: 47.8 us -> 45.2 us  [move(): return lax.ppermute(value, ('lat', 'lon'), pairs)]
  transfers between devices with their start and end apart: 21 -> 17, of which waited for: 20 -> 16; matrix products, arithmetic and copies ran while one was open for 0% -> 1% of each run, Pallas kernels for 1% -> 1%
where the time goes in v9:
time: 167 us; the launch traced here: 166 us
  starting transfers between devices  62.8 us (38%)
  waiting for transfers between devices  55.9 us (33%)
  blocking collectives  26.2 us (16%)
  Pallas kernels  18.1 us (11%)
    ppermute x16, starting transfers between devices, move(): return lax.ppermute(value, ('lat', 'lon'), pairs)  55.2 us
    ppermute x16, waiting for transfers between devices, move(): return lax.ppermute(value, ('lat', 'lon'), pairs)  45.2 us
    all_gather x2, blocking collectives, swap_cores(): lax.all_gather(give, 'lon', axis_index_groups=[[i, i + 1] for i in range(...  14.7 us
    all_to_all x1, blocking collectives, along_y(): return lax.all_to_all(value, ('lat', 'lon'), 0, 0, axis_index_groups=groups)  11.6 us
    pallas_call x1, Pallas kernels, middle(): pl.pallas_call(functools.partial(middle_kernel, step), out_shape=jax.Shap...  10.8 us
    all_to_all x1, waiting for transfers between devices, along_y(): return lax.all_to_all(value, ('lat', 'lon'), 0, 0, axis_index_groups=groups)  10.7 us
    all_to_all x1, starting transfers between devices, along_y(): return lax.all_to_all(value, ('lat', 'lon'), 0, 0, axis_index_groups=groups)  7.66 us
  transfers between devices with their start and end apart: 17, of which 16 were waited for; matrix products, arithmetic and copies ran while one was open for 1% of the time, Pallas kernels for 1%

profile of v9, /device:TPU:1, one launch (start us, length us, event | category | flops | bytes accessed | tf_op | source)
XLA Modules:
  0.0 166.0 jit_solution(13252378318030454173)
XLA Ops:
  0.0 1.8 %shard_map.64 = bf16[8,192,128]{2,1,0:T(8,128)(2,1)} custom-call(s32[1]{0:T(128)} %bitcast.1.mine, s32[4]{0:T(128)} %bitcast.66, s32[4]{0:T(128)} %bitcast.67, bf16[8,72,128]{2,1,0:T(8,128)(2,1)} %bitcast.61, f32[72,128]{1,0:T(8,128)} %bitcast.65, bf16[4,72,72]{2,1,0:T(8,128)(2,1)} %bitcast.64), custom_call_target="tpu_custom_call" | custom-call | bytes 1000000 | tf_op jit(solution)/shard_map/pallas_call | solution.py:45
  1.8 7.7 %all-to-all-start = ((bf16[8,192,128]{2,1,0:T(8,128)(2,1)}), bf16[8,192,128]{2,1,0:T(8,128)(2,1)S(1)}, u32[]{:S(2)}, u32[]{:S(2)}) async-start(bf16[8,192,128]{2,1,0:T(8,128)(2,1)} %shard_map.64), calls=%async_computation | async-start | bytes 786432 | tf_op jit(solution)/shard_map/all_to_all | solution.py:263
  9.5 10.7 %all-to-all-done = bf16[8,192,128]{2,1,0:T(8,128)(2,1)S(1)} async-done(((bf16[8,192,128]{2,1,0:T(8,128)(2,1)}), bf16[8,192,128]{2,1,0:T(8,128)(2,1)S(1)}, u32[]{:S(2)}, u32[]{:S(2)}) %all-to-all-start) | async-done | bytes 393248 | tf_op jit(solution)/shard_map/all_to_all | solution.py:263
  20.2 12.7 %all-gather = bf16[8,192,128]{2,1,0:T(8,128)(2,1)S(1)} all-gather(bf16[4,192,128]{2,1,0:T(8,128)(2,1)S(1)} %broadcast_select_fusion), channel_id=2, replica_groups={{0,1},{2,3},{4,5},{6,7},{8,9},{10,11},{12,13},{14,15},{16,17},{18,19},{..., dimensions={0}, use_global_device_ids=true | all-gather | bytes 589824 | tf_op jit(solution)/shard_map/all_gather | solution.py:269
  33.2 2.1 %collective-permute-start.1 = (bf16[4,152,128]{2,1,0:T(8,128)(2,1)S(1)}, bf16[4,152,128]{2,1,0:T(8,128)(2,1)S(1)}, u32[]{:S(2)}, u32[]{:S(2)}) collective-permute-start(bf16[4,152,128]{2,1,0:T(8,128)(2,1)S(1)} %bitcast.59), channel_id=1, source_target_pairs={{0,24},{2,26},{4,28},{6,30},{512,536},{514,538},{516,540},{518,542... | collective-permute-start | bytes 466952 | tf_op jit(solution)/shard_map/ppermute | solution.py:242
  35.2 3.4 %collective-permute-start = (bf16[4,152,128]{2,1,0:T(8,128)(2,1)S(1)}, bf16[4,152,128]{2,1,0:T(8,128)(2,1)S(1)}, u32[]{:S(2)}, u32[]{:S(2)}) collective-permute-start(bf16[4,152,128]{2,1,0:T(8,128)(2,1)S(1)} %bitcast.58), channel_id=1, source_target_pairs={{0,8},{2,10},{4,12},{6,14},{512,520},{514,522},{516,524},{518,526}... | collective-permute-start | bytes 466952 | tf_op jit(solution)/shard_map/ppermute | solution.py:242
  38.7 1.7 %collective-permute-done.1 = bf16[4,152,128]{2,1,0:T(8,128)(2,1)S(1)} collective-permute-done((bf16[4,152,128]{2,1,0:T(8,128)(2,1)S(1)}, bf16[4,152,128]{2,1,0:T(8,128)(2,1)S(1)}, u32[]{:S(2)}, u32[]{:S(2)}) %collective-permute-start.1) | collective-permute-done | bytes 155680 | tf_op jit(solution)/shard_map/ppermute | solution.py:242
  40.4 3.1 %collective-permute-done = bf16[4,152,128]{2,1,0:T(8,128)(2,1)S(1)} collective-permute-done((bf16[4,152,128]{2,1,0:T(8,128)(2,1)S(1)}, bf16[4,152,128]{2,1,0:T(8,128)(2,1)S(1)}, u32[]{:S(2)}, u32[]{:S(2)}) %collective-permute-start) | collective-permute-done | bytes 155680 | tf_op jit(solution)/shard_map/ppermute | solution.py:242
  43.7 15.4 %collective-permute-start.3 = (bf16[17,72,128]{2,1,0:T(8,128)(2,1)S(1)}, bf16[17,72,128]{2,1,0:T(8,128)(2,1)S(1)}, u32[]{:S(2)}, u32[]{:S(2)}) collective-permute-start(bf16[17,72,128]{2,1,0:T(8,128)(2,1)S(1)} %pad_maximum_fusion.6), channel_id=1, source_target_pairs={{32,0},{34,2},{36,4},{38,6},{544,512},{546,514},{548,516},{550,518... | collective-permute-start | bytes 940040 | tf_op jit(solution)/shard_map/ppermute | solution.py:242
  59.1 1.9 %collective-permute-start.2 = (bf16[17,72,128]{2,1,0:T(8,128)(2,1)S(1)}, bf16[17,72,128]{2,1,0:T(8,128)(2,1)S(1)}, u32[]{:S(2)}, u32[]{:S(2)}) collective-permute-start(bf16[17,72,128]{2,1,0:T(8,128)(2,1)S(1)} %pad_maximum_fusion.6), channel_id=1, source_target_pairs={{0,32},{2,34},{4,36},{6,38},{512,544},{514,546},{516,548},{518,550... | collective-permute-start | bytes 940040 | tf_op jit(solution)/shard_map/ppermute | solution.py:242
  61.2 0.8 shard_map.65.weights
  62.0 1.0 collective-permute-done.3.south
  63.0 5.6 %collective-permute-done.2.north = bf16[17,72,128]{2,1,0:T(8,128)(2,1)S(1)} collective-permute-done((bf16[17,72,128]{2,1,0:T(8,128)(2,1)S(1)}, bf16[17,72,128]{2,1,0:T(8,128)(2,1)S(1)}, u32[]{:S(2)}, u32[]{:S(2)}) %collective-permute-start.2) | collective-permute-done | bytes 313376 | tf_op jit(solution)/shard_map/ppermute | solution.py:242
  68.6 0.7 shard_map.66.own
  69.3 2.9 %collective-permute-start.5 = (bf16[17,72,128]{2,1,0:T(8,128)(2,1)S(1)}, bf16[17,72,128]{2,1,0:T(8,128)(2,1)S(1)}, u32[]{:S(2)}, u32[]{:S(2)}) collective-permute-start(bf16[17,72,128]{2,1,0:T(8,128)(2,1)S(1)} %pad_maximum_fusion.7), channel_id=1, source_target_pairs={{32,0},{34,2},{36,4},{38,6},{544,512},{546,514},{548,516},{550,518... | collective-permute-start | bytes 940040 | tf_op jit(solution)/shard_map/ppermute | solution.py:242
  72.2 2.3 %collective-permute-start.4 = (bf16[17,72,128]{2,1,0:T(8,128)(2,1)S(1)}, bf16[17,72,128]{2,1,0:T(8,128)(2,1)S(1)}, u32[]{:S(2)}, u32[]{:S(2)}) collective-permute-start(bf16[17,72,128]{2,1,0:T(8,128)(2,1)S(1)} %pad_maximum_fusion.7), channel_id=1, source_target_pairs={{0,32},{2,34},{4,36},{6,38},{512,544},{514,546},{516,548},{518,550... | collective-permute-start | bytes 940040 | tf_op jit(solution)/shard_map/ppermute | solution.py:242
  74.7 5.0 %collective-permute-done.5.south = bf16[17,72,128]{2,1,0:T(8,128)(2,1)S(1)} collective-permute-done((bf16[17,72,128]{2,1,0:T(8,128)(2,1)S(1)}, bf16[17,72,128]{2,1,0:T(8,128)(2,1)S(1)}, u32[]{:S(2)}, u32[]{:S(2)}) %collective-permute-start.5) | collective-permute-done | bytes 313376 | tf_op jit(solution)/shard_map/ppermute | solution.py:242
  79.7 2.0 %collective-permute-done.4.north = bf16[17,72,128]{2,1,0:T(8,128)(2,1)S(1)} collective-permute-done((bf16[17,72,128]{2,1,0:T(8,128)(2,1)S(1)}, bf16[17,72,128]{2,1,0:T(8,128)(2,1)S(1)}, u32[]{:S(2)}, u32[]{:S(2)}) %collective-permute-start.4) | collective-permute-done | bytes 313376 | tf_op jit(solution)/shard_map/ppermute | solution.py:242
  81.7 0.6 shard_map.67.own
  82.4 1.9 %collective-permute-start.7 = (bf16[18,72,128]{2,1,0:T(8,128)(2,1)S(1)}, bf16[18,72,128]{2,1,0:T(8,128)(2,1)S(1)}, u32[]{:S(2)}, u32[]{:S(2)}) collective-permute-start(bf16[18,72,128]{2,1,0:T(8,128)(2,1)S(1)} %pad_maximum_fusion.5), channel_id=1, source_target_pairs={{32,0},{34,2},{36,4},{38,6},{544,512},{546,514},{548,516},{550,518... | collective-permute-start | bytes 995336 | tf_op jit(solution)/shard_map/ppermute | solution.py:242
  84.3 0.3 shard_map.69.turned.table
  84.6 0.8 shard_map.71.rest_1_.rest_3_
  85.7 3.5 %collective-permute-start.6 = (bf16[18,72,128]{2,1,0:T(8,128)(2,1)S(1)}, bf16[18,72,128]{2,1,0:T(8,128)(2,1)S(1)}, u32[]{:S(2)}, u32[]{:S(2)}) collective-permute-start(bf16[18,72,128]{2,1,0:T(8,128)(2,1)S(1)} %pad_maximum_fusion.5), channel_id=1, source_target_pairs={{0,32},{2,34},{4,36},{6,38},{512,544},{514,546},{516,548},{518,550... | collective-permute-start | bytes 995336 | tf_op jit(solution)/shard_map/ppermute | solution.py:242
  89.3 1.0 collective-permute-done.7.south
  90.5 5.0 %collective-permute-done.6.north = bf16[18,72,128]{2,1,0:T(8,128)(2,1)S(1)} collective-permute-done((bf16[18,72,128]{2,1,0:T(8,128)(2,1)S(1)}, bf16[18,72,128]{2,1,0:T(8,128)(2,1)S(1)}, u32[]{:S(2)}, u32[]{:S(2)}) %collective-permute-start.6) | collective-permute-done | bytes 331808 | tf_op jit(solution)/shard_map/ppermute | solution.py:242
  95.7 0.6 shard_map.68
  96.3 1.9 %collective-permute-start.9 = (bf16[5,72,128]{2,1,0:T(8,128)(2,1)S(1)}, bf16[5,72,128]{2,1,0:T(8,128)(2,1)S(1)}, u32[]{:S(2)}, u32[]{:S(2)}) collective-permute-start(bf16[5,72,128]{2,1,0:T(8,128)(2,1)S(1)} %get-tuple-element.29), channel_id=1, source_target_pairs={{0,24},{2,26},{4,28},{6,30},{512,536},{514,538},{516,540},{518,542... | collective-permute-start | bytes 276488 | tf_op jit(solution)/shard_map/ppermute | solution.py:242
  98.3 3.4 %collective-permute-start.8 = (bf16[5,72,128]{2,1,0:T(8,128)(2,1)S(1)}, bf16[5,72,128]{2,1,0:T(8,128)(2,1)S(1)}, u32[]{:S(2)}, u32[]{:S(2)}) collective-permute-start(bf16[5,72,128]{2,1,0:T(8,128)(2,1)S(1)} %get-tuple-element.30), channel_id=1, source_target_pairs={{0,8},{2,10},{4,12},{6,14},{512,520},{514,522},{516,524},{518,526}... | collective-permute-start | bytes 276488 | tf_op jit(solution)/shard_map/ppermute | solution.py:242
  101.8 2.9 %collective-permute-done.8 = bf16[5,72,128]{2,1,0:T(8,128)(2,1)S(1)} collective-permute-done((bf16[5,72,128]{2,1,0:T(8,128)(2,1)S(1)}, bf16[5,72,128]{2,1,0:T(8,128)(2,1)S(1)}, u32[]{:S(2)}, u32[]{:S(2)}) %collective-permute-start.8) | collective-permute-done | bytes 92192 | tf_op jit(solution)/shard_map/ppermute | solution.py:242
  104.8 10.8 %shard_map.70.rest_0_ = bf16[14,72,128]{2,1,0:T(8,128)(2,1)S(1)} custom-call(s32[3,16]{1,0:T(4,128)S(1)} %pad_add_fusion.par, bf16[17,72,128]{2,1,0:T(8,128)(2,1)S(1)} %pad_maximum_fusion.8.line, bf16[19,72,128]{2,1,0:T(8,128)(2,1)S(1)} %pad_maximum_fusion.3.above, bf16[19,72,128]{2,1,0:T(8,128)(2,1)S(1)} %pad_maximum_fusion.2.beside, ...), custom_call_target="tpu_custom_call" | custom-call | flops 480000000 | bytes 4000000 | tf_op jit(solution)/shard_map/pallas_call | solution.py:214
  115.7 0.6 shard_map.72
  116.3 4.0 %collective-permute-start.10 = (bf16[12,72,128]{2,1,0:T(8,128)(2,1)S(1)}, bf16[12,72,128]{2,1,0:T(8,128)(2,1)S(1)}, u32[]{:S(2)}, u32[]{:S(2)}) collective-permute-start(bf16[12,72,128]{2,1,0:T(8,128)(2,1)S(1)} %get-tuple-element.15), channel_id=1, source_target_pairs={{32,0},{34,2},{36,4},{38,6},{544,512},{546,514},{548,516},{550,518... | collective-permute-start | bytes 663560 | tf_op jit(solution)/shard_map/ppermute | solution.py:242
  120.3 1.9 %collective-permute-start.11 = (bf16[12,72,128]{2,1,0:T(8,128)(2,1)S(1)}, bf16[12,72,128]{2,1,0:T(8,128)(2,1)S(1)}, u32[]{:S(2)}, u32[]{:S(2)}) collective-permute-start(bf16[12,72,128]{2,1,0:T(8,128)(2,1)S(1)} %get-tuple-element.16), channel_id=1, source_target_pairs={{0,32},{2,34},{4,36},{6,38},{512,544},{514,546},{516,548},{518,550... | collective-permute-start | bytes 663560 | tf_op jit(solution)/shard_map/ppermute | solution.py:242
  122.2 2.0 %collective-permute-done.10.rest_1_ = bf16[12,72,128]{2,1,0:T(8,128)(2,1)S(1)} collective-permute-done((bf16[12,72,128]{2,1,0:T(8,128)(2,1)S(1)}, bf16[12,72,128]{2,1,0:T(8,128)(2,1)S(1)}, u32[]{:S(2)}, u32[]{:S(2)}) %collective-permute-start.10) | collective-permute-done | bytes 221216 | tf_op jit(solution)/shard_map/ppermute | solution.py:242
  124.3 4.5 %collective-permute-done.11.rest_2_ = bf16[12,72,128]{2,1,0:T(8,128)(2,1)S(1)} collective-permute-done((bf16[12,72,128]{2,1,0:T(8,128)(2,1)S(1)}, bf16[12,72,128]{2,1,0:T(8,128)(2,1)S(1)}, u32[]{:S(2)}, u32[]{:S(2)}) %collective-permute-start.11) | collective-permute-done | bytes 221216 | tf_op jit(solution)/shard_map/ppermute | solution.py:242
  128.8 0.6 shard_map.73
  129.3 3.1 %collective-permute-start.12 = (bf16[10,72,128]{2,1,0:T(8,128)(2,1)S(1)}, bf16[10,72,128]{2,1,0:T(8,128)(2,1)S(1)}, u32[]{:S(2)}, u32[]{:S(2)}) collective-permute-start(bf16[10,72,128]{2,1,0:T(8,128)(2,1)S(1)} %get-tuple-element.18), channel_id=1, source_target_pairs={{32,0},{34,2},{36,4},{38,6},{544,512},{546,514},{548,516},{550,518... | collective-permute-start | bytes 552968 | tf_op jit(solution)/shard_map/ppermute | solution.py:242
  132.5 2.2 %collective-permute-start.13 = (bf16[10,72,128]{2,1,0:T(8,128)(2,1)S(1)}, bf16[10,72,128]{2,1,0:T(8,128)(2,1)S(1)}, u32[]{:S(2)}, u32[]{:S(2)}) collective-permute-start(bf16[10,72,128]{2,1,0:T(8,128)(2,1)S(1)} %get-tuple-element.19), channel_id=1, source_target_pairs={{0,32},{2,34},{4,36},{6,38},{512,544},{514,546},{516,548},{518,550... | collective-permute-start | bytes 552968 | tf_op jit(solution)/shard_map/ppermute | solution.py:242
  134.6 1.0 collective-permute-done.12.rest_1_
  135.6 4.9 %collective-permute-done.13.rest_2_ = bf16[10,72,128]{2,1,0:T(8,128)(2,1)S(1)} collective-permute-done((bf16[10,72,128]{2,1,0:T(8,128)(2,1)S(1)}, bf16[10,72,128]{2,1,0:T(8,128)(2,1)S(1)}, u32[]{:S(2)}, u32[]{:S(2)}) %collective-permute-start.13) | collective-permute-done | bytes 184352 | tf_op jit(solution)/shard_map/ppermute | solution.py:242
  140.5 0.5 shard_map.74
  141.1 3.0 %collective-permute-start.14 = (bf16[8,72,128]{2,1,0:T(8,128)(2,1)S(1)}, bf16[8,72,128]{2,1,0:T(8,128)(2,1)S(1)}, u32[]{:S(2)}, u32[]{:S(2)}) collective-permute-start(bf16[8,72,128]{2,1,0:T(8,128)(2,1)S(1)} %get-tuple-element.21), channel_id=1, source_target_pairs={{32,0},{34,2},{36,4},{38,6},{544,512},{546,514},{548,516},{550,518... | collective-permute-start | bytes 442376 | tf_op jit(solution)/shard_map/ppermute | solution.py:242
  144.1 2.3 %collective-permute-start.15 = (bf16[8,72,128]{2,1,0:T(8,128)(2,1)S(1)}, bf16[8,72,128]{2,1,0:T(8,128)(2,1)S(1)}, u32[]{:S(2)}, u32[]{:S(2)}) collective-permute-start(bf16[8,72,128]{2,1,0:T(8,128)(2,1)S(1)} %get-tuple-element.22), channel_id=1, source_target_pairs={{0,32},{2,34},{4,36},{6,38},{512,544},{514,546},{516,548},{518,550... | collective-permute-start | bytes 442376 | tf_op jit(solution)/shard_map/ppermute | solution.py:242
  146.4 0.6 collective-permute-done.14
  147.0 4.8 %collective-permute-done.15 = bf16[8,72,128]{2,1,0:T(8,128)(2,1)S(1)} collective-permute-done((bf16[8,72,128]{2,1,0:T(8,128)(2,1)S(1)}, bf16[8,72,128]{2,1,0:T(8,128)(2,1)S(1)}, u32[]{:S(2)}, u32[]{:S(2)}) %collective-permute-start.15) | collective-permute-done | bytes 147488 | tf_op jit(solution)/shard_map/ppermute | solution.py:242
  151.8 1.9 %all-gather.1 = bf16[8,1,72,128]{3,2,1,0:T(8,128)(2,1)S(1)} all-gather(bf16[4,1,72,128]{3,2,1,0:T(8,128)(2,1)S(1)} %bitcast_select_fusion), channel_id=3, replica_groups={{0,1},{2,3},{4,5},{6,7},{8,9},{10,11},{12,13},{14,15},{16,17},{18,19},{..., dimensions={0}, use_global_device_ids=true | all-gather | bytes 221184 | tf_op jit(solution)/shard_map/all_gather | solution.py:269
  153.8 11.6 %all_to_all.10 = bf16[8,72,128]{2,1,0:T(8,128)(2,1)S(1)} all-to-all(bf16[8,72,128]{2,1,0:T(8,128)(2,1)S(1)} %pad_maximum_fusion.10), channel_id=1, replica_groups={{0,2,4,6,512,514,516,518},{1,3,5,7,513,515,517,519},{8,10,12,14,520,522..., dimensions={0} | all-to-all | bytes 294912 | tf_op jit(solution)/shard_map/all_to_all | solution.py:263
  165.4 0.7 copy.24
  (72 shorter events, 1.7 us)
Async XLA Ops:
  1.8 18.4 %all-to-all-start = ((bf16[8,192,128]{2,1,0:T(8,128)(2,1)}), bf16[8,192,128]{2,1,0:T(8,128)(2,1)S(1)}, u32[]{:S(2)}, u32[]{:S(2)}) async-start(bf16[8,192,128]{2,1,0:T(8,128)(2,1)} %shard_map.64), calls=%async_computation | async-start | bytes 786432 | tf_op jit(solution)/shard_map/all_to_all | solution.py:263
  33.1 28.1 %copy-start = (bf16[16,160,128]{2,1,0:T(8,128)(2,1)S(1)}, bf16[16,160,128]{2,1,0:T(8,128)(2,1)}, u32[]{:S(2)}) copy-start(bf16[16,160,128]{2,1,0:T(8,128)(2,1)} %table.5) | copy-start | bytes 1966084
  33.2 7.3 %collective-permute-start.1 = (bf16[4,152,128]{2,1,0:T(8,128)(2,1)S(1)}, bf16[4,152,128]{2,1,0:T(8,128)(2,1)S(1)}, u32[]{:S(2)}, u32[]{:S(2)}) collective-permute-start(bf16[4,152,128]{2,1,0:T(8,128)(2,1)S(1)} %bitcast.59), channel_id=1, source_target_pairs={{0,24},{2,26},{4,28},{6,30},{512,536},{514,538},{516,540},{518,542... | collective-permute-start | bytes 466952 | tf_op jit(solution)/shard_map/ppermute | solution.py:242
  35.2 8.3 %collective-permute-start = (bf16[4,152,128]{2,1,0:T(8,128)(2,1)S(1)}, bf16[4,152,128]{2,1,0:T(8,128)(2,1)S(1)}, u32[]{:S(2)}, u32[]{:S(2)}) collective-permute-start(bf16[4,152,128]{2,1,0:T(8,128)(2,1)S(1)} %bitcast.58), channel_id=1, source_target_pairs={{0,8},{2,10},{4,12},{6,14},{512,520},{514,522},{516,524},{518,526}... | collective-permute-start | bytes 466952 | tf_op jit(solution)/shard_map/ppermute | solution.py:242
  43.7 19.2 %collective-permute-start.3 = (bf16[17,72,128]{2,1,0:T(8,128)(2,1)S(1)}, bf16[17,72,128]{2,1,0:T(8,128)(2,1)S(1)}, u32[]{:S(2)}, u32[]{:S(2)}) collective-permute-start(bf16[17,72,128]{2,1,0:T(8,128)(2,1)S(1)} %pad_maximum_fusion.6), channel_id=1, source_target_pairs={{32,0},{34,2},{36,4},{38,6},{544,512},{546,514},{548,516},{550,518... | collective-permute-start | bytes 940040 | tf_op jit(solution)/shard_map/ppermute | solution.py:242
  59.1 9.5 %collective-permute-start.2 = (bf16[17,72,128]{2,1,0:T(8,128)(2,1)S(1)}, bf16[17,72,128]{2,1,0:T(8,128)(2,1)S(1)}, u32[]{:S(2)}, u32[]{:S(2)}) collective-permute-start(bf16[17,72,128]{2,1,0:T(8,128)(2,1)S(1)} %pad_maximum_fusion.6), channel_id=1, source_target_pairs={{0,32},{2,34},{4,36},{6,38},{512,544},{514,546},{516,548},{518,550... | collective-permute-start | bytes 940040 | tf_op jit(solution)/shard_map/ppermute | solution.py:242
  63.0 22.7 %copy-start.3 = (bf16[17,72,128]{2,1,0:T(8,128)(2,1)}, bf16[17,72,128]{2,1,0:T(8,128)(2,1)S(1)}, u32[]{:S(2)}) copy-start(bf16[17,72,128]{2,1,0:T(8,128)(2,1)S(1)} %collective-permute-done.3.south) | copy-start | bytes 940036
  68.6 17.1 %copy-start.4 = (bf16[17,72,128]{2,1,0:T(8,128)(2,1)}, bf16[17,72,128]{2,1,0:T(8,128)(2,1)S(1)}, u32[]{:S(2)}) copy-start(bf16[17,72,128]{2,1,0:T(8,128)(2,1)S(1)} %collective-permute-done.2.north) | copy-start | bytes 940036
  69.3 10.4 %collective-permute-start.5 = (bf16[17,72,128]{2,1,0:T(8,128)(2,1)S(1)}, bf16[17,72,128]{2,1,0:T(8,128)(2,1)S(1)}, u32[]{:S(2)}, u32[]{:S(2)}) collective-permute-start(bf16[17,72,128]{2,1,0:T(8,128)(2,1)S(1)} %pad_maximum_fusion.7), channel_id=1, source_target_pairs={{32,0},{34,2},{36,4},{38,6},{544,512},{546,514},{548,516},{550,518... | collective-permute-start | bytes 940040 | tf_op jit(solution)/shard_map/ppermute | solution.py:242
  72.2 9.5 %collective-permute-start.4 = (bf16[17,72,128]{2,1,0:T(8,128)(2,1)S(1)}, bf16[17,72,128]{2,1,0:T(8,128)(2,1)S(1)}, u32[]{:S(2)}, u32[]{:S(2)}) collective-permute-start(bf16[17,72,128]{2,1,0:T(8,128)(2,1)S(1)} %pad_maximum_fusion.7), channel_id=1, source_target_pairs={{0,32},{2,34},{4,36},{6,38},{512,544},{514,546},{516,548},{518,550... | collective-permute-start | bytes 940040 | tf_op jit(solution)/shard_map/ppermute | solution.py:242
  79.7 9.6 %copy-start.1 = (bf16[17,72,128]{2,1,0:T(8,128)(2,1)}, bf16[17,72,128]{2,1,0:T(8,128)(2,1)S(1)}, u32[]{:S(2)}) copy-start(bf16[17,72,128]{2,1,0:T(8,128)(2,1)S(1)} %collective-permute-done.5.south) | copy-start | bytes 940036
  81.7 7.5 %copy-start.2 = (bf16[17,72,128]{2,1,0:T(8,128)(2,1)}, bf16[17,72,128]{2,1,0:T(8,128)(2,1)S(1)}, u32[]{:S(2)}) copy-start(bf16[17,72,128]{2,1,0:T(8,128)(2,1)S(1)} %collective-permute-done.4.north) | copy-start | bytes 940036
  82.4 7.9 %collective-permute-start.7 = (bf16[18,72,128]{2,1,0:T(8,128)(2,1)S(1)}, bf16[18,72,128]{2,1,0:T(8,128)(2,1)S(1)}, u32[]{:S(2)}, u32[]{:S(2)}) collective-permute-start(bf16[18,72,128]{2,1,0:T(8,128)(2,1)S(1)} %pad_maximum_fusion.5), channel_id=1, source_target_pairs={{32,0},{34,2},{36,4},{38,6},{544,512},{546,514},{548,516},{550,518... | collective-permute-start | bytes 995336 | tf_op jit(solution)/shard_map/ppermute | solution.py:242
  85.7 16.0 %slice-start.2 = ((bf16[17,72,128]{2,1,0:T(8,128)(2,1)}), bf16[4,72,128]{2,1,0:T(8,128)(2,1)S(1)}, s32[]{:S(2)}) async-start(bf16[17,72,128]{2,1,0:T(8,128)(2,1)} %copy-done.3), calls=%async_computation.4 | async-start | bytes 147456 | tf_op jit(solution)/shard_map/slice | solution.py:312
  85.7 16.0 %slice-start.3 = ((bf16[17,72,128]{2,1,0:T(8,128)(2,1)}), bf16[4,72,128]{2,1,0:T(8,128)(2,1)S(1)}, s32[]{:S(2)}) async-start(bf16[17,72,128]{2,1,0:T(8,128)(2,1)} %copy-done.4), calls=%async_computation.5 | async-start | bytes 147456 | tf_op jit(solution)/shard_map/slice | solution.py:311
  85.7 9.8 %collective-permute-start.6 = (bf16[18,72,128]{2,1,0:T(8,128)(2,1)S(1)}, bf16[18,72,128]{2,1,0:T(8,128)(2,1)S(1)}, u32[]{:S(2)}, u32[]{:S(2)}) collective-permute-start(bf16[18,72,128]{2,1,0:T(8,128)(2,1)S(1)} %pad_maximum_fusion.5), channel_id=1, source_target_pairs={{0,32},{2,34},{4,36},{6,38},{512,544},{514,546},{516,548},{518,550... | collective-permute-start | bytes 995336 | tf_op jit(solution)/shard_map/ppermute | solution.py:242
  89.2 12.4 %slice-start = ((bf16[17,72,128]{2,1,0:T(8,128)(2,1)}), bf16[6,72,128]{2,1,0:T(8,128)(2,1)S(1)}, s32[]{:S(2)}) async-start(bf16[17,72,128]{2,1,0:T(8,128)(2,1)} %copy-done.1), calls=%async_computation.2 | async-start | bytes 221184 | tf_op jit(solution)/shard_map/slice | solution.py:312
  89.2 12.5 %slice-start.1 = ((bf16[17,72,128]{2,1,0:T(8,128)(2,1)}), bf16[6,72,128]{2,1,0:T(8,128)(2,1)S(1)}, s32[]{:S(2)}) async-start(bf16[17,72,128]{2,1,0:T(8,128)(2,1)} %copy-done.2), calls=%async_computation.3 | async-start | bytes 221184 | tf_op jit(solution)/shard_map/slice | solution.py:311
  96.3 5.5 %collective-permute-start.9 = (bf16[5,72,128]{2,1,0:T(8,128)(2,1)S(1)}, bf16[5,72,128]{2,1,0:T(8,128)(2,1)S(1)}, u32[]{:S(2)}, u32[]{:S(2)}) collective-permute-start(bf16[5,72,128]{2,1,0:T(8,128)(2,1)S(1)} %get-tuple-element.29), channel_id=1, source_target_pairs={{0,24},{2,26},{4,28},{6,30},{512,536},{514,538},{516,540},{518,542... | collective-permute-start | bytes 276488 | tf_op jit(solution)/shard_map/ppermute | solution.py:242
  98.3 6.5 %collective-permute-start.8 = (bf16[5,72,128]{2,1,0:T(8,128)(2,1)S(1)}, bf16[5,72,128]{2,1,0:T(8,128)(2,1)S(1)}, u32[]{:S(2)}, u32[]{:S(2)}) collective-permute-start(bf16[5,72,128]{2,1,0:T(8,128)(2,1)S(1)} %get-tuple-element.30), channel_id=1, source_target_pairs={{0,8},{2,10},{4,12},{6,14},{512,520},{514,522},{516,524},{518,526}... | collective-permute-start | bytes 276488 | tf_op jit(solution)/shard_map/ppermute | solution.py:242
  116.3 8.0 %collective-permute-start.10 = (bf16[12,72,128]{2,1,0:T(8,128)(2,1)S(1)}, bf16[12,72,128]{2,1,0:T(8,128)(2,1)S(1)}, u32[]{:S(2)}, u32[]{:S(2)}) collective-permute-start(bf16[12,72,128]{2,1,0:T(8,128)(2,1)S(1)} %get-tuple-element.15), channel_id=1, source_target_pairs={{32,0},{34,2},{36,4},{38,6},{544,512},{546,514},{548,516},{550,518... | collective-permute-start | bytes 663560 | tf_op jit(solution)/shard_map/ppermute | solution.py:242
  120.3 8.5 %collective-permute-start.11 = (bf16[12,72,128]{2,1,0:T(8,128)(2,1)S(1)}, bf16[12,72,128]{2,1,0:T(8,128)(2,1)S(1)}, u32[]{:S(2)}, u32[]{:S(2)}) collective-permute-start(bf16[12,72,128]{2,1,0:T(8,128)(2,1)S(1)} %get-tuple-element.16), channel_id=1, source_target_pairs={{0,32},{2,34},{4,36},{6,38},{512,544},{514,546},{516,548},{518,550... | collective-permute-start | bytes 663560 | tf_op jit(solution)/shard_map/ppermute | solution.py:242
  129.3 6.3 %collective-permute-start.12 = (bf16[10,72,128]{2,1,0:T(8,128)(2,1)S(1)}, bf16[10,72,128]{2,1,0:T(8,128)(2,1)S(1)}, u32[]{:S(2)}, u32[]{:S(2)}) collective-permute-start(bf16[10,72,128]{2,1,0:T(8,128)(2,1)S(1)} %get-tuple-element.18), channel_id=1, source_target_pairs={{32,0},{34,2},{36,4},{38,6},{544,512},{546,514},{548,516},{550,518... | collective-permute-start | bytes 552968 | tf_op jit(solution)/shard_map/ppermute | solution.py:242
  132.5 8.1 %collective-permute-start.13 = (bf16[10,72,128]{2,1,0:T(8,128)(2,1)S(1)}, bf16[10,72,128]{2,1,0:T(8,128)(2,1)S(1)}, u32[]{:S(2)}, u32[]{:S(2)}) collective-permute-start(bf16[10,72,128]{2,1,0:T(8,128)(2,1)S(1)} %get-tuple-element.19), channel_id=1, source_target_pairs={{0,32},{2,34},{4,36},{6,38},{512,544},{514,546},{516,548},{518,550... | collective-permute-start | bytes 552968 | tf_op jit(solution)/shard_map/ppermute | solution.py:242
  141.1 5.9 %collective-permute-start.14 = (bf16[8,72,128]{2,1,0:T(8,128)(2,1)S(1)}, bf16[8,72,128]{2,1,0:T(8,128)(2,1)S(1)}, u32[]{:S(2)}, u32[]{:S(2)}) collective-permute-start(bf16[8,72,128]{2,1,0:T(8,128)(2,1)S(1)} %get-tuple-element.21), channel_id=1, source_target_pairs={{32,0},{34,2},{36,4},{38,6},{544,512},{546,514},{548,516},{550,518... | collective-permute-start | bytes 442376 | tf_op jit(solution)/shard_map/ppermute | solution.py:242
  144.1 7.7 %collective-permute-start.15 = (bf16[8,72,128]{2,1,0:T(8,128)(2,1)S(1)}, bf16[8,72,128]{2,1,0:T(8,128)(2,1)S(1)}, u32[]{:S(2)}, u32[]{:S(2)}) collective-permute-start(bf16[8,72,128]{2,1,0:T(8,128)(2,1)S(1)} %get-tuple-element.22), channel_id=1, source_target_pairs={{0,32},{2,34},{4,36},{6,38},{512,544},{514,546},{516,548},{518,550... | collective-permute-start | bytes 442376 | tf_op jit(solution)/shard_map/ppermute | solution.py:242

commit v10 on v9

--- a/solution.py
+++ b/solution.py
@@ -179,47 +179,44 @@
     )(marks, *parts, weights, mix)
 
 
-def middle_kernel(step, par, line, above, beside, below, table, turned, out, spreads):
+def middle_kernel(step, par, line, above, beside, below, marks, table, turned, out, cots, spreads):
     reads = spreads.shape[0]
     shape = line.shape[1:]
     levels, cols = shape
     rightward = right_lanes(shape)
-    rows = (above, beside, below)
-    marks = [jnp.concatenate([row[reads + 1].astype(F32), row[reads + 2].astype(F32)]) for row in rows]
-    mixing = [row[reads][:, :levels] for row in rows]
-    unmixing = [row[reads].astype(F32).T[:levels].astype(BF16) for row in rows]
-    count = 2 * (step + 1)
-    for p in range(reads):
-        left = p - 1 if p > 0 else reads
-        right = p + 1 if p < reads - 1 else reads
-        window = jnp.concatenate([line[p], jnp.where(rightward, line[right], line[left])], axis=1)
-        total = jnp.zeros((levels, 2 * cols), F32)
-        for i, row in enumerate(rows):
-            which = par[i, p]
-            interp = jnp.dot(window, window_weights(table[which]), preferred_element_type=F32).astype(BF16)
-            mixed = jnp.dot(mixing[i], interp, preferred_element_type=F32).astype(BF16)
+    for i, row in enumerate((above, beside, below)):
+        mixing = row[reads][:, :levels]
+        unmixing = row[reads].astype(F32).T[:levels].astype(BF16)
+        for p in range(reads):
+            left = p - 1 if p > 0 else reads
+            right = p + 1 if p < reads - 1 else reads
+            window = jnp.concatenate([line[p], jnp.where(rightward, line[right], line[left])], axis=1)
+            weights = window_weights(table[par[i, p]])
+            interp = jnp.dot(window, weights, preferred_element_type=F32).astype(BF16)
+            mixed = jnp.dot(mixing, interp, preferred_element_type=F32).astype(BF16)
+            way = jnp.broadcast_to(marks[i, p][step : step + 1].astype(F32), shape)
             cot = row[p].astype(F32) * mixed.astype(F32)
-            way = jnp.broadcast_to(marks[i][count * p + step : count * p + step + 1], shape)
-            cot = jnp.where(way == 2 - i, cot, 0.0).astype(BF16)
-            back = jnp.dot(unmixing[i], cot, preferred_element_type=F32).astype(BF16)
-            total += jnp.dot(back, turned[which], preferred_element_type=F32)
-        spreads[p] = total
+            cots[p] = jnp.where(way == 2 - i, cot, 0.0).astype(BF16)
+        for p in range(reads):
+            back = jnp.dot(unmixing, cots[p], preferred_element_type=F32).astype(BF16)
+            spread = jnp.dot(back, turned[par[i, p]], preferred_element_type=F32)
+            spreads[p] = spread if i == 0 else spreads[p] + spread
     for p in range(1, reads - 1):
         edges = jnp.where(rightward, spreads[p - 1, :, cols:], spreads[p + 1, :, cols:])
         out[p - 1] = (spreads[p, :, :cols] + edges).astype(BF16)
 
 
-def middle(step, par, line, rows, table, turned):
+def middle(step, par, line, rows, marks, table, turned):
     reads, (levels, cols) = par.shape[1], line.shape[1:]
     return pl.pallas_call(
         functools.partial(middle_kernel, step),
         out_shape=jax.ShapeDtypeStruct((reads - 2, levels, cols), BF16),
-        in_specs=[SMEM] + [VMEM] * 6,
-        out_specs=VMEM,
-        scratch_shapes=[pltpu.VMEM((reads, levels, 2 * cols), F32)],
+        in_specs=[SMEM] + [VMEM] * 7,
+        out_specs=VMEM,
+        scratch_shapes=[pltpu.VMEM((reads, levels, cols), BF16), pltpu.VMEM((reads, levels, 2 * cols), F32)],
         compiler_params=pltpu.CompilerParams(vmem_limit_bytes=LIMIT),
         cost_estimate=pl.CostEstimate(flops=reads * 30_000_000, bytes_accessed=4_000_000, transcendentals=0),
-    )(par, line, *rows, table, turned)
+    )(par, line, *rows, marks, table, turned)
 
 
 def homes():
@@ -318,12 +315,9 @@
     line = jnp.concatenate([west[1:], state, east[:-1], outer[None]])
     rows = (jnp.concatenate(above), beside, jnp.concatenate(below))
 
-    def chosen(row):
-        numbers = row[span + 1 :].reshape(-1, cols)[: span * count].reshape(span, count, cols)[:, -1]
-        return jnp.max(numbers.astype(F32), axis=1).astype(jnp.int32)
-
-    par = jnp.stack([chosen(row) for row in rows])
-    parts = (middle(last, par, line, rows, interp_table, table),)
+    marks_of = jnp.stack([row[span + 1 :].reshape(-1, cols)[: span * count].reshape(span, count, cols) for row in rows])
+    par = jnp.max(marks_of[:, :, -1].astype(F32), axis=2).astype(jnp.int32)
+    parts = (middle(last, par, line, rows, marks_of, interp_table, table),)
     for step in reversed(range(last)):
         north, stay, south = adjoint(step, marks, parts, turned, mix)
         parts = (stay, from_lat(north, 1), from_lat(south, -1))

time: 167 us -> 156 us (0.934)
  waiting for transfers between devices: 55.9 us -> 45.7 us
  Pallas kernels: 18.1 us -> 10.3 us
  starting transfers between devices: 62.8 us -> 70.5 us
    ppermute x16, waiting for transfers between devices: 45.2 us -> 35 us  [move(): return lax.ppermute(value, ('lat', 'lon'), pairs)]
    pallas_call x1, Pallas kernels: 10.8 us -> 3.05 us  [middle(): pl.pallas_call(functools.partial(middle_kernel, step), out_shape=jax.Shap...]
    ppermute x16, starting transfers between devices: 55.2 us -> 62.8 us  [move(): return lax.ppermute(value, ('lat', 'lon'), pairs)]
  transfers between devices with their start and end apart: 17 -> 17, of which waited for: 16 -> 16; matrix products, arithmetic and copies ran while one was open for 1% -> 0% of each run, Pallas kernels for 1% -> 1%
where the time goes in v10:
time: 156 us; the launch traced here: 155 us
  starting transfers between devices  70.5 us (45%)
  waiting for transfers between devices  45.7 us (29%)
  blocking collectives  26.2 us (17%)
  Pallas kernels  10.3 us (7%)
    ppermute x16, starting transfers between devices, move(): return lax.ppermute(value, ('lat', 'lon'), pairs)  62.8 us
    ppermute x16, waiting for transfers between devices, move(): return lax.ppermute(value, ('lat', 'lon'), pairs)  35 us
    all_gather x2, blocking collectives, swap_cores(): lax.all_gather(give, 'lon', axis_index_groups=[[i, i + 1] for i in range(...  14.7 us
    all_to_all x1, blocking collectives, along_y(): return lax.all_to_all(value, ('lat', 'lon'), 0, 0, axis_index_groups=groups)  11.6 us
    all_to_all x1, waiting for transfers between devices, along_y(): return lax.all_to_all(value, ('lat', 'lon'), 0, 0, axis_index_groups=groups)  10.7 us
    all_to_all x1, starting transfers between devices, along_y(): return lax.all_to_all(value, ('lat', 'lon'), 0, 0, axis_index_groups=groups)  7.66 us
  transfers between devices with their start and end apart: 17, of which 16 were waited for; matrix products, arithmetic and copies ran while one was open for 0% of the time, Pallas kernels for 1%

profile of v10, /device:TPU:1, one launch (start us, length us, event | category | flops | bytes accessed | tf_op | source)
XLA Modules:
  0.0 155.2 jit_solution(16766026466012096003)
XLA Ops:
  0.0 1.8 %shard_map.64 = bf16[8,192,128]{2,1,0:T(8,128)(2,1)} custom-call(s32[1]{0:T(128)} %bitcast.1.mine, s32[4]{0:T(128)} %bitcast.62, s32[4]{0:T(128)} %bitcast.63, bf16[8,72,128]{2,1,0:T(8,128)(2,1)} %bitcast.57, f32[72,128]{1,0:T(8,128)} %bitcast.61, bf16[4,72,72]{2,1,0:T(8,128)(2,1)} %bitcast.60), custom_call_target="tpu_custom_call" | custom-call | bytes 1000000 | tf_op jit(solution)/shard_map/pallas_call | solution.py:45
  1.8 7.7 %all-to-all-start = ((bf16[8,192,128]{2,1,0:T(8,128)(2,1)}), bf16[8,192,128]{2,1,0:T(8,128)(2,1)S(1)}, u32[]{:S(2)}, u32[]{:S(2)}) async-start(bf16[8,192,128]{2,1,0:T(8,128)(2,1)} %shard_map.64), calls=%async_computation | async-start | bytes 786432 | tf_op jit(solution)/shard_map/all_to_all | solution.py:260
  9.5 10.7 %all-to-all-done = bf16[8,192,128]{2,1,0:T(8,128)(2,1)S(1)} async-done(((bf16[8,192,128]{2,1,0:T(8,128)(2,1)}), bf16[8,192,128]{2,1,0:T(8,128)(2,1)S(1)}, u32[]{:S(2)}, u32[]{:S(2)}) %all-to-all-start) | async-done | bytes 393248 | tf_op jit(solution)/shard_map/all_to_all | solution.py:260
  20.2 12.7 %all-gather = bf16[8,192,128]{2,1,0:T(8,128)(2,1)S(1)} all-gather(bf16[4,192,128]{2,1,0:T(8,128)(2,1)S(1)} %broadcast_select_fusion), channel_id=2, replica_groups={{0,1},{2,3},{4,5},{6,7},{8,9},{10,11},{12,13},{14,15},{16,17},{18,19},{..., dimensions={0}, use_global_device_ids=true | all-gather | bytes 589824 | tf_op jit(solution)/shard_map/all_gather | solution.py:266
  33.1 2.1 %collective-permute-start = (bf16[4,152,128]{2,1,0:T(8,128)(2,1)S(1)}, bf16[4,152,128]{2,1,0:T(8,128)(2,1)S(1)}, u32[]{:S(2)}, u32[]{:S(2)}) collective-permute-start(bf16[4,152,128]{2,1,0:T(8,128)(2,1)S(1)} %bitcast.54), channel_id=1, source_target_pairs={{0,8},{2,10},{4,12},{6,14},{512,520},{514,522},{516,524},{518,526}... | collective-permute-start | bytes 466952 | tf_op jit(solution)/shard_map/ppermute | solution.py:239
  35.2 4.6 %collective-permute-start.1 = (bf16[4,152,128]{2,1,0:T(8,128)(2,1)S(1)}, bf16[4,152,128]{2,1,0:T(8,128)(2,1)S(1)}, u32[]{:S(2)}, u32[]{:S(2)}) collective-permute-start(bf16[4,152,128]{2,1,0:T(8,128)(2,1)S(1)} %bitcast.55), channel_id=1, source_target_pairs={{0,24},{2,26},{4,28},{6,30},{512,536},{514,538},{516,540},{518,542... | collective-permute-start | bytes 466952 | tf_op jit(solution)/shard_map/ppermute | solution.py:239
  39.9 1.7 %collective-permute-done = bf16[4,152,128]{2,1,0:T(8,128)(2,1)S(1)} collective-permute-done((bf16[4,152,128]{2,1,0:T(8,128)(2,1)S(1)}, bf16[4,152,128]{2,1,0:T(8,128)(2,1)S(1)}, u32[]{:S(2)}, u32[]{:S(2)}) %collective-permute-start) | collective-permute-done | bytes 155680 | tf_op jit(solution)/shard_map/ppermute | solution.py:239
  41.6 0.9 collective-permute-done.1
  42.6 1.9 %collective-permute-start.2 = (bf16[17,72,128]{2,1,0:T(8,128)(2,1)S(1)}, bf16[17,72,128]{2,1,0:T(8,128)(2,1)S(1)}, u32[]{:S(2)}, u32[]{:S(2)}) collective-permute-start(bf16[17,72,128]{2,1,0:T(8,128)(2,1)S(1)} %pad_maximum_fusion.6), channel_id=1, source_target_pairs={{0,32},{2,34},{4,36},{6,38},{512,544},{514,546},{516,548},{518,550... | collective-permute-start | bytes 940040 | tf_op jit(solution)/shard_map/ppermute | solution.py:239
  44.5 14.0 %collective-permute-start.3 = (bf16[17,72,128]{2,1,0:T(8,128)(2,1)S(1)}, bf16[17,72,128]{2,1,0:T(8,128)(2,1)S(1)}, u32[]{:S(2)}, u32[]{:S(2)}) collective-permute-start(bf16[17,72,128]{2,1,0:T(8,128)(2,1)S(1)} %pad_maximum_fusion.6), channel_id=1, source_target_pairs={{32,0},{34,2},{36,4},{38,6},{544,512},{546,514},{548,516},{550,518... | collective-permute-start | bytes 940040 | tf_op jit(solution)/shard_map/ppermute | solution.py:239
  58.6 0.8 shard_map.65.weights
  59.4 1.8 %collective-permute-done.2.north = bf16[17,72,128]{2,1,0:T(8,128)(2,1)S(1)} collective-permute-done((bf16[17,72,128]{2,1,0:T(8,128)(2,1)S(1)}, bf16[17,72,128]{2,1,0:T(8,128)(2,1)S(1)}, u32[]{:S(2)}, u32[]{:S(2)}) %collective-permute-start.2) | collective-permute-done | bytes 313376 | tf_op jit(solution)/shard_map/ppermute | solution.py:239
  61.1 1.2 collective-permute-done.3.south
  62.3 0.7 shard_map.66.own
  63.0 1.9 %collective-permute-start.4 = (bf16[17,72,128]{2,1,0:T(8,128)(2,1)S(1)}, bf16[17,72,128]{2,1,0:T(8,128)(2,1)S(1)}, u32[]{:S(2)}, u32[]{:S(2)}) collective-permute-start(bf16[17,72,128]{2,1,0:T(8,128)(2,1)S(1)} %pad_maximum_fusion.7), channel_id=1, source_target_pairs={{0,32},{2,34},{4,36},{6,38},{512,544},{514,546},{516,548},{518,550... | collective-permute-start | bytes 940040 | tf_op jit(solution)/shard_map/ppermute | solution.py:239
  65.0 5.6 %collective-permute-start.5 = (bf16[17,72,128]{2,1,0:T(8,128)(2,1)S(1)}, bf16[17,72,128]{2,1,0:T(8,128)(2,1)S(1)}, u32[]{:S(2)}, u32[]{:S(2)}) collective-permute-start(bf16[17,72,128]{2,1,0:T(8,128)(2,1)S(1)} %pad_maximum_fusion.7), channel_id=1, source_target_pairs={{32,0},{34,2},{36,4},{38,6},{544,512},{546,514},{548,516},{550,518... | collective-permute-start | bytes 940040 | tf_op jit(solution)/shard_map/ppermute | solution.py:239
  70.7 2.6 %collective-permute-done.4.north = bf16[17,72,128]{2,1,0:T(8,128)(2,1)S(1)} collective-permute-done((bf16[17,72,128]{2,1,0:T(8,128)(2,1)S(1)}, bf16[17,72,128]{2,1,0:T(8,128)(2,1)S(1)}, u32[]{:S(2)}, u32[]{:S(2)}) %collective-permute-start.4) | collective-permute-done | bytes 313376 | tf_op jit(solution)/shard_map/ppermute | solution.py:239
  73.2 1.2 collective-permute-done.5.south
  74.4 0.6 shard_map.67.own
  75.1 5.6 %collective-permute-start.7 = (bf16[18,72,128]{2,1,0:T(8,128)(2,1)S(1)}, bf16[18,72,128]{2,1,0:T(8,128)(2,1)S(1)}, u32[]{:S(2)}, u32[]{:S(2)}) collective-permute-start(bf16[18,72,128]{2,1,0:T(8,128)(2,1)S(1)} %pad_maximum_fusion.5), channel_id=1, source_target_pairs={{32,0},{34,2},{36,4},{38,6},{544,512},{546,514},{548,516},{550,518... | collective-permute-start | bytes 995336 | tf_op jit(solution)/shard_map/ppermute | solution.py:239
  80.7 1.9 %collective-permute-start.6 = (bf16[18,72,128]{2,1,0:T(8,128)(2,1)S(1)}, bf16[18,72,128]{2,1,0:T(8,128)(2,1)S(1)}, u32[]{:S(2)}, u32[]{:S(2)}) collective-permute-start(bf16[18,72,128]{2,1,0:T(8,128)(2,1)S(1)} %pad_maximum_fusion.5), channel_id=1, source_target_pairs={{0,32},{2,34},{4,36},{6,38},{512,544},{514,546},{516,548},{518,550... | collective-permute-start | bytes 995336 | tf_op jit(solution)/shard_map/ppermute | solution.py:239
  82.6 0.3 shard_map.69.turned.table
  83.0 0.8 shard_map.71.rest_1_.rest_3_
  83.9 0.9 collective-permute-done.7.south
  84.8 5.6 %collective-permute-done.6.north = bf16[18,72,128]{2,1,0:T(8,128)(2,1)S(1)} collective-permute-done((bf16[18,72,128]{2,1,0:T(8,128)(2,1)S(1)}, bf16[18,72,128]{2,1,0:T(8,128)(2,1)S(1)}, u32[]{:S(2)}, u32[]{:S(2)}) %collective-permute-start.6) | collective-permute-done | bytes 331808 | tf_op jit(solution)/shard_map/ppermute | solution.py:239
  90.4 0.6 shard_map.68
  91.0 3.1 %collective-permute-start.8 = (bf16[5,72,128]{2,1,0:T(8,128)(2,1)S(1)}, bf16[5,72,128]{2,1,0:T(8,128)(2,1)S(1)}, u32[]{:S(2)}, u32[]{:S(2)}) collective-permute-start(bf16[5,72,128]{2,1,0:T(8,128)(2,1)S(1)} %get-tuple-element.30), channel_id=1, source_target_pairs={{0,8},{2,10},{4,12},{6,14},{512,520},{514,522},{516,524},{518,526}... | collective-permute-start | bytes 276488 | tf_op jit(solution)/shard_map/ppermute | solution.py:239
  94.1 3.7 %collective-permute-start.9 = (bf16[5,72,128]{2,1,0:T(8,128)(2,1)S(1)}, bf16[5,72,128]{2,1,0:T(8,128)(2,1)S(1)}, u32[]{:S(2)}, u32[]{:S(2)}) collective-permute-start(bf16[5,72,128]{2,1,0:T(8,128)(2,1)S(1)} %get-tuple-element.29), channel_id=1, source_target_pairs={{0,24},{2,26},{4,28},{6,30},{512,536},{514,538},{516,540},{518,542... | collective-permute-start | bytes 276488 | tf_op jit(solution)/shard_map/ppermute | solution.py:239
  97.9 0.2 slice_reduce_fusion
  98.3 1.1 collective-permute-done.9
  99.5 3.0 %shard_map.70.rest_0_ = bf16[14,72,128]{2,1,0:T(8,128)(2,1)S(1)} custom-call(s32[3,16]{1,0:T(4,128)S(1)} %convert_convert_fusion.1.par, bf16[17,72,128]{2,1,0:T(8,128)(2,1)S(1)} %pad_maximum_fusion.8.line, bf16[19,72,128]{2,1,0:T(8,128)(2,1)S(1)} %pad_maximum_fusion.3.above, bf16[19,72,128]{2,1,0:T(8,128)(2,1)S(1)} %fusion.1.beside, ...), custom_call_target="tpu_custom_call" | custom-call | flops 480000000 | bytes 4000000 | tf_op jit(solution)/shard_map/pallas_call | solution.py:211
  102.5 0.6 shard_map.72
  103.1 4.7 %collective-permute-start.10 = (bf16[12,72,128]{2,1,0:T(8,128)(2,1)S(1)}, bf16[12,72,128]{2,1,0:T(8,128)(2,1)S(1)}, u32[]{:S(2)}, u32[]{:S(2)}) collective-permute-start(bf16[12,72,128]{2,1,0:T(8,128)(2,1)S(1)} %get-tuple-element.15), channel_id=1, source_target_pairs={{32,0},{34,2},{36,4},{38,6},{544,512},{546,514},{548,516},{550,518... | collective-permute-start | bytes 663560 | tf_op jit(solution)/shard_map/ppermute | solution.py:239
  107.8 1.9 %collective-permute-start.11 = (bf16[12,72,128]{2,1,0:T(8,128)(2,1)S(1)}, bf16[12,72,128]{2,1,0:T(8,128)(2,1)S(1)}, u32[]{:S(2)}, u32[]{:S(2)}) collective-permute-start(bf16[12,72,128]{2,1,0:T(8,128)(2,1)S(1)} %get-tuple-element.16), channel_id=1, source_target_pairs={{0,32},{2,34},{4,36},{6,38},{512,544},{514,546},{516,548},{518,550... | collective-permute-start | bytes 663560 | tf_op jit(solution)/shard_map/ppermute | solution.py:239
  109.8 0.9 collective-permute-done.10.rest_1_
  110.7 5.6 %collective-permute-done.11.rest_2_ = bf16[12,72,128]{2,1,0:T(8,128)(2,1)S(1)} collective-permute-done((bf16[12,72,128]{2,1,0:T(8,128)(2,1)S(1)}, bf16[12,72,128]{2,1,0:T(8,128)(2,1)S(1)}, u32[]{:S(2)}, u32[]{:S(2)}) %collective-permute-start.11) | collective-permute-done | bytes 221216 | tf_op jit(solution)/shard_map/ppermute | solution.py:239
  116.3 0.6 shard_map.73
  116.9 3.1 %collective-permute-start.12 = (bf16[10,72,128]{2,1,0:T(8,128)(2,1)S(1)}, bf16[10,72,128]{2,1,0:T(8,128)(2,1)S(1)}, u32[]{:S(2)}, u32[]{:S(2)}) collective-permute-start(bf16[10,72,128]{2,1,0:T(8,128)(2,1)S(1)} %get-tuple-element.18), channel_id=1, source_target_pairs={{32,0},{34,2},{36,4},{38,6},{544,512},{546,514},{548,516},{550,518... | collective-permute-start | bytes 552968 | tf_op jit(solution)/shard_map/ppermute | solution.py:239
  120.0 2.2 %collective-permute-start.13 = (bf16[10,72,128]{2,1,0:T(8,128)(2,1)S(1)}, bf16[10,72,128]{2,1,0:T(8,128)(2,1)S(1)}, u32[]{:S(2)}, u32[]{:S(2)}) collective-permute-start(bf16[10,72,128]{2,1,0:T(8,128)(2,1)S(1)} %get-tuple-element.19), channel_id=1, source_target_pairs={{0,32},{2,34},{4,36},{6,38},{512,544},{514,546},{516,548},{518,550... | collective-permute-start | bytes 552968 | tf_op jit(solution)/shard_map/ppermute | solution.py:239
  122.2 1.0 collective-permute-done.12.rest_1_
  123.2 4.9 %collective-permute-done.13.rest_2_ = bf16[10,72,128]{2,1,0:T(8,128)(2,1)S(1)} collective-permute-done((bf16[10,72,128]{2,1,0:T(8,128)(2,1)S(1)}, bf16[10,72,128]{2,1,0:T(8,128)(2,1)S(1)}, u32[]{:S(2)}, u32[]{:S(2)}) %collective-permute-start.13) | collective-permute-done | bytes 184352 | tf_op jit(solution)/shard_map/ppermute | solution.py:239
  128.1 0.5 shard_map.74
  128.6 4.6 %collective-permute-start.14 = (bf16[8,72,128]{2,1,0:T(8,128)(2,1)S(1)}, bf16[8,72,128]{2,1,0:T(8,128)(2,1)S(1)}, u32[]{:S(2)}, u32[]{:S(2)}) collective-permute-start(bf16[8,72,128]{2,1,0:T(8,128)(2,1)S(1)} %get-tuple-element.21), channel_id=1, source_target_pairs={{32,0},{34,2},{36,4},{38,6},{544,512},{546,514},{548,516},{550,518... | collective-permute-start | bytes 442376 | tf_op jit(solution)/shard_map/ppermute | solution.py:239
  133.2 1.9 %collective-permute-start.15 = (bf16[8,72,128]{2,1,0:T(8,128)(2,1)S(1)}, bf16[8,72,128]{2,1,0:T(8,128)(2,1)S(1)}, u32[]{:S(2)}, u32[]{:S(2)}) collective-permute-start(bf16[8,72,128]{2,1,0:T(8,128)(2,1)S(1)} %get-tuple-element.22), channel_id=1, source_target_pairs={{0,32},{2,34},{4,36},{6,38},{512,544},{514,546},{516,548},{518,550... | collective-permute-start | bytes 442376 | tf_op jit(solution)/shard_map/ppermute | solution.py:239
  135.3 5.6 %collective-permute-done.15 = bf16[8,72,128]{2,1,0:T(8,128)(2,1)S(1)} collective-permute-done((bf16[8,72,128]{2,1,0:T(8,128)(2,1)S(1)}, bf16[8,72,128]{2,1,0:T(8,128)(2,1)S(1)}, u32[]{:S(2)}, u32[]{:S(2)}) %collective-permute-start.15) | collective-permute-done | bytes 147488 | tf_op jit(solution)/shard_map/ppermute | solution.py:239
  141.0 1.9 %all-gather.1 = bf16[8,1,72,128]{3,2,1,0:T(8,128)(2,1)S(1)} all-gather(bf16[4,1,72,128]{3,2,1,0:T(8,128)(2,1)S(1)} %bitcast_select_fusion), channel_id=3, replica_groups={{0,1},{2,3},{4,5},{6,7},{8,9},{10,11},{12,13},{14,15},{16,17},{18,19},{..., dimensions={0}, use_global_device_ids=true | all-gather | bytes 221184 | tf_op jit(solution)/shard_map/all_gather | solution.py:266
  142.9 11.6 %all_to_all.10 = bf16[8,72,128]{2,1,0:T(8,128)(2,1)S(1)} all-to-all(bf16[8,72,128]{2,1,0:T(8,128)(2,1)S(1)} %pad_maximum_fusion.11), channel_id=1, replica_groups={{0,2,4,6,512,514,516,518},{1,3,5,7,513,515,517,519},{8,10,12,14,520,522..., dimensions={0} | all-to-all | bytes 294912 | tf_op jit(solution)/shard_map/all_to_all | solution.py:260
  154.5 0.7 copy.24
  (66 shorter events, 1.1 us)
Async XLA Ops:
  1.8 18.4 %all-to-all-start = ((bf16[8,192,128]{2,1,0:T(8,128)(2,1)}), bf16[8,192,128]{2,1,0:T(8,128)(2,1)S(1)}, u32[]{:S(2)}, u32[]{:S(2)}) async-start(bf16[8,192,128]{2,1,0:T(8,128)(2,1)} %shard_map.64), calls=%async_computation | async-start | bytes 786432 | tf_op jit(solution)/shard_map/all_to_all | solution.py:260
  33.0 25.5 %copy-start = (bf16[16,160,128]{2,1,0:T(8,128)(2,1)S(1)}, bf16[16,160,128]{2,1,0:T(8,128)(2,1)}, u32[]{:S(2)}) copy-start(bf16[16,160,128]{2,1,0:T(8,128)(2,1)} %table.5) | copy-start | bytes 1966084
  33.1 8.5 %collective-permute-start = (bf16[4,152,128]{2,1,0:T(8,128)(2,1)S(1)}, bf16[4,152,128]{2,1,0:T(8,128)(2,1)S(1)}, u32[]{:S(2)}, u32[]{:S(2)}) collective-permute-start(bf16[4,152,128]{2,1,0:T(8,128)(2,1)S(1)} %bitcast.54), channel_id=1, source_target_pairs={{0,8},{2,10},{4,12},{6,14},{512,520},{514,522},{516,524},{518,526}... | collective-permute-start | bytes 466952 | tf_op jit(solution)/shard_map/ppermute | solution.py:239
  35.2 7.3 %collective-permute-start.1 = (bf16[4,152,128]{2,1,0:T(8,128)(2,1)S(1)}, bf16[4,152,128]{2,1,0:T(8,128)(2,1)S(1)}, u32[]{:S(2)}, u32[]{:S(2)}) collective-permute-start(bf16[4,152,128]{2,1,0:T(8,128)(2,1)S(1)} %bitcast.55), channel_id=1, source_target_pairs={{0,24},{2,26},{4,28},{6,30},{512,536},{514,538},{516,540},{518,542... | collective-permute-start | bytes 466952 | tf_op jit(solution)/shard_map/ppermute | solution.py:239
  42.6 18.6 %collective-permute-start.2 = (bf16[17,72,128]{2,1,0:T(8,128)(2,1)S(1)}, bf16[17,72,128]{2,1,0:T(8,128)(2,1)S(1)}, u32[]{:S(2)}, u32[]{:S(2)}) collective-permute-start(bf16[17,72,128]{2,1,0:T(8,128)(2,1)S(1)} %pad_maximum_fusion.6), channel_id=1, source_target_pairs={{0,32},{2,34},{4,36},{6,38},{512,544},{514,546},{516,548},{518,550... | collective-permute-start | bytes 940040 | tf_op jit(solution)/shard_map/ppermute | solution.py:239
  44.5 17.8 %collective-permute-start.3 = (bf16[17,72,128]{2,1,0:T(8,128)(2,1)S(1)}, bf16[17,72,128]{2,1,0:T(8,128)(2,1)S(1)}, u32[]{:S(2)}, u32[]{:S(2)}) collective-permute-start(bf16[17,72,128]{2,1,0:T(8,128)(2,1)S(1)} %pad_maximum_fusion.6), channel_id=1, source_target_pairs={{32,0},{34,2},{36,4},{38,6},{544,512},{546,514},{548,516},{550,518... | collective-permute-start | bytes 940040 | tf_op jit(solution)/shard_map/ppermute | solution.py:239
  61.1 22.7 %copy-start.3 = (bf16[17,72,128]{2,1,0:T(8,128)(2,1)}, bf16[17,72,128]{2,1,0:T(8,128)(2,1)S(1)}, u32[]{:S(2)}) copy-start(bf16[17,72,128]{2,1,0:T(8,128)(2,1)S(1)} %collective-permute-done.2.north) | copy-start | bytes 940036
  62.3 21.5 %copy-start.4 = (bf16[17,72,128]{2,1,0:T(8,128)(2,1)}, bf16[17,72,128]{2,1,0:T(8,128)(2,1)S(1)}, u32[]{:S(2)}) copy-start(bf16[17,72,128]{2,1,0:T(8,128)(2,1)S(1)} %collective-permute-done.3.south) | copy-start | bytes 940036
  63.0 10.2 %collective-permute-start.4 = (bf16[17,72,128]{2,1,0:T(8,128)(2,1)S(1)}, bf16[17,72,128]{2,1,0:T(8,128)(2,1)S(1)}, u32[]{:S(2)}, u32[]{:S(2)}) collective-permute-start(bf16[17,72,128]{2,1,0:T(8,128)(2,1)S(1)} %pad_maximum_fusion.7), channel_id=1, source_target_pairs={{0,32},{2,34},{4,36},{6,38},{512,544},{514,546},{516,548},{518,550... | collective-permute-start | bytes 940040 | tf_op jit(solution)/shard_map/ppermute | solution.py:239
  65.0 9.5 %collective-permute-start.5 = (bf16[17,72,128]{2,1,0:T(8,128)(2,1)S(1)}, bf16[17,72,128]{2,1,0:T(8,128)(2,1)S(1)}, u32[]{:S(2)}, u32[]{:S(2)}) collective-permute-start(bf16[17,72,128]{2,1,0:T(8,128)(2,1)S(1)} %pad_maximum_fusion.7), channel_id=1, source_target_pairs={{32,0},{34,2},{36,4},{38,6},{544,512},{546,514},{548,516},{550,518... | collective-permute-start | bytes 940040 | tf_op jit(solution)/shard_map/ppermute | solution.py:239
  73.2 10.6 %copy-start.1 = (bf16[17,72,128]{2,1,0:T(8,128)(2,1)}, bf16[17,72,128]{2,1,0:T(8,128)(2,1)S(1)}, u32[]{:S(2)}) copy-start(bf16[17,72,128]{2,1,0:T(8,128)(2,1)S(1)} %collective-permute-done.4.north) | copy-start | bytes 940036
  74.4 9.4 %copy-start.2 = (bf16[17,72,128]{2,1,0:T(8,128)(2,1)}, bf16[17,72,128]{2,1,0:T(8,128)(2,1)S(1)}, u32[]{:S(2)}) copy-start(bf16[17,72,128]{2,1,0:T(8,128)(2,1)S(1)} %collective-permute-done.5.south) | copy-start | bytes 940036
  75.1 9.6 %collective-permute-start.7 = (bf16[18,72,128]{2,1,0:T(8,128)(2,1)S(1)}, bf16[18,72,128]{2,1,0:T(8,128)(2,1)S(1)}, u32[]{:S(2)}, u32[]{:S(2)}) collective-permute-start(bf16[18,72,128]{2,1,0:T(8,128)(2,1)S(1)} %pad_maximum_fusion.5), channel_id=1, source_target_pairs={{32,0},{34,2},{36,4},{38,6},{544,512},{546,514},{548,516},{550,518... | collective-permute-start | bytes 995336 | tf_op jit(solution)/shard_map/ppermute | solution.py:239
  80.7 9.6 %collective-permute-start.6 = (bf16[18,72,128]{2,1,0:T(8,128)(2,1)S(1)}, bf16[18,72,128]{2,1,0:T(8,128)(2,1)S(1)}, u32[]{:S(2)}, u32[]{:S(2)}) collective-permute-start(bf16[18,72,128]{2,1,0:T(8,128)(2,1)S(1)} %pad_maximum_fusion.5), channel_id=1, source_target_pairs={{0,32},{2,34},{4,36},{6,38},{512,544},{514,546},{516,548},{518,550... | collective-permute-start | bytes 995336 | tf_op jit(solution)/shard_map/ppermute | solution.py:239
  83.8 14.3 %slice-start.3 = ((bf16[17,72,128]{2,1,0:T(8,128)(2,1)}), bf16[4,72,128]{2,1,0:T(8,128)(2,1)S(1)}, s32[]{:S(2)}) async-start(bf16[17,72,128]{2,1,0:T(8,128)(2,1)} %copy-done.4), calls=%async_computation.5 | async-start | bytes 147456 | tf_op jit(solution)/shard_map/slice | solution.py:309
  83.9 14.3 %slice-start.2 = ((bf16[17,72,128]{2,1,0:T(8,128)(2,1)}), bf16[4,72,128]{2,1,0:T(8,128)(2,1)S(1)}, s32[]{:S(2)}) async-start(bf16[17,72,128]{2,1,0:T(8,128)(2,1)} %copy-done.3), calls=%async_computation.4 | async-start | bytes 147456 | tf_op jit(solution)/shard_map/slice | solution.py:308
  83.9 14.2 %slice-start.1 = ((bf16[17,72,128]{2,1,0:T(8,128)(2,1)}), bf16[6,72,128]{2,1,0:T(8,128)(2,1)S(1)}, s32[]{:S(2)}) async-start(bf16[17,72,128]{2,1,0:T(8,128)(2,1)} %copy-done.2), calls=%async_computation.3 | async-start | bytes 221184 | tf_op jit(solution)/shard_map/slice | solution.py:309
  83.9 14.3 %slice-start = ((bf16[17,72,128]{2,1,0:T(8,128)(2,1)}), bf16[6,72,128]{2,1,0:T(8,128)(2,1)S(1)}, s32[]{:S(2)}) async-start(bf16[17,72,128]{2,1,0:T(8,128)(2,1)} %copy-done.1), calls=%async_computation.2 | async-start | bytes 221184 | tf_op jit(solution)/shard_map/slice | solution.py:308
  91.0 7.3 %collective-permute-start.8 = (bf16[5,72,128]{2,1,0:T(8,128)(2,1)S(1)}, bf16[5,72,128]{2,1,0:T(8,128)(2,1)S(1)}, u32[]{:S(2)}, u32[]{:S(2)}) collective-permute-start(bf16[5,72,128]{2,1,0:T(8,128)(2,1)S(1)} %get-tuple-element.30), channel_id=1, source_target_pairs={{0,8},{2,10},{4,12},{6,14},{512,520},{514,522},{516,524},{518,526}... | collective-permute-start | bytes 276488 | tf_op jit(solution)/shard_map/ppermute | solution.py:239
  94.1 5.3 %collective-permute-start.9 = (bf16[5,72,128]{2,1,0:T(8,128)(2,1)S(1)}, bf16[5,72,128]{2,1,0:T(8,128)(2,1)S(1)}, u32[]{:S(2)}, u32[]{:S(2)}) collective-permute-start(bf16[5,72,128]{2,1,0:T(8,128)(2,1)S(1)} %get-tuple-element.29), channel_id=1, source_target_pairs={{0,24},{2,26},{4,28},{6,30},{512,536},{514,538},{516,540},{518,542... | collective-permute-start | bytes 276488 | tf_op jit(solution)/shard_map/ppermute | solution.py:239
  103.1 7.6 %collective-permute-start.10 = (bf16[12,72,128]{2,1,0:T(8,128)(2,1)S(1)}, bf16[12,72,128]{2,1,0:T(8,128)(2,1)S(1)}, u32[]{:S(2)}, u32[]{:S(2)}) collective-permute-start(bf16[12,72,128]{2,1,0:T(8,128)(2,1)S(1)} %get-tuple-element.15), channel_id=1, source_target_pairs={{32,0},{34,2},{36,4},{38,6},{544,512},{546,514},{548,516},{550,518... | collective-permute-start | bytes 663560 | tf_op jit(solution)/shard_map/ppermute | solution.py:239
  107.8 8.5 %collective-permute-start.11 = (bf16[12,72,128]{2,1,0:T(8,128)(2,1)S(1)}, bf16[12,72,128]{2,1,0:T(8,128)(2,1)S(1)}, u32[]{:S(2)}, u32[]{:S(2)}) collective-permute-start(bf16[12,72,128]{2,1,0:T(8,128)(2,1)S(1)} %get-tuple-element.16), channel_id=1, source_target_pairs={{0,32},{2,34},{4,36},{6,38},{512,544},{514,546},{516,548},{518,550... | collective-permute-start | bytes 663560 | tf_op jit(solution)/shard_map/ppermute | solution.py:239
  116.9 6.3 %collective-permute-start.12 = (bf16[10,72,128]{2,1,0:T(8,128)(2,1)S(1)}, bf16[10,72,128]{2,1,0:T(8,128)(2,1)S(1)}, u32[]{:S(2)}, u32[]{:S(2)}) collective-permute-start(bf16[10,72,128]{2,1,0:T(8,128)(2,1)S(1)} %get-tuple-element.18), channel_id=1, source_target_pairs={{32,0},{34,2},{36,4},{38,6},{544,512},{546,514},{548,516},{550,518... | collective-permute-start | bytes 552968 | tf_op jit(solution)/shard_map/ppermute | solution.py:239
  120.0 8.1 %collective-permute-start.13 = (bf16[10,72,128]{2,1,0:T(8,128)(2,1)S(1)}, bf16[10,72,128]{2,1,0:T(8,128)(2,1)S(1)}, u32[]{:S(2)}, u32[]{:S(2)}) collective-permute-start(bf16[10,72,128]{2,1,0:T(8,128)(2,1)S(1)} %get-tuple-element.19), channel_id=1, source_target_pairs={{0,32},{2,34},{4,36},{6,38},{512,544},{514,546},{516,548},{518,550... | collective-permute-start | bytes 552968 | tf_op jit(solution)/shard_map/ppermute | solution.py:239
  128.6 6.7 %collective-permute-start.14 = (bf16[8,72,128]{2,1,0:T(8,128)(2,1)S(1)}, bf16[8,72,128]{2,1,0:T(8,128)(2,1)S(1)}, u32[]{:S(2)}, u32[]{:S(2)}) collective-permute-start(bf16[8,72,128]{2,1,0:T(8,128)(2,1)S(1)} %get-tuple-element.21), channel_id=1, source_target_pairs={{32,0},{34,2},{36,4},{38,6},{544,512},{546,514},{548,516},{550,518... | collective-permute-start | bytes 442376 | tf_op jit(solution)/shard_map/ppermute | solution.py:239
  133.2 7.7 %collective-permute-start.15 = (bf16[8,72,128]{2,1,0:T(8,128)(2,1)S(1)}, bf16[8,72,128]{2,1,0:T(8,128)(2,1)S(1)}, u32[]{:S(2)}, u32[]{:S(2)}) collective-permute-start(bf16[8,72,128]{2,1,0:T(8,128)(2,1)S(1)} %get-tuple-element.22), channel_id=1, source_target_pairs={{0,32},{2,34},{4,36},{6,38},{512,544},{514,546},{516,548},{518,550... | collective-permute-start | bytes 442376 | tf_op jit(solution)/shard_map/ppermute | solution.py:239

commit v11 on v10

--- a/solution.py
+++ b/solution.py
@@ -290,8 +290,6 @@
     par = jnp.max(marks.astype(F32), axis=2).astype(jnp.int32)
     last = steps - 1
     weights = choose(par, interp_table, last, lambda step: 2 + step)
-    table = turn(interp_table)
-    turned = choose(par, table, last, lambda step: reach - 1 - step)
 
     span = line.shape[0]
     room = -(-span * count // levels) * levels - span * count
@@ -310,7 +308,10 @@
         outs = run + 2 * (last - 1 - step)
         state = forward(step, outs, step < last - 1, marks, (state, north, south), weights, mix)
 
+    state, par, raw = lax.optimization_barrier((state, par, interp_table))
     west, east = from_lon(state[-reach - 1 :], -run), from_lon(state[: reach + 1], run)
+    table = turn(raw)
+    turned = choose(par, table, last, lambda step: reach - 1 - step)
     outer = jnp.where(right_lanes((levels, cols)), east[-1], west[0])
     line = jnp.concatenate([west[1:], state, east[:-1], outer[None]])
     rows = (jnp.concatenate(above), beside, jnp.concatenate(below))

time: 156 us -> 158 us (1.013)
  waiting for transfers between devices: 45.7 us -> 55 us
  starting transfers between devices: 70.5 us -> 62.8 us
    ppermute x16, waiting for transfers between devices: 35 us -> 44.3 us  [move(): return lax.ppermute(value, ('lat', 'lon'), pairs)]
    ppermute x16, starting transfers between devices: 62.8 us -> 55.2 us  [move(): return lax.ppermute(value, ('lat', 'lon'), pairs)]
  transfers between devices with their start and end apart: 17 -> 17, of which waited for: 16 -> 15; matrix products, arithmetic and copies ran while one was open for 0% -> 0% of each run, Pallas kernels for 1% -> 1%
where the time goes in v11:
time: 158 us; the launch traced here: 157 us
  starting transfers between devices  62.8 us (40%)
  waiting for transfers between devices  55 us (35%)
  blocking collectives  26.2 us (17%)
  Pallas kernels  10.4 us (7%)
    ppermute x16, starting transfers between devices, move(): return lax.ppermute(value, ('lat', 'lon'), pairs)  55.2 us
    ppermute x16, waiting for transfers between devices, move(): return lax.ppermute(value, ('lat', 'lon'), pairs)  44.3 us
    all_gather x2, blocking collectives, swap_cores(): lax.all_gather(give, 'lon', axis_index_groups=[[i, i + 1] for i in range(...  14.7 us
    all_to_all x1, blocking collectives, along_y(): return lax.all_to_all(value, ('lat', 'lon'), 0, 0, axis_index_groups=groups)  11.6 us
    all_to_all x1, waiting for transfers between devices, along_y(): return lax.all_to_all(value, ('lat', 'lon'), 0, 0, axis_index_groups=groups)  10.7 us
    all_to_all x1, starting transfers between devices, along_y(): return lax.all_to_all(value, ('lat', 'lon'), 0, 0, axis_index_groups=groups)  7.66 us
  transfers between devices with their start and end apart: 17, of which 15 were waited for; matrix products, arithmetic and copies ran while one was open for 0% of the time, Pallas kernels for 1%

profile of v11, /device:TPU:1, one launch (start us, length us, event | category | flops | bytes accessed | tf_op | source)
XLA Modules:
  0.0 156.8 jit_solution(8149476897343337763)
XLA Ops:
  0.0 1.8 %shard_map.64 = bf16[8,192,128]{2,1,0:T(8,128)(2,1)} custom-call(s32[1]{0:T(128)} %bitcast.1.mine, s32[4]{0:T(128)} %bitcast.62, s32[4]{0:T(128)} %bitcast.63, bf16[8,72,128]{2,1,0:T(8,128)(2,1)} %bitcast.57, f32[72,128]{1,0:T(8,128)} %bitcast.61, bf16[4,72,72]{2,1,0:T(8,128)(2,1)} %bitcast.60), custom_call_target="tpu_custom_call" | custom-call | bytes 1000000 | tf_op jit(solution)/shard_map/pallas_call | solution.py:45
  1.8 7.7 %all-to-all-start = ((bf16[8,192,128]{2,1,0:T(8,128)(2,1)}), bf16[8,192,128]{2,1,0:T(8,128)(2,1)S(1)}, u32[]{:S(2)}, u32[]{:S(2)}) async-start(bf16[8,192,128]{2,1,0:T(8,128)(2,1)} %shard_map.64), calls=%async_computation | async-start | bytes 786432 | tf_op jit(solution)/shard_map/all_to_all | solution.py:260
  9.5 10.7 %all-to-all-done = bf16[8,192,128]{2,1,0:T(8,128)(2,1)S(1)} async-done(((bf16[8,192,128]{2,1,0:T(8,128)(2,1)}), bf16[8,192,128]{2,1,0:T(8,128)(2,1)S(1)}, u32[]{:S(2)}, u32[]{:S(2)}) %all-to-all-start) | async-done | bytes 393248 | tf_op jit(solution)/shard_map/all_to_all | solution.py:260
  20.2 12.7 %all-gather = bf16[8,192,128]{2,1,0:T(8,128)(2,1)S(1)} all-gather(bf16[4,192,128]{2,1,0:T(8,128)(2,1)S(1)} %broadcast_select_fusion), channel_id=2, replica_groups={{0,1},{2,3},{4,5},{6,7},{8,9},{10,11},{12,13},{14,15},{16,17},{18,19},{..., dimensions={0}, use_global_device_ids=true | all-gather | bytes 589824 | tf_op jit(solution)/shard_map/all_gather | solution.py:266
  33.2 2.1 %collective-permute-start.1 = (bf16[4,152,128]{2,1,0:T(8,128)(2,1)S(1)}, bf16[4,152,128]{2,1,0:T(8,128)(2,1)S(1)}, u32[]{:S(2)}, u32[]{:S(2)}) collective-permute-start(bf16[4,152,128]{2,1,0:T(8,128)(2,1)S(1)} %bitcast.54), channel_id=1, source_target_pairs={{0,24},{2,26},{4,28},{6,30},{512,536},{514,538},{516,540},{518,542... | collective-permute-start | bytes 466952 | tf_op jit(solution)/shard_map/ppermute | solution.py:239
  35.2 3.4 %collective-permute-start = (bf16[4,152,128]{2,1,0:T(8,128)(2,1)S(1)}, bf16[4,152,128]{2,1,0:T(8,128)(2,1)S(1)}, u32[]{:S(2)}, u32[]{:S(2)}) collective-permute-start(bf16[4,152,128]{2,1,0:T(8,128)(2,1)S(1)} %bitcast.55), channel_id=1, source_target_pairs={{0,8},{2,10},{4,12},{6,14},{512,520},{514,522},{516,524},{518,526}... | collective-permute-start | bytes 466952 | tf_op jit(solution)/shard_map/ppermute | solution.py:239
  38.7 4.8 %collective-permute-done = bf16[4,152,128]{2,1,0:T(8,128)(2,1)S(1)} collective-permute-done((bf16[4,152,128]{2,1,0:T(8,128)(2,1)S(1)}, bf16[4,152,128]{2,1,0:T(8,128)(2,1)S(1)}, u32[]{:S(2)}, u32[]{:S(2)}) %collective-permute-start) | collective-permute-done | bytes 155680 | tf_op jit(solution)/shard_map/ppermute | solution.py:239
  43.7 15.4 %collective-permute-start.3 = (bf16[17,72,128]{2,1,0:T(8,128)(2,1)S(1)}, bf16[17,72,128]{2,1,0:T(8,128)(2,1)S(1)}, u32[]{:S(2)}, u32[]{:S(2)}) collective-permute-start(bf16[17,72,128]{2,1,0:T(8,128)(2,1)S(1)} %pad_maximum_fusion.6), channel_id=1, source_target_pairs={{32,0},{34,2},{36,4},{38,6},{544,512},{546,514},{548,516},{550,518... | collective-permute-start | bytes 940040 | tf_op jit(solution)/shard_map/ppermute | solution.py:239
  59.0 1.9 %collective-permute-start.2 = (bf16[17,72,128]{2,1,0:T(8,128)(2,1)S(1)}, bf16[17,72,128]{2,1,0:T(8,128)(2,1)S(1)}, u32[]{:S(2)}, u32[]{:S(2)}) collective-permute-start(bf16[17,72,128]{2,1,0:T(8,128)(2,1)S(1)} %pad_maximum_fusion.6), channel_id=1, source_target_pairs={{0,32},{2,34},{4,36},{6,38},{512,544},{514,546},{516,548},{518,550... | collective-permute-start | bytes 940040 | tf_op jit(solution)/shard_map/ppermute | solution.py:239
  61.1 0.8 shard_map.65.weights
  61.9 1.0 collective-permute-done.3.south
  62.9 5.6 %collective-permute-done.2.north = bf16[17,72,128]{2,1,0:T(8,128)(2,1)S(1)} collective-permute-done((bf16[17,72,128]{2,1,0:T(8,128)(2,1)S(1)}, bf16[17,72,128]{2,1,0:T(8,128)(2,1)S(1)}, u32[]{:S(2)}, u32[]{:S(2)}) %collective-permute-start.2) | collective-permute-done | bytes 313376 | tf_op jit(solution)/shard_map/ppermute | solution.py:239
  68.5 0.7 shard_map.66.own
  69.2 2.9 %collective-permute-start.5 = (bf16[17,72,128]{2,1,0:T(8,128)(2,1)S(1)}, bf16[17,72,128]{2,1,0:T(8,128)(2,1)S(1)}, u32[]{:S(2)}, u32[]{:S(2)}) collective-permute-start(bf16[17,72,128]{2,1,0:T(8,128)(2,1)S(1)} %pad_maximum_fusion.7), channel_id=1, source_target_pairs={{32,0},{34,2},{36,4},{38,6},{544,512},{546,514},{548,516},{550,518... | collective-permute-start | bytes 940040 | tf_op jit(solution)/shard_map/ppermute | solution.py:239
  72.2 2.3 %collective-permute-start.4 = (bf16[17,72,128]{2,1,0:T(8,128)(2,1)S(1)}, bf16[17,72,128]{2,1,0:T(8,128)(2,1)S(1)}, u32[]{:S(2)}, u32[]{:S(2)}) collective-permute-start(bf16[17,72,128]{2,1,0:T(8,128)(2,1)S(1)} %pad_maximum_fusion.7), channel_id=1, source_target_pairs={{0,32},{2,34},{4,36},{6,38},{512,544},{514,546},{516,548},{518,550... | collective-permute-start | bytes 940040 | tf_op jit(solution)/shard_map/ppermute | solution.py:239
  74.6 5.0 %collective-permute-done.5.south = bf16[17,72,128]{2,1,0:T(8,128)(2,1)S(1)} collective-permute-done((bf16[17,72,128]{2,1,0:T(8,128)(2,1)S(1)}, bf16[17,72,128]{2,1,0:T(8,128)(2,1)S(1)}, u32[]{:S(2)}, u32[]{:S(2)}) %collective-permute-start.5) | collective-permute-done | bytes 313376 | tf_op jit(solution)/shard_map/ppermute | solution.py:239
  79.6 2.0 %collective-permute-done.4.north = bf16[17,72,128]{2,1,0:T(8,128)(2,1)S(1)} collective-permute-done((bf16[17,72,128]{2,1,0:T(8,128)(2,1)S(1)}, bf16[17,72,128]{2,1,0:T(8,128)(2,1)S(1)}, u32[]{:S(2)}, u32[]{:S(2)}) %collective-permute-start.4) | collective-permute-done | bytes 313376 | tf_op jit(solution)/shard_map/ppermute | solution.py:239
  81.6 0.6 shard_map.67.own
  82.3 1.9 %collective-permute-start.7 = (bf16[18,72,128]{2,1,0:T(8,128)(2,1)S(1)}, bf16[18,72,128]{2,1,0:T(8,128)(2,1)S(1)}, u32[]{:S(2)}, u32[]{:S(2)}) collective-permute-start(bf16[18,72,128]{2,1,0:T(8,128)(2,1)S(1)} %pad_maximum_fusion.5), channel_id=1, source_target_pairs={{32,0},{34,2},{36,4},{38,6},{544,512},{546,514},{548,516},{550,518... | collective-permute-start | bytes 995336 | tf_op jit(solution)/shard_map/ppermute | solution.py:239
  84.2 3.4 %collective-permute-start.6 = (bf16[18,72,128]{2,1,0:T(8,128)(2,1)S(1)}, bf16[18,72,128]{2,1,0:T(8,128)(2,1)S(1)}, u32[]{:S(2)}, u32[]{:S(2)}) collective-permute-start(bf16[18,72,128]{2,1,0:T(8,128)(2,1)S(1)} %pad_maximum_fusion.5), channel_id=1, source_target_pairs={{0,32},{2,34},{4,36},{6,38},{512,544},{514,546},{516,548},{518,550... | collective-permute-start | bytes 995336 | tf_op jit(solution)/shard_map/ppermute | solution.py:239
  87.6 2.5 %collective-permute-done.7.south = bf16[18,72,128]{2,1,0:T(8,128)(2,1)S(1)} collective-permute-done((bf16[18,72,128]{2,1,0:T(8,128)(2,1)S(1)}, bf16[18,72,128]{2,1,0:T(8,128)(2,1)S(1)}, u32[]{:S(2)}, u32[]{:S(2)}) %collective-permute-start.7) | collective-permute-done | bytes 331808 | tf_op jit(solution)/shard_map/ppermute | solution.py:239
  90.2 3.7 %collective-permute-done.6.north = bf16[18,72,128]{2,1,0:T(8,128)(2,1)S(1)} collective-permute-done((bf16[18,72,128]{2,1,0:T(8,128)(2,1)S(1)}, bf16[18,72,128]{2,1,0:T(8,128)(2,1)S(1)}, u32[]{:S(2)}, u32[]{:S(2)}) %collective-permute-start.6) | collective-permute-done | bytes 331808 | tf_op jit(solution)/shard_map/ppermute | solution.py:239
  93.9 0.6 shard_map.68
  94.5 0.2 slice_reduce_fusion
  94.8 2.1 %collective-permute-start.9 = (bf16[5,72,128]{2,1,0:T(8,128)(2,1)S(1)}, bf16[5,72,128]{2,1,0:T(8,128)(2,1)S(1)}, u32[]{:S(2)}, u32[]{:S(2)}) collective-permute-start(bf16[5,72,128]{2,1,0:T(8,128)(2,1)S(1)} %get-tuple-element.35), channel_id=1, source_target_pairs={{0,24},{2,26},{4,28},{6,30},{512,536},{514,538},{516,540},{518,542... | collective-permute-start | bytes 276488 | tf_op jit(solution)/shard_map/ppermute | solution.py:239
  96.8 3.4 %collective-permute-start.8 = (bf16[5,72,128]{2,1,0:T(8,128)(2,1)S(1)}, bf16[5,72,128]{2,1,0:T(8,128)(2,1)S(1)}, u32[]{:S(2)}, u32[]{:S(2)}) collective-permute-start(bf16[5,72,128]{2,1,0:T(8,128)(2,1)S(1)} %get-tuple-element.36), channel_id=1, source_target_pairs={{0,8},{2,10},{4,12},{6,14},{512,520},{514,522},{516,524},{518,526}... | collective-permute-start | bytes 276488 | tf_op jit(solution)/shard_map/ppermute | solution.py:239
  100.2 0.3 shard_map.69.turned.table
  100.6 0.8 shard_map.71.rest_1_.rest_3_
  101.6 1.8 %collective-permute-done.8 = bf16[5,72,128]{2,1,0:T(8,128)(2,1)S(1)} collective-permute-done((bf16[5,72,128]{2,1,0:T(8,128)(2,1)S(1)}, bf16[5,72,128]{2,1,0:T(8,128)(2,1)S(1)}, u32[]{:S(2)}, u32[]{:S(2)}) %collective-permute-start.8) | collective-permute-done | bytes 92192 | tf_op jit(solution)/shard_map/ppermute | solution.py:239
  103.4 3.0 %shard_map.70.rest_0_ = bf16[14,72,128]{2,1,0:T(8,128)(2,1)S(1)} custom-call(s32[3,16]{1,0:T(4,128)S(1)} %convert_convert_fusion.1.par, bf16[17,72,128]{2,1,0:T(8,128)(2,1)S(1)} %pad_maximum_fusion.8.line, bf16[19,72,128]{2,1,0:T(8,128)(2,1)S(1)} %pad_maximum_fusion.3.above, bf16[19,72,128]{2,1,0:T(8,128)(2,1)S(1)} %fusion.1.beside, ...), custom_call_target="tpu_custom_call" | custom-call | flops 480000000 | bytes 4000000 | tf_op jit(solution)/shard_map/pallas_call | solution.py:211
  106.5 0.6 shard_map.72
  107.1 4.0 %collective-permute-start.10 = (bf16[12,72,128]{2,1,0:T(8,128)(2,1)S(1)}, bf16[12,72,128]{2,1,0:T(8,128)(2,1)S(1)}, u32[]{:S(2)}, u32[]{:S(2)}) collective-permute-start(bf16[12,72,128]{2,1,0:T(8,128)(2,1)S(1)} %get-tuple-element.21), channel_id=1, source_target_pairs={{32,0},{34,2},{36,4},{38,6},{544,512},{546,514},{548,516},{550,518... | collective-permute-start | bytes 663560 | tf_op jit(solution)/shard_map/ppermute | solution.py:239
  111.1 1.9 %collective-permute-start.11 = (bf16[12,72,128]{2,1,0:T(8,128)(2,1)S(1)}, bf16[12,72,128]{2,1,0:T(8,128)(2,1)S(1)}, u32[]{:S(2)}, u32[]{:S(2)}) collective-permute-start(bf16[12,72,128]{2,1,0:T(8,128)(2,1)S(1)} %get-tuple-element.22), channel_id=1, source_target_pairs={{0,32},{2,34},{4,36},{6,38},{512,544},{514,546},{516,548},{518,550... | collective-permute-start | bytes 663560 | tf_op jit(solution)/shard_map/ppermute | solution.py:239
  113.0 2.6 %collective-permute-done.10.rest_1_ = bf16[12,72,128]{2,1,0:T(8,128)(2,1)S(1)} collective-permute-done((bf16[12,72,128]{2,1,0:T(8,128)(2,1)S(1)}, bf16[12,72,128]{2,1,0:T(8,128)(2,1)S(1)}, u32[]{:S(2)}, u32[]{:S(2)}) %collective-permute-start.10) | collective-permute-done | bytes 221216 | tf_op jit(solution)/shard_map/ppermute | solution.py:239
  115.6 3.9 %collective-permute-done.11.rest_2_ = bf16[12,72,128]{2,1,0:T(8,128)(2,1)S(1)} collective-permute-done((bf16[12,72,128]{2,1,0:T(8,128)(2,1)S(1)}, bf16[12,72,128]{2,1,0:T(8,128)(2,1)S(1)}, u32[]{:S(2)}, u32[]{:S(2)}) %collective-permute-start.11) | collective-permute-done | bytes 221216 | tf_op jit(solution)/shard_map/ppermute | solution.py:239
  119.6 0.6 shard_map.73
  120.1 3.1 %collective-permute-start.12 = (bf16[10,72,128]{2,1,0:T(8,128)(2,1)S(1)}, bf16[10,72,128]{2,1,0:T(8,128)(2,1)S(1)}, u32[]{:S(2)}, u32[]{:S(2)}) collective-permute-start(bf16[10,72,128]{2,1,0:T(8,128)(2,1)S(1)} %get-tuple-element.24), channel_id=1, source_target_pairs={{32,0},{34,2},{36,4},{38,6},{544,512},{546,514},{548,516},{550,518... | collective-permute-start | bytes 552968 | tf_op jit(solution)/shard_map/ppermute | solution.py:239
  123.2 2.2 %collective-permute-start.13 = (bf16[10,72,128]{2,1,0:T(8,128)(2,1)S(1)}, bf16[10,72,128]{2,1,0:T(8,128)(2,1)S(1)}, u32[]{:S(2)}, u32[]{:S(2)}) collective-permute-start(bf16[10,72,128]{2,1,0:T(8,128)(2,1)S(1)} %get-tuple-element.25), channel_id=1, source_target_pairs={{0,32},{2,34},{4,36},{6,38},{512,544},{514,546},{516,548},{518,550... | collective-permute-start | bytes 552968 | tf_op jit(solution)/shard_map/ppermute | solution.py:239
  125.4 2.1 %collective-permute-done.12.rest_1_ = bf16[10,72,128]{2,1,0:T(8,128)(2,1)S(1)} collective-permute-done((bf16[10,72,128]{2,1,0:T(8,128)(2,1)S(1)}, bf16[10,72,128]{2,1,0:T(8,128)(2,1)S(1)}, u32[]{:S(2)}, u32[]{:S(2)}) %collective-permute-start.12) | collective-permute-done | bytes 184352 | tf_op jit(solution)/shard_map/ppermute | solution.py:239
  127.6 3.7 %collective-permute-done.13.rest_2_ = bf16[10,72,128]{2,1,0:T(8,128)(2,1)S(1)} collective-permute-done((bf16[10,72,128]{2,1,0:T(8,128)(2,1)S(1)}, bf16[10,72,128]{2,1,0:T(8,128)(2,1)S(1)}, u32[]{:S(2)}, u32[]{:S(2)}) %collective-permute-start.13) | collective-permute-done | bytes 184352 | tf_op jit(solution)/shard_map/ppermute | solution.py:239
  131.3 0.5 shard_map.74
  131.8 3.0 %collective-permute-start.14 = (bf16[8,72,128]{2,1,0:T(8,128)(2,1)S(1)}, bf16[8,72,128]{2,1,0:T(8,128)(2,1)S(1)}, u32[]{:S(2)}, u32[]{:S(2)}) collective-permute-start(bf16[8,72,128]{2,1,0:T(8,128)(2,1)S(1)} %get-tuple-element.27), channel_id=1, source_target_pairs={{32,0},{34,2},{36,4},{38,6},{544,512},{546,514},{548,516},{550,518... | collective-permute-start | bytes 442376 | tf_op jit(solution)/shard_map/ppermute | solution.py:239
  134.9 2.3 %collective-permute-start.15 = (bf16[8,72,128]{2,1,0:T(8,128)(2,1)S(1)}, bf16[8,72,128]{2,1,0:T(8,128)(2,1)S(1)}, u32[]{:S(2)}, u32[]{:S(2)}) collective-permute-start(bf16[8,72,128]{2,1,0:T(8,128)(2,1)S(1)} %get-tuple-element.28), channel_id=1, source_target_pairs={{0,32},{2,34},{4,36},{6,38},{512,544},{514,546},{516,548},{518,550... | collective-permute-start | bytes 442376 | tf_op jit(solution)/shard_map/ppermute | solution.py:239
  137.1 0.6 collective-permute-done.14
  137.7 4.8 %collective-permute-done.15 = bf16[8,72,128]{2,1,0:T(8,128)(2,1)S(1)} collective-permute-done((bf16[8,72,128]{2,1,0:T(8,128)(2,1)S(1)}, bf16[8,72,128]{2,1,0:T(8,128)(2,1)S(1)}, u32[]{:S(2)}, u32[]{:S(2)}) %collective-permute-start.15) | collective-permute-done | bytes 147488 | tf_op jit(solution)/shard_map/ppermute | solution.py:239
  142.6 1.9 %all-gather.1 = bf16[8,1,72,128]{3,2,1,0:T(8,128)(2,1)S(1)} all-gather(bf16[4,1,72,128]{3,2,1,0:T(8,128)(2,1)S(1)} %bitcast_select_fusion), channel_id=3, replica_groups={{0,1},{2,3},{4,5},{6,7},{8,9},{10,11},{12,13},{14,15},{16,17},{18,19},{..., dimensions={0}, use_global_device_ids=true | all-gather | bytes 221184 | tf_op jit(solution)/shard_map/all_gather | solution.py:266
  144.6 11.6 %all_to_all.10 = bf16[8,72,128]{2,1,0:T(8,128)(2,1)S(1)} all-to-all(bf16[8,72,128]{2,1,0:T(8,128)(2,1)S(1)} %pad_maximum_fusion.11), channel_id=1, replica_groups={{0,2,4,6,512,514,516,518},{1,3,5,7,513,515,517,519},{8,10,12,14,520,522..., dimensions={0} | all-to-all | bytes 294912 | tf_op jit(solution)/shard_map/all_to_all | solution.py:260
  156.2 0.7 copy.24
  (66 shorter events, 0.9 us)
Async XLA Ops:
  1.8 18.4 %all-to-all-start = ((bf16[8,192,128]{2,1,0:T(8,128)(2,1)}), bf16[8,192,128]{2,1,0:T(8,128)(2,1)S(1)}, u32[]{:S(2)}, u32[]{:S(2)}) async-start(bf16[8,192,128]{2,1,0:T(8,128)(2,1)} %shard_map.64), calls=%async_computation | async-start | bytes 786432 | tf_op jit(solution)/shard_map/all_to_all | solution.py:260
  33.0 28.0 %copy-start = (bf16[16,160,128]{2,1,0:T(8,128)(2,1)S(1)}, bf16[16,160,128]{2,1,0:T(8,128)(2,1)}, u32[]{:S(2)}) copy-start(bf16[16,160,128]{2,1,0:T(8,128)(2,1)} %table.4) | copy-start | bytes 1966084
  33.2 10.4 %collective-permute-start.1 = (bf16[4,152,128]{2,1,0:T(8,128)(2,1)S(1)}, bf16[4,152,128]{2,1,0:T(8,128)(2,1)S(1)}, u32[]{:S(2)}, u32[]{:S(2)}) collective-permute-start(bf16[4,152,128]{2,1,0:T(8,128)(2,1)S(1)} %bitcast.54), channel_id=1, source_target_pairs={{0,24},{2,26},{4,28},{6,30},{512,536},{514,538},{516,540},{518,542... | collective-permute-start | bytes 466952 | tf_op jit(solution)/shard_map/ppermute | solution.py:239
  35.2 8.3 %collective-permute-start = (bf16[4,152,128]{2,1,0:T(8,128)(2,1)S(1)}, bf16[4,152,128]{2,1,0:T(8,128)(2,1)S(1)}, u32[]{:S(2)}, u32[]{:S(2)}) collective-permute-start(bf16[4,152,128]{2,1,0:T(8,128)(2,1)S(1)} %bitcast.55), channel_id=1, source_target_pairs={{0,8},{2,10},{4,12},{6,14},{512,520},{514,522},{516,524},{518,526}... | collective-permute-start | bytes 466952 | tf_op jit(solution)/shard_map/ppermute | solution.py:239
  43.7 19.2 %collective-permute-start.3 = (bf16[17,72,128]{2,1,0:T(8,128)(2,1)S(1)}, bf16[17,72,128]{2,1,0:T(8,128)(2,1)S(1)}, u32[]{:S(2)}, u32[]{:S(2)}) collective-permute-start(bf16[17,72,128]{2,1,0:T(8,128)(2,1)S(1)} %pad_maximum_fusion.6), channel_id=1, source_target_pairs={{32,0},{34,2},{36,4},{38,6},{544,512},{546,514},{548,516},{550,518... | collective-permute-start | bytes 940040 | tf_op jit(solution)/shard_map/ppermute | solution.py:239
  59.0 9.5 %collective-permute-start.2 = (bf16[17,72,128]{2,1,0:T(8,128)(2,1)S(1)}, bf16[17,72,128]{2,1,0:T(8,128)(2,1)S(1)}, u32[]{:S(2)}, u32[]{:S(2)}) collective-permute-start(bf16[17,72,128]{2,1,0:T(8,128)(2,1)S(1)} %pad_maximum_fusion.6), channel_id=1, source_target_pairs={{0,32},{2,34},{4,36},{6,38},{512,544},{514,546},{516,548},{518,550... | collective-permute-start | bytes 940040 | tf_op jit(solution)/shard_map/ppermute | solution.py:239
  62.9 24.7 %copy-start.3 = (bf16[17,72,128]{2,1,0:T(8,128)(2,1)}, bf16[17,72,128]{2,1,0:T(8,128)(2,1)S(1)}, u32[]{:S(2)}) copy-start(bf16[17,72,128]{2,1,0:T(8,128)(2,1)S(1)} %collective-permute-done.3.south) | copy-start | bytes 940036
  68.5 19.1 %copy-start.4 = (bf16[17,72,128]{2,1,0:T(8,128)(2,1)}, bf16[17,72,128]{2,1,0:T(8,128)(2,1)S(1)}, u32[]{:S(2)}) copy-start(bf16[17,72,128]{2,1,0:T(8,128)(2,1)S(1)} %collective-permute-done.2.north) | copy-start | bytes 940036
  69.2 10.4 %collective-permute-start.5 = (bf16[17,72,128]{2,1,0:T(8,128)(2,1)S(1)}, bf16[17,72,128]{2,1,0:T(8,128)(2,1)S(1)}, u32[]{:S(2)}, u32[]{:S(2)}) collective-permute-start(bf16[17,72,128]{2,1,0:T(8,128)(2,1)S(1)} %pad_maximum_fusion.7), channel_id=1, source_target_pairs={{32,0},{34,2},{36,4},{38,6},{544,512},{546,514},{548,516},{550,518... | collective-permute-start | bytes 940040 | tf_op jit(solution)/shard_map/ppermute | solution.py:239
  72.2 9.5 %collective-permute-start.4 = (bf16[17,72,128]{2,1,0:T(8,128)(2,1)S(1)}, bf16[17,72,128]{2,1,0:T(8,128)(2,1)S(1)}, u32[]{:S(2)}, u32[]{:S(2)}) collective-permute-start(bf16[17,72,128]{2,1,0:T(8,128)(2,1)S(1)} %pad_maximum_fusion.7), channel_id=1, source_target_pairs={{0,32},{2,34},{4,36},{6,38},{512,544},{514,546},{516,548},{518,550... | collective-permute-start | bytes 940040 | tf_op jit(solution)/shard_map/ppermute | solution.py:239
  79.6 14.9 %copy-start.1 = (bf16[17,72,128]{2,1,0:T(8,128)(2,1)}, bf16[17,72,128]{2,1,0:T(8,128)(2,1)S(1)}, u32[]{:S(2)}) copy-start(bf16[17,72,128]{2,1,0:T(8,128)(2,1)S(1)} %collective-permute-done.5.south) | copy-start | bytes 940036
  81.6 12.9 %copy-start.2 = (bf16[17,72,128]{2,1,0:T(8,128)(2,1)}, bf16[17,72,128]{2,1,0:T(8,128)(2,1)S(1)}, u32[]{:S(2)}) copy-start(bf16[17,72,128]{2,1,0:T(8,128)(2,1)S(1)} %collective-permute-done.4.north) | copy-start | bytes 940036
  82.3 7.9 %collective-permute-start.7 = (bf16[18,72,128]{2,1,0:T(8,128)(2,1)S(1)}, bf16[18,72,128]{2,1,0:T(8,128)(2,1)S(1)}, u32[]{:S(2)}, u32[]{:S(2)}) collective-permute-start(bf16[18,72,128]{2,1,0:T(8,128)(2,1)S(1)} %pad_maximum_fusion.5), channel_id=1, source_target_pairs={{32,0},{34,2},{36,4},{38,6},{544,512},{546,514},{548,516},{550,518... | collective-permute-start | bytes 995336 | tf_op jit(solution)/shard_map/ppermute | solution.py:239
  84.2 9.6 %collective-permute-start.6 = (bf16[18,72,128]{2,1,0:T(8,128)(2,1)S(1)}, bf16[18,72,128]{2,1,0:T(8,128)(2,1)S(1)}, u32[]{:S(2)}, u32[]{:S(2)}) collective-permute-start(bf16[18,72,128]{2,1,0:T(8,128)(2,1)S(1)} %pad_maximum_fusion.5), channel_id=1, source_target_pairs={{0,32},{2,34},{4,36},{6,38},{512,544},{514,546},{516,548},{518,550... | collective-permute-start | bytes 995336 | tf_op jit(solution)/shard_map/ppermute | solution.py:239
  94.8 6.7 %slice-start = ((bf16[17,72,128]{2,1,0:T(8,128)(2,1)}), bf16[6,72,128]{2,1,0:T(8,128)(2,1)S(1)}, s32[]{:S(2)}) async-start(bf16[17,72,128]{2,1,0:T(8,128)(2,1)} %copy-done.1), calls=%async_computation.2 | async-start | bytes 221184 | tf_op jit(solution)/shard_map/slice | solution.py:307
  94.8 6.7 %slice-start.2 = ((bf16[17,72,128]{2,1,0:T(8,128)(2,1)}), bf16[4,72,128]{2,1,0:T(8,128)(2,1)S(1)}, s32[]{:S(2)}) async-start(bf16[17,72,128]{2,1,0:T(8,128)(2,1)} %copy-done.3), calls=%async_computation.4 | async-start | bytes 147456 | tf_op jit(solution)/shard_map/slice | solution.py:307
  94.8 6.8 %collective-permute-start.9 = (bf16[5,72,128]{2,1,0:T(8,128)(2,1)S(1)}, bf16[5,72,128]{2,1,0:T(8,128)(2,1)S(1)}, u32[]{:S(2)}, u32[]{:S(2)}) collective-permute-start(bf16[5,72,128]{2,1,0:T(8,128)(2,1)S(1)} %get-tuple-element.35), channel_id=1, source_target_pairs={{0,24},{2,26},{4,28},{6,30},{512,536},{514,538},{516,540},{518,542... | collective-permute-start | bytes 276488 | tf_op jit(solution)/shard_map/ppermute | solution.py:239
  96.8 6.5 %collective-permute-start.8 = (bf16[5,72,128]{2,1,0:T(8,128)(2,1)S(1)}, bf16[5,72,128]{2,1,0:T(8,128)(2,1)S(1)}, u32[]{:S(2)}, u32[]{:S(2)}) collective-permute-start(bf16[5,72,128]{2,1,0:T(8,128)(2,1)S(1)} %get-tuple-element.36), channel_id=1, source_target_pairs={{0,8},{2,10},{4,12},{6,14},{512,520},{514,522},{516,524},{518,526}... | collective-permute-start | bytes 276488 | tf_op jit(solution)/shard_map/ppermute | solution.py:239
  100.6 1.0 slice-start.1
  100.6 1.0 slice-start.3
  107.1 8.5 %collective-permute-start.10 = (bf16[12,72,128]{2,1,0:T(8,128)(2,1)S(1)}, bf16[12,72,128]{2,1,0:T(8,128)(2,1)S(1)}, u32[]{:S(2)}, u32[]{:S(2)}) collective-permute-start(bf16[12,72,128]{2,1,0:T(8,128)(2,1)S(1)} %get-tuple-element.21), channel_id=1, source_target_pairs={{32,0},{34,2},{36,4},{38,6},{544,512},{546,514},{548,516},{550,518... | collective-permute-start | bytes 663560 | tf_op jit(solution)/shard_map/ppermute | solution.py:239
  111.1 8.5 %collective-permute-start.11 = (bf16[12,72,128]{2,1,0:T(8,128)(2,1)S(1)}, bf16[12,72,128]{2,1,0:T(8,128)(2,1)S(1)}, u32[]{:S(2)}, u32[]{:S(2)}) collective-permute-start(bf16[12,72,128]{2,1,0:T(8,128)(2,1)S(1)} %get-tuple-element.22), channel_id=1, source_target_pairs={{0,32},{2,34},{4,36},{6,38},{512,544},{514,546},{516,548},{518,550... | collective-permute-start | bytes 663560 | tf_op jit(solution)/shard_map/ppermute | solution.py:239
  120.1 7.4 %collective-permute-start.12 = (bf16[10,72,128]{2,1,0:T(8,128)(2,1)S(1)}, bf16[10,72,128]{2,1,0:T(8,128)(2,1)S(1)}, u32[]{:S(2)}, u32[]{:S(2)}) collective-permute-start(bf16[10,72,128]{2,1,0:T(8,128)(2,1)S(1)} %get-tuple-element.24), channel_id=1, source_target_pairs={{32,0},{34,2},{36,4},{38,6},{544,512},{546,514},{548,516},{550,518... | collective-permute-start | bytes 552968 | tf_op jit(solution)/shard_map/ppermute | solution.py:239
  123.2 8.1 %collective-permute-start.13 = (bf16[10,72,128]{2,1,0:T(8,128)(2,1)S(1)}, bf16[10,72,128]{2,1,0:T(8,128)(2,1)S(1)}, u32[]{:S(2)}, u32[]{:S(2)}) collective-permute-start(bf16[10,72,128]{2,1,0:T(8,128)(2,1)S(1)} %get-tuple-element.25), channel_id=1, source_target_pairs={{0,32},{2,34},{4,36},{6,38},{512,544},{514,546},{516,548},{518,550... | collective-permute-start | bytes 552968 | tf_op jit(solution)/shard_map/ppermute | solution.py:239
  131.8 5.9 %collective-permute-start.14 = (bf16[8,72,128]{2,1,0:T(8,128)(2,1)S(1)}, bf16[8,72,128]{2,1,0:T(8,128)(2,1)S(1)}, u32[]{:S(2)}, u32[]{:S(2)}) collective-permute-start(bf16[8,72,128]{2,1,0:T(8,128)(2,1)S(1)} %get-tuple-element.27), channel_id=1, source_target_pairs={{32,0},{34,2},{36,4},{38,6},{544,512},{546,514},{548,516},{550,518... | collective-permute-start | bytes 442376 | tf_op jit(solution)/shard_map/ppermute | solution.py:239
  134.9 7.7 %collective-permute-start.15 = (bf16[8,72,128]{2,1,0:T(8,128)(2,1)S(1)}, bf16[8,72,128]{2,1,0:T(8,128)(2,1)S(1)}, u32[]{:S(2)}, u32[]{:S(2)}) collective-permute-start(bf16[8,72,128]{2,1,0:T(8,128)(2,1)S(1)} %get-tuple-element.28), channel_id=1, source_target_pairs={{0,32},{2,34},{4,36},{6,38},{512,544},{514,546},{516,548},{518,550... | collective-permute-start | bytes 442376 | tf_op jit(solution)/shard_map/ppermute | solution.py:239
